TPU v7x, 256 devices: a whole 4x4x8 slice. The times are simulated.
256 devices in a mesh: ta: 2 (over x_lo), ha: 4 (over x_hi, core), wa: 32 (over z, y).
Axes of the slice: x: 4 (x_hi: 2, x_lo: 2; x = x_hi * 2 + x_lo), y: 4, z: 8, core: 2. Of those that a mesh axis runs over, the one named last changes fastest.
Arguments:
- queries: bfloat16 [32, 2, 4, 192, 1536], P('wa', 'ta', 'ha'), may hold values from -5 to 5
- keys_values: bfloat16 [2, 32, 2, 4, 192, 1536], P(None, 'wa', 'ta', 'ha'), may hold values from -5 to 5
- upstream: bfloat16 [32, 2, 4, 192, 1536], P('wa', 'ta', 'ha'), may hold values from -1.5 to 1.5
- out_weight: bfloat16 [32, 1536, 1536], P(None, 'wa'), may hold values from -1.25 to 1.25
- block_pick: int32 [1], replicated, may hold values from 0 to 31
Outputs:
- mixed: bfloat16 [32, 2, 4, 192, 1536], P('wa', 'ta', 'ha')
- grad_queries: bfloat16 [32, 2, 4, 192, 1536], P('wa', 'ta', 'ha')
- grad_keys_values: bfloat16 [2, 32, 2, 4, 192, 1536], P(None, 'wa', 'ta', 'ha')
- grad_weight: float32 [1536, 1536], P('wa')
All inputs are finite; a program needn't handle non-finite values.
Results may differ from a plain program's by a relative error of at most 0.029.
Values may be sent and summed in bfloat16 or wider, within the bound.
No kernel may reach another device: no remote copies, remote signals or barrier semaphores. Data moves between devices by JAX's collectives and lax.ppermute only.
A program may use at most 128 MiB of HBM per device.

v0:
```python
import jax
import jax.numpy as jnp
from jax import lax
from jax.sharding import PartitionSpec as P

HEADS = 12
HEAD_DIM = 128


def padded_2(block, sides, width):
    for axis, dim in sides:
        count = lax.axis_size(axis)
        forward = [(i, i + 1) for i in range(count - 1)]
        backward = [(target, source) for source, target in forward]
        low = lax.ppermute(
            lax.slice_in_dim(block, block.shape[dim] - width, None, axis=dim), axis, forward
        )
        high = lax.ppermute(lax.slice_in_dim(block, 0, width, axis=dim), axis, backward)
        block = jnp.concatenate([low, block, high], axis=dim)
    return block


def from_behind(x, axis, by):
    count = lax.axis_size(axis)
    pairs = [(i, i + by) for i in range(count) if 0 <= i + by < count]
    return lax.ppermute(x, axis, pairs)


def attend_forward(queries, keys, values, live):
    scale = HEAD_DIM ** (-0.5)
    scores = jnp.einsum("qhd,khd->hqk", queries, keys, preferred_element_type=jnp.float32) * scale
    scores = jnp.where(live[None, None, :], scores, -jnp.inf)
    top = jnp.max(scores, axis=-1, keepdims=True)
    weights = jnp.exp(scores - top)
    probs = weights / jnp.sum(weights, axis=-1, keepdims=True)
    probs_b = probs.astype(jnp.bfloat16)
    attention = jnp.einsum("hqk,khd->qhd", probs_b, values, preferred_element_type=jnp.float32)
    return (probs, probs_b, attention.astype(jnp.bfloat16))


def per_device(queries, keys_values, upstream, out_weight, block_pick):
    samples = queries.shape[0]
    tile = queries.shape[3]
    width = queries.shape[4]
    dout = upstream.shape[4]
    here_t = lax.axis_index("ta")
    here_h = lax.axis_index("ha")
    slots_live = jnp.stack(
        [
            here_t >= 0,
            here_t > 0,
            here_t < lax.axis_size("ta") - 1,
            here_h > 0,
            here_h < lax.axis_size("ha") - 1,
        ]
    )
    live = jnp.repeat(slots_live, tile)
    padded = padded_2(keys_values, (("ta", 2), ("ha", 3)), 1)
    parts = [
        padded[:, :, 1, 1],
        padded[:, :, 0, 1],
        padded[:, :, 2, 1],
        padded[:, :, 1, 0],
        padded[:, :, 1, 2],
    ]
    window = jnp.concatenate(parts, axis=2)
    keys = window[0].reshape(samples, 5 * tile, HEADS, HEAD_DIM)
    values = window[1].reshape(samples, 5 * tile, HEADS, HEAD_DIM)
    heads_q = queries.reshape(samples, tile, HEADS, HEAD_DIM)

    def forward_only(triple):
        return attend_forward(triple[0], triple[1], triple[2], live)[2]

    def backward_tile(quad):
        tile_q, tile_k, tile_v, d_att = quad
        scale = HEAD_DIM ** (-0.5)
        probs, probs_b, attention = attend_forward(tile_q, tile_k, tile_v, live)
        delta = jnp.sum(d_att.astype(jnp.float32) * attention.astype(jnp.float32), axis=-1)
        delta = jnp.swapaxes(delta, 0, 1)[..., None]
        d_probs = jnp.einsum("qhd,khd->hqk", d_att, tile_v, preferred_element_type=jnp.float32)
        d_scores = (probs * (d_probs - delta)).astype(jnp.bfloat16)
        grad_q = (
            jnp.einsum("hqk,khd->qhd", d_scores, tile_k, preferred_element_type=jnp.float32) * scale
        )
        key_terms = (
            jnp.einsum("hqk,qhd->khd", d_scores, tile_q, preferred_element_type=jnp.float32) * scale
        )
        value_terms = jnp.einsum("hqk,qhd->khd", probs_b, d_att, preferred_element_type=jnp.float32)
        terms = jnp.stack([key_terms, value_terms]).reshape((2, 5 * tile, width))
        own_terms = terms[:, :tile]
        sent_terms = terms[:, tile:].astype(jnp.bfloat16).reshape(2, 4, tile, width)
        return (grad_q.astype(jnp.bfloat16), own_terms, sent_terms)

    attention = lax.map(forward_only, (heads_q, keys, values))
    flat = attention.reshape(samples * tile, width)
    up_flat = upstream.reshape(samples * tile, dout)
    panel = lax.dynamic_index_in_dim(out_weight, block_pick[0], 0, keepdims=False)
    full = lax.all_gather(panel, "wa", axis=0, tiled=True)
    mixed = jnp.dot(flat, full, preferred_element_type=jnp.float32).astype(jnp.bfloat16)
    d_attention = lax.dot_general(
        up_flat, full, (((1,), (1,)), ((), ())), preferred_element_type=jnp.float32
    ).astype(jnp.bfloat16)
    d_heads = d_attention.reshape(samples, tile, HEADS, HEAD_DIM)
    grad_q, own_terms, sent_terms = lax.map(backward_tile, (heads_q, keys, values, d_heads))
    total = jnp.moveaxis(own_terms, 0, 1)
    sent_terms = jnp.moveaxis(sent_terms, 0, 1)
    for offset, slot in ((-1, 0), (1, 1)):
        total = total + from_behind(sent_terms[:, :, slot], "ta", offset).astype(jnp.float32)
    for offset, slot in ((-1, 2), (1, 3)):
        total = total + from_behind(sent_terms[:, :, slot], "ha", offset).astype(jnp.float32)
    grad_keys_values = total.astype(jnp.bfloat16).reshape(keys_values.shape)
    block_sum = lax.psum_scatter(
        lax.dot_general(
            flat, up_flat, (((0,), (0,)), ((), ())), preferred_element_type=jnp.float32
        ).astype(jnp.bfloat16),
        "wa",
        scatter_dimension=0,
        tiled=True,
    )
    grad_weight = lax.psum(block_sum, ("ta", "ha")).astype(jnp.float32)
    return (
        mixed.reshape(upstream.shape),
        grad_q.reshape(queries.shape),
        grad_keys_values,
        grad_weight,
    )


def solution(mesh):
    return jax.shard_map(
        per_device,
        mesh=mesh,
        in_specs=(
            P("wa", "ta", "ha", None, None),
            P(None, "wa", "ta", "ha", None, None),
            P("wa", "ta", "ha", None, None),
            P(None, "wa", None),
            P(),
        ),
        out_specs=(
            P("wa", "ta", "ha", None, None),
            P("wa", "ta", "ha", None, None),
            P(None, "wa", "ta", "ha", None, None),
            P("wa", None),
        ),
        check_vma=False,
    )
```

profile of v0, /device:TPU:1, one launch (start us, length us, event | category | flops | bytes accessed | tf_op | source)
XLA Modules:
  0.0 432.7 jit_solution(8942150616990557122)
XLA Ops:
  10.9 4.1 collective-permute-start
  15.0 21.0 %collective-permute-done.1 = bf16[2,1,1,1,192,1536]{5,4,0,3,2,1:T(8,128)(2,1)S(1)} collective-permute-done((bf16[2,1,1,1,192,1536]{5,4,0,3,2,1:T(8,128)(2,1)}, bf16[2,1,1,1,192,1536]{5,4,0,3,2,1:T(8,128)(2,1)S(1)}, u32[]{:S(2)}, u32[]{:S(2)}) %collective-permute-start.1) | collective-permute-done | bytes 1179680 | tf_op jit(solution)/shard_map/ppermute | solution.py:18
  41.0 4.4 %copy.68 = bf16[2,1,3,1,192,1536]{5,4,0,3,2,1:T(8,128)(2,1)} copy(bf16[2,1,3,1,192,1536]{5,4,3,2,1,0:T(8,128)(2,1)} %pad_maximum_fusion.1) | data formatting | bytes 7077888 | tf_op jit(solution)/shard_map/concatenate | solution.py:19
  45.5 9.8 %collective-permute-start.2 = (bf16[2,1,3,1,192,1536]{5,4,0,3,2,1:T(8,128)(2,1)}, bf16[2,1,3,1,192,1536]{5,4,0,3,2,1:T(8,128)(2,1)}, u32[]{:S(2)}, u32[]{:S(2)}) collective-permute-start(bf16[2,1,3,1,192,1536]{5,4,0,3,2,1:T(8,128)(2,1)} %copy.68), channel_id=1, source_target_pairs={{0,32},{32,64},{64,96},{1,33},{33,65},{65,97},{2,34},{34,66},{66,9... | collective-permute-start | bytes 10616840 | tf_op jit(solution)/shard_map/ppermute | solution.py:15
  60.3 33.7 %collective-permute-done.2 = bf16[2,1,3,1,192,1536]{5,4,0,3,2,1:T(8,128)(2,1)} collective-permute-done((bf16[2,1,3,1,192,1536]{5,4,0,3,2,1:T(8,128)(2,1)}, bf16[2,1,3,1,192,1536]{5,4,0,3,2,1:T(8,128)(2,1)}, u32[]{:S(2)}, u32[]{:S(2)}) %collective-permute-start.2) | collective-permute-done | bytes 3538976 | tf_op jit(solution)/shard_map/ppermute | solution.py:15
  95.3 4.6 %collective-permute-done.3 = bf16[2,1,3,1,192,1536]{5,4,3,2,1,0:T(8,128)(2,1)} collective-permute-done((bf16[2,1,3,1,192,1536]{5,4,3,2,1,0:T(8,128)(2,1)}, bf16[2,1,3,1,192,1536]{5,4,3,2,1,0:T(8,128)(2,1)}, u32[]{:S(2)}, u32[]{:S(2)}) %collective-permute-start.3) | collective-permute-done | bytes 3538976 | tf_op jit(solution)/shard_map/ppermute | solution.py:18
  103.2 4.6 %copy.70 = bf16[1,1,960,1536]{2,3,1,0:T(8,128)(2,1)} copy(bf16[1,1,960,1536]{3,2,0,1:T(8,128)(2,1)} %get-tuple-element.61) | data formatting | bytes 5898240 | tf_op jit(solution)/shard_map/slice | solution.py:67
  110.8 9.0 %fusion.61 = (f32[12,192]{1,0:T(8,128)S(1)}, f32[12,192,960]{2,1,0:T(8,128)}) fusion(pred[960]{0:T(1024)(128)(4,1)S(1)} %broadcast_in_dim.53, bf16[960,12,128]{0,2,1:T(8,128)(2,1)} %bitcast.143, bf16[192,12,128]{2,1,0:T(8,128)(2,1)} %squeeze.65), kind=kOutput, calls=%fused_computation.71 | convolution fusion | flops 575079360 | bytes 12396480 | tf_op jit(solution)/shard_map/while/body/eval_jaxpr/sub | solution.py:34
  119.8 7.0 %fusion.13 = bf16[12,192,960]{2,1,0:T(8,128)(2,1)} fusion(f32[12,192,960]{2,1,0:T(8,128)} %get-tuple-element.68, f32[12,192]{1,0:T(8,128)S(1)} %get-tuple-element.67), kind=kLoop, calls=%fused_computation.21 | loop fusion | flops 4423680 | bytes 13280256 | tf_op jit(solution)/shard_map/while/body/eval_jaxpr/convert_element_type | solution.py:36
  126.8 4.2 fusion.32
  134.4 3.6 convolution_convert_fusion
  138.3 5.7 %multiply_convert_fusion = bf16[12,192,960]{2,1,0:T(8,128)(2,1)S(1)} fusion(f32[12,192]{1,0:T(8,128)S(1)} %bitcast.147, f32[12,192,960]{2,1,0:T(8,128)} %get-tuple-element.68, f32[12,192]{1,0:T(8,128)S(1)} %get-tuple-element.67, bf16[960,12,128]{0,2,1:T(8,128)(2,1)} %bitcast.146, bf16[24,12,8,128]{3,2,1,0:T(8,128)(2,1)S(1)} %fusion.32), kind=kOutput, calls=%fused_computation.9 | convolution fusion | flops 575078400 | bytes 16828416 | tf_op jit(solution)/shard_map/while/body/eval_jaxpr/qhd,khd->hqk/dot_general | solution.py:80
  146.3 4.5 %multiply_bitcast_fusion = f32[960,12,128]{2,0,1:T(8,128)} fusion(bf16[12,192,960]{2,1,0:T(8,128)(2,1)S(1)} %multiply_convert_fusion, bf16[192,12,128]{2,1,0:T(8,128)(2,1)S(1)} %copy-done.7), kind=kOutput, calls=%fused_computation.12 | convolution fusion | flops 567705600 | bytes 10911744 | tf_op jit(solution)/shard_map/while/body/eval_jaxpr/hqk,qhd->khd/dot_general | solution.py:86
  150.8 6.6 %copy.81 = f32[960,12,128]{0,2,1:T(8,128)} copy(f32[960,12,128]{2,0,1:T(8,128)} %multiply_bitcast_fusion) | data formatting | bytes 11796480 | tf_op jit(solution)/shard_map/while/body/eval_jaxpr/mul | solution.py:86
  157.4 6.6 %copy.84 = f32[1,960,1536]{2,1,0:T(8,128)} copy(f32[1,960,1536]{1,2,0:T(8,128)} %bitcast.136) | data formatting | bytes 11796480 | tf_op jit(solution)/shard_map/while/body/eval_jaxpr/stack | solution.py:89
  164.0 6.8 %convolution_bitcast_fusion = f32[960,12,128]{2,0,1:T(8,128)} fusion(bf16[12,192,960]{2,1,0:T(8,128)(2,1)} %fusion.13, bf16[24,12,8,128]{3,2,1,0:T(8,128)(2,1)S(1)} %fusion.32), kind=kOutput, calls=%fused_computation.23 | convolution fusion | flops 566231040 | bytes 10911744 | tf_op jit(solution)/shard_map/while/body/eval_jaxpr/hqk,qhd->khd/dot_general | solution.py:88
  170.8 6.5 %copy.83 = f32[960,12,128]{0,2,1:T(8,128)} copy(f32[960,12,128]{2,0,1:T(8,128)} %convolution_bitcast_fusion) | data formatting | bytes 11796480 | tf_op jit(solution)/shard_map/while/body/eval_jaxpr/hqk,qhd->khd/transpose | solution.py:88
  177.3 6.6 %copy.85 = f32[1,960,1536]{2,1,0:T(8,128)} copy(f32[1,960,1536]{1,2,0:T(8,128)} %bitcast.137) | data formatting | bytes 11796480 | tf_op jit(solution)/shard_map/while/body/eval_jaxpr/stack | solution.py:89
  183.9 4.6 %fusion.1 = bf16[2,768,1536]{2,1,0:T(8,128)(2,1)S(1)} fusion(f32[1,960,1536]{2,1,0:T(8,128)} %copy.85, f32[1,960,1536]{2,1,0:T(8,128)} %copy.84), kind=kLoop, calls=%fused_computation.4 | loop fusion | flops 9437184 | bytes 16515072 | tf_op jit(solution)/shard_map/convert
  197.7 5.1 %collective-permute-start.5 = (bf16[2,1,192,1536]{3,2,1,0:T(8,128)(2,1)}, bf16[2,1,192,1536]{3,2,1,0:T(8,128)(2,1)}, u32[]{:S(2)}, u32[]{:S(2)}) collective-permute-start(bf16[2,1,192,1536]{3,2,1,0:T(8,128)(2,1)} %get-tuple-element.66), channel_id=1, source_target_pairs={{0,128},{1,129},{2,130},{3,131},{4,132},{5,133},{6,134},{7,135},{8... | collective-permute-start | bytes 3538952 | tf_op jit(solution)/shard_map/ppermute | solution.py:26
  205.9 4.3 fusion.20
  210.1 148.1 %reduce-scatter.2.cloned.1.call-done = bf16[48,1536]{1,0:T(8,128)(2,1)} async-done(((bf16[1536,1536]{1,0:T(8,128)(2,1)}), bf16[48,1536]{1,0:T(8,128)(2,1)}) %reduce-scatter.2.cloned.1.call-update) | async-done | bytes 147472 | tf_op jit(solution)/shard_map/reduce_scatter | solution.py:112
  358.3 4.5 %fusion.37 = bf16[2,1,1,1,192,1536]{5,4,3,2,1,0:T(8,128)(2,1)} fusion(bf16[2,1,192,1536]{3,2,1,0:T(8,128)(2,1)} %collective-permute-done.7, bf16[2,1,192,1536]{3,2,1,0:T(8,128)(2,1)} %collective-permute-done.6, bf16[2,1,192,1536]{3,2,1,0:T(8,128)(2,1)} %collective-permute-done.5, bf16[2,1,192,1536]{3,2,1,0:T(8,128)(2,1)S(1)} %collective-permute-done.4, ...), kind=kLoop, calls=%fused_computation.51 | loop fusion | flops 5898240 | bytes 17694720
  362.9 61.7 %all-reduce.2.cloned.1.call-done = bf16[48,1536]{1,0:T(8,128)(2,1)} async-done(((bf16[48,1536]{1,0:T(8,128)(2,1)}), bf16[48,1536]{1,0:T(8,128)(2,1)}) %all-reduce.2.cloned.1.call-update) | async-done | bytes 147472 | tf_op jit(solution)/shard_map/psum | solution.py:120
  (59 shorter events, 40.4 us)
Async XLA Ops:
  7.2 119.6 %copy-start = (bf16[1,1,1,192,1536]{4,3,2,1,0:T(8,128)(2,1)S(1)}, bf16[1,1,1,192,1536]{4,3,2,1,0:T(8,128)(2,1)}, u32[]{:S(2)}) copy-start(bf16[1,1,1,192,1536]{4,3,2,1,0:T(8,128)(2,1)} %param.7) | copy-start | bytes 1769476
  7.2 119.6 %all-gather.3.cloned.1.call-start = ((), (), s32[]{:S(2)}) async-start(), calls=%async_computation.3 | async-start | bytes 4866048 | tf_op jit(solution)/shard_map/all_gather | solution.py:98
  9.5 348.7 %reduce-scatter.2.cloned.1.call-start = ((), (), s32[]{:S(2)}) async-start(), calls=%async_computation.1 | async-start | bytes 4866048 | tf_op jit(solution)/shard_map/reduce_scatter | solution.py:112
  9.6 26.4 %collective-permute-start.1 = (bf16[2,1,1,1,192,1536]{5,4,0,3,2,1:T(8,128)(2,1)}, bf16[2,1,1,1,192,1536]{5,4,0,3,2,1:T(8,128)(2,1)S(1)}, u32[]{:S(2)}, u32[]{:S(2)}) collective-permute-start(bf16[2,1,1,1,192,1536]{5,4,0,3,2,1:T(8,128)(2,1)} %bitcast.139), channel_id=1, source_target_pairs={{128,0},{129,1},{130,2},{131,3},{132,4},{133,5},{134,6},{135,7},{1... | collective-permute-start | bytes 3538952 | tf_op jit(solution)/shard_map/ppermute | solution.py:18
  10.9 26.1 %collective-permute-start = (bf16[2,1,1,1,192,1536]{5,4,3,2,1,0:T(8,128)(2,1)}, bf16[2,1,1,1,192,1536]{5,4,3,2,1,0:T(8,128)(2,1)S(1)}, u32[]{:S(2)}, u32[]{:S(2)}) collective-permute-start(bf16[2,1,1,1,192,1536]{5,4,3,2,1,0:T(8,128)(2,1)} %param.6), channel_id=1, source_target_pairs={{0,128},{1,129},{2,130},{3,131},{4,132},{5,133},{6,134},{7,135},{8... | collective-permute-start | bytes 3538952 | tf_op jit(solution)/shard_map/ppermute | solution.py:15
  37.0 1.0 copy-start.4
  41.0 16.4 %copy-start.8 = (bf16[1,1,1,192,1536]{4,3,2,1,0:T(8,128)(2,1)S(1)}, bf16[1,1,1,192,1536]{4,3,2,1,0:T(8,128)(2,1)}, u32[]{:S(2)}) copy-start(bf16[1,1,1,192,1536]{4,3,2,1,0:T(8,128)(2,1)} %param.5) | copy-start | bytes 1769476
  41.0 17.7 %copy-start.3 = (bf16[2,1,1,1,192,1536]{5,4,3,2,1,0:T(8,128)(2,1)S(1)}, bf16[2,1,1,1,192,1536]{5,4,3,2,1,0:T(8,128)(2,1)}, u32[]{:S(2)}) copy-start(bf16[2,1,1,1,192,1536]{5,4,3,2,1,0:T(8,128)(2,1)} %param.6) | copy-start | bytes 3538948
  45.5 48.5 %collective-permute-start.2 = (bf16[2,1,3,1,192,1536]{5,4,0,3,2,1:T(8,128)(2,1)}, bf16[2,1,3,1,192,1536]{5,4,0,3,2,1:T(8,128)(2,1)}, u32[]{:S(2)}, u32[]{:S(2)}) collective-permute-start(bf16[2,1,3,1,192,1536]{5,4,0,3,2,1:T(8,128)(2,1)} %copy.68), channel_id=1, source_target_pairs={{0,32},{32,64},{64,96},{1,33},{33,65},{65,97},{2,34},{34,66},{66,9... | collective-permute-start | bytes 10616840 | tf_op jit(solution)/shard_map/ppermute | solution.py:15
  55.3 44.6 %collective-permute-start.3 = (bf16[2,1,3,1,192,1536]{5,4,3,2,1,0:T(8,128)(2,1)}, bf16[2,1,3,1,192,1536]{5,4,3,2,1,0:T(8,128)(2,1)}, u32[]{:S(2)}, u32[]{:S(2)}) collective-permute-start(bf16[2,1,3,1,192,1536]{5,4,3,2,1,0:T(8,128)(2,1)} %pad_maximum_fusion.1), channel_id=1, source_target_pairs={{32,0},{64,32},{96,64},{33,1},{65,33},{97,65},{34,2},{66,34},{98,6... | collective-permute-start | bytes 10616840 | tf_op jit(solution)/shard_map/ppermute | solution.py:18
  126.8 4.2 copy-start.2
  138.1 286.5 %all-reduce.2.cloned.1.call-start = ((), (), s32[]{:S(2)}) async-start(), calls=%async_computation.2 | async-start | bytes 294912 | tf_op jit(solution)/shard_map/psum | solution.py:120
  138.3 8.0 %copy-start.7 = (bf16[192,12,128]{2,1,0:T(8,128)(2,1)S(1)}, bf16[192,12,128]{2,1,0:T(8,128)(2,1)}, u32[]{:S(2)}) copy-start(bf16[192,12,128]{2,1,0:T(8,128)(2,1)} %squeeze.65) | copy-start | bytes 1769476
  144.1 2.2 copy-start.5
  177.3 25.5 %slice-start = ((s8[4718592]{0:T(1024)(128)(4,1)}), s8[524288]{0:T(1024)(128)(4,1)S(1)}, s32[]{:S(2)}) async-start(s8[4718592]{0:T(1024)(128)(4,1)} %bitcast.141), calls=%async_computation.4 | async-start | bytes 1048576
  183.9 18.9 %slice-start.1 = ((s8[4718592]{0:T(1024)(128)(4,1)}), s8[4194304]{0:T(1024)(128)(4,1)S(1)}, s32[]{:S(2)}) async-start(s8[4718592]{0:T(1024)(128)(4,1)} %bitcast.141), calls=%async_computation.5 | async-start | bytes 8388608
  188.5 14.3 %copy-start.6 = (bf16[1,1,960,1536]{2,3,1,0:T(8,128)(2,1)S(1)}, bf16[1,1,960,1536]{2,3,1,0:T(8,128)(2,1)}, u32[]{:S(2)}) copy-start(bf16[1,1,960,1536]{2,3,1,0:T(8,128)(2,1)} %copy.70) | copy-start | bytes 8847364
  191.0 167.3 %collective-permute-start.4 = (bf16[2,1,192,1536]{3,2,1,0:T(8,128)(2,1)}, bf16[2,1,192,1536]{3,2,1,0:T(8,128)(2,1)S(1)}, u32[]{:S(2)}, u32[]{:S(2)}) collective-permute-start(bf16[2,1,192,1536]{3,2,1,0:T(8,128)(2,1)} %get-tuple-element.63), channel_id=1, source_target_pairs={{128,0},{129,1},{130,2},{131,3},{132,4},{133,5},{134,6},{135,7},{1... | collective-permute-start | bytes 3538952 | tf_op jit(solution)/shard_map/ppermute | solution.py:26
  192.4 165.9 %collective-permute-start.7 = (bf16[2,1,192,1536]{3,2,1,0:T(8,128)(2,1)}, bf16[2,1,192,1536]{3,2,1,0:T(8,128)(2,1)}, u32[]{:S(2)}, u32[]{:S(2)}) collective-permute-start(bf16[2,1,192,1536]{3,2,1,0:T(8,128)(2,1)} %get-tuple-element.64), channel_id=1, source_target_pairs={{0,32},{32,64},{64,96},{1,33},{33,65},{65,97},{2,34},{34,66},{66,9... | collective-permute-start | bytes 3538952 | tf_op jit(solution)/shard_map/ppermute | solution.py:26
  194.3 164.0 %collective-permute-start.6 = (bf16[2,1,192,1536]{3,2,1,0:T(8,128)(2,1)}, bf16[2,1,192,1536]{3,2,1,0:T(8,128)(2,1)}, u32[]{:S(2)}, u32[]{:S(2)}) collective-permute-start(bf16[2,1,192,1536]{3,2,1,0:T(8,128)(2,1)} %get-tuple-element.65), channel_id=1, source_target_pairs={{32,0},{64,32},{96,64},{33,1},{65,33},{97,65},{34,2},{66,34},{98,6... | collective-permute-start | bytes 3538952 | tf_op jit(solution)/shard_map/ppermute | solution.py:26
  197.7 160.6 %collective-permute-start.5 = (bf16[2,1,192,1536]{3,2,1,0:T(8,128)(2,1)}, bf16[2,1,192,1536]{3,2,1,0:T(8,128)(2,1)}, u32[]{:S(2)}, u32[]{:S(2)}) collective-permute-start(bf16[2,1,192,1536]{3,2,1,0:T(8,128)(2,1)} %get-tuple-element.66), channel_id=1, source_target_pairs={{0,128},{1,129},{2,130},{3,131},{4,132},{5,133},{6,134},{7,135},{8... | collective-permute-start | bytes 3538952 | tf_op jit(solution)/shard_map/ppermute | solution.py:26
  358.3 67.9 %copy-start.1 = (bf16[1,1,1,192,1536]{4,3,2,1,0:T(8,128)(2,1)S(1)}, bf16[1,1,1,192,1536]{4,3,2,1,0:T(8,128)(2,1)}, u32[]{:S(2)}) copy-start(bf16[1,1,1,192,1536]{4,3,2,1,0:T(8,128)(2,1)} %param.7) | copy-start | bytes 1769476
Sparse Core Ops, SparseCore 0:
  11.2 84.6 all-gather.2
  138.2 220.0 reduce-scatter.1
  360.6 63.9 all-reduce.1
where the time goes:
time: 435 us; the launch traced here: 433 us
  waiting for transfers between devices  270 us (62%)
  local copies, waits for them, and re-layouts  55 us (13%)
  matrix products  43 us (10%)
  starting transfers between devices  29.3 us (7%)
  other arithmetic  20.7 us (5%)
  between operations  14.7 us (3%)
    reduce_scatter x1, waiting for transfers between devices, per_device(): lax.psum_scatter(lax.dot_general(flat, up_flat, (((0,), (0,)), ((), ())),...  148 us
    psum x1, waiting for transfers between devices, per_device(): grad_weight = lax.psum(block_sum, ('ta', 'ha')).astype(jnp.float32)  61.7 us
    ppermute x2, waiting for transfers between devices, padded_2(): lax.ppermute(lax.slice_in_dim(block, block.shape[dim] - width, None, axis...  34.6 us
    ppermute x2, waiting for transfers between devices, padded_2(): lax.ppermute(lax.slice_in_dim(block, 0, width, axis=dim), axis, backward)  25.5 us
    ppermute x2, starting transfers between devices, padded_2(): lax.ppermute(lax.slice_in_dim(block, block.shape[dim] - width, None, axis...  13.9 us
    another operation x2, local copies, waits for them, and re-layouts, backward_tile(): terms = jnp.stack([key_terms, value_terms]).reshape((2, 5 * tile, width))  13.2 us
    ppermute x4, starting transfers between devices, from_behind(): return lax.ppermute(x, axis, pairs)  11.8 us
    sub x1, matrix products, attend_forward(): weights = jnp.exp(scores - top)  9.05 us
  transfers between devices with their start and end apart: 11, of which 6 were waited for; matrix products, arithmetic and copies ran while one was open for 23% of the time, Pallas kernels for 0%

commit v1 on v0

v1 whole, which is shorter than its diff:
```python
import functools

import jax
import jax.numpy as jnp
from jax import lax
from jax.experimental import pallas as pl
from jax.experimental.pallas import tpu as pltpu
from jax.sharding import Mesh, PartitionSpec as P

HEADS = 12
HEAD_DIM = 128
SCALE = HEAD_DIM ** (-0.5)
TILE = 192
SLOTS = 4
PER_STEP = 2
NT = (((1,), (1,)), ((), ()))
TN = (((0,), (0,)), ((), ()))
F32 = jnp.float32
BF16 = jnp.bfloat16


def window_of(refs, which, cols):
    return jnp.concatenate([ref[which, :, cols] for ref in refs], axis=0)


def probs_of(q, k, bound):
    scores = lax.dot_general(q, k, NT, preferred_element_type=F32)
    column = lax.broadcasted_iota(jnp.int32, scores.shape, 1)
    scores = jnp.where(column < bound, scores, -1e30)
    top = jnp.max(scores, axis=1, keepdims=True)
    weights = jnp.exp((scores - top) * SCALE)
    return weights * (1.0 / jnp.sum(weights, axis=1, keepdims=True))


def forward_kernel(bound_ref, q_ref, own_ref, time_ref, core_ref, cross_ref, out_ref):
    kv = (own_ref, time_ref, core_ref, cross_ref)
    for h in range(PER_STEP):
        cols = slice(h * HEAD_DIM, (h + 1) * HEAD_DIM)
        k = window_of(kv, 0, cols)
        v = window_of(kv, 1, cols)
        probs = probs_of(q_ref[:, cols], k, bound_ref[0])
        out = jnp.dot(probs.astype(BF16), v, preferred_element_type=F32)
        out_ref[:, cols] = out.astype(BF16)


def backward_kernel(
    bound_ref, q_ref, own_ref, time_ref, core_ref, cross_ref, att_ref, d_ref,
    gq_ref, g_own_ref, g_time_ref, g_core_ref, g_cross_ref,
):
    kv = (own_ref, time_ref, core_ref, cross_ref)
    outs = (g_own_ref, g_time_ref, g_core_ref, g_cross_ref)
    for h in range(PER_STEP):
        cols = slice(h * HEAD_DIM, (h + 1) * HEAD_DIM)
        q = q_ref[:, cols]
        k = window_of(kv, 0, cols)
        v = window_of(kv, 1, cols)
        d = d_ref[:, cols]
        probs = probs_of(q, k, bound_ref[0])
        delta = jnp.sum(d.astype(F32) * att_ref[:, cols].astype(F32), axis=1, keepdims=True)
        d_probs = lax.dot_general(d, v, NT, preferred_element_type=F32)
        d_scores = (probs * (d_probs - delta)).astype(BF16)
        value_terms = lax.dot_general(probs.astype(BF16), d, TN, preferred_element_type=F32)
        key_terms = lax.dot_general(d_scores, q, TN, preferred_element_type=F32) * SCALE
        gq = jnp.dot(d_scores, k, preferred_element_type=F32) * SCALE
        gq_ref[:, cols] = gq.astype(BF16)
        for s, ref in enumerate(outs):
            rows = slice(s * TILE, (s + 1) * TILE)
            ref[0, :, cols] = key_terms[rows].astype(ref.dtype)
            ref[1, :, cols] = value_terms[rows].astype(ref.dtype)


def flat_spec(first):
    return pl.BlockSpec((TILE, PER_STEP * HEAD_DIM), lambda i, b: (0, i + first))


def pair_spec(first):
    return pl.BlockSpec((2, TILE, PER_STEP * HEAD_DIM), lambda i, b: (0, 0, i + first))


def attention_forward(bound, q, kvs, heads):
    steps = heads // PER_STEP
    width = heads * HEAD_DIM
    return pl.pallas_call(
        forward_kernel,
        grid_spec=pltpu.PrefetchScalarGridSpec(
            num_scalar_prefetch=1,
            grid=(steps,),
            in_specs=[flat_spec(0)] + [pair_spec(0)] * 4,
            out_specs=flat_spec(0),
        ),
        out_shape=jax.ShapeDtypeStruct((TILE, width), BF16),
        compiler_params=pltpu.CompilerParams(vmem_limit_bytes=32 * 1024 * 1024),
        cost_estimate=pl.CostEstimate(
            flops=4 * heads * TILE * SLOTS * TILE * HEAD_DIM,
            bytes_accessed=2 * TILE * width * 10,
            transcendentals=heads * TILE * SLOTS * TILE,
        ),
    )(bound, q, *kvs)


def attention_backward(bound, q, kvs, att, d, first, heads):
    steps = heads // PER_STEP
    width = heads * HEAD_DIM
    at = first // PER_STEP
    return pl.pallas_call(
        backward_kernel,
        grid_spec=pltpu.PrefetchScalarGridSpec(
            num_scalar_prefetch=1,
            grid=(steps,),
            in_specs=[flat_spec(at)] + [pair_spec(at)] * 4 + [flat_spec(at)] * 2,
            out_specs=[flat_spec(0)] + [pair_spec(0)] * 4,
        ),
        out_shape=[jax.ShapeDtypeStruct((TILE, width), BF16), jax.ShapeDtypeStruct((2, TILE, width), F32)]
        + [jax.ShapeDtypeStruct((2, TILE, width), BF16)] * 3,
        compiler_params=pltpu.CompilerParams(vmem_limit_bytes=32 * 1024 * 1024),
        cost_estimate=pl.CostEstimate(
            flops=12 * heads * TILE * SLOTS * TILE * HEAD_DIM,
            bytes_accessed=2 * TILE * width * 24,
            transcendentals=heads * TILE * SLOTS * TILE,
        ),
    )(bound, q, *kvs, att, d)


SWAP = [(0, 1), (1, 0)]
CROSS = [(1, 2), (2, 1)]


def exchange(time, core, cross):
    return (
        lax.ppermute(time, "xl", SWAP),
        lax.ppermute(core, "co", SWAP),
        lax.ppermute(cross, ("xh", "co"), CROSS),
    )


def per_device(queries, keys_values, upstream, out_weight, block_pick):
    width = queries.shape[4]
    dout = upstream.shape[4]
    half = dout // 2
    ny = lax.axis_size("y")
    nz = lax.axis_size("z")
    xh = lax.axis_index("xh")
    co = lax.axis_index("co")
    y = lax.axis_index("y")
    q = queries.reshape(TILE, width)
    kv = keys_values.reshape(2, TILE, width)
    up = upstream.reshape(TILE, dout)

    has_cross = xh != co
    bound = jnp.where(has_cross, SLOTS * TILE, (SLOTS - 1) * TILE).astype(jnp.int32).reshape(1)

    panel = lax.dynamic_slice(out_weight, (block_pick[0], 0, co * half), (1, out_weight.shape[1], half))[0]
    w_mine = lax.all_gather(panel, ("z", "y"), axis=0, tiled=True)
    kvs = (kv,) + exchange(kv, kv, kv)
    w_mate = lax.ppermute(w_mine, "co", SWAP)

    up_mine = lax.dynamic_slice_in_dim(up, co * half, half, axis=1)
    up_mate = lax.dynamic_slice_in_dim(up, (1 - co) * half, half, axis=1)
    up_from_mate = lax.ppermute(up_mate, "co", SWAP)

    att = attention_forward(bound, q, kvs, HEADS)
    att_mate = lax.ppermute(att, "co", SWAP)

    d_att = (
        lax.dot_general(up_mine, w_mine, NT, preferred_element_type=F32)
        + lax.dot_general(up_mate, w_mate, NT, preferred_element_type=F32)
    ).astype(BF16)

    grad = lax.dot_general(att, up_mine, TN, preferred_element_type=F32) + lax.dot_general(
        att_mate, up_from_mate, TN, preferred_element_type=F32
    )
    rows = out_weight.shape[1]
    grad = grad.reshape(nz, ny, rows, half)
    total_w = lax.dynamic_index_in_dim(grad, y, 1, keepdims=False)
    grad_b = grad.astype(BF16)
    for k in range(1, ny):
        piece = lax.dynamic_index_in_dim(grad_b, lax.rem(y + k, ny), 1, keepdims=False)
        got = lax.ppermute(piece, "y", [(i, (i + k) % ny) for i in range(ny)])
        total_w = total_w + got.astype(F32)
    over_z = lax.all_to_all(total_w.astype(BF16), "z", split_axis=0, concat_axis=0, tiled=True)
    over_z = jnp.sum(over_z.astype(F32), axis=0).astype(BF16)
    x_near = lax.ppermute(over_z, "xl", SWAP)
    x_far = lax.ppermute(over_z, "xh", SWAP)
    x_both = lax.ppermute(over_z, ("xl", "xh"), [(i, 3 - i) for i in range(4)])
    mine = (over_z.astype(F32) + x_near.astype(F32)) + (x_far.astype(F32) + x_both.astype(F32))
    mate = lax.ppermute(mine, "co", SWAP)
    first = co == 0
    grad_weight = jnp.concatenate(
        [jnp.where(first, mine, mate), jnp.where(first, mate, mine)], axis=1
    )

    parts = 2
    heads = HEADS // parts
    gq_parts, gkv_parts = [], []
    for c in range(parts):
        gq, own, to_time, to_core, to_cross = attention_backward(
            bound, q, kvs, att, d_att, c * heads, heads
        )
        gq_parts.append(gq)
        from_time, from_core, from_cross = exchange(to_time, to_core, to_cross)
        gkv_parts.append(
            own + from_time.astype(F32) + from_core.astype(F32) + from_cross.astype(F32)
        )
    grad_q = jnp.concatenate(gq_parts, axis=1)
    grad_kv = jnp.concatenate([p.astype(BF16) for p in gkv_parts], axis=2)

    m_mine = jnp.dot(att, w_mine, preferred_element_type=F32).astype(BF16)
    m_mate = jnp.dot(att, w_mate, preferred_element_type=F32).astype(BF16)
    mixed = jnp.concatenate(
        [jnp.where(first, m_mine, m_mate), jnp.where(first, m_mate, m_mine)], axis=1
    )
    return (
        mixed.reshape(upstream.shape),
        grad_q.reshape(queries.shape),
        grad_kv.reshape(keys_values.shape),
        grad_weight,
    )


def solution(mesh):
    fine = Mesh(mesh.devices.reshape(2, 2, 2, 8, 4), ("xl", "xh", "co", "z", "y"))
    wa = ("z", "y")
    ha = ("xh", "co")
    return jax.shard_map(
        per_device,
        mesh=fine,
        in_specs=(
            P(wa, "xl", ha, None, None),
            P(None, wa, "xl", ha, None, None),
            P(wa, "xl", ha, None, None),
            P(None, wa, None),
            P(),
        ),
        out_specs=(
            P(wa, "xl", ha, None, None),
            P(wa, "xl", ha, None, None),
            P(None, wa, "xl", ha, None, None),
            P(wa, None),
        ),
        check_vma=False,
    )
```

time: 435 us -> 213 us (0.49)
  waiting for transfers between devices: 270 us -> 80.5 us
  local copies, waits for them, and re-layouts: 55 us -> 7.75 us
  matrix products: 43 us -> 11.3 us
  blocking collectives: 0 us -> 25.2 us
  Pallas kernels: 0 us -> 21.6 us
  starting transfers between devices: 29.3 us -> 40.5 us
  other arithmetic: 20.7 us -> 10.1 us
    reduce_scatter x1 -> x0, waiting for transfers between devices: 148 us -> none  [per_device(): lax.psum_scatter(lax.dot_general(flat, up_flat, (((0,), (0,)), ((), ())),...]
    psum x1 -> x0, waiting for transfers between devices: 61.7 us -> none  [per_device(): grad_weight = lax.psum(block_sum, ('ta', 'ha')).astype(jnp.float32)]
    all_to_all x0 -> x1, blocking collectives: none -> 25.2 us  [per_device(): lax.all_to_all(total_w.astype(BF16), 'z', split_axis=0, concat_axis=0, ti...]
    dot_general x8 -> x6, matrix products: 34 us -> 11.3 us  [the longest x1 2.81 us: per_device(): lax.dot_general(up_mate, w_mate, NT, preferred_element_type=F32)]
    pallas_call x0 -> x3, Pallas kernels: none -> 21.6 us  [the longest x2 13.6 us: attention_backward(): pl.pallas_call(backward_kernel, grid_spec=pltpu.PrefetchScalarGridSpec(nu...]
    another operation x3 -> x0, local copies, waits for them, and re-layouts: 13.3 us -> none  [the longest x2 13.2 us: backward_tile(): terms = jnp.stack([key_terms, value_terms]).reshape((2, 5 * tile, width))]
    all_gather x1, waiting for transfers between devices: 0.01 us -> 13 us  [per_device(): w_mine = lax.all_gather(panel, ('z', 'y'), axis=0, tiled=True)]
    ppermute x8 -> x19, starting transfers between devices: 29 us -> 40.5 us  [the longest x1 13.3 us: per_device(): w_mate = lax.ppermute(w_mine, 'co', SWAP)]
  transfers between devices with their start and end apart: 11 -> 20, of which waited for: 6 -> 12; matrix products, arithmetic and copies ran while one was open for 23% -> 9% of each run, Pallas kernels for 0% -> 7%
where the time goes in v1:
time: 213 us; the launch traced here: 212 us
  waiting for transfers between devices  80.5 us (38%)
  starting transfers between devices  40.5 us (19%)
  blocking collectives  25.2 us (12%)
  Pallas kernels  21.6 us (10%)
  between operations  15 us (7%)
  matrix products  11.3 us (5%)
  other arithmetic  10.1 us (5%)
  local copies, waits for them, and re-layouts  7.75 us (4%)
    ppermute x3, waiting for transfers between devices, exchange(): lax.ppermute(time, 'xl', SWAP)  29.9 us
    ppermute x3, waiting for transfers between devices, exchange(): lax.ppermute(cross, ('xh', 'co'), CROSS)  28.3 us
    all_to_all x1, blocking collectives, per_device(): lax.all_to_all(total_w.astype(BF16), 'z', split_axis=0, concat_axis=0, ti...  25.2 us
    pallas_call x2, Pallas kernels, attention_backward(): pl.pallas_call(backward_kernel, grid_spec=pltpu.PrefetchScalarGridSpec(nu...  13.6 us
    ppermute x1, starting transfers between devices, per_device(): w_mate = lax.ppermute(w_mine, 'co', SWAP)  13.3 us
    all_gather x1, waiting for transfers between devices, per_device(): w_mine = lax.all_gather(panel, ('z', 'y'), axis=0, tiled=True)  13 us
    ppermute x3, starting transfers between devices, exchange(): lax.ppermute(cross, ('xh', 'co'), CROSS)  11.7 us
    pallas_call x1, Pallas kernels, attention_forward(): pl.pallas_call(forward_kernel, grid_spec=pltpu.PrefetchScalarGridSpec(num...  8.08 us
  transfers between devices with their start and end apart: 20, of which 12 were waited for; matrix products, arithmetic and copies ran while one was open for 9% of the time, Pallas kernels for 7%

profile of v1, /device:TPU:1, one launch (start us, length us, event | category | flops | bytes accessed | tf_op | source)
XLA Modules:
  0.0 212.1 jit_solution(9012588677963219118)
XLA Ops:
  9.5 2.1 %collective-permute-start = (bf16[2,192,1536]{2,1,0:T(8,128)(2,1)}, bf16[2,192,1536]{2,1,0:T(8,128)(2,1)S(1)}, u32[]{:S(2)}, u32[]{:S(2)}) collective-permute-start(bf16[2,192,1536]{2,1,0:T(8,128)(2,1)} %bitcast.52), channel_id=1, source_target_pairs={{0,128},{128,0},{1,129},{129,1},{2,130},{130,2},{3,131},{131,3},{4... | collective-permute-start | bytes 3538952 | tf_op jit(solution)/shard_map/ppermute | solution.py:130
  12.9 3.9 %collective-permute-start.2 = (bf16[2,192,1536]{2,1,0:T(8,128)(2,1)}, bf16[2,192,1536]{2,1,0:T(8,128)(2,1)}, u32[]{:S(2)}, u32[]{:S(2)}) collective-permute-start(bf16[2,192,1536]{2,1,0:T(8,128)(2,1)} %bitcast.54), channel_id=1, source_target_pairs={{32,64},{64,32},{33,65},{65,33},{34,66},{66,34},{35,67},{67,35},{3... | collective-permute-start | bytes 3538952 | tf_op jit(solution)/shard_map/ppermute | solution.py:132
  16.8 19.5 %collective-permute-done.time_ref = bf16[2,192,1536]{2,1,0:T(8,128)(2,1)S(1)} collective-permute-done((bf16[2,192,1536]{2,1,0:T(8,128)(2,1)}, bf16[2,192,1536]{2,1,0:T(8,128)(2,1)S(1)}, u32[]{:S(2)}, u32[]{:S(2)}) %collective-permute-start) | collective-permute-done | bytes 1179680 | tf_op jit(solution)/shard_map/ppermute | solution.py:130
  36.3 17.0 %collective-permute-done.2.cross_ref = bf16[2,192,1536]{2,1,0:T(8,128)(2,1)} collective-permute-done((bf16[2,192,1536]{2,1,0:T(8,128)(2,1)}, bf16[2,192,1536]{2,1,0:T(8,128)(2,1)}, u32[]{:S(2)}, u32[]{:S(2)}) %collective-permute-start.2) | collective-permute-done | bytes 1179680 | tf_op jit(solution)/shard_map/ppermute | solution.py:132
  55.6 8.1 %shard_map.84.att_ref = bf16[192,1536]{1,0:T(8,128)(2,1)S(1)} custom-call(s32[1]{0:T(128)} %bitcast.bound_ref, bf16[192,1536]{1,0:T(8,128)(2,1)S(1)} %bitcast.58, bf16[2,192,1536]{2,1,0:T(8,128)(2,1)S(1)} %bitcast.55, bf16[2,192,1536]{2,1,0:T(8,128)(2,1)S(1)} %collective-permute-done.time_ref, bf16[2,192,1536]{2,1,0:T(8,128)(2,1)S(1)} %collective-permute-done.1.core_ref, ...), custom_call_target="tpu_custom_call" | custom-call | flops 905969664 | bytes 5898240 | tf_op jit(solution)/shard_map/pallas_call | solution.py:83
  66.6 2.0 fusion.13
  72.8 2.7 %collective-permute-start.14 = (bf16[8,48,768]{2,1,0:T(8,128)(2,1)}, bf16[8,48,768]{2,1,0:T(8,128)(2,1)}, u32[]{:S(2)}, u32[]{:S(2)}) collective-permute-start(bf16[8,48,768]{2,1,0:T(8,128)(2,1)} %get-tuple-element.29), channel_id=1, source_target_pairs={{0,3},{1,0},{2,1},{3,2},{4,7},{5,4},{6,5},{7,6},{8,11},{9,8},{10,9... | collective-permute-start | bytes 1769480 | tf_op jit(solution)/shard_map/ppermute | solution.py:178
  76.6 13.0 %all-gather.3.cloned.1.call-done = bf16[1,1536,768]{2,1,0:T(8,128)(2,1)} async-done(((bf16[1,48,768]{2,1,0:T(8,128)(2,1)}), bf16[1,1536,768]{2,1,0:T(8,128)(2,1)}) %all-gather.3.cloned.1.call-update) | async-done | bytes 2359312 | tf_op jit(solution)/shard_map/all_gather | solution.py:153
  89.6 13.3 %collective-permute-start.3 = (bf16[1536,768]{1,0:T(8,128)(2,1)}, bf16[1536,768]{1,0:T(8,128)(2,1)}, u32[]{:S(2)}, u32[]{:S(2)}) collective-permute-start(bf16[1536,768]{1,0:T(8,128)(2,1)} %bitcast.63), channel_id=1, source_target_pairs={{0,32},{32,0},{1,33},{33,1},{2,34},{34,2},{3,35},{35,3},{4,36},{36... | collective-permute-start | bytes 7077896 | tf_op jit(solution)/shard_map/ppermute | solution.py:155
  104.3 2.1 collective-permute-done.12
  106.3 2.1 fusion.3
  108.4 25.2 %all_to_all.5 = bf16[8,48,768]{2,1,0:T(8,128)(2,1)} all-to-all(bf16[8,48,768]{2,1,0:T(8,128)(2,1)S(1)} %fusion.3), channel_id=1, replica_groups=mesh['xl'=2,'xh'=2,'co'=2,'z'=8,'y'=4] {'z'}, dimensions={0} | all-to-all | bytes 1179648 | tf_op jit(solution)/shard_map/all_to_all | solution.py:180
  138.7 2.2 %collective-permute-done.17 = bf16[48,768]{1,0:T(8,128)(2,1)S(1)} collective-permute-done((bf16[48,768]{1,0:T(8,128)(2,1)}, bf16[48,768]{1,0:T(8,128)(2,1)S(1)}, u32[]{:S(2)}, u32[]{:S(2)}) %collective-permute-start.17) | collective-permute-done | bytes 73760 | tf_op jit(solution)/shard_map/ppermute | solution.py:184
  143.3 2.8 %collective-permute-start.18 = (f32[48,768]{1,0:T(8,128)}, f32[48,768]{1,0:T(8,128)}, u32[]{:S(2)}, u32[]{:S(2)}) collective-permute-start(f32[48,768]{1,0:T(8,128)} %add_add_fusion), channel_id=1, source_target_pairs={{0,32},{32,0},{1,33},{33,1},{2,34},{34,2},{3,35},{35,3},{4,36},{36... | collective-permute-start | bytes 442376 | tf_op jit(solution)/shard_map/ppermute | solution.py:186
  148.4 2.6 %fusion.5 = f32[192,1536]{1,0:T(8,128)S(1)} fusion(bf16[1,1,1,192,1536]{4,3,2,1,0:T(8,128)(2,1)S(1)} %copy-done, s32[]{:T(128)S(6)} %select_n.55, bf16[1,1536,768]{2,1,0:T(8,128)(2,1)} %all-gather.3.cloned.1.call-done), kind=kOutput, calls=%fused_computation.19 | convolution fusion | flops 452984832 | bytes 3833860 | tf_op jit(solution)/shard_map/dot_general | solution.py:165
  151.0 2.8 %fusion.d_ref = bf16[192,1536]{1,0:T(8,128)(2,1)S(1)} fusion(f32[192,1536]{1,0:T(8,128)S(1)} %fusion.5, bf16[192,768]{1,0:T(8,128)(2,1)} %dynamic-slice_bitcast_fusion.3, bf16[1536,768]{1,0:T(8,128)(2,1)} %collective-permute-done.3), kind=kOutput, calls=%fused_computation.2 | convolution fusion | flops 453574656 | bytes 4423680 | tf_op jit(solution)/shard_map/dot_general | solution.py:166
  153.9 6.8 %shard_map.86 = (bf16[192,768]{1,0:T(8,128)(2,1)S(1)}, f32[2,192,768]{2,1,0:T(8,128)S(1)}, bf16[2,192,768]{2,1,0:T(8,128)(2,1)S(1)}, bf16[2,192,768]{2,1,0:T(8,128)(2,1)S(1)}, bf16[2,192,768]{2,1,0:T(8,128)(2,1)S(1)}) custom-call(s32[1]{0:T(128)} %bitcast.bound_ref, bf16[192,1536]{1,0:T(8,128)(2,1)S(1)} %bitcast.59, bf16[2,192,1536]{2,1,0:T(8,128)(2,1)S(1)} %bitcast.56, ...), custom_call_target="tpu_custom_call" | custom-call | flops 1358954496 | bytes 7077888 | tf_op jit(solution)/shard_map/pallas_call | solution.py:105
  160.7 3.2 %collective-permute-start.9 = (bf16[2,192,768]{2,1,0:T(8,128)(2,1)S(1)}, bf16[2,192,768]{2,1,0:T(8,128)(2,1)S(1)}, u32[]{:S(2)}, u32[]{:S(2)}) collective-permute-start(bf16[2,192,768]{2,1,0:T(8,128)(2,1)S(1)} %get-tuple-element.23), channel_id=1, source_target_pairs={{32,64},{64,32},{33,65},{65,33},{34,66},{66,34},{35,67},{67,35},{3... | collective-permute-start | bytes 1769480 | tf_op jit(solution)/shard_map/ppermute | solution.py:132
  165.8 6.8 %shard_map.85 = (bf16[192,768]{1,0:T(8,128)(2,1)S(1)}, f32[2,192,768]{2,1,0:T(8,128)S(1)}, bf16[2,192,768]{2,1,0:T(8,128)(2,1)S(1)}, bf16[2,192,768]{2,1,0:T(8,128)(2,1)S(1)}, bf16[2,192,768]{2,1,0:T(8,128)(2,1)S(1)}) custom-call(s32[1]{0:T(128)} %bitcast.bound_ref, bf16[192,1536]{1,0:T(8,128)(2,1)S(1)} %bitcast.60, bf16[2,192,1536]{2,1,0:T(8,128)(2,1)S(1)} %bitcast.57, ...), custom_call_target="tpu_custom_call" | custom-call | flops 1358954496 | bytes 7077888 | tf_op jit(solution)/shard_map/pallas_call | solution.py:105
  172.6 4.6 %collective-permute-start.6 = (bf16[2,192,768]{2,1,0:T(8,128)(2,1)S(1)}, bf16[2,192,768]{2,1,0:T(8,128)(2,1)S(1)}, u32[]{:S(2)}, u32[]{:S(2)}) collective-permute-start(bf16[2,192,768]{2,1,0:T(8,128)(2,1)S(1)} %get-tuple-element.19), channel_id=1, source_target_pairs={{32,64},{64,32},{33,65},{65,33},{34,66},{66,34},{35,67},{67,35},{3... | collective-permute-start | bytes 1769480 | tf_op jit(solution)/shard_map/ppermute | solution.py:132
  177.2 2.4 %convolution_convert_fusion = bf16[192,768]{1,0:T(8,128)(2,1)S(1)} fusion(bf16[192,1536]{1,0:T(8,128)(2,1)S(1)} %shard_map.84.att_ref, bf16[1536,768]{1,0:T(8,128)(2,1)} %collective-permute-done.3), kind=kOutput, calls=%fused_computation.3 | convolution fusion | flops 453132288 | bytes 3244032 | tf_op jit(solution)/shard_map/dot_general | solution.py:208
  181.9 5.2 %collective-permute-done.7 = bf16[2,192,768]{2,1,0:T(8,128)(2,1)S(1)} collective-permute-done((bf16[2,192,768]{2,1,0:T(8,128)(2,1)S(1)}, bf16[2,192,768]{2,1,0:T(8,128)(2,1)S(1)}, u32[]{:S(2)}, u32[]{:S(2)}) %collective-permute-start.7) | collective-permute-done | bytes 589856 | tf_op jit(solution)/shard_map/ppermute | solution.py:130
  187.3 11.3 %collective-permute-done.6 = bf16[2,192,768]{2,1,0:T(8,128)(2,1)S(1)} collective-permute-done((bf16[2,192,768]{2,1,0:T(8,128)(2,1)S(1)}, bf16[2,192,768]{2,1,0:T(8,128)(2,1)S(1)}, u32[]{:S(2)}, u32[]{:S(2)}) %collective-permute-start.6) | collective-permute-done | bytes 589856 | tf_op jit(solution)/shard_map/ppermute | solution.py:132
  198.7 5.2 %collective-permute-done.4 = bf16[2,192,768]{2,1,0:T(8,128)(2,1)S(1)} collective-permute-done((bf16[2,192,768]{2,1,0:T(8,128)(2,1)S(1)}, bf16[2,192,768]{2,1,0:T(8,128)(2,1)S(1)}, u32[]{:S(2)}, u32[]{:S(2)}) %collective-permute-start.4) | collective-permute-done | bytes 589856 | tf_op jit(solution)/shard_map/ppermute | solution.py:130
  (54 shorter events, 30.3 us)
Async XLA Ops:
  7.2 56.6 %copy-start = (bf16[1,1,1,192,1536]{4,3,2,1,0:T(8,128)(2,1)S(1)}, bf16[1,1,1,192,1536]{4,3,2,1,0:T(8,128)(2,1)}, u32[]{:S(2)}) copy-start(bf16[1,1,1,192,1536]{4,3,2,1,0:T(8,128)(2,1)} %param.7) | copy-start | bytes 1769476
  7.2 82.4 %all-gather.3.cloned.1.call-start = ((), (), s32[]{:S(2)}) async-start(), calls=%async_computation.1 | async-start | bytes 2433024 | tf_op jit(solution)/shard_map/all_gather | solution.py:153
  9.5 26.8 %collective-permute-start = (bf16[2,192,1536]{2,1,0:T(8,128)(2,1)}, bf16[2,192,1536]{2,1,0:T(8,128)(2,1)S(1)}, u32[]{:S(2)}, u32[]{:S(2)}) collective-permute-start(bf16[2,192,1536]{2,1,0:T(8,128)(2,1)} %bitcast.52), channel_id=1, source_target_pairs={{0,128},{128,0},{1,129},{129,1},{2,130},{130,2},{3,131},{131,3},{4... | collective-permute-start | bytes 3538952 | tf_op jit(solution)/shard_map/ppermute | solution.py:130
  11.6 24.7 %collective-permute-start.1 = (bf16[2,192,1536]{2,1,0:T(8,128)(2,1)}, bf16[2,192,1536]{2,1,0:T(8,128)(2,1)S(1)}, u32[]{:S(2)}, u32[]{:S(2)}) collective-permute-start(bf16[2,192,1536]{2,1,0:T(8,128)(2,1)} %bitcast.53), channel_id=1, source_target_pairs={{0,32},{32,0},{1,33},{33,1},{2,34},{34,2},{3,35},{35,3},{4,36},{36... | collective-permute-start | bytes 3538952 | tf_op jit(solution)/shard_map/ppermute | solution.py:131
  12.9 40.3 %collective-permute-start.2 = (bf16[2,192,1536]{2,1,0:T(8,128)(2,1)}, bf16[2,192,1536]{2,1,0:T(8,128)(2,1)}, u32[]{:S(2)}, u32[]{:S(2)}) collective-permute-start(bf16[2,192,1536]{2,1,0:T(8,128)(2,1)} %bitcast.54), channel_id=1, source_target_pairs={{32,64},{64,32},{33,65},{65,33},{34,66},{66,34},{35,67},{67,35},{3... | collective-permute-start | bytes 3538952 | tf_op jit(solution)/shard_map/ppermute | solution.py:132
  63.7 2.9 %collective-permute-start.10 = (bf16[192,1536]{1,0:T(8,128)(2,1)S(1)}, bf16[192,1536]{1,0:T(8,128)(2,1)}, u32[]{:S(2)}, u32[]{:S(2)}) collective-permute-start(bf16[192,1536]{1,0:T(8,128)(2,1)S(1)} %shard_map.84.att_ref), channel_id=1, source_target_pairs={{0,32},{32,0},{1,33},{33,1},{2,34},{34,2},{3,35},{35,3},{4,36},{36... | collective-permute-start | bytes 1769480 | tf_op jit(solution)/shard_map/ppermute | solution.py:162
  64.5 2.0 collective-permute-start.11
  72.8 31.5 %collective-permute-start.14 = (bf16[8,48,768]{2,1,0:T(8,128)(2,1)}, bf16[8,48,768]{2,1,0:T(8,128)(2,1)}, u32[]{:S(2)}, u32[]{:S(2)}) collective-permute-start(bf16[8,48,768]{2,1,0:T(8,128)(2,1)} %get-tuple-element.29), channel_id=1, source_target_pairs={{0,3},{1,0},{2,1},{3,2},{4,7},{5,4},{6,5},{7,6},{8,11},{9,8},{10,9... | collective-permute-start | bytes 1769480 | tf_op jit(solution)/shard_map/ppermute | solution.py:178
  75.5 28.7 %collective-permute-start.13 = (bf16[8,48,768]{2,1,0:T(8,128)(2,1)}, bf16[8,48,768]{2,1,0:T(8,128)(2,1)}, u32[]{:S(2)}, u32[]{:S(2)}) collective-permute-start(bf16[8,48,768]{2,1,0:T(8,128)(2,1)} %get-tuple-element.30), channel_id=1, source_target_pairs={{0,2},{1,3},{2,0},{3,1},{4,6},{5,7},{6,4},{7,5},{8,10},{9,11},{10,... | collective-permute-start | bytes 1769480 | tf_op jit(solution)/shard_map/ppermute | solution.py:178
  75.9 30.5 %collective-permute-start.12 = (bf16[8,48,768]{2,1,0:T(8,128)(2,1)}, bf16[8,48,768]{2,1,0:T(8,128)(2,1)}, u32[]{:S(2)}, u32[]{:S(2)}) collective-permute-start(bf16[8,48,768]{2,1,0:T(8,128)(2,1)} %get-tuple-element.28), channel_id=1, source_target_pairs={{0,1},{1,2},{2,3},{3,0},{4,5},{5,6},{6,7},{7,4},{8,9},{9,10},{10,1... | collective-permute-start | bytes 1769480 | tf_op jit(solution)/shard_map/ppermute | solution.py:178
  89.6 61.4 %collective-permute-start.3 = (bf16[1536,768]{1,0:T(8,128)(2,1)}, bf16[1536,768]{1,0:T(8,128)(2,1)}, u32[]{:S(2)}, u32[]{:S(2)}) collective-permute-start(bf16[1536,768]{1,0:T(8,128)(2,1)} %bitcast.63), channel_id=1, source_target_pairs={{0,32},{32,0},{1,33},{33,1},{2,34},{34,2},{3,35},{35,3},{4,36},{36... | collective-permute-start | bytes 7077896 | tf_op jit(solution)/shard_map/ppermute | solution.py:155
  135.4 5.4 %collective-permute-start.17 = (bf16[48,768]{1,0:T(8,128)(2,1)}, bf16[48,768]{1,0:T(8,128)(2,1)S(1)}, u32[]{:S(2)}, u32[]{:S(2)}) collective-permute-start(bf16[48,768]{1,0:T(8,128)(2,1)} %reduce_sum.12), channel_id=1, source_target_pairs={{0,192},{64,128},{128,64},{192,0},{1,193},{65,129},{129,65},{193,1... | collective-permute-start | bytes 221192 | tf_op jit(solution)/shard_map/ppermute | solution.py:184
  135.4 5.4 %collective-permute-start.16 = (bf16[48,768]{1,0:T(8,128)(2,1)}, bf16[48,768]{1,0:T(8,128)(2,1)S(1)}, u32[]{:S(2)}, u32[]{:S(2)}) collective-permute-start(bf16[48,768]{1,0:T(8,128)(2,1)} %reduce_sum.12), channel_id=1, source_target_pairs={{0,64},{64,0},{1,65},{65,1},{2,66},{66,2},{3,67},{67,3},{4,68},{68... | collective-permute-start | bytes 221192 | tf_op jit(solution)/shard_map/ppermute | solution.py:183
  137.0 4.7 %collective-permute-start.15 = (bf16[48,768]{1,0:T(8,128)(2,1)}, bf16[48,768]{1,0:T(8,128)(2,1)S(1)}, u32[]{:S(2)}, u32[]{:S(2)}) collective-permute-start(bf16[48,768]{1,0:T(8,128)(2,1)} %reduce_sum.12), channel_id=1, source_target_pairs={{0,128},{128,0},{1,129},{129,1},{2,130},{130,2},{3,131},{131,3},{4... | collective-permute-start | bytes 221192 | tf_op jit(solution)/shard_map/ppermute | solution.py:182
  143.3 4.1 %collective-permute-start.18 = (f32[48,768]{1,0:T(8,128)}, f32[48,768]{1,0:T(8,128)}, u32[]{:S(2)}, u32[]{:S(2)}) collective-permute-start(f32[48,768]{1,0:T(8,128)} %add_add_fusion), channel_id=1, source_target_pairs={{0,32},{32,0},{1,33},{33,1},{2,34},{34,2},{3,35},{35,3},{4,36},{36... | collective-permute-start | bytes 442376 | tf_op jit(solution)/shard_map/ppermute | solution.py:186
  151.0 2.9 %copy-start.2 = (bf16[2,1,1,1,192,1536]{5,4,3,2,1,0:T(8,128)(2,1)S(1)}, bf16[2,1,1,1,192,1536]{5,4,3,2,1,0:T(8,128)(2,1)}, u32[]{:S(2)}) copy-start(bf16[2,1,1,1,192,1536]{5,4,3,2,1,0:T(8,128)(2,1)} %param.6) | copy-start | bytes 3538948
  151.0 2.9 %copy-start.4 = (bf16[1,1,1,192,1536]{4,3,2,1,0:T(8,128)(2,1)S(1)}, bf16[1,1,1,192,1536]{4,3,2,1,0:T(8,128)(2,1)}, u32[]{:S(2)}) copy-start(bf16[1,1,1,192,1536]{4,3,2,1,0:T(8,128)(2,1)} %param.5) | copy-start | bytes 1769476
  160.7 19.0 %collective-permute-start.9 = (bf16[2,192,768]{2,1,0:T(8,128)(2,1)S(1)}, bf16[2,192,768]{2,1,0:T(8,128)(2,1)S(1)}, u32[]{:S(2)}, u32[]{:S(2)}) collective-permute-start(bf16[2,192,768]{2,1,0:T(8,128)(2,1)S(1)} %get-tuple-element.23), channel_id=1, source_target_pairs={{32,64},{64,32},{33,65},{65,33},{34,66},{66,34},{35,67},{67,35},{3... | collective-permute-start | bytes 1769480 | tf_op jit(solution)/shard_map/ppermute | solution.py:132
  164.7 17.2 %collective-permute-start.8 = (bf16[2,192,768]{2,1,0:T(8,128)(2,1)S(1)}, bf16[2,192,768]{2,1,0:T(8,128)(2,1)S(1)}, u32[]{:S(2)}, u32[]{:S(2)}) collective-permute-start(bf16[2,192,768]{2,1,0:T(8,128)(2,1)S(1)} %get-tuple-element.22), channel_id=1, source_target_pairs={{0,32},{32,0},{1,33},{33,1},{2,34},{34,2},{3,35},{35,3},{4,36},{36... | collective-permute-start | bytes 1769480 | tf_op jit(solution)/shard_map/ppermute | solution.py:131
  164.7 22.4 %collective-permute-start.7 = (bf16[2,192,768]{2,1,0:T(8,128)(2,1)S(1)}, bf16[2,192,768]{2,1,0:T(8,128)(2,1)S(1)}, u32[]{:S(2)}, u32[]{:S(2)}) collective-permute-start(bf16[2,192,768]{2,1,0:T(8,128)(2,1)S(1)} %get-tuple-element.21), channel_id=1, source_target_pairs={{0,128},{128,0},{1,129},{129,1},{2,130},{130,2},{3,131},{131,3},{4... | collective-permute-start | bytes 1769480 | tf_op jit(solution)/shard_map/ppermute | solution.py:130
  172.6 26.1 %collective-permute-start.6 = (bf16[2,192,768]{2,1,0:T(8,128)(2,1)S(1)}, bf16[2,192,768]{2,1,0:T(8,128)(2,1)S(1)}, u32[]{:S(2)}, u32[]{:S(2)}) collective-permute-start(bf16[2,192,768]{2,1,0:T(8,128)(2,1)S(1)} %get-tuple-element.19), channel_id=1, source_target_pairs={{32,64},{64,32},{33,65},{65,33},{34,66},{66,34},{35,67},{67,35},{3... | collective-permute-start | bytes 1769480 | tf_op jit(solution)/shard_map/ppermute | solution.py:132
  177.1 3.0 %copy-start.6 = (bf16[1,1536,768]{2,1,0:T(8,128)(2,1)S(1)}, bf16[1,1536,768]{2,1,0:T(8,128)(2,1)}, u32[]{:S(2)}) copy-start(bf16[1,1536,768]{2,1,0:T(8,128)(2,1)} %all-gather.3.cloned.1.call-done) | copy-start | bytes 7077892
  177.1 21.6 %collective-permute-start.5 = (bf16[2,192,768]{2,1,0:T(8,128)(2,1)S(1)}, bf16[2,192,768]{2,1,0:T(8,128)(2,1)S(1)}, u32[]{:S(2)}, u32[]{:S(2)}) collective-permute-start(bf16[2,192,768]{2,1,0:T(8,128)(2,1)S(1)} %get-tuple-element.18), channel_id=1, source_target_pairs={{0,32},{32,0},{1,33},{33,1},{2,34},{34,2},{3,35},{35,3},{4,36},{36... | collective-permute-start | bytes 1769480 | tf_op jit(solution)/shard_map/ppermute | solution.py:131
  179.7 24.2 %collective-permute-start.4 = (bf16[2,192,768]{2,1,0:T(8,128)(2,1)S(1)}, bf16[2,192,768]{2,1,0:T(8,128)(2,1)S(1)}, u32[]{:S(2)}, u32[]{:S(2)}) collective-permute-start(bf16[2,192,768]{2,1,0:T(8,128)(2,1)S(1)} %get-tuple-element.17), channel_id=1, source_target_pairs={{0,128},{128,0},{1,129},{129,1},{2,130},{130,2},{3,131},{131,3},{4... | collective-permute-start | bytes 1769480 | tf_op jit(solution)/shard_map/ppermute | solution.py:130
  (3 other events, 4.5 us)
Sparse Core Ops, SparseCore 0:
  10.6 78.9 all-gather.2

commit v2 on v1

v2 whole, which is shorter than its diff:
```python
import functools

import jax
import jax.numpy as jnp
from jax import lax
from jax.experimental import pallas as pl
from jax.experimental.pallas import tpu as pltpu
from jax.sharding import Mesh, PartitionSpec as P

HEADS = 12
HEAD_DIM = 128
SCALE = HEAD_DIM ** (-0.5)
TILE = 192
SLOTS = 4
PER_STEP = 3
GROUP = PER_STEP * HEAD_DIM
NT = (((1,), (1,)), ((), ()))
TN = (((0,), (0,)), ((), ()))
F32 = jnp.float32
BF16 = jnp.bfloat16
PARAMS = pltpu.CompilerParams(vmem_limit_bytes=40 * 1024 * 1024)


def window_of(refs, which, cols):
    return jnp.concatenate([ref[which, :, cols] for ref in refs], axis=0)


def probs_of(q, k, bound):
    scores = lax.dot_general(q, k, NT, preferred_element_type=F32)
    column = lax.broadcasted_iota(jnp.int32, scores.shape, 1)
    scores = jnp.where(column < bound, scores, -1e30)
    top = jnp.max(scores, axis=1, keepdims=True)
    weights = jnp.exp((scores - top) * SCALE)
    return weights * (1.0 / jnp.sum(weights, axis=1, keepdims=True))


def forward_kernel(bound_ref, q_ref, own_ref, time_ref, core_ref, cross_ref, out_ref):
    kv = (own_ref, time_ref, core_ref, cross_ref)
    for h in range(PER_STEP):
        cols = slice(h * HEAD_DIM, (h + 1) * HEAD_DIM)
        k = window_of(kv, 0, cols)
        v = window_of(kv, 1, cols)
        probs = probs_of(q_ref[:, cols], k, bound_ref[0])
        out = jnp.dot(probs.astype(BF16), v, preferred_element_type=F32)
        out_ref[:, cols] = out.astype(BF16)


def backward_kernel(group, scalar_ref, q_ref, own_ref, time_ref, core_ref, cross_ref, att_ref, *rest):
    pieces, gq_ref, outs, d_ref = rest[:4], rest[4], rest[5:9], rest[9]
    kv = (own_ref, time_ref, core_ref, cross_ref)
    at = lax.rem(group + pl.program_id(0) - scalar_ref[1] + 4, 4)
    for i in range(4):

        @pl.when(at == i)
        def _():
            d_ref[...] = pieces[i][...]

    for h in range(PER_STEP):
        cols = slice(h * HEAD_DIM, (h + 1) * HEAD_DIM)
        q = q_ref[:, cols]
        k = window_of(kv, 0, cols)
        v = window_of(kv, 1, cols)
        d = d_ref[:, cols]
        probs = probs_of(q, k, scalar_ref[0])
        delta = jnp.sum(d.astype(F32) * att_ref[:, cols].astype(F32), axis=1, keepdims=True)
        d_probs = lax.dot_general(d, v, NT, preferred_element_type=F32)
        d_scores = (probs * (d_probs - delta)).astype(BF16)
        value_terms = lax.dot_general(probs.astype(BF16), d, TN, preferred_element_type=F32)
        key_terms = lax.dot_general(d_scores, q, TN, preferred_element_type=F32) * SCALE
        gq = jnp.dot(d_scores, k, preferred_element_type=F32) * SCALE
        gq_ref[:, cols] = gq.astype(BF16)
        for s, ref in enumerate(outs):
            rows = slice(s * TILE, (s + 1) * TILE)
            ref[0, :, cols] = key_terms[rows].astype(ref.dtype)
            ref[1, :, cols] = value_terms[rows].astype(ref.dtype)


def flat_spec(first):
    return pl.BlockSpec((TILE, GROUP), lambda i, b: (0, i + first))


def pair_spec(first):
    return pl.BlockSpec((2, TILE, GROUP), lambda i, b: (0, 0, i + first))


def whole(shape):
    return pl.BlockSpec(shape, lambda *_: (0,) * len(shape))


def attention_forward(scalars, q, kvs, first, groups):
    return pl.pallas_call(
        forward_kernel,
        grid_spec=pltpu.PrefetchScalarGridSpec(
            num_scalar_prefetch=1,
            grid=(groups,),
            in_specs=[flat_spec(first), pair_spec(first), pair_spec(0), pair_spec(first), pair_spec(0)],
            out_specs=flat_spec(0),
        ),
        out_shape=jax.ShapeDtypeStruct((TILE, groups * GROUP), BF16),
        compiler_params=PARAMS,
        cost_estimate=pl.CostEstimate(
            flops=4 * groups * TILE * SLOTS * TILE * GROUP,
            bytes_accessed=20 * TILE * groups * GROUP,
            transcendentals=groups * PER_STEP * TILE * SLOTS * TILE,
        ),
    )(scalars, q, *kvs)


def attention_backward(scalars, q, kvs, att, pieces, first, groups):
    width = groups * GROUP
    return pl.pallas_call(
        functools.partial(backward_kernel, first),
        grid_spec=pltpu.PrefetchScalarGridSpec(
            num_scalar_prefetch=1,
            grid=(groups,),
            in_specs=[flat_spec(first), pair_spec(first), pair_spec(0), pair_spec(first), pair_spec(0), flat_spec(0)]
            + [whole((TILE, GROUP))] * 4,
            out_specs=[flat_spec(0)] + [pair_spec(0)] * 4,
            scratch_shapes=[pltpu.VMEM((TILE, GROUP), BF16)],
        ),
        out_shape=[jax.ShapeDtypeStruct((TILE, width), BF16), jax.ShapeDtypeStruct((2, TILE, width), F32)]
        + [jax.ShapeDtypeStruct((2, TILE, width), BF16)] * 3,
        compiler_params=PARAMS,
        cost_estimate=pl.CostEstimate(
            flops=12 * groups * TILE * SLOTS * TILE * GROUP,
            bytes_accessed=48 * TILE * width,
            transcendentals=groups * PER_STEP * TILE * SLOTS * TILE,
        ),
    )(scalars, q, *kvs, att, *pieces)


def ordered_kernel(scalar_ref, *refs):
    pieces, out_ref = refs[:-1], refs[-1]
    rows = pieces[0].shape[0]
    count = len(pieces)
    for k, piece in enumerate(pieces):
        row = pl.multiple_of(lax.rem(scalar_ref[2] - k + count, count) * rows, 16)
        out_ref[pl.ds(row, rows), :] = piece[...]


def ordered(scalars, pieces):
    rows, cols = pieces[0].shape
    return pl.pallas_call(
        ordered_kernel,
        grid_spec=pltpu.PrefetchScalarGridSpec(
            num_scalar_prefetch=1,
            grid=(1,),
            in_specs=[whole((rows, cols))] * len(pieces),
            out_specs=whole((rows * len(pieces), cols)),
        ),
        out_shape=jax.ShapeDtypeStruct((rows * len(pieces), cols), BF16),
        compiler_params=PARAMS,
        cost_estimate=pl.CostEstimate(
            flops=0, bytes_accessed=4 * rows * cols * len(pieces), transcendentals=0
        ),
    )(scalars, *pieces)


def d_attention_kernel(scalar_ref, *refs):
    ups, mine_ref, mate_ref, outs, weight_ref = refs[:4], refs[4], refs[5], refs[6:10], refs[10]
    co = scalar_ref[3]
    half = mine_ref.shape[1]
    for side, ref in enumerate((mine_ref, mate_ref)):
        column = pl.multiple_of((co if side == 0 else 1 - co) * half, 128)
        weight_ref[:, pl.ds(column, half)] = ref[...]
    for up, out in zip(ups, outs):
        out[...] = lax.dot_general(
            up[...], weight_ref[...], NT, preferred_element_type=F32
        ).astype(BF16)


def d_attention(scalars, ups, w_mine, w_mate):
    dout = ups[0].shape[1]
    return pl.pallas_call(
        d_attention_kernel,
        grid_spec=pltpu.PrefetchScalarGridSpec(
            num_scalar_prefetch=1,
            grid=(1,),
            in_specs=[whole((TILE, dout))] * 4 + [whole(w_mine.shape)] * 2,
            out_specs=[whole((TILE, GROUP))] * 4 + [whole((GROUP, dout))],
        ),
        out_shape=[jax.ShapeDtypeStruct((TILE, GROUP), BF16)] * 4
        + [jax.ShapeDtypeStruct((GROUP, dout), BF16)],
        compiler_params=PARAMS,
        cost_estimate=pl.CostEstimate(
            flops=8 * TILE * GROUP * dout, bytes_accessed=8 * TILE * dout + 4 * GROUP * dout, transcendentals=0
        ),
    )(scalars, *ups, w_mine, w_mate)


def gradient_kernel(scalar_ref, *refs):
    atts, ups, out_ref = refs[:4], refs[4:8], refs[8]
    total = lax.dot_general(atts[0][...], ups[0][...], TN, preferred_element_type=F32)
    for k in range(1, 4):
        total += lax.dot_general(atts[k][...], ups[k][...], TN, preferred_element_type=F32)
    out_ref[...] = total.astype(out_ref.dtype)


def weight_gradient(scalars, atts, ups, mate, kind):
    half = ups[0].shape[1] // 2
    step = 256
    steps = half // step

    def column(i, b):
        co = 1 - b[3] if mate else b[3]
        return (0, co * steps + i)

    return pl.pallas_call(
        gradient_kernel,
        grid_spec=pltpu.PrefetchScalarGridSpec(
            num_scalar_prefetch=1,
            grid=(steps,),
            in_specs=[whole((TILE, GROUP))] * 4 + [pl.BlockSpec((TILE, step), column)] * 4,
            out_specs=pl.BlockSpec((GROUP, step), lambda i, b: (0, i)),
        ),
        out_shape=jax.ShapeDtypeStruct((GROUP, half), kind),
        compiler_params=PARAMS,
        cost_estimate=pl.CostEstimate(
            flops=8 * TILE * GROUP * half, bytes_accessed=8 * TILE * (GROUP + half), transcendentals=0
        ),
    )(scalars, *atts, *ups)


def mixed_kernel(*refs):
    atts, weight_ref, outs = refs[:4], refs[4], refs[5:]
    for att, out in zip(atts, outs):
        out[...] = jnp.dot(att[...], weight_ref[...], preferred_element_type=F32).astype(out.dtype)


def mixed_parts(atts, weight):
    dout = weight.shape[1]
    step = 512
    return pl.pallas_call(
        mixed_kernel,
        grid=(dout // step,),
        in_specs=[whole((TILE, GROUP))] * 4 + [pl.BlockSpec((GROUP, step), lambda i: (0, i))],
        out_specs=[pl.BlockSpec((TILE, step), lambda i: (0, i))] * 4,
        out_shape=[jax.ShapeDtypeStruct((TILE, dout), F32)]
        + [jax.ShapeDtypeStruct((TILE, dout), BF16)] * 3,
        compiler_params=PARAMS,
        cost_estimate=pl.CostEstimate(
            flops=8 * TILE * GROUP * dout, bytes_accessed=10 * TILE * dout, transcendentals=0
        ),
    )(*atts, weight)


SWAP = [(0, 1), (1, 0)]
CROSS = [(1, 2), (2, 1)]


def shifted(x, axis, by):
    count = lax.axis_size(axis)
    return lax.ppermute(x, axis, [(i, (i + by) % count) for i in range(count)])


def per_device(queries, keys_values, upstream, out_weight, block_pick):
    width = queries.shape[4]
    dout = upstream.shape[4]
    half = dout // 2
    rows = out_weight.shape[1]
    ny = lax.axis_size("y")
    nz = lax.axis_size("z")
    wa = ("z", "y")
    y = lax.axis_index("y")
    z = lax.axis_index("z")
    co = lax.axis_index("co")
    first = co == 0
    q = queries.reshape(TILE, width)
    kv = keys_values.reshape(2, TILE, width)
    up = upstream.reshape(TILE, dout)

    has_cross = lax.axis_index("xh") != co
    bound = jnp.where(has_cross, SLOTS * TILE, (SLOTS - 1) * TILE)
    scalars = jnp.stack([bound, y, z, co]).astype(jnp.int32)

    parts = 2
    groups = HEADS // PER_STEP // parts
    part = groups * GROUP
    pieces = [lax.slice_in_dim(kv, c * part, (c + 1) * part, axis=2) for c in range(parts)]
    from_core = lax.ppermute(kv, "co", SWAP)
    kvs = []
    for piece in pieces:
        from_time = lax.ppermute(piece, "xl", SWAP)
        from_cross = lax.ppermute(piece, ("xh", "co"), CROSS)
        kvs.append((kv, from_time, from_core, from_cross))

    panel = lax.dynamic_slice(out_weight, (block_pick[0], 0, co * half), (1, rows, half))[0]
    w_pieces = [
        lax.ppermute(panel, wa, [(s, ny * ((s + k) % nz) + s // nz) for s in range(nz * ny)])
        for k in range(nz)
    ]
    w_mine = ordered(scalars, w_pieces)
    ups = [up] + [shifted(up, "y", k) for k in range(1, ny)]
    w_mate = lax.ppermute(w_mine, "co", SWAP)
    *d_parts, w_rows = d_attention(scalars, ups, w_mine, w_mate)
    d_pieces = d_parts[:1] + [shifted(d_parts[k], "y", -k) for k in range(1, ny)]

    att_parts = [
        attention_forward(scalars, q, kvs[c], c * groups, groups) for c in range(parts)
    ]
    att = jnp.concatenate(att_parts, axis=1)
    att_y = [
        lax.dynamic_slice_in_dim(att, lax.rem(y + k, ny) * GROUP, GROUP, axis=1) for k in range(ny)
    ]
    att_y = att_y[:1] + [shifted(att_y[k], "y", k) for k in range(1, ny)]

    grad_mate = weight_gradient(scalars, att_y, ups, True, BF16)
    grad_mine = weight_gradient(scalars, att_y, ups, False, F32)
    from_mate = lax.ppermute(grad_mate, "co", SWAP)
    grad = (grad_mine + from_mate.astype(F32)).astype(BF16).reshape(nz, rows, half)
    over_z = 0.0
    for k in range(nz):
        piece = lax.dynamic_index_in_dim(grad, lax.rem(z + k, nz), 0, keepdims=False)
        pairs = [(ny * zz + yy, nz * yy + (zz + k) % nz) for zz in range(nz) for yy in range(ny)]
        over_z = over_z + lax.ppermute(piece, wa, pairs).astype(F32)
    over_z = over_z.astype(BF16)
    x_near = lax.ppermute(over_z, "xl", SWAP)
    x_far = lax.ppermute(over_z, "xh", SWAP)
    x_both = lax.ppermute(over_z, ("xl", "xh"), [(i, 3 - i) for i in range(4)])
    mine = (over_z.astype(F32) + x_near.astype(F32)) + (x_far.astype(F32) + x_both.astype(F32))
    mate = lax.ppermute(mine, "co", SWAP)
    grad_weight = jnp.concatenate(
        [jnp.where(first, mine, mate), jnp.where(first, mate, mine)], axis=1
    )

    gq_parts, gkv_parts = [], []
    for c in range(parts):
        gq, own, to_time, to_core, to_cross = attention_backward(
            scalars, q, kvs[c], att_parts[c], d_pieces, c * groups, groups
        )
        gq_parts.append(gq)
        terms = (
            lax.ppermute(to_time, "xl", SWAP),
            lax.ppermute(to_cross, ("xh", "co"), CROSS),
            lax.ppermute(to_core, "co", SWAP),
        )
        gkv_parts.append(own + sum(t.astype(F32) for t in terms))
    grad_q = jnp.concatenate(gq_parts, axis=1)
    grad_kv = jnp.concatenate([p.astype(BF16) for p in gkv_parts], axis=2)

    m_mine, *m_others = mixed_parts(att_y, w_rows)
    for k in range(1, ny):
        m_mine = m_mine + shifted(m_others[k - 1], "y", -k).astype(F32)
    return (
        m_mine.astype(BF16).reshape(upstream.shape),
        grad_q.reshape(queries.shape),
        grad_kv.reshape(keys_values.shape),
        grad_weight,
    )


def solution(mesh):
    fine = Mesh(mesh.devices.reshape(2, 2, 2, 8, 4), ("xl", "xh", "co", "z", "y"))
    wa = ("z", "y")
    ha = ("xh", "co")
    return jax.shard_map(
        per_device,
        mesh=fine,
        in_specs=(
            P(wa, "xl", ha, None, None),
            P(None, wa, "xl", ha, None, None),
            P(wa, "xl", ha, None, None),
            P(None, wa, None),
            P(),
        ),
        out_specs=(
            P(wa, "xl", ha, None, None),
            P(wa, "xl", ha, None, None),
            P(None, wa, "xl", ha, None, None),
            P(wa, None),
        ),
        check_vma=False,
    )
```

time: 213 us -> 267 us (1.25); the launches traced: 212 us -> 262 us
  starting transfers between devices: 40.5 us -> 139 us
  waiting for transfers between devices: 80.5 us -> 43.8 us
  blocking collectives: 25.2 us -> 0 us
  local copies, waits for them, and re-layouts: 7.75 us -> 32.3 us
  Pallas kernels: 21.6 us -> 36.9 us
  between operations: 15 us -> 1.99 us
  matrix products: 11.3 us -> 0 us
  other arithmetic: 10.1 us -> 7.29 us
    ppermute x14 -> x40, starting transfers between devices: 21.1 us -> 130 us  [the longest x8 40.2 us: per_device(): lax.ppermute(panel, wa, [(s, ny * ((s + k) % nz) + s // nz) for s in rang...]
    all_to_all x1 -> x0, blocking collectives: 25.2 us -> none  [per_device(): lax.all_to_all(total_w.astype(BF16), 'z', split_axis=0, concat_axis=0, ti...]
    unnamed x14 -> x108, local copies, waits for them, and re-layouts: 4.25 us -> 29.2 us
    ppermute x14 -> x40, waiting for transfers between devices: 63.1 us -> 40.8 us  [the longest x12 28.2 us: shifted(): return lax.ppermute(x, axis, [(i, (i + by) % count) for i in range(count)])]
    pallas_call x2 -> x7, Pallas kernels: 13.6 us -> 27.2 us  [the longest x2 15.2 us: attention_backward(): pl.pallas_call(functools.partial(backward_kernel, first), grid_spec=pltpu...]
    ppermute x1, starting transfers between devices: 13.3 us -> 0.01 us  [per_device(): w_mate = lax.ppermute(w_mine, 'co', SWAP)]
    all_gather x1 -> x0, waiting for transfers between devices: 13 us -> none  [per_device(): w_mine = lax.all_gather(panel, ('z', 'y'), axis=0, tiled=True)]
    dot_general x6 -> x0, matrix products: 11.3 us -> none  [the longest x1 2.81 us: per_device(): lax.dot_general(up_mate, w_mate, NT, preferred_element_type=F32)]
  transfers between devices with their start and end apart: 20 -> 45, of which waited for: 12 -> 14; matrix products, arithmetic and copies ran while one was open for 9% -> 4% of each run, Pallas kernels for 7% -> 14%
where the time goes in v2:
time: 267 us; the launch traced here: 262 us
  starting transfers between devices  139 us (52%)
  waiting for transfers between devices  43.8 us (16%)
  Pallas kernels  36.9 us (14%)
  local copies, waits for them, and re-layouts  32.3 us (12%)
  other arithmetic  7.29 us (3%)
    ppermute x8, starting transfers between devices, per_device(): lax.ppermute(panel, wa, [(s, ny * ((s + k) % nz) + s // nz) for s in rang...  40.2 us
    ppermute x8, starting transfers between devices, per_device(): over_z = over_z + lax.ppermute(piece, wa, pairs).astype(F32)  33.5 us
    unnamed x108, local copies, waits for them, and re-layouts  29.2 us
    ppermute x12, waiting for transfers between devices, shifted(): return lax.ppermute(x, axis, [(i, (i + by) % count) for i in range(count)])  28.2 us
    ppermute x12, starting transfers between devices, shifted(): return lax.ppermute(x, axis, [(i, (i + by) % count) for i in range(count)])  26.9 us
    pallas_call x2, Pallas kernels, attention_backward(): pl.pallas_call(functools.partial(backward_kernel, first), grid_spec=pltpu...  15.2 us
    ppermute x8, waiting for transfers between devices, per_device(): lax.ppermute(panel, wa, [(s, ny * ((s + k) % nz) + s // nz) for s in rang...  12.5 us
    ppermute x2, starting transfers between devices, per_device(): from_cross = lax.ppermute(piece, ('xh', 'co'), CROSS)  11.5 us
  transfers between devices with their start and end apart: 45, of which 14 were waited for; matrix products, arithmetic and copies ran while one was open for 4% of the time, Pallas kernels for 14%

profile of v2, /device:TPU:1, one launch (start us, length us, event | category | flops | bytes accessed | tf_op | source)
XLA Modules:
  0.0 261.7 jit_solution(4594024787011935079)
XLA Ops:
  6.3 8.6 %collective-permute-start.12 = (bf16[48,768]{1,0:T(8,128)(2,1)S(1)}, bf16[48,768]{1,0:T(8,128)(2,1)S(1)}, u32[]{:S(2)}, u32[]{:S(2)}) collective-permute-start(bf16[48,768]{1,0:T(8,128)(2,1)S(1)} %dynamic-slice_bitcast_fusion.8), channel_id=1, source_target_pairs={{0,4},{1,8},{2,12},{3,16},{4,20},{5,24},{6,28},{7,0},{8,5},{9,9},{... | collective-permute-start | bytes 221192 | tf_op jit(solution)/shard_map/ppermute | solution.py:289
  18.3 5.1 %collective-permute-start.4 = (bf16[2,192,768]{2,1,0:T(8,128)(2,1)S(1)}, bf16[2,192,768]{2,1,0:T(8,128)(2,1)S(1)}, u32[]{:S(2)}, u32[]{:S(2)}) collective-permute-start(bf16[2,192,768]{2,1,0:T(8,128)(2,1)S(1)} %get-tuple-element.46), channel_id=1, source_target_pairs={{32,64},{64,32},{33,65},{65,33},{34,66},{66,34},{35,67},{67,35},{3... | collective-permute-start | bytes 1769480 | tf_op jit(solution)/shard_map/ppermute | solution.py:284
  24.0 4.4 %collective-permute-start.13 = (bf16[48,768]{1,0:T(8,128)(2,1)S(1)}, bf16[48,768]{1,0:T(8,128)(2,1)S(1)}, u32[]{:S(2)}, u32[]{:S(2)}) collective-permute-start(bf16[48,768]{1,0:T(8,128)(2,1)S(1)} %dynamic-slice_bitcast_fusion.8), channel_id=1, source_target_pairs={{0,8},{1,12},{2,16},{3,20},{4,24},{5,28},{6,0},{7,4},{8,9},{9,13},... | collective-permute-start | bytes 221192 | tf_op jit(solution)/shard_map/ppermute | solution.py:289
  29.1 5.6 %collective-permute-start.14 = (bf16[48,768]{1,0:T(8,128)(2,1)S(1)}, bf16[48,768]{1,0:T(8,128)(2,1)S(1)}, u32[]{:S(2)}, u32[]{:S(2)}) collective-permute-start(bf16[48,768]{1,0:T(8,128)(2,1)S(1)} %dynamic-slice_bitcast_fusion.8), channel_id=1, source_target_pairs={{0,12},{1,16},{2,20},{3,24},{4,28},{5,0},{6,4},{7,8},{8,13},{9,17}... | collective-permute-start | bytes 221192 | tf_op jit(solution)/shard_map/ppermute | solution.py:289
  35.3 8.1 %collective-permute-start.15 = (bf16[48,768]{1,0:T(8,128)(2,1)S(1)}, bf16[48,768]{1,0:T(8,128)(2,1)S(1)}, u32[]{:S(2)}, u32[]{:S(2)}) collective-permute-start(bf16[48,768]{1,0:T(8,128)(2,1)S(1)} %dynamic-slice_bitcast_fusion.8), channel_id=1, source_target_pairs={{0,16},{1,20},{2,24},{3,28},{4,0},{5,4},{6,8},{7,12},{8,17},{9,21}... | collective-permute-start | bytes 221192 | tf_op jit(solution)/shard_map/ppermute | solution.py:289
  52.3 4.9 %collective-permute-start.17 = (bf16[48,768]{1,0:T(8,128)(2,1)S(1)}, bf16[48,768]{1,0:T(8,128)(2,1)S(1)}, u32[]{:S(2)}, u32[]{:S(2)}) collective-permute-start(bf16[48,768]{1,0:T(8,128)(2,1)S(1)} %dynamic-slice_bitcast_fusion.8), channel_id=1, source_target_pairs={{0,24},{1,28},{2,0},{3,4},{4,8},{5,12},{6,16},{7,20},{8,25},{9,29}... | collective-permute-start | bytes 221192 | tf_op jit(solution)/shard_map/ppermute | solution.py:289
  57.3 7.1 %collective-permute-done.17.refs_6_ = bf16[48,768]{1,0:T(8,128)(2,1)S(1)} collective-permute-done((bf16[48,768]{1,0:T(8,128)(2,1)S(1)}, bf16[48,768]{1,0:T(8,128)(2,1)S(1)}, u32[]{:S(2)}, u32[]{:S(2)}) %collective-permute-start.17) | collective-permute-done | bytes 73760 | tf_op jit(solution)/shard_map/ppermute | solution.py:289
  71.9 6.4 %collective-permute-start.2 = (bf16[2,192,768]{2,1,0:T(8,128)(2,1)}, bf16[2,192,768]{2,1,0:T(8,128)(2,1)}, u32[]{:S(2)}, u32[]{:S(2)}) collective-permute-start(bf16[2,192,768]{2,1,0:T(8,128)(2,1)} %get-tuple-element.47), channel_id=1, source_target_pairs={{32,64},{64,32},{33,65},{65,33},{34,66},{66,34},{35,67},{67,35},{3... | collective-permute-start | bytes 1769480 | tf_op jit(solution)/shard_map/ppermute | solution.py:284
  79.1 4.5 %collective-permute-start.10 = (bf16[192,1536]{1,0:T(8,128)(2,1)S(1)}, bf16[192,1536]{1,0:T(8,128)(2,1)S(1)}, u32[]{:S(2)}, u32[]{:S(2)}) collective-permute-start(bf16[192,1536]{1,0:T(8,128)(2,1)S(1)} %bitcast.44), channel_id=1, source_target_pairs={{0,3},{1,0},{2,1},{3,2},{4,7},{5,4},{6,5},{7,6},{8,11},{9,8},{10,9... | collective-permute-start | bytes 1769480 | tf_op jit(solution)/shard_map/ppermute | solution.py:253
  85.3 6.7 %collective-permute-start.9 = (bf16[192,1536]{1,0:T(8,128)(2,1)S(1)}, bf16[192,1536]{1,0:T(8,128)(2,1)S(1)}, u32[]{:S(2)}, u32[]{:S(2)}) collective-permute-start(bf16[192,1536]{1,0:T(8,128)(2,1)S(1)} %bitcast.46), channel_id=1, source_target_pairs={{0,2},{1,3},{2,0},{3,1},{4,6},{5,7},{6,4},{7,5},{8,10},{9,11},{10,... | collective-permute-start | bytes 1769480 | tf_op jit(solution)/shard_map/ppermute | solution.py:253
  103.7 4.8 %shard_map.85.att_ref = bf16[192,768]{1,0:T(8,128)(2,1)S(1)} custom-call(s32[4]{0:T(128)S(1)} %pad_add_fusion.bound_ref.scalar_ref, bf16[192,1536]{1,0:T(8,128)(2,1)S(1)} %bitcast.50, bf16[2,192,1536]{2,1,0:T(8,128)(2,1)S(1)} %bitcast.40, bf16[2,192,768]{2,1,0:T(8,128)(2,1)S(1)} %copy-done.12, bf16[2,192,1536]{2,1,0:T(8,128)(2,1)} %collective-permute-done.1.core_ref, ...), custom_call_target="tpu_custom_call" | custom-call | flops 452984832 | bytes 2949120 | tf_op jit(solution)/shard_map/pallas_call | solution.py:91
  108.5 4.9 %shard_map.84.att_ref = bf16[192,768]{1,0:T(8,128)(2,1)S(1)} custom-call(s32[4]{0:T(128)S(1)} %pad_add_fusion.bound_ref.scalar_ref, bf16[192,1536]{1,0:T(8,128)(2,1)S(1)} %bitcast.51, bf16[2,192,1536]{2,1,0:T(8,128)(2,1)S(1)} %bitcast.41, bf16[2,192,768]{2,1,0:T(8,128)(2,1)S(1)} %copy-done.18, bf16[2,192,1536]{2,1,0:T(8,128)(2,1)} %collective-permute-done.1.core_ref, ...), custom_call_target="tpu_custom_call" | custom-call | flops 452984832 | bytes 2949120 | tf_op jit(solution)/shard_map/pallas_call | solution.py:91
  135.6 5.7 %collective-permute-done.23.rest_1_ = bf16[192,384]{1,0:T(8,128)(2,1)S(1)} collective-permute-done((bf16[192,384]{1,0:T(8,128)(2,1)S(1)}, bf16[192,384]{1,0:T(8,128)(2,1)S(1)}, u32[]{:S(2)}, u32[]{:S(2)}) %collective-permute-start.23) | collective-permute-done | bytes 147488 | tf_op jit(solution)/shard_map/ppermute | solution.py:253
  144.9 8.0 %shard_map.89 = (bf16[192,768]{1,0:T(8,128)(2,1)S(1)}, f32[2,192,768]{2,1,0:T(8,128)S(1)}, bf16[2,192,768]{2,1,0:T(8,128)(2,1)}, bf16[2,192,768]{2,1,0:T(8,128)(2,1)S(1)}, bf16[2,192,768]{2,1,0:T(8,128)(2,1)}) custom-call(s32[4]{0:T(128)S(1)} %pad_add_fusion.bound_ref.scalar_ref, bf16[192,1536]{1,0:T(8,128)(2,1)S(1)} %bitcast.52, ...), custom_call_target="tpu_custom_call" | custom-call | flops 1358954496 | bytes 7077888 | tf_op jit(solution)/shard_map/pallas_call | solution.py:111
  156.0 4.4 %collective-permute-start.27 = (bf16[2,192,768]{2,1,0:T(8,128)(2,1)}, bf16[2,192,768]{2,1,0:T(8,128)(2,1)}, u32[]{:S(2)}, u32[]{:S(2)}) collective-permute-start(bf16[2,192,768]{2,1,0:T(8,128)(2,1)} %get-tuple-element.36), channel_id=1, source_target_pairs={{32,64},{64,32},{33,65},{65,33},{34,66},{66,34},{35,67},{67,35},{3... | collective-permute-start | bytes 1769480 | tf_op jit(solution)/shard_map/ppermute | solution.py:334
  168.3 7.2 %shard_map.90 = (bf16[192,768]{1,0:T(8,128)(2,1)S(1)}, f32[2,192,768]{2,1,0:T(8,128)S(1)}, bf16[2,192,768]{2,1,0:T(8,128)(2,1)S(1)}, bf16[2,192,768]{2,1,0:T(8,128)(2,1)S(1)}, bf16[2,192,768]{2,1,0:T(8,128)(2,1)S(1)}) custom-call(s32[4]{0:T(128)S(1)} %pad_add_fusion.bound_ref.scalar_ref, bf16[192,1536]{1,0:T(8,128)(2,1)S(1)} %bitcast.53, ...), custom_call_target="tpu_custom_call" | custom-call | flops 1358954496 | bytes 7077888 | tf_op jit(solution)/shard_map/pallas_call | solution.py:111
  183.3 9.1 %collective-permute-start.35 = (bf16[48,768]{1,0:T(8,128)(2,1)S(1)}, bf16[48,768]{1,0:T(8,128)(2,1)S(1)}, u32[]{:S(2)}, u32[]{:S(2)}) collective-permute-start(bf16[48,768]{1,0:T(8,128)(2,1)S(1)} %get-tuple-element.54), channel_id=1, source_target_pairs={{0,2},{1,10},{2,18},{3,26},{4,3},{5,11},{6,19},{7,27},{8,4},{9,12}... | collective-permute-start | bytes 221192 | tf_op jit(solution)/shard_map/ppermute | solution.py:315
  195.5 6.1 %collective-permute-start.30 = (bf16[2,192,768]{2,1,0:T(8,128)(2,1)S(1)}, bf16[2,192,768]{2,1,0:T(8,128)(2,1)S(1)}, u32[]{:S(2)}, u32[]{:S(2)}) collective-permute-start(bf16[2,192,768]{2,1,0:T(8,128)(2,1)S(1)} %get-tuple-element.40), channel_id=1, source_target_pairs={{32,64},{64,32},{33,65},{65,33},{34,66},{66,34},{35,67},{67,35},{3... | collective-permute-start | bytes 1769480 | tf_op jit(solution)/shard_map/ppermute | solution.py:334
  202.0 4.9 %collective-permute-start.37 = (bf16[48,768]{1,0:T(8,128)(2,1)S(1)}, bf16[48,768]{1,0:T(8,128)(2,1)S(1)}, u32[]{:S(2)}, u32[]{:S(2)}) collective-permute-start(bf16[48,768]{1,0:T(8,128)(2,1)S(1)} %get-tuple-element.52), channel_id=1, source_target_pairs={{0,4},{1,12},{2,20},{3,28},{4,5},{5,13},{6,21},{7,29},{8,6},{9,14}... | collective-permute-start | bytes 221192 | tf_op jit(solution)/shard_map/ppermute | solution.py:315
  206.9 4.4 %collective-permute-start.38 = (bf16[48,768]{1,0:T(8,128)(2,1)S(1)}, bf16[48,768]{1,0:T(8,128)(2,1)S(1)}, u32[]{:S(2)}, u32[]{:S(2)}) collective-permute-start(bf16[48,768]{1,0:T(8,128)(2,1)S(1)} %get-tuple-element.51), channel_id=1, source_target_pairs={{0,5},{1,13},{2,21},{3,29},{4,6},{5,14},{6,22},{7,30},{8,7},{9,15}... | collective-permute-start | bytes 221192 | tf_op jit(solution)/shard_map/ppermute | solution.py:315
  213.3 5.9 %collective-permute-start.39 = (bf16[48,768]{1,0:T(8,128)(2,1)S(1)}, bf16[48,768]{1,0:T(8,128)(2,1)S(1)}, u32[]{:S(2)}, u32[]{:S(2)}) collective-permute-start(bf16[48,768]{1,0:T(8,128)(2,1)S(1)} %get-tuple-element.50), channel_id=1, source_target_pairs={{0,6},{1,14},{2,22},{3,30},{4,7},{5,15},{6,23},{7,31},{8,0},{9,8},... | collective-permute-start | bytes 221192 | tf_op jit(solution)/shard_map/ppermute | solution.py:315
  227.9 5.5 %collective-permute-start.21 = (bf16[192,1536]{1,0:T(8,128)(2,1)S(1)}, bf16[192,1536]{1,0:T(8,128)(2,1)S(1)}, u32[]{:S(2)}, u32[]{:S(2)}) collective-permute-start(bf16[192,1536]{1,0:T(8,128)(2,1)S(1)} %get-tuple-element.26), channel_id=1, source_target_pairs={{0,2},{1,3},{2,0},{3,1},{4,6},{5,7},{6,4},{7,5},{8,10},{9,11},{10,... | collective-permute-start | bytes 1769480 | tf_op jit(solution)/shard_map/ppermute | solution.py:253
  242.8 5.0 %collective-permute-start.44 = (f32[48,768]{1,0:T(8,128)S(1)}, f32[48,768]{1,0:T(8,128)S(1)}, u32[]{:S(2)}, u32[]{:S(2)}) collective-permute-start(f32[48,768]{1,0:T(8,128)S(1)} %add_add_fusion), channel_id=1, source_target_pairs={{0,32},{32,0},{1,33},{33,1},{2,34},{34,2},{3,35},{35,3},{4,36},{36... | collective-permute-start | bytes 442376 | tf_op jit(solution)/shard_map/ppermute | solution.py:321
  247.8 12.1 %collective-permute-done.22 = bf16[192,1536]{1,0:T(8,128)(2,1)S(1)} collective-permute-done((bf16[192,1536]{1,0:T(8,128)(2,1)S(1)}, bf16[192,1536]{1,0:T(8,128)(2,1)S(1)}, u32[]{:S(2)}, u32[]{:S(2)}) %collective-permute-start.22) | collective-permute-done | bytes 589856 | tf_op jit(solution)/shard_map/ppermute | solution.py:253
  (198 shorter events, 110.4 us)
Async XLA Ops:
  0.6 99.9 %collective-permute-start.1 = (bf16[2,192,1536]{2,1,0:T(8,128)(2,1)}, bf16[2,192,1536]{2,1,0:T(8,128)(2,1)}, u32[]{:S(2)}, u32[]{:S(2)}) collective-permute-start(bf16[2,192,1536]{2,1,0:T(8,128)(2,1)} %bitcast.38), channel_id=1, source_target_pairs={{0,32},{32,0},{1,33},{33,1},{2,34},{34,2},{3,35},{35,3},{4,36},{36... | collective-permute-start | bytes 3538952 | tf_op jit(solution)/shard_map/ppermute | solution.py:280
  5.5 17.9 %collective-permute-start.11 = (bf16[48,768]{1,0:T(8,128)(2,1)S(1)}, bf16[48,768]{1,0:T(8,128)(2,1)S(1)}, u32[]{:S(2)}, u32[]{:S(2)}) collective-permute-start(bf16[48,768]{1,0:T(8,128)(2,1)S(1)} %dynamic-slice_bitcast_fusion.8), channel_id=1, source_target_pairs={{0,0},{1,4},{2,8},{3,12},{4,16},{5,20},{6,24},{7,28},{8,1},{9,5},{... | collective-permute-start | bytes 221192 | tf_op jit(solution)/shard_map/ppermute | solution.py:289
  6.3 22.2 %collective-permute-start.12 = (bf16[48,768]{1,0:T(8,128)(2,1)S(1)}, bf16[48,768]{1,0:T(8,128)(2,1)S(1)}, u32[]{:S(2)}, u32[]{:S(2)}) collective-permute-start(bf16[48,768]{1,0:T(8,128)(2,1)S(1)} %dynamic-slice_bitcast_fusion.8), channel_id=1, source_target_pairs={{0,4},{1,8},{2,12},{3,16},{4,20},{5,24},{6,28},{7,0},{8,5},{9,9},{... | collective-permute-start | bytes 221192 | tf_op jit(solution)/shard_map/ppermute | solution.py:289
  17.1 61.2 %collective-permute-start.3 = (bf16[2,192,768]{2,1,0:T(8,128)(2,1)S(1)}, bf16[2,192,768]{2,1,0:T(8,128)(2,1)S(1)}, u32[]{:S(2)}, u32[]{:S(2)}) collective-permute-start(bf16[2,192,768]{2,1,0:T(8,128)(2,1)S(1)} %get-tuple-element.46), channel_id=1, source_target_pairs={{0,128},{128,0},{1,129},{129,1},{2,130},{130,2},{3,131},{131,3},{4... | collective-permute-start | bytes 1769480 | tf_op jit(solution)/shard_map/ppermute | solution.py:283
  18.3 65.3 %collective-permute-start.4 = (bf16[2,192,768]{2,1,0:T(8,128)(2,1)S(1)}, bf16[2,192,768]{2,1,0:T(8,128)(2,1)S(1)}, u32[]{:S(2)}, u32[]{:S(2)}) collective-permute-start(bf16[2,192,768]{2,1,0:T(8,128)(2,1)S(1)} %get-tuple-element.46), channel_id=1, source_target_pairs={{32,64},{64,32},{33,65},{65,33},{34,66},{66,34},{35,67},{67,35},{3... | collective-permute-start | bytes 1769480 | tf_op jit(solution)/shard_map/ppermute | solution.py:284
  44.0 40.4 %collective-permute-start = (bf16[2,192,768]{2,1,0:T(8,128)(2,1)}, bf16[2,192,768]{2,1,0:T(8,128)(2,1)S(1)}, u32[]{:S(2)}, u32[]{:S(2)}) collective-permute-start(bf16[2,192,768]{2,1,0:T(8,128)(2,1)} %get-tuple-element.47), channel_id=1, source_target_pairs={{0,128},{128,0},{1,129},{129,1},{2,130},{130,2},{3,131},{131,3},{4... | collective-permute-start | bytes 1769480 | tf_op jit(solution)/shard_map/ppermute | solution.py:283
  71.9 36.7 %collective-permute-start.2 = (bf16[2,192,768]{2,1,0:T(8,128)(2,1)}, bf16[2,192,768]{2,1,0:T(8,128)(2,1)}, u32[]{:S(2)}, u32[]{:S(2)}) collective-permute-start(bf16[2,192,768]{2,1,0:T(8,128)(2,1)} %get-tuple-element.47), channel_id=1, source_target_pairs={{32,64},{64,32},{33,65},{65,33},{34,66},{66,34},{35,67},{67,35},{3... | collective-permute-start | bytes 1769480 | tf_op jit(solution)/shard_map/ppermute | solution.py:284
  79.1 34.7 %collective-permute-start.10 = (bf16[192,1536]{1,0:T(8,128)(2,1)S(1)}, bf16[192,1536]{1,0:T(8,128)(2,1)S(1)}, u32[]{:S(2)}, u32[]{:S(2)}) collective-permute-start(bf16[192,1536]{1,0:T(8,128)(2,1)S(1)} %bitcast.44), channel_id=1, source_target_pairs={{0,3},{1,0},{2,1},{3,2},{4,7},{5,4},{6,5},{7,6},{8,11},{9,8},{10,9... | collective-permute-start | bytes 1769480 | tf_op jit(solution)/shard_map/ppermute | solution.py:253
  84.4 31.2 %collective-permute-start.8 = (bf16[192,1536]{1,0:T(8,128)(2,1)S(1)}, bf16[192,1536]{1,0:T(8,128)(2,1)S(1)}, u32[]{:S(2)}, u32[]{:S(2)}) collective-permute-start(bf16[192,1536]{1,0:T(8,128)(2,1)S(1)} %bitcast.45), channel_id=1, source_target_pairs={{0,1},{1,2},{2,3},{3,0},{4,5},{5,6},{6,7},{7,4},{8,9},{9,10},{10,1... | collective-permute-start | bytes 1769480 | tf_op jit(solution)/shard_map/ppermute | solution.py:253
  85.3 31.3 %collective-permute-start.9 = (bf16[192,1536]{1,0:T(8,128)(2,1)S(1)}, bf16[192,1536]{1,0:T(8,128)(2,1)S(1)}, u32[]{:S(2)}, u32[]{:S(2)}) collective-permute-start(bf16[192,1536]{1,0:T(8,128)(2,1)S(1)} %bitcast.46), channel_id=1, source_target_pairs={{0,2},{1,3},{2,0},{3,1},{4,6},{5,7},{6,4},{7,5},{8,10},{9,11},{10,... | collective-permute-start | bytes 1769480 | tf_op jit(solution)/shard_map/ppermute | solution.py:253
  100.5 27.8 %collective-permute-start.19 = (bf16[384,768]{1,0:T(8,128)(2,1)}, bf16[384,768]{1,0:T(8,128)(2,1)}, u32[]{:S(2)}, u32[]{:S(2)}) collective-permute-start(bf16[384,768]{1,0:T(8,128)(2,1)} %shard_map.86.refs_4_), channel_id=1, source_target_pairs={{0,32},{32,0},{1,33},{33,1},{2,34},{34,2},{3,35},{35,3},{4,36},{36... | collective-permute-start | bytes 1769480 | tf_op jit(solution)/shard_map/ppermute | solution.py:294
  126.4 51.3 %collective-permute-start.32 = (bf16[384,768]{1,0:T(8,128)(2,1)}, bf16[384,768]{1,0:T(8,128)(2,1)}, u32[]{:S(2)}, u32[]{:S(2)}) collective-permute-start(bf16[384,768]{1,0:T(8,128)(2,1)} %shard_map.92), channel_id=1, source_target_pairs={{0,32},{32,0},{1,33},{33,1},{2,34},{34,2},{3,35},{35,3},{4,36},{36... | collective-permute-start | bytes 1769480 | tf_op jit(solution)/shard_map/ppermute | solution.py:309
  155.5 27.8 %collective-permute-start.26 = (bf16[2,192,768]{2,1,0:T(8,128)(2,1)}, bf16[2,192,768]{2,1,0:T(8,128)(2,1)}, u32[]{:S(2)}, u32[]{:S(2)}) collective-permute-start(bf16[2,192,768]{2,1,0:T(8,128)(2,1)} %get-tuple-element.35), channel_id=1, source_target_pairs={{0,128},{128,0},{1,129},{129,1},{2,130},{130,2},{3,131},{131,3},{4... | collective-permute-start | bytes 1769480 | tf_op jit(solution)/shard_map/ppermute | solution.py:333
  156.0 36.4 %collective-permute-start.27 = (bf16[2,192,768]{2,1,0:T(8,128)(2,1)}, bf16[2,192,768]{2,1,0:T(8,128)(2,1)}, u32[]{:S(2)}, u32[]{:S(2)}) collective-permute-start(bf16[2,192,768]{2,1,0:T(8,128)(2,1)} %get-tuple-element.36), channel_id=1, source_target_pairs={{32,64},{64,32},{33,65},{65,33},{34,66},{66,34},{35,67},{67,35},{3... | collective-permute-start | bytes 1769480 | tf_op jit(solution)/shard_map/ppermute | solution.py:334
  160.4 34.8 %collective-permute-start.28 = (bf16[2,192,768]{2,1,0:T(8,128)(2,1)}, bf16[2,192,768]{2,1,0:T(8,128)(2,1)S(1)}, u32[]{:S(2)}, u32[]{:S(2)}) collective-permute-start(bf16[2,192,768]{2,1,0:T(8,128)(2,1)} %copy-done.45), channel_id=1, source_target_pairs={{0,32},{32,0},{1,33},{33,1},{2,34},{34,2},{3,35},{35,3},{4,36},{36... | collective-permute-start | bytes 1769480 | tf_op jit(solution)/shard_map/ppermute | solution.py:335
  179.8 21.8 %collective-permute-start.34 = (bf16[48,768]{1,0:T(8,128)(2,1)S(1)}, bf16[48,768]{1,0:T(8,128)(2,1)S(1)}, u32[]{:S(2)}, u32[]{:S(2)}) collective-permute-start(bf16[48,768]{1,0:T(8,128)(2,1)S(1)} %get-tuple-element.55), channel_id=1, source_target_pairs={{0,1},{1,9},{2,17},{3,25},{4,2},{5,10},{6,18},{7,26},{8,3},{9,11},... | collective-permute-start | bytes 221192 | tf_op jit(solution)/shard_map/ppermute | solution.py:315
  183.3 18.7 %collective-permute-start.35 = (bf16[48,768]{1,0:T(8,128)(2,1)S(1)}, bf16[48,768]{1,0:T(8,128)(2,1)S(1)}, u32[]{:S(2)}, u32[]{:S(2)}) collective-permute-start(bf16[48,768]{1,0:T(8,128)(2,1)S(1)} %get-tuple-element.54), channel_id=1, source_target_pairs={{0,2},{1,10},{2,18},{3,26},{4,3},{5,11},{6,19},{7,27},{8,4},{9,12}... | collective-permute-start | bytes 221192 | tf_op jit(solution)/shard_map/ppermute | solution.py:315
  195.2 38.3 %collective-permute-start.29 = (bf16[2,192,768]{2,1,0:T(8,128)(2,1)S(1)}, bf16[2,192,768]{2,1,0:T(8,128)(2,1)S(1)}, u32[]{:S(2)}, u32[]{:S(2)}) collective-permute-start(bf16[2,192,768]{2,1,0:T(8,128)(2,1)S(1)} %get-tuple-element.39), channel_id=1, source_target_pairs={{0,128},{128,0},{1,129},{129,1},{2,130},{130,2},{3,131},{131,3},{4... | collective-permute-start | bytes 1769480 | tf_op jit(solution)/shard_map/ppermute | solution.py:333
  195.5 38.6 %collective-permute-start.30 = (bf16[2,192,768]{2,1,0:T(8,128)(2,1)S(1)}, bf16[2,192,768]{2,1,0:T(8,128)(2,1)S(1)}, u32[]{:S(2)}, u32[]{:S(2)}) collective-permute-start(bf16[2,192,768]{2,1,0:T(8,128)(2,1)S(1)} %get-tuple-element.40), channel_id=1, source_target_pairs={{32,64},{64,32},{33,65},{65,33},{34,66},{66,34},{35,67},{67,35},{3... | collective-permute-start | bytes 1769480 | tf_op jit(solution)/shard_map/ppermute | solution.py:334
  201.7 34.3 %collective-permute-start.31 = (bf16[2,192,768]{2,1,0:T(8,128)(2,1)S(1)}, bf16[2,192,768]{2,1,0:T(8,128)(2,1)S(1)}, u32[]{:S(2)}, u32[]{:S(2)}) collective-permute-start(bf16[2,192,768]{2,1,0:T(8,128)(2,1)S(1)} %get-tuple-element.41), channel_id=1, source_target_pairs={{0,32},{32,0},{1,33},{33,1},{2,34},{34,2},{3,35},{35,3},{4,36},{36... | collective-permute-start | bytes 1769480 | tf_op jit(solution)/shard_map/ppermute | solution.py:335
  223.8 24.0 %collective-permute-start.20 = (bf16[192,1536]{1,0:T(8,128)(2,1)S(1)}, bf16[192,1536]{1,0:T(8,128)(2,1)S(1)}, u32[]{:S(2)}, u32[]{:S(2)}) collective-permute-start(bf16[192,1536]{1,0:T(8,128)(2,1)S(1)} %get-tuple-element.25), channel_id=1, source_target_pairs={{0,3},{1,0},{2,1},{3,2},{4,7},{5,4},{6,5},{7,6},{8,11},{9,8},{10,9... | collective-permute-start | bytes 1769480 | tf_op jit(solution)/shard_map/ppermute | solution.py:253
  227.9 19.9 %collective-permute-start.21 = (bf16[192,1536]{1,0:T(8,128)(2,1)S(1)}, bf16[192,1536]{1,0:T(8,128)(2,1)S(1)}, u32[]{:S(2)}, u32[]{:S(2)}) collective-permute-start(bf16[192,1536]{1,0:T(8,128)(2,1)S(1)} %get-tuple-element.26), channel_id=1, source_target_pairs={{0,2},{1,3},{2,0},{3,1},{4,6},{5,7},{6,4},{7,5},{8,10},{9,11},{10,... | collective-permute-start | bytes 1769480 | tf_op jit(solution)/shard_map/ppermute | solution.py:253
  233.5 26.3 %collective-permute-start.22 = (bf16[192,1536]{1,0:T(8,128)(2,1)S(1)}, bf16[192,1536]{1,0:T(8,128)(2,1)S(1)}, u32[]{:S(2)}, u32[]{:S(2)}) collective-permute-start(bf16[192,1536]{1,0:T(8,128)(2,1)S(1)} %get-tuple-element.27), channel_id=1, source_target_pairs={{0,1},{1,2},{2,3},{3,0},{4,5},{5,6},{6,7},{7,4},{8,9},{9,10},{10,1... | collective-permute-start | bytes 1769480 | tf_op jit(solution)/shard_map/ppermute | solution.py:253
  242.8 18.2 %collective-permute-start.44 = (f32[48,768]{1,0:T(8,128)S(1)}, f32[48,768]{1,0:T(8,128)S(1)}, u32[]{:S(2)}, u32[]{:S(2)}) collective-permute-start(f32[48,768]{1,0:T(8,128)S(1)} %add_add_fusion), channel_id=1, source_target_pairs={{0,32},{32,0},{1,33},{33,1},{2,34},{34,2},{3,35},{35,3},{4,36},{36... | collective-permute-start | bytes 442376 | tf_op jit(solution)/shard_map/ppermute | solution.py:321
  (75 other events, 573.1 us)

commit v3 on v1

v3 whole, which is shorter than its diff:
```python
import jax
import jax.numpy as jnp
from jax import lax
from jax.experimental import pallas as pl
from jax.experimental.pallas import tpu as pltpu
from jax.sharding import Mesh, PartitionSpec as P

HEADS = 12
HEAD_DIM = 128
SCALE = HEAD_DIM ** (-0.5)
TILE = 192
SLOTS = 4
PER_STEP = 3
GROUP = PER_STEP * HEAD_DIM
ROWS = 48
NY = 4
PAD = 256
MASKED = 512
NT = (((1,), (1,)), ((), ()))
TN = (((0,), (0,)), ((), ()))
F32 = jnp.float32
BF16 = jnp.bfloat16
PARAMS = pltpu.CompilerParams(vmem_limit_bytes=56 * 1024 * 1024)


def window_of(refs, which, cols):
    return jnp.concatenate([ref[which, :, cols] for ref in refs], axis=0)


def probs_of(q, k, bound):
    scores = lax.dot_general(q, k, NT, preferred_element_type=F32)
    tail = scores[:, MASKED:]
    column = lax.broadcasted_iota(jnp.int32, tail.shape, 1)
    tail = jnp.where(column + MASKED < bound, tail, -1e30)
    scores = jnp.concatenate([scores[:, :MASKED], tail], axis=1)
    top = jnp.max(scores, axis=1, keepdims=True)
    weights = jnp.exp((scores - top) * SCALE)
    return weights * (1.0 / jnp.sum(weights, axis=1, keepdims=True))


def forward_kernel(scalar_ref, q_ref, own_ref, time_ref, core_ref, cross_ref, out_ref, out_t_ref, probs_ref):
    kv = (own_ref, time_ref, core_ref, cross_ref)
    for h in range(PER_STEP):
        cols = slice(h * HEAD_DIM, (h + 1) * HEAD_DIM)
        k = window_of(kv, 0, cols)
        v = window_of(kv, 1, cols)
        probs = probs_of(q_ref[:, cols], k, scalar_ref[0])
        probs_b = probs.astype(BF16)
        probs_ref[h] = probs_b
        out = jnp.dot(probs_b, v, preferred_element_type=F32)
        out_ref[:, cols] = out.astype(BF16)
    flipped = out_ref[...].astype(F32).T.astype(BF16)
    for b in range(GROUP // ROWS):
        block = flipped[b * ROWS : (b + 1) * ROWS]
        out_t_ref[b % NY, b // NY] = jnp.concatenate([block, jnp.zeros((ROWS, PAD - TILE), BF16)], axis=1)


def backward_kernel(
    scalar_ref, q_ref, own_ref, time_ref, core_ref, cross_ref, att_ref, d_ref, probs_ref,
    gq_ref, g_own_ref, g_time_ref, g_core_ref, g_cross_ref,
):
    kv = (own_ref, time_ref, core_ref, cross_ref)
    outs = (g_own_ref, g_time_ref, g_core_ref, g_cross_ref)
    flipped = jnp.concatenate(
        [d_ref[b % NY, b // NY] for b in range(GROUP // ROWS)], axis=0
    )
    d_all = flipped.astype(F32).T[:TILE].astype(BF16)
    for h in range(PER_STEP):
        cols = slice(h * HEAD_DIM, (h + 1) * HEAD_DIM)
        q = q_ref[:, cols]
        k = window_of(kv, 0, cols)
        v = window_of(kv, 1, cols)
        d = d_all[:, cols]
        probs = probs_ref[h]
        delta = jnp.sum(d.astype(F32) * att_ref[:, cols].astype(F32), axis=1, keepdims=True)
        d_probs = lax.dot_general(d, v, NT, preferred_element_type=F32)
        d_scores = (probs.astype(F32) * (d_probs - delta)).astype(BF16)
        value_terms = lax.dot_general(probs, d, TN, preferred_element_type=F32)
        key_terms = lax.dot_general(d_scores, q, TN, preferred_element_type=F32) * SCALE
        gq = jnp.dot(d_scores, k, preferred_element_type=F32) * SCALE
        gq_ref[:, cols] = gq.astype(BF16)
        for s, ref in enumerate(outs):
            rows = slice(s * TILE, (s + 1) * TILE)
            ref[0, :, cols] = key_terms[rows].astype(ref.dtype)
            ref[1, :, cols] = value_terms[rows].astype(ref.dtype)


def flat_spec(first):
    return pl.BlockSpec((TILE, GROUP), lambda i, b: (0, i + first))


def pair_spec(first):
    return pl.BlockSpec((2, TILE, GROUP), lambda i, b: (0, 0, i + first))


def turned_spec(first):
    return pl.BlockSpec((NY, GROUP // ROWS // NY, ROWS, PAD), lambda i, b: (0, i + first, 0, 0))


def probs_spec(first):
    return pl.BlockSpec((PER_STEP, TILE, SLOTS * TILE), lambda i, b: (i + first, 0, 0))


def whole(shape):
    return pl.BlockSpec(shape, lambda *_: (0,) * len(shape))


def attention_forward(scalars, q, kvs):
    groups = HEADS // PER_STEP
    return pl.pallas_call(
        forward_kernel,
        grid_spec=pltpu.PrefetchScalarGridSpec(
            num_scalar_prefetch=1,
            grid=(groups,),
            in_specs=[flat_spec(0)] + [pair_spec(0)] * 4,
            out_specs=[flat_spec(0), turned_spec(0), probs_spec(0)],
        ),
        out_shape=[
            jax.ShapeDtypeStruct((TILE, groups * GROUP), BF16),
            jax.ShapeDtypeStruct((NY, groups * GROUP // ROWS // NY, ROWS, PAD), BF16),
            jax.ShapeDtypeStruct((HEADS, TILE, SLOTS * TILE), BF16),
        ],
        compiler_params=PARAMS,
        cost_estimate=pl.CostEstimate(
            flops=4 * groups * TILE * SLOTS * TILE * GROUP,
            bytes_accessed=20 * TILE * groups * GROUP,
            transcendentals=groups * PER_STEP * TILE * SLOTS * TILE,
        ),
    )(scalars, q, *kvs)


def attention_backward(scalars, q, kvs, att, d, probs, first, groups):
    width = groups * GROUP
    return pl.pallas_call(
        backward_kernel,
        grid_spec=pltpu.PrefetchScalarGridSpec(
            num_scalar_prefetch=1,
            grid=(groups,),
            in_specs=[flat_spec(first)] + [pair_spec(first)] * 4 + [flat_spec(first), turned_spec(first), probs_spec(first)],
            out_specs=[flat_spec(0)] + [pair_spec(0)] * 4,
        ),
        out_shape=[jax.ShapeDtypeStruct((TILE, width), BF16)]
        + [jax.ShapeDtypeStruct((2, TILE, width), BF16)] * 4,
        compiler_params=PARAMS,
        cost_estimate=pl.CostEstimate(
            flops=12 * groups * TILE * SLOTS * TILE * GROUP,
            bytes_accessed=48 * TILE * width,
            transcendentals=groups * PER_STEP * TILE * SLOTS * TILE,
        ),
    )(scalars, q, *kvs, att, d, probs)


def d_attention_kernel(scalar_ref, up_ref, mine_ref, mate_ref, out_ref, weight_ref):
    half = mine_ref.shape[1]

    @pl.when(pl.program_id(0) == 0)
    def _():
        for side, ref in enumerate((mine_ref, mate_ref)):
            co = scalar_ref[1] if side == 0 else 1 - scalar_ref[1]
            weight_ref[:, pl.ds(pl.multiple_of(co * half, 128), half)] = ref[...]

    out = lax.dot_general(weight_ref[...], up_ref[0], NT, preferred_element_type=F32)
    out_ref[0] = jnp.concatenate(
        [out.astype(BF16), jnp.zeros((out.shape[0], PAD - TILE), BF16)], axis=1
    )


def d_attention(scalars, ups, w_mine, w_mate):
    dout = ups.shape[2]
    rows = w_mine.shape[0]
    return pl.pallas_call(
        d_attention_kernel,
        grid_spec=pltpu.PrefetchScalarGridSpec(
            num_scalar_prefetch=1,
            grid=(NY,),
            in_specs=[pl.BlockSpec((1, TILE, dout), lambda i, b: (i, 0, 0))] + [whole(w_mine.shape)] * 2,
            out_specs=[pl.BlockSpec((1, rows, PAD), lambda i, b: (i, 0, 0)), whole((rows, dout))],
        ),
        out_shape=[
            jax.ShapeDtypeStruct((NY, rows, PAD), BF16),
            jax.ShapeDtypeStruct((rows, dout), BF16),
        ],
        compiler_params=PARAMS,
        cost_estimate=pl.CostEstimate(
            flops=8 * TILE * rows * dout, bytes_accessed=8 * TILE * dout + 4 * rows * dout, transcendentals=0
        ),
    )(scalars, ups, w_mine, w_mate)


def gradient_kernel(scalar_ref, att_ref, mine_ref, mate_ref, out_mine_ref, out_mate_ref):
    for up_ref, out_ref in ((mine_ref, out_mine_ref), (mate_ref, out_mate_ref)):
        total = jnp.dot(att_ref[0][:, :TILE], up_ref[0], preferred_element_type=F32)
        for k in range(1, NY):
            total += jnp.dot(att_ref[k][:, :TILE], up_ref[k], preferred_element_type=F32)
        out_ref[...] = total.astype(out_ref.dtype)


def weight_gradient(scalars, atts, ups):
    half = ups.shape[2] // 2
    rows = atts.shape[1]
    step = 256
    steps = half // step
    return pl.pallas_call(
        gradient_kernel,
        grid_spec=pltpu.PrefetchScalarGridSpec(
            num_scalar_prefetch=1,
            grid=(steps,),
            in_specs=[
                whole(atts.shape),
                pl.BlockSpec((NY, TILE, step), lambda i, b: (0, 0, b[1] * steps + i)),
                pl.BlockSpec((NY, TILE, step), lambda i, b: (0, 0, (1 - b[1]) * steps + i)),
            ],
            out_specs=[pl.BlockSpec((rows, step), lambda i, b: (0, i))] * 2,
        ),
        out_shape=[jax.ShapeDtypeStruct((rows, half), BF16)] * 2,
        compiler_params=PARAMS,
        cost_estimate=pl.CostEstimate(
            flops=16 * TILE * rows * half, bytes_accessed=16 * TILE * (rows + half), transcendentals=0
        ),
    )(scalars, atts, ups, ups)


def mixed_kernel(att_ref, weight_ref, out_ref):
    att = att_ref[0][:, :TILE]
    out_ref[0] = lax.dot_general(att, weight_ref[...], TN, preferred_element_type=F32).astype(BF16)


def mixed_parts(atts, weight):
    rows, dout = weight.shape
    return pl.pallas_call(
        mixed_kernel,
        grid=(NY,),
        in_specs=[pl.BlockSpec((1, rows, PAD), lambda i: (i, 0, 0)), whole((rows, dout))],
        out_specs=pl.BlockSpec((1, TILE, dout), lambda i: (i, 0, 0)),
        out_shape=jax.ShapeDtypeStruct((NY, TILE, dout), BF16),
        compiler_params=PARAMS,
        cost_estimate=pl.CostEstimate(
            flops=8 * TILE * rows * dout, bytes_accessed=10 * TILE * dout, transcendentals=0
        ),
    )(atts, weight)


SWAP = [(0, 1), (1, 0)]
CROSS = [(1, 2), (2, 1)]


def swapped(x, axis):
    return lax.all_to_all(x, axis, split_axis=0, concat_axis=0, tiled=True)


def per_device(queries, keys_values, upstream, out_weight, block_pick):
    width = queries.shape[4]
    dout = upstream.shape[4]
    half = dout // 2
    rows = out_weight.shape[1]
    ny = lax.axis_size("y")
    nz = lax.axis_size("z")
    co = lax.axis_index("co")
    first = co == 0
    q = queries.reshape(TILE, width)
    kv = keys_values.reshape(2, TILE, width)
    up = upstream.reshape(TILE, dout)

    has_cross = lax.axis_index("xh") != co
    bound = jnp.where(has_cross, SLOTS * TILE, (SLOTS - 1) * TILE)
    scalars = jnp.stack([bound, co]).astype(jnp.int32)

    from_time = lax.ppermute(kv, "xl", SWAP)
    from_cross = lax.ppermute(kv, ("xh", "co"), CROSS)
    from_core = lax.ppermute(kv, "co", SWAP)
    kvs = (kv, from_time, from_core, from_cross)

    panel = lax.dynamic_slice(out_weight, (block_pick[0], 0, co * half), (1, rows, half))
    w_mine = swapped(jnp.broadcast_to(panel, (nz, rows, half)), "z").reshape(nz * rows, half)
    ups = swapped(jnp.broadcast_to(up[None], (ny, TILE, dout)), "y")
    w_mate = lax.ppermute(w_mine, "co", SWAP)
    d_parts, w_rows = d_attention(scalars, ups, w_mine, w_mate)
    d_turned = swapped(d_parts, "y").reshape(ny, nz, rows, PAD)

    kvs, d_parts = lax.optimization_barrier((kvs, d_parts))
    att, att_turned, probs = attention_forward(scalars, q, kvs)
    atts = swapped(att_turned.reshape(ny, nz * rows, PAD), "y")

    parts = 2
    groups = HEADS // PER_STEP // parts

    def backward(c):
        gq, own, to_time, to_core, to_cross = attention_backward(
            scalars, q, kvs, att, d_turned, probs, c * groups, groups
        )
        terms = (
            lax.ppermute(to_time, "xl", SWAP),
            lax.ppermute(to_cross, ("xh", "co"), CROSS),
            lax.ppermute(to_core, "co", SWAP),
        )
        return gq, own.astype(F32) + sum(t.astype(F32) for t in terms)

    gq_0, gkv_0 = backward(0)
    atts, gq_0 = lax.optimization_barrier((atts, gq_0))
    grad_mine, grad_mate = weight_gradient(scalars, atts, ups)
    from_mate = lax.ppermute(grad_mate, "co", SWAP)
    atts, w_rows, grad_mine = lax.optimization_barrier((atts, w_rows, grad_mine))
    mixed = mixed_parts(atts, w_rows)
    grad = (grad_mine.astype(F32) + from_mate.astype(F32)).astype(BF16).reshape(nz, rows, half)
    probs, grad, mixed = lax.optimization_barrier((probs, grad, mixed))
    gq_1, gkv_1 = backward(1)
    gq_parts, gkv_parts = (gq_0, gq_1), (gkv_0, gkv_1)
    over_z = jnp.sum(swapped(grad, "z").astype(F32), axis=0).astype(BF16)
    x_near = lax.ppermute(over_z, "xl", SWAP)
    x_far = lax.ppermute(over_z, "xh", SWAP)
    x_both = lax.ppermute(over_z, ("xl", "xh"), [(i, 3 - i) for i in range(4)])
    mine = (over_z.astype(F32) + x_near.astype(F32)) + (x_far.astype(F32) + x_both.astype(F32))
    mate = lax.ppermute(mine, "co", SWAP)
    grad_weight = jnp.concatenate(
        [jnp.where(first, mine, mate), jnp.where(first, mate, mine)], axis=1
    )

    mixed = jnp.sum(swapped(mixed, "y").astype(F32), axis=0).astype(BF16)
    grad_q = jnp.concatenate(gq_parts, axis=1)
    grad_kv = jnp.concatenate([p.astype(BF16) for p in gkv_parts], axis=2)
    return (
        mixed.reshape(upstream.shape),
        grad_q.reshape(queries.shape),
        grad_kv.reshape(keys_values.shape),
        grad_weight,
    )


def solution(mesh):
    fine = Mesh(mesh.devices.reshape(2, 2, 2, 8, 4), ("xl", "xh", "co", "z", "y"))
    wa = ("z", "y")
    ha = ("xh", "co")
    return jax.shard_map(
        per_device,
        mesh=fine,
        in_specs=(
            P(wa, "xl", ha, None, None),
            P(None, wa, "xl", ha, None, None),
            P(wa, "xl", ha, None, None),
            P(None, wa, None),
            P(),
        ),
        out_specs=(
            P(wa, "xl", ha, None, None),
            P(wa, "xl", ha, None, None),
            P(None, wa, "xl", ha, None, None),
            P(wa, None),
        ),
        check_vma=False,
    )
```

time: 213 us -> 174 us (0.82)
  waiting for transfers between devices: 80.5 us -> 47.1 us
  Pallas kernels: 21.6 us -> 39.3 us
  between operations: 15 us -> 1.56 us
  matrix products: 11.3 us -> 0 us
    ppermute x14 -> x10, waiting for transfers between devices: 63.1 us -> 22.2 us  [the longest x2 12.6 us: backward(): lax.ppermute(to_cross, ('xh', 'co'), CROSS)]
    all_to_all x0 -> x5, waiting for transfers between devices: none -> 22.3 us  [swapped(): return lax.all_to_all(x, axis, split_axis=0, concat_axis=0, tiled=True)]
    all_to_all x0 -> x5, starting transfers between devices: none -> 19.7 us  [swapped(): return lax.all_to_all(x, axis, split_axis=0, concat_axis=0, tiled=True)]
    pallas_call x0 -> x3, Pallas kernels: none -> 16 us  [the longest x1 5.7 us: d_attention(): pl.pallas_call(d_attention_kernel, grid_spec=pltpu.PrefetchScalarGridSpec...]
    all_gather x1 -> x0, waiting for transfers between devices: 13 us -> none  [per_device(): w_mine = lax.all_gather(panel, ('z', 'y'), axis=0, tiled=True)]
    ppermute x1, starting transfers between devices: 13.3 us -> 0.69 us  [per_device(): w_mate = lax.ppermute(w_mine, 'co', SWAP)]
    dot_general x6 -> x0, matrix products: 11.3 us -> none  [the longest x1 2.81 us: per_device(): lax.dot_general(up_mate, w_mate, NT, preferred_element_type=F32)]
    ppermute x14 -> x10, starting transfers between devices: 21.1 us -> 17.8 us  [the longest x2 7.93 us: backward(): lax.ppermute(to_cross, ('xh', 'co'), CROSS)]
  transfers between devices with their start and end apart: 20 -> 20, of which waited for: 12 -> 9; matrix products, arithmetic and copies ran while one was open for 9% -> 5% of each run, Pallas kernels for 7% -> 20%
where the time goes in v3:
time: 174 us; the launch traced here: 173 us
  waiting for transfers between devices  47.1 us (27%)
  starting transfers between devices  41.5 us (24%)
  Pallas kernels  39.3 us (23%)
  blocking collectives  26.4 us (15%)
  other arithmetic  11.2 us (6%)
  local copies, waits for them, and re-layouts  5.76 us (3%)
    all_to_all x1, blocking collectives, swapped(): return lax.all_to_all(x, axis, split_axis=0, concat_axis=0, tiled=True)  26.4 us
    all_to_all x5, waiting for transfers between devices, swapped(): return lax.all_to_all(x, axis, split_axis=0, concat_axis=0, tiled=True)  22.3 us
    all_to_all x5, starting transfers between devices, swapped(): return lax.all_to_all(x, axis, split_axis=0, concat_axis=0, tiled=True)  19.7 us
    pallas_call x2, Pallas kernels, attention_backward(): pl.pallas_call(backward_kernel, grid_spec=pltpu.PrefetchScalarGridSpec(nu...  13.5 us
    ppermute x2, waiting for transfers between devices, backward(): lax.ppermute(to_cross, ('xh', 'co'), CROSS)  12.6 us
    pallas_call x1, Pallas kernels, attention_forward(): pl.pallas_call(forward_kernel, grid_spec=pltpu.PrefetchScalarGridSpec(num...  9.82 us
    ppermute x1, waiting for transfers between devices, per_device(): from_time = lax.ppermute(kv, 'xl', SWAP)  9.57 us
    ppermute x2, starting transfers between devices, backward(): lax.ppermute(to_cross, ('xh', 'co'), CROSS)  7.93 us
  transfers between devices with their start and end apart: 20, of which 9 were waited for; matrix products, arithmetic and copies ran while one was open for 5% of the time, Pallas kernels for 20%

profile of v3, /device:TPU:1, one launch (start us, length us, event | category | flops | bytes accessed | tf_op | source)
XLA Modules:
  0.0 172.7 jit_solution(4517030172949634373)
XLA Ops:
  2.3 26.4 %all_to_all.30 = bf16[8,48,768]{2,1,0:T(8,128)(2,1)} all-to-all(bf16[8,48,768]{2,1,0:T(8,128)(2,1)S(1)} %broadcast_in_dim.17), channel_id=1, replica_groups=mesh['xl'=2,'xh'=2,'co'=2,'z'=8,'y'=4] {'z'}, dimensions={0} | all-to-all | bytes 1179648 | tf_op jit(solution)/shard_map/all_to_all | solution.py:248
  30.3 4.3 %all-to-all-start = ((bf16[4,192,1536]{2,1,0:T(8,128)(2,1)}), bf16[4,192,1536]{2,1,0:T(8,128)(2,1)S(1)}, u32[]{:S(2)}, u32[]{:S(2)}) async-start(bf16[4,192,1536]{2,1,0:T(8,128)(2,1)} %broadcast_in_dim.15), calls=%async_computation | async-start | bytes 4718592 | tf_op jit(solution)/shard_map/all_to_all | solution.py:248
  34.6 7.2 %collective-permute-start.2 = (bf16[2,192,1536]{2,1,0:T(8,128)(2,1)S(1)}, bf16[2,192,1536]{2,1,0:T(8,128)(2,1)}, u32[]{:S(2)}, u32[]{:S(2)}) collective-permute-start(bf16[2,192,1536]{2,1,0:T(8,128)(2,1)S(1)} %bitcast.25), channel_id=1, source_target_pairs={{32,64},{64,32},{33,65},{65,33},{34,66},{66,34},{35,67},{67,35},{3... | collective-permute-start | bytes 3538952 | tf_op jit(solution)/shard_map/ppermute | solution.py:269
  43.6 2.3 %collective-permute-done.3.mate_ref = bf16[384,768]{1,0:T(8,128)(2,1)} collective-permute-done((bf16[384,768]{1,0:T(8,128)(2,1)}, bf16[384,768]{1,0:T(8,128)(2,1)}, u32[]{:S(2)}, u32[]{:S(2)}) %collective-permute-start.3) | collective-permute-done | bytes 589856 | tf_op jit(solution)/shard_map/ppermute | solution.py:276
  45.9 15.1 %all-to-all-done.up_ref.mine_ref.mate_ref = bf16[4,192,1536]{2,1,0:T(8,128)(2,1)S(1)} async-done(((bf16[4,192,1536]{2,1,0:T(8,128)(2,1)}), bf16[4,192,1536]{2,1,0:T(8,128)(2,1)S(1)}, u32[]{:S(2)}, u32[]{:S(2)}) %all-to-all-start) | async-done | bytes 2359328 | tf_op jit(solution)/shard_map/all_to_all | solution.py:248
  62.5 5.7 %shard_map.84 = (bf16[4,384,256]{2,1,0:T(8,128)(2,1)}, bf16[384,1536]{1,0:T(8,128)(2,1)}) custom-call(s32[2]{0:T(128)} %pad_add_fusion.scalar_ref, bf16[4,192,1536]{2,1,0:T(8,128)(2,1)} %copy-done, bf16[384,768]{1,0:T(8,128)(2,1)} %bitcast.34, bf16[384,768]{1,0:T(8,128)(2,1)} %collective-permute-done.3.mate_ref), custom_call_target="tpu_custom_call" | custom-call | flops 905969664 | bytes 4718592 | tf_op jit(solution)/shard_map/pallas_call | solution.py:171
  68.2 3.5 %all-to-all-start.3 = ((bf16[4,384,256]{2,1,0:T(8,128)(2,1)}), bf16[4,384,256]{2,1,0:T(8,128)(2,1)S(1)}, u32[]{:S(2)}, u32[]{:S(2)}) async-start(bf16[4,384,256]{2,1,0:T(8,128)(2,1)} %get-tuple-element.33), calls=%async_computation.3 | async-start | bytes 1572864 | tf_op jit(solution)/shard_map/all_to_all | solution.py:248
  71.7 9.6 %collective-permute-done.time_ref = bf16[2,192,1536]{2,1,0:T(8,128)(2,1)} collective-permute-done((bf16[2,192,1536]{2,1,0:T(8,128)(2,1)S(1)}, bf16[2,192,1536]{2,1,0:T(8,128)(2,1)}, u32[]{:S(2)}, u32[]{:S(2)}) %collective-permute-start) | collective-permute-done | bytes 1179680 | tf_op jit(solution)/shard_map/ppermute | solution.py:268
  81.3 9.8 %shard_map.85 = (bf16[192,1536]{1,0:T(8,128)(2,1)}, bf16[4,8,48,256]{3,2,1,0:T(8,128)(2,1)}, bf16[12,192,768]{2,1,0:T(8,128)(2,1)}) custom-call(s32[2]{0:T(128)} %pad_add_fusion.scalar_ref, bf16[192,1536]{1,0:T(8,128)(2,1)} %bitcast.30, bf16[2,192,1536]{2,1,0:T(8,128)(2,1)} %bitcast.22, bf16[2,192,1536]{2,1,0:T(8,128)(2,1)} %collective-permute-done.time_ref, ...), custom_call_target="tpu_custom_call" | custom-call | flops 905969664 | bytes 5898240 | tf_op jit(solution)/shard_map/pallas_call | solution.py:110
  91.1 4.5 %all-to-all-start.2 = ((bf16[4,384,256]{2,1,0:T(8,128)(2,1)}), bf16[4,384,256]{2,1,0:T(8,128)(2,1)S(1)}, u32[]{:S(2)}, u32[]{:S(2)}) async-start(bf16[4,384,256]{2,1,0:T(8,128)(2,1)} %bitcast.35), calls=%async_computation.2 | async-start | bytes 1572864 | tf_op jit(solution)/shard_map/all_to_all | solution.py:248
  95.6 6.7 %shard_map.86 = (bf16[192,768]{1,0:T(8,128)(2,1)}, bf16[2,192,768]{2,1,0:T(8,128)(2,1)}, bf16[2,192,768]{2,1,0:T(8,128)(2,1)}, bf16[2,192,768]{2,1,0:T(8,128)(2,1)}, bf16[2,192,768]{2,1,0:T(8,128)(2,1)}) custom-call(s32[2]{0:T(128)} %pad_add_fusion.scalar_ref, bf16[192,1536]{1,0:T(8,128)(2,1)} %bitcast.31, bf16[2,192,1536]{2,1,0:T(8,128)(2,1)} %bitcast.23, ...), custom_call_target="tpu_custom_call" | custom-call | flops 1358954496 | bytes 7077888 | tf_op jit(solution)/shard_map/pallas_call | solution.py:134
  104.9 5.3 %shard_map.87 = (bf16[384,768]{1,0:T(8,128)(2,1)}, bf16[384,768]{1,0:T(8,128)(2,1)}) custom-call(s32[2]{0:T(128)} %pad_add_fusion.scalar_ref, bf16[4,384,256]{2,1,0:T(8,128)(2,1)} %copy-done.3, bf16[4,192,1536]{2,1,0:T(8,128)(2,1)} %copy-done, bf16[4,192,1536]{2,1,0:T(8,128)(2,1)} %copy-done), custom_call_target="tpu_custom_call" | custom-call | flops 905969664 | bytes 3538944 | tf_op jit(solution)/shard_map/pallas_call | solution.py:203
  110.2 5.0 %shard_map.88 = bf16[4,192,1536]{2,1,0:T(8,128)(2,1)} custom-call(bf16[4,384,256]{2,1,0:T(8,128)(2,1)} %copy-done.3, bf16[384,1536]{1,0:T(8,128)(2,1)} %get-tuple-element.48.weight_ref), custom_call_target="tpu_custom_call" | custom-call | flops 905969664 | bytes 2949120 | tf_op jit(solution)/shard_map/pallas_call | solution.py:230
  116.2 3.5 %all-to-all-start.5 = ((bf16[8,48,768]{2,1,0:T(8,128)(2,1)}), bf16[8,48,768]{2,1,0:T(8,128)(2,1)S(1)}, u32[]{:S(2)}, u32[]{:S(2)}) async-start(bf16[8,48,768]{2,1,0:T(8,128)(2,1)} %bitcast.10), calls=%async_computation.5 | async-start | bytes 1179648 | tf_op jit(solution)/shard_map/all_to_all | solution.py:248
  121.0 4.3 %collective-permute-start.6 = (bf16[2,192,768]{2,1,0:T(8,128)(2,1)}, bf16[2,192,768]{2,1,0:T(8,128)(2,1)S(1)}, u32[]{:S(2)}, u32[]{:S(2)}) collective-permute-start(bf16[2,192,768]{2,1,0:T(8,128)(2,1)} %get-tuple-element.55), channel_id=1, source_target_pairs={{32,64},{64,32},{33,65},{65,33},{34,66},{66,34},{35,67},{67,35},{3... | collective-permute-start | bytes 1769480 | tf_op jit(solution)/shard_map/ppermute | solution.py:293
  125.4 6.7 %shard_map.89 = (bf16[192,768]{1,0:T(8,128)(2,1)}, bf16[2,192,768]{2,1,0:T(8,128)(2,1)}, bf16[2,192,768]{2,1,0:T(8,128)(2,1)}, bf16[2,192,768]{2,1,0:T(8,128)(2,1)}, bf16[2,192,768]{2,1,0:T(8,128)(2,1)}) custom-call(s32[2]{0:T(128)} %pad_add_fusion.scalar_ref, bf16[192,1536]{1,0:T(8,128)(2,1)} %bitcast.32, bf16[2,192,1536]{2,1,0:T(8,128)(2,1)} %bitcast.24, ...), custom_call_target="tpu_custom_call" | custom-call | flops 1358954496 | bytes 7077888 | tf_op jit(solution)/shard_map/pallas_call | solution.py:134
  132.5 3.6 %collective-permute-start.9 = (bf16[2,192,768]{2,1,0:T(8,128)(2,1)}, bf16[2,192,768]{2,1,0:T(8,128)(2,1)}, u32[]{:S(2)}, u32[]{:S(2)}) collective-permute-start(bf16[2,192,768]{2,1,0:T(8,128)(2,1)} %get-tuple-element.59), channel_id=1, source_target_pairs={{32,64},{64,32},{33,65},{65,33},{34,66},{66,34},{35,67},{67,35},{3... | collective-permute-start | bytes 1769480 | tf_op jit(solution)/shard_map/ppermute | solution.py:293
  136.6 2.4 %all-to-all-done.5 = bf16[8,48,768]{2,1,0:T(8,128)(2,1)S(1)} async-done(((bf16[8,48,768]{2,1,0:T(8,128)(2,1)}), bf16[8,48,768]{2,1,0:T(8,128)(2,1)S(1)}, u32[]{:S(2)}, u32[]{:S(2)}) %all-to-all-start.5) | async-done | bytes 589856 | tf_op jit(solution)/shard_map/all_to_all | solution.py:248
  139.1 3.8 %all-to-all-start.4 = ((bf16[4,192,1536]{2,1,0:T(8,128)(2,1)}), bf16[4,192,1536]{2,1,0:T(8,128)(2,1)S(1)}, u32[]{:S(2)}, u32[]{:S(2)}) async-start(bf16[4,192,1536]{2,1,0:T(8,128)(2,1)} %shard_map.88), calls=%async_computation.4 | async-start | bytes 4718592 | tf_op jit(solution)/shard_map/all_to_all | solution.py:248
  142.9 2.0 %maximum_bitcast_fusion.1 = bf16[1,1,1,192,1536]{4,3,2,1,0:T(8,128)(2,1)} fusion(bf16[192,768]{1,0:T(8,128)(2,1)} %get-tuple-element.52, bf16[192,768]{1,0:T(8,128)(2,1)} %get-tuple-element.50), kind=kLoop, calls=%fused_computation.4 | loop fusion | flops 1179648 | bytes 1179648 | tf_op jit(solution)/shard_map/reshape | solution.py:323
  144.9 4.6 %collective-permute-done.6 = bf16[2,192,768]{2,1,0:T(8,128)(2,1)S(1)} collective-permute-done((bf16[2,192,768]{2,1,0:T(8,128)(2,1)}, bf16[2,192,768]{2,1,0:T(8,128)(2,1)S(1)}, u32[]{:S(2)}, u32[]{:S(2)}) %collective-permute-start.6) | collective-permute-done | bytes 589856 | tf_op jit(solution)/shard_map/ppermute | solution.py:293
  152.7 2.4 %collective-permute-start.12 = (bf16[48,768]{1,0:T(8,128)(2,1)}, bf16[48,768]{1,0:T(8,128)(2,1)S(1)}, u32[]{:S(2)}, u32[]{:S(2)}) collective-permute-start(bf16[48,768]{1,0:T(8,128)(2,1)} %reduce_sum.25), channel_id=1, source_target_pairs={{0,64},{64,0},{1,65},{65,1},{2,66},{66,2},{3,67},{67,3},{4,68},{68... | collective-permute-start | bytes 221192 | tf_op jit(solution)/shard_map/ppermute | solution.py:310
  156.0 8.0 %collective-permute-done.9 = bf16[2,192,768]{2,1,0:T(8,128)(2,1)} collective-permute-done((bf16[2,192,768]{2,1,0:T(8,128)(2,1)}, bf16[2,192,768]{2,1,0:T(8,128)(2,1)}, u32[]{:S(2)}, u32[]{:S(2)}) %collective-permute-start.9) | collective-permute-done | bytes 589856 | tf_op jit(solution)/shard_map/ppermute | solution.py:293
  168.2 3.2 %all-to-all-done.4 = bf16[4,192,1536]{2,1,0:T(8,128)(2,1)S(1)} async-done(((bf16[4,192,1536]{2,1,0:T(8,128)(2,1)}), bf16[4,192,1536]{2,1,0:T(8,128)(2,1)S(1)}, u32[]{:S(2)}, u32[]{:S(2)}) %all-to-all-start.4) | async-done | bytes 2359328 | tf_op jit(solution)/shard_map/all_to_all | solution.py:248
  (57 shorter events, 21.1 us)
Async XLA Ops:
  0.6 28.0 %copy-start.5 = (bf16[1,1,1,192,1536]{4,3,2,1,0:T(8,128)(2,1)S(1)}, bf16[1,1,1,192,1536]{4,3,2,1,0:T(8,128)(2,1)}, u32[]{:S(2)}) copy-start(bf16[1,1,1,192,1536]{4,3,2,1,0:T(8,128)(2,1)} %param.7) | copy-start | bytes 1769476
  30.3 30.8 %all-to-all-start = ((bf16[4,192,1536]{2,1,0:T(8,128)(2,1)}), bf16[4,192,1536]{2,1,0:T(8,128)(2,1)S(1)}, u32[]{:S(2)}, u32[]{:S(2)}) async-start(bf16[4,192,1536]{2,1,0:T(8,128)(2,1)} %broadcast_in_dim.15), calls=%async_computation | async-start | bytes 4718592 | tf_op jit(solution)/shard_map/all_to_all | solution.py:248
  34.6 37.1 %collective-permute-start.2 = (bf16[2,192,1536]{2,1,0:T(8,128)(2,1)S(1)}, bf16[2,192,1536]{2,1,0:T(8,128)(2,1)}, u32[]{:S(2)}, u32[]{:S(2)}) collective-permute-start(bf16[2,192,1536]{2,1,0:T(8,128)(2,1)S(1)} %bitcast.25), channel_id=1, source_target_pairs={{32,64},{64,32},{33,65},{65,33},{34,66},{66,34},{35,67},{67,35},{3... | collective-permute-start | bytes 3538952 | tf_op jit(solution)/shard_map/ppermute | solution.py:269
  41.8 29.9 %collective-permute-start.1 = (bf16[2,192,1536]{2,1,0:T(8,128)(2,1)S(1)}, bf16[2,192,1536]{2,1,0:T(8,128)(2,1)}, u32[]{:S(2)}, u32[]{:S(2)}) collective-permute-start(bf16[2,192,1536]{2,1,0:T(8,128)(2,1)S(1)} %bitcast.26), channel_id=1, source_target_pairs={{0,32},{32,0},{1,33},{33,1},{2,34},{34,2},{3,35},{35,3},{4,36},{36... | collective-permute-start | bytes 3538952 | tf_op jit(solution)/shard_map/ppermute | solution.py:270
  41.9 39.4 %collective-permute-start = (bf16[2,192,1536]{2,1,0:T(8,128)(2,1)S(1)}, bf16[2,192,1536]{2,1,0:T(8,128)(2,1)}, u32[]{:S(2)}, u32[]{:S(2)}) collective-permute-start(bf16[2,192,1536]{2,1,0:T(8,128)(2,1)S(1)} %bitcast.27), channel_id=1, source_target_pairs={{0,128},{128,0},{1,129},{129,1},{2,130},{130,2},{3,131},{131,3},{4... | collective-permute-start | bytes 3538952 | tf_op jit(solution)/shard_map/ppermute | solution.py:268
  42.3 3.6 %collective-permute-start.3 = (bf16[384,768]{1,0:T(8,128)(2,1)}, bf16[384,768]{1,0:T(8,128)(2,1)}, u32[]{:S(2)}, u32[]{:S(2)}) collective-permute-start(bf16[384,768]{1,0:T(8,128)(2,1)} %bitcast.33), channel_id=1, source_target_pairs={{0,32},{32,0},{1,33},{33,1},{2,34},{34,2},{3,35},{35,3},{4,36},{36... | collective-permute-start | bytes 1769480 | tf_op jit(solution)/shard_map/ppermute | solution.py:276
  68.2 22.9 %all-to-all-start.3 = ((bf16[4,384,256]{2,1,0:T(8,128)(2,1)}), bf16[4,384,256]{2,1,0:T(8,128)(2,1)S(1)}, u32[]{:S(2)}, u32[]{:S(2)}) async-start(bf16[4,384,256]{2,1,0:T(8,128)(2,1)} %get-tuple-element.33), calls=%async_computation.3 | async-start | bytes 1572864 | tf_op jit(solution)/shard_map/all_to_all | solution.py:248
  91.1 4.5 %copy-start.2 = (bf16[4,384,256]{2,1,0:T(8,128)(2,1)}, bf16[4,384,256]{2,1,0:T(8,128)(2,1)S(1)}, u32[]{:S(2)}) copy-start(bf16[4,384,256]{2,1,0:T(8,128)(2,1)S(1)} %all-to-all-done.3) | copy-start | bytes 2359300
  91.1 12.9 %all-to-all-start.2 = ((bf16[4,384,256]{2,1,0:T(8,128)(2,1)}), bf16[4,384,256]{2,1,0:T(8,128)(2,1)S(1)}, u32[]{:S(2)}, u32[]{:S(2)}) async-start(bf16[4,384,256]{2,1,0:T(8,128)(2,1)} %bitcast.35), calls=%async_computation.2 | async-start | bytes 1572864 | tf_op jit(solution)/shard_map/all_to_all | solution.py:248
  110.2 5.0 %collective-permute-start.4 = (bf16[384,768]{1,0:T(8,128)(2,1)}, bf16[384,768]{1,0:T(8,128)(2,1)S(1)}, u32[]{:S(2)}, u32[]{:S(2)}) collective-permute-start(bf16[384,768]{1,0:T(8,128)(2,1)} %get-tuple-element.46), channel_id=1, source_target_pairs={{0,32},{32,0},{1,33},{33,1},{2,34},{34,2},{3,35},{35,3},{4,36},{36... | collective-permute-start | bytes 1769480 | tf_op jit(solution)/shard_map/ppermute | solution.py:301
  110.2 5.0 %copy-start.4 = (bf16[384,768]{1,0:T(8,128)(2,1)S(1)}, bf16[384,768]{1,0:T(8,128)(2,1)}, u32[]{:S(2)}) copy-start(bf16[384,768]{1,0:T(8,128)(2,1)} %get-tuple-element.45) | copy-start | bytes 1769476
  116.2 22.9 %all-to-all-start.5 = ((bf16[8,48,768]{2,1,0:T(8,128)(2,1)}), bf16[8,48,768]{2,1,0:T(8,128)(2,1)S(1)}, u32[]{:S(2)}, u32[]{:S(2)}) async-start(bf16[8,48,768]{2,1,0:T(8,128)(2,1)} %bitcast.10), calls=%async_computation.5 | async-start | bytes 1179648 | tf_op jit(solution)/shard_map/all_to_all | solution.py:248
  119.8 16.4 %collective-permute-start.5 = (bf16[2,192,768]{2,1,0:T(8,128)(2,1)S(1)}, bf16[2,192,768]{2,1,0:T(8,128)(2,1)}, u32[]{:S(2)}, u32[]{:S(2)}) collective-permute-start(bf16[2,192,768]{2,1,0:T(8,128)(2,1)S(1)} %copy-done.9), channel_id=1, source_target_pairs={{0,128},{128,0},{1,129},{129,1},{2,130},{130,2},{3,131},{131,3},{4... | collective-permute-start | bytes 1769480 | tf_op jit(solution)/shard_map/ppermute | solution.py:292
  121.0 28.4 %collective-permute-start.6 = (bf16[2,192,768]{2,1,0:T(8,128)(2,1)}, bf16[2,192,768]{2,1,0:T(8,128)(2,1)S(1)}, u32[]{:S(2)}, u32[]{:S(2)}) collective-permute-start(bf16[2,192,768]{2,1,0:T(8,128)(2,1)} %get-tuple-element.55), channel_id=1, source_target_pairs={{32,64},{64,32},{33,65},{65,33},{34,66},{66,34},{35,67},{67,35},{3... | collective-permute-start | bytes 1769480 | tf_op jit(solution)/shard_map/ppermute | solution.py:293
  125.3 24.1 %collective-permute-start.7 = (bf16[2,192,768]{2,1,0:T(8,128)(2,1)}, bf16[2,192,768]{2,1,0:T(8,128)(2,1)}, u32[]{:S(2)}, u32[]{:S(2)}) collective-permute-start(bf16[2,192,768]{2,1,0:T(8,128)(2,1)} %get-tuple-element.56), channel_id=1, source_target_pairs={{0,32},{32,0},{1,33},{33,1},{2,34},{34,2},{3,35},{35,3},{4,36},{36... | collective-permute-start | bytes 1769480 | tf_op jit(solution)/shard_map/ppermute | solution.py:294
  132.1 23.0 %collective-permute-start.8 = (bf16[2,192,768]{2,1,0:T(8,128)(2,1)}, bf16[2,192,768]{2,1,0:T(8,128)(2,1)}, u32[]{:S(2)}, u32[]{:S(2)}) collective-permute-start(bf16[2,192,768]{2,1,0:T(8,128)(2,1)} %get-tuple-element.58), channel_id=1, source_target_pairs={{0,128},{128,0},{1,129},{129,1},{2,130},{130,2},{3,131},{131,3},{4... | collective-permute-start | bytes 1769480 | tf_op jit(solution)/shard_map/ppermute | solution.py:292
  132.5 31.5 %collective-permute-start.9 = (bf16[2,192,768]{2,1,0:T(8,128)(2,1)}, bf16[2,192,768]{2,1,0:T(8,128)(2,1)}, u32[]{:S(2)}, u32[]{:S(2)}) collective-permute-start(bf16[2,192,768]{2,1,0:T(8,128)(2,1)} %get-tuple-element.59), channel_id=1, source_target_pairs={{32,64},{64,32},{33,65},{65,33},{34,66},{66,34},{35,67},{67,35},{3... | collective-permute-start | bytes 1769480 | tf_op jit(solution)/shard_map/ppermute | solution.py:293
  136.2 27.8 %collective-permute-start.10 = (bf16[2,192,768]{2,1,0:T(8,128)(2,1)}, bf16[2,192,768]{2,1,0:T(8,128)(2,1)}, u32[]{:S(2)}, u32[]{:S(2)}) collective-permute-start(bf16[2,192,768]{2,1,0:T(8,128)(2,1)} %get-tuple-element.60), channel_id=1, source_target_pairs={{0,32},{32,0},{1,33},{33,1},{2,34},{34,2},{3,35},{35,3},{4,36},{36... | collective-permute-start | bytes 1769480 | tf_op jit(solution)/shard_map/ppermute | solution.py:294
  139.1 32.4 %all-to-all-start.4 = ((bf16[4,192,1536]{2,1,0:T(8,128)(2,1)}), bf16[4,192,1536]{2,1,0:T(8,128)(2,1)S(1)}, u32[]{:S(2)}, u32[]{:S(2)}) async-start(bf16[4,192,1536]{2,1,0:T(8,128)(2,1)} %shard_map.88), calls=%async_computation.4 | async-start | bytes 4718592 | tf_op jit(solution)/shard_map/all_to_all | solution.py:248
  142.9 7.4 %copy-start.6 = (bf16[2,192,768]{2,1,0:T(8,128)(2,1)S(1)}, bf16[2,192,768]{2,1,0:T(8,128)(2,1)}, u32[]{:S(2)}) copy-start(bf16[2,192,768]{2,1,0:T(8,128)(2,1)} %get-tuple-element.53) | copy-start | bytes 1769476
  152.7 13.2 %collective-permute-start.13 = (bf16[48,768]{1,0:T(8,128)(2,1)}, bf16[48,768]{1,0:T(8,128)(2,1)S(1)}, u32[]{:S(2)}, u32[]{:S(2)}) collective-permute-start(bf16[48,768]{1,0:T(8,128)(2,1)} %reduce_sum.25), channel_id=1, source_target_pairs={{0,192},{64,128},{128,64},{192,0},{1,193},{65,129},{129,65},{193,1... | collective-permute-start | bytes 221192 | tf_op jit(solution)/shard_map/ppermute | solution.py:311
  152.7 13.2 %collective-permute-start.12 = (bf16[48,768]{1,0:T(8,128)(2,1)}, bf16[48,768]{1,0:T(8,128)(2,1)S(1)}, u32[]{:S(2)}, u32[]{:S(2)}) collective-permute-start(bf16[48,768]{1,0:T(8,128)(2,1)} %reduce_sum.25), channel_id=1, source_target_pairs={{0,64},{64,0},{1,65},{65,1},{2,66},{66,2},{3,67},{67,3},{4,68},{68... | collective-permute-start | bytes 221192 | tf_op jit(solution)/shard_map/ppermute | solution.py:310
  155.1 10.8 %collective-permute-start.11 = (bf16[48,768]{1,0:T(8,128)(2,1)}, bf16[48,768]{1,0:T(8,128)(2,1)S(1)}, u32[]{:S(2)}, u32[]{:S(2)}) collective-permute-start(bf16[48,768]{1,0:T(8,128)(2,1)} %reduce_sum.25), channel_id=1, source_target_pairs={{0,128},{128,0},{1,129},{129,1},{2,130},{130,2},{3,131},{131,3},{4... | collective-permute-start | bytes 221192 | tf_op jit(solution)/shard_map/ppermute | solution.py:309
  166.0 1.5 collective-permute-start.14
  (6 other events, 14.0 us)

commit v4 on v3

--- a/solution.py
+++ b/solution.py
@@ -150,31 +150,33 @@
     )(scalars, q, *kvs, att, d, probs)
 
 
-def d_attention_kernel(scalar_ref, up_ref, mine_ref, mate_ref, out_ref, weight_ref):
+def source(scalar_ref, k):
+    return lax.rem(scalar_ref[2] - k + NY, NY)
+
+
+def d_attention_kernel(scalar_ref, *refs):
+    ups, mine_ref, mate_ref, out_ref, weight_ref = refs[:NY], *refs[NY:]
     half = mine_ref.shape[1]
-
-    @pl.when(pl.program_id(0) == 0)
-    def _():
-        for side, ref in enumerate((mine_ref, mate_ref)):
-            co = scalar_ref[1] if side == 0 else 1 - scalar_ref[1]
-            weight_ref[:, pl.ds(pl.multiple_of(co * half, 128), half)] = ref[...]
-
-    out = lax.dot_general(weight_ref[...], up_ref[0], NT, preferred_element_type=F32)
-    out_ref[0] = jnp.concatenate(
-        [out.astype(BF16), jnp.zeros((out.shape[0], PAD - TILE), BF16)], axis=1
-    )
+    for side, ref in enumerate((mine_ref, mate_ref)):
+        co = scalar_ref[1] if side == 0 else 1 - scalar_ref[1]
+        weight_ref[:, pl.ds(pl.multiple_of(co * half, 128), half)] = ref[...]
+    for k, up in enumerate(ups):
+        out = lax.dot_general(weight_ref[...], up[...], NT, preferred_element_type=F32)
+        out_ref[source(scalar_ref, k)] = jnp.concatenate(
+            [out.astype(BF16), jnp.zeros((out.shape[0], PAD - TILE), BF16)], axis=1
+        )
 
 
 def d_attention(scalars, ups, w_mine, w_mate):
-    dout = ups.shape[2]
+    dout = ups[0].shape[1]
     rows = w_mine.shape[0]
     return pl.pallas_call(
         d_attention_kernel,
         grid_spec=pltpu.PrefetchScalarGridSpec(
             num_scalar_prefetch=1,
-            grid=(NY,),
-            in_specs=[pl.BlockSpec((1, TILE, dout), lambda i, b: (i, 0, 0))] + [whole(w_mine.shape)] * 2,
-            out_specs=[pl.BlockSpec((1, rows, PAD), lambda i, b: (i, 0, 0)), whole((rows, dout))],
+            grid=(1,),
+            in_specs=[whole((TILE, dout))] * NY + [whole(w_mine.shape)] * 2,
+            out_specs=[whole((NY, rows, PAD)), whole((rows, dout))],
         ),
         out_shape=[
             jax.ShapeDtypeStruct((NY, rows, PAD), BF16),
@@ -184,32 +186,32 @@
         cost_estimate=pl.CostEstimate(
             flops=8 * TILE * rows * dout, bytes_accessed=8 * TILE * dout + 4 * rows * dout, transcendentals=0
         ),
-    )(scalars, ups, w_mine, w_mate)
-
-
-def gradient_kernel(scalar_ref, att_ref, mine_ref, mate_ref, out_mine_ref, out_mate_ref):
-    for up_ref, out_ref in ((mine_ref, out_mine_ref), (mate_ref, out_mate_ref)):
-        total = jnp.dot(att_ref[0][:, :TILE], up_ref[0], preferred_element_type=F32)
-        for k in range(1, NY):
-            total += jnp.dot(att_ref[k][:, :TILE], up_ref[k], preferred_element_type=F32)
+    )(scalars, *ups, w_mine, w_mate)
+
+
+def gradient_kernel(scalar_ref, att_ref, *refs):
+    ups, outs = refs[: 2 * NY], refs[2 * NY :]
+    for side, out_ref in enumerate(outs):
+        total = 0.0
+        for k in range(NY):
+            att = att_ref[source(scalar_ref, k)][:, :TILE]
+            total += jnp.dot(att, ups[side * NY + k][...], preferred_element_type=F32)
         out_ref[...] = total.astype(out_ref.dtype)
 
 
 def weight_gradient(scalars, atts, ups):
-    half = ups.shape[2] // 2
+    half = ups[0].shape[1] // 2
     rows = atts.shape[1]
     step = 256
     steps = half // step
+    mine = pl.BlockSpec((TILE, step), lambda i, b: (0, b[1] * steps + i))
+    mate = pl.BlockSpec((TILE, step), lambda i, b: (0, (1 - b[1]) * steps + i))
     return pl.pallas_call(
         gradient_kernel,
         grid_spec=pltpu.PrefetchScalarGridSpec(
             num_scalar_prefetch=1,
             grid=(steps,),
-            in_specs=[
-                whole(atts.shape),
-                pl.BlockSpec((NY, TILE, step), lambda i, b: (0, 0, b[1] * steps + i)),
-                pl.BlockSpec((NY, TILE, step), lambda i, b: (0, 0, (1 - b[1]) * steps + i)),
-            ],
+            in_specs=[whole(atts.shape)] + [mine] * NY + [mate] * NY,
             out_specs=[pl.BlockSpec((rows, step), lambda i, b: (0, i))] * 2,
         ),
         out_shape=[jax.ShapeDtypeStruct((rows, half), BF16)] * 2,
@@ -217,31 +219,42 @@
         cost_estimate=pl.CostEstimate(
             flops=16 * TILE * rows * half, bytes_accessed=16 * TILE * (rows + half), transcendentals=0
         ),
-    )(scalars, atts, ups, ups)
-
-
-def mixed_kernel(att_ref, weight_ref, out_ref):
-    att = att_ref[0][:, :TILE]
-    out_ref[0] = lax.dot_general(att, weight_ref[...], TN, preferred_element_type=F32).astype(BF16)
-
-
-def mixed_parts(atts, weight):
+    )(scalars, atts, *ups, *ups)
+
+
+def mixed_kernel(scalar_ref, att_ref, weight_ref, *outs):
+    for k, out_ref in enumerate(outs):
+        att = att_ref[source(scalar_ref, k)][:, :TILE]
+        out = lax.dot_general(att, weight_ref[...], TN, preferred_element_type=F32)
+        out_ref[...] = out.astype(BF16)
+
+
+def mixed_parts(scalars, atts, weight):
     rows, dout = weight.shape
+    step = 512
     return pl.pallas_call(
         mixed_kernel,
-        grid=(NY,),
-        in_specs=[pl.BlockSpec((1, rows, PAD), lambda i: (i, 0, 0)), whole((rows, dout))],
-        out_specs=pl.BlockSpec((1, TILE, dout), lambda i: (i, 0, 0)),
-        out_shape=jax.ShapeDtypeStruct((NY, TILE, dout), BF16),
+        grid_spec=pltpu.PrefetchScalarGridSpec(
+            num_scalar_prefetch=1,
+            grid=(dout // step,),
+            in_specs=[whole(atts.shape), pl.BlockSpec((rows, step), lambda i, b: (0, i))],
+            out_specs=[pl.BlockSpec((TILE, step), lambda i, b: (0, i))] * NY,
+        ),
+        out_shape=[jax.ShapeDtypeStruct((TILE, dout), BF16)] * NY,
         compiler_params=PARAMS,
         cost_estimate=pl.CostEstimate(
             flops=8 * TILE * rows * dout, bytes_accessed=10 * TILE * dout, transcendentals=0
         ),
-    )(atts, weight)
+    )(scalars, atts, weight)
 
 
 SWAP = [(0, 1), (1, 0)]
 CROSS = [(1, 2), (2, 1)]
+
+
+def shifted(x, axis, by):
+    count = lax.axis_size(axis)
+    return lax.ppermute(x, axis, [(i, (i + by) % count) for i in range(count)])
 
 
 def swapped(x, axis):
@@ -263,7 +276,7 @@
 
     has_cross = lax.axis_index("xh") != co
     bound = jnp.where(has_cross, SLOTS * TILE, (SLOTS - 1) * TILE)
-    scalars = jnp.stack([bound, co]).astype(jnp.int32)
+    scalars = jnp.stack([bound, co, lax.axis_index("y")]).astype(jnp.int32)
 
     from_time = lax.ppermute(kv, "xl", SWAP)
     from_cross = lax.ppermute(kv, ("xh", "co"), CROSS)
@@ -272,7 +285,7 @@
 
     panel = lax.dynamic_slice(out_weight, (block_pick[0], 0, co * half), (1, rows, half))
     w_mine = swapped(jnp.broadcast_to(panel, (nz, rows, half)), "z").reshape(nz * rows, half)
-    ups = swapped(jnp.broadcast_to(up[None], (ny, TILE, dout)), "y")
+    ups = [up] + [shifted(up, "y", k) for k in (1, 2, 3)]
     w_mate = lax.ppermute(w_mine, "co", SWAP)
     d_parts, w_rows = d_attention(scalars, ups, w_mine, w_mate)
     d_turned = swapped(d_parts, "y").reshape(ny, nz, rows, PAD)
@@ -293,18 +306,22 @@
             lax.ppermute(to_cross, ("xh", "co"), CROSS),
             lax.ppermute(to_core, "co", SWAP),
         )
-        return gq, own.astype(F32) + sum(t.astype(F32) for t in terms)
-
-    gq_0, gkv_0 = backward(0)
+        return gq, own, terms
+
+    gq_0, own_0, terms_0 = backward(0)
     atts, gq_0 = lax.optimization_barrier((atts, gq_0))
     grad_mine, grad_mate = weight_gradient(scalars, atts, ups)
     from_mate = lax.ppermute(grad_mate, "co", SWAP)
     atts, w_rows, grad_mine = lax.optimization_barrier((atts, w_rows, grad_mine))
-    mixed = mixed_parts(atts, w_rows)
+    mixed = mixed_parts(scalars, atts, w_rows)
     grad = (grad_mine.astype(F32) + from_mate.astype(F32)).astype(BF16).reshape(nz, rows, half)
-    probs, grad, mixed = lax.optimization_barrier((probs, grad, mixed))
-    gq_1, gkv_1 = backward(1)
-    gq_parts, gkv_parts = (gq_0, gq_1), (gkv_0, gkv_1)
+    probs, grad, mixed, terms_0 = lax.optimization_barrier((probs, grad, mixed, terms_0))
+    gq_1, own_1, terms_1 = backward(1)
+    gkv_parts = [
+        own.astype(F32) + sum(t.astype(F32) for t in terms)
+        for own, terms in ((own_0, terms_0), (own_1, terms_1))
+    ]
+    gq_parts = (gq_0, gq_1)
     over_z = jnp.sum(swapped(grad, "z").astype(F32), axis=0).astype(BF16)
     x_near = lax.ppermute(over_z, "xl", SWAP)
     x_far = lax.ppermute(over_z, "xh", SWAP)
@@ -315,7 +332,8 @@
         [jnp.where(first, mine, mate), jnp.where(first, mate, mine)], axis=1
     )
 
-    mixed = jnp.sum(swapped(mixed, "y").astype(F32), axis=0).astype(BF16)
+    back = [shifted(mixed[k], "y", -k).astype(F32) for k in (1, 2, 3)]
+    mixed = (mixed[0].astype(F32) + sum(back)).astype(BF16)
     grad_q = jnp.concatenate(gq_parts, axis=1)
     grad_kv = jnp.concatenate([p.astype(BF16) for p in gkv_parts], axis=2)
     return (

time: 174 us -> 159 us (0.914)
  blocking collectives: 26.4 us -> 0 us
  starting transfers between devices: 41.5 us -> 67.3 us
  waiting for transfers between devices: 47.1 us -> 37.2 us
  local copies, waits for them, and re-layouts: 5.76 us -> 3.28 us
  other arithmetic: 11.2 us -> 8.79 us
    all_to_all x1 -> x0, blocking collectives: 26.4 us -> none  [swapped(): return lax.all_to_all(x, axis, split_axis=0, concat_axis=0, tiled=True)]
    all_to_all x5 -> x4, waiting for transfers between devices: 22.3 us -> 5.28 us  [swapped(): return lax.all_to_all(x, axis, split_axis=0, concat_axis=0, tiled=True)]
    ppermute x0 -> x6, waiting for transfers between devices: none -> 9.86 us  [shifted(): return lax.ppermute(x, axis, [(i, (i + by) % count) for i in range(count)])]
    ppermute x1, starting transfers between devices: 0.69 us -> 9.86 us  [per_device(): w_mate = lax.ppermute(w_mine, 'co', SWAP)]
    all_to_all x5 -> x4, starting transfers between devices: 19.7 us -> 25.8 us  [swapped(): return lax.all_to_all(x, axis, split_axis=0, concat_axis=0, tiled=True)]
    ppermute x1, starting transfers between devices: 0.01 us -> 5.33 us  [per_device(): from_mate = lax.ppermute(grad_mate, 'co', SWAP)]
    ppermute x0 -> x6, starting transfers between devices: none -> 4.76 us  [shifted(): return lax.ppermute(x, axis, [(i, (i + by) % count) for i in range(count)])]
    ppermute x1, waiting for transfers between devices: 9.57 us -> 6.07 us  [per_device(): from_time = lax.ppermute(kv, 'xl', SWAP)]
  transfers between devices with their start and end apart: 20 -> 25, of which waited for: 9 -> 13; matrix products, arithmetic and copies ran while one was open for 5% -> 5% of each run, Pallas kernels for 20% -> 21%
where the time goes in v4:
time: 159 us; the launch traced here: 157 us
  starting transfers between devices  67.3 us (42%)
  Pallas kernels  39.3 us (25%)
  waiting for transfers between devices  37.2 us (23%)
  other arithmetic  8.79 us (6%)
  local copies, waits for them, and re-layouts  3.28 us (2%)
  between operations  1.59 us (1%)
    all_to_all x4, starting transfers between devices, swapped(): return lax.all_to_all(x, axis, split_axis=0, concat_axis=0, tiled=True)  25.8 us
    pallas_call x2, Pallas kernels, attention_backward(): pl.pallas_call(backward_kernel, grid_spec=pltpu.PrefetchScalarGridSpec(nu...  13.6 us
    ppermute x2, waiting for transfers between devices, backward(): lax.ppermute(to_cross, ('xh', 'co'), CROSS)  9.92 us
    pallas_call x1, Pallas kernels, attention_forward(): pl.pallas_call(forward_kernel, grid_spec=pltpu.PrefetchScalarGridSpec(num...  9.87 us
    ppermute x1, starting transfers between devices, per_device(): w_mate = lax.ppermute(w_mine, 'co', SWAP)  9.86 us
    ppermute x6, waiting for transfers between devices, shifted(): return lax.ppermute(x, axis, [(i, (i + by) % count) for i in range(count)])  9.86 us
    ppermute x2, starting transfers between devices, backward(): lax.ppermute(to_cross, ('xh', 'co'), CROSS)  9.56 us
    ppermute x1, waiting for transfers between devices, per_device(): from_time = lax.ppermute(kv, 'xl', SWAP)  6.07 us
  transfers between devices with their start and end apart: 25, of which 13 were waited for; matrix products, arithmetic and copies ran while one was open for 5% of the time, Pallas kernels for 21%

profile of v4, /device:TPU:1, one launch (start us, length us, event | category | flops | bytes accessed | tf_op | source)
XLA Modules:
  0.0 157.4 jit_solution(13899017307248744426)
XLA Ops:
  3.1 9.0 %all-to-all-start = ((bf16[8,48,768]{2,1,0:T(8,128)(2,1)}), bf16[8,48,768]{2,1,0:T(8,128)(2,1)}, u32[]{:S(2)}, u32[]{:S(2)}) async-start(bf16[8,48,768]{2,1,0:T(8,128)(2,1)} %broadcast_in_dim.8), calls=%async_computation | async-start | bytes 1179648 | tf_op jit(solution)/shard_map/all_to_all | solution.py:261
  12.2 2.7 %collective-permute-start.5 = (bf16[192,1536]{1,0:T(8,128)(2,1)}, bf16[192,1536]{1,0:T(8,128)(2,1)}, u32[]{:S(2)}, u32[]{:S(2)}) collective-permute-start(bf16[192,1536]{1,0:T(8,128)(2,1)} %bitcast.5.refs_0_.refs_4_), channel_id=1, source_target_pairs={{0,3},{1,0},{2,1},{3,2},{4,7},{5,4},{6,5},{7,6},{8,11},{9,8},{10,9... | collective-permute-start | bytes 1769480 | tf_op jit(solution)/shard_map/ppermute | solution.py:257
  15.2 6.0 %collective-permute-start.2 = (bf16[2,192,1536]{2,1,0:T(8,128)(2,1)S(1)}, bf16[2,192,1536]{2,1,0:T(8,128)(2,1)S(1)}, u32[]{:S(2)}, u32[]{:S(2)}) collective-permute-start(bf16[2,192,1536]{2,1,0:T(8,128)(2,1)S(1)} %bitcast.27), channel_id=1, source_target_pairs={{32,64},{64,32},{33,65},{65,33},{34,66},{66,34},{35,67},{67,35},{3... | collective-permute-start | bytes 3538952 | tf_op jit(solution)/shard_map/ppermute | solution.py:282
  21.8 6.1 %collective-permute-done.5.refs_3_.refs_7_ = bf16[192,1536]{1,0:T(8,128)(2,1)} collective-permute-done((bf16[192,1536]{1,0:T(8,128)(2,1)}, bf16[192,1536]{1,0:T(8,128)(2,1)}, u32[]{:S(2)}, u32[]{:S(2)}) %collective-permute-start.5) | collective-permute-done | bytes 589856 | tf_op jit(solution)/shard_map/ppermute | solution.py:257
  27.9 2.4 %collective-permute-done.4.refs_2_.refs_6_ = bf16[192,1536]{1,0:T(8,128)(2,1)} collective-permute-done((bf16[192,1536]{1,0:T(8,128)(2,1)}, bf16[192,1536]{1,0:T(8,128)(2,1)}, u32[]{:S(2)}, u32[]{:S(2)}) %collective-permute-start.4) | collective-permute-done | bytes 589856 | tf_op jit(solution)/shard_map/ppermute | solution.py:257
  31.6 9.9 %collective-permute-start.6 = (bf16[384,768]{1,0:T(8,128)(2,1)}, bf16[384,768]{1,0:T(8,128)(2,1)}, u32[]{:S(2)}, u32[]{:S(2)}) collective-permute-start(bf16[384,768]{1,0:T(8,128)(2,1)} %bitcast.8.refs_4_), channel_id=1, source_target_pairs={{0,32},{32,0},{1,33},{33,1},{2,34},{34,2},{3,35},{35,3},{4,36},{36... | collective-permute-start | bytes 1769480 | tf_op jit(solution)/shard_map/ppermute | solution.py:289
  43.5 4.9 %shard_map.84 = (bf16[4,384,256]{2,1,0:T(8,128)(2,1)}, bf16[384,1536]{1,0:T(8,128)(2,1)}) custom-call(s32[3]{0:T(128)} %pad_add_fusion.scalar_ref, bf16[192,1536]{1,0:T(8,128)(2,1)} %bitcast.5.refs_0_.refs_4_, bf16[192,1536]{1,0:T(8,128)(2,1)} %collective-permute-done.3.refs_1_.refs_5_, bf16[192,1536]{1,0:T(8,128)(2,1)} %collective-permute-done.4.refs_2_.refs_6_, ...), custom_call_target="tpu_custom_call" | custom-call | flops 905969664 | bytes 4718592 | tf_op jit(solution)/shard_map/pallas_call | solution.py:173
  48.4 6.1 %all-to-all-start.2 = ((bf16[4,384,256]{2,1,0:T(8,128)(2,1)}), bf16[4,384,256]{2,1,0:T(8,128)(2,1)}, u32[]{:S(2)}, u32[]{:S(2)}) async-start(bf16[4,384,256]{2,1,0:T(8,128)(2,1)} %get-tuple-element.43), calls=%async_computation.2 | async-start | bytes 1572864 | tf_op jit(solution)/shard_map/all_to_all | solution.py:261
  54.5 6.1 %collective-permute-done.time_ref = bf16[2,192,1536]{2,1,0:T(8,128)(2,1)} collective-permute-done((bf16[2,192,1536]{2,1,0:T(8,128)(2,1)S(1)}, bf16[2,192,1536]{2,1,0:T(8,128)(2,1)}, u32[]{:S(2)}, u32[]{:S(2)}) %collective-permute-start) | collective-permute-done | bytes 1179680 | tf_op jit(solution)/shard_map/ppermute | solution.py:281
  60.6 9.9 %shard_map.85 = (bf16[192,1536]{1,0:T(8,128)(2,1)}, bf16[4,8,48,256]{3,2,1,0:T(8,128)(2,1)}, bf16[12,192,768]{2,1,0:T(8,128)(2,1)}) custom-call(s32[3]{0:T(128)} %pad_add_fusion.scalar_ref, bf16[192,1536]{1,0:T(8,128)(2,1)} %bitcast.30, bf16[2,192,1536]{2,1,0:T(8,128)(2,1)} %bitcast.24, bf16[2,192,1536]{2,1,0:T(8,128)(2,1)} %collective-permute-done.time_ref, ...), custom_call_target="tpu_custom_call" | custom-call | flops 905969664 | bytes 5898240 | tf_op jit(solution)/shard_map/pallas_call | solution.py:110
  70.4 3.9 %all-to-all-start.1 = ((bf16[4,384,256]{2,1,0:T(8,128)(2,1)}), bf16[4,384,256]{2,1,0:T(8,128)(2,1)S(1)}, u32[]{:S(2)}, u32[]{:S(2)}) async-start(bf16[4,384,256]{2,1,0:T(8,128)(2,1)} %bitcast.33), calls=%async_computation.1 | async-start | bytes 1572864 | tf_op jit(solution)/shard_map/all_to_all | solution.py:261
  74.3 6.7 %shard_map.86 = (bf16[192,768]{1,0:T(8,128)(2,1)}, bf16[2,192,768]{2,1,0:T(8,128)(2,1)}, bf16[2,192,768]{2,1,0:T(8,128)(2,1)}, bf16[2,192,768]{2,1,0:T(8,128)(2,1)}, bf16[2,192,768]{2,1,0:T(8,128)(2,1)}) custom-call(s32[3]{0:T(128)} %pad_add_fusion.scalar_ref, bf16[192,1536]{1,0:T(8,128)(2,1)} %bitcast.31, bf16[2,192,1536]{2,1,0:T(8,128)(2,1)} %bitcast.25, ...), custom_call_target="tpu_custom_call" | custom-call | flops 1358954496 | bytes 7077888 | tf_op jit(solution)/shard_map/pallas_call | solution.py:134
  83.6 5.8 %shard_map.87 = (bf16[384,768]{1,0:T(8,128)(2,1)}, bf16[384,768]{1,0:T(8,128)(2,1)}) custom-call(s32[3]{0:T(128)} %pad_add_fusion.scalar_ref, bf16[4,384,256]{2,1,0:T(8,128)(2,1)} %copy-done.3, bf16[192,1536]{1,0:T(8,128)(2,1)} %bitcast.5.refs_0_.refs_4_, bf16[192,1536]{1,0:T(8,128)(2,1)} %collective-permute-done.3.refs_1_.refs_5_, ...), custom_call_target="tpu_custom_call" | custom-call | flops 905969664 | bytes 3538944 | tf_op jit(solution)/shard_map/pallas_call | solution.py:209
  89.3 5.3 %collective-permute-start.7 = (bf16[384,768]{1,0:T(8,128)(2,1)}, bf16[384,768]{1,0:T(8,128)(2,1)S(1)}, u32[]{:S(2)}, u32[]{:S(2)}) collective-permute-start(bf16[384,768]{1,0:T(8,128)(2,1)} %get-tuple-element.56), channel_id=1, source_target_pairs={{0,32},{32,0},{1,33},{33,1},{2,34},{34,2},{3,35},{35,3},{4,36},{36... | collective-permute-start | bytes 1769480 | tf_op jit(solution)/shard_map/ppermute | solution.py:314
  95.9 4.6 %collective-permute-start.9 = (bf16[2,192,768]{2,1,0:T(8,128)(2,1)S(1)}, bf16[2,192,768]{2,1,0:T(8,128)(2,1)S(1)}, u32[]{:S(2)}, u32[]{:S(2)}) collective-permute-start(bf16[2,192,768]{2,1,0:T(8,128)(2,1)S(1)} %copy-done.11), channel_id=1, source_target_pairs={{32,64},{64,32},{33,65},{65,33},{34,66},{66,34},{35,67},{67,35},{3... | collective-permute-start | bytes 1769480 | tf_op jit(solution)/shard_map/ppermute | solution.py:306
  100.6 5.1 %shard_map.88 = (bf16[192,1536]{1,0:T(8,128)(2,1)}, bf16[192,1536]{1,0:T(8,128)(2,1)}, bf16[192,1536]{1,0:T(8,128)(2,1)}, bf16[192,1536]{1,0:T(8,128)(2,1)}) custom-call(s32[3]{0:T(128)} %pad_add_fusion.scalar_ref, bf16[4,384,256]{2,1,0:T(8,128)(2,1)} %copy-done.3, bf16[384,1536]{1,0:T(8,128)(2,1)} %get-tuple-element.58.weight_ref), custom_call_target="tpu_custom_call" | custom-call | flops 905969664 | bytes 2949120 | tf_op jit(solution)/shard_map/pallas_call | solution.py:235
  106.7 2.9 %collective-permute-done.8 = bf16[2,192,768]{2,1,0:T(8,128)(2,1)S(1)} collective-permute-done((bf16[2,192,768]{2,1,0:T(8,128)(2,1)S(1)}, bf16[2,192,768]{2,1,0:T(8,128)(2,1)S(1)}, u32[]{:S(2)}, u32[]{:S(2)}) %collective-permute-start.8) | collective-permute-done | bytes 589856 | tf_op jit(solution)/shard_map/ppermute | solution.py:305
  109.6 9.1 %collective-permute-done.9 = bf16[2,192,768]{2,1,0:T(8,128)(2,1)S(1)} collective-permute-done((bf16[2,192,768]{2,1,0:T(8,128)(2,1)S(1)}, bf16[2,192,768]{2,1,0:T(8,128)(2,1)S(1)}, u32[]{:S(2)}, u32[]{:S(2)}) %collective-permute-start.9) | collective-permute-done | bytes 589856 | tf_op jit(solution)/shard_map/ppermute | solution.py:306
  120.3 6.9 %shard_map.89 = (bf16[192,768]{1,0:T(8,128)(2,1)}, bf16[2,192,768]{2,1,0:T(8,128)(2,1)}, bf16[2,192,768]{2,1,0:T(8,128)(2,1)}, bf16[2,192,768]{2,1,0:T(8,128)(2,1)}, bf16[2,192,768]{2,1,0:T(8,128)(2,1)}) custom-call(s32[3]{0:T(128)} %pad_add_fusion.scalar_ref, bf16[192,1536]{1,0:T(8,128)(2,1)} %bitcast.32, bf16[2,192,1536]{2,1,0:T(8,128)(2,1)} %bitcast.26, ...), custom_call_target="tpu_custom_call" | custom-call | flops 1358954496 | bytes 7077888 | tf_op jit(solution)/shard_map/pallas_call | solution.py:134
  127.2 6.8 %all-to-all-start.3 = ((bf16[8,48,768]{2,1,0:T(8,128)(2,1)}), bf16[8,48,768]{2,1,0:T(8,128)(2,1)S(1)}, u32[]{:S(2)}, u32[]{:S(2)}) async-start(bf16[8,48,768]{2,1,0:T(8,128)(2,1)} %bitcast.11), calls=%async_computation.3 | async-start | bytes 1179648 | tf_op jit(solution)/shard_map/all_to_all | solution.py:261
  134.0 5.0 %collective-permute-start.15 = (bf16[2,192,768]{2,1,0:T(8,128)(2,1)}, bf16[2,192,768]{2,1,0:T(8,128)(2,1)}, u32[]{:S(2)}, u32[]{:S(2)}) collective-permute-start(bf16[2,192,768]{2,1,0:T(8,128)(2,1)} %get-tuple-element.79), channel_id=1, source_target_pairs={{32,64},{64,32},{33,65},{65,33},{34,66},{66,34},{35,67},{67,35},{3... | collective-permute-start | bytes 1769480 | tf_op jit(solution)/shard_map/ppermute | solution.py:306
  142.3 2.5 %fusion = bf16[1,1,1,192,1536]{4,3,2,1,0:T(8,128)(2,1)} fusion(bf16[192,1536]{1,0:T(8,128)(2,1)} %collective-permute-done.13, bf16[192,1536]{1,0:T(8,128)(2,1)} %collective-permute-done.12, bf16[192,1536]{1,0:T(8,128)(2,1)} %collective-permute-done.11, bf16[192,1536]{1,0:T(8,128)(2,1)S(1)} %copy-done.6), kind=kLoop, calls=%fused_computation.5 | loop fusion | flops 2359296 | bytes 2949120 | tf_op jit(solution)/shard_map/reshape | solution.py:340
  144.8 2.3 %all-to-all-done.3 = bf16[8,48,768]{2,1,0:T(8,128)(2,1)S(1)} async-done(((bf16[8,48,768]{2,1,0:T(8,128)(2,1)}), bf16[8,48,768]{2,1,0:T(8,128)(2,1)S(1)}, u32[]{:S(2)}, u32[]{:S(2)}) %all-to-all-start.3) | async-done | bytes 589856 | tf_op jit(solution)/shard_map/all_to_all | solution.py:261
  147.3 3.0 %collective-permute-start.18 = (bf16[48,768]{1,0:T(8,128)(2,1)S(1)}, bf16[48,768]{1,0:T(8,128)(2,1)S(1)}, u32[]{:S(2)}, u32[]{:S(2)}) collective-permute-start(bf16[48,768]{1,0:T(8,128)(2,1)S(1)} %reduce_sum.12), channel_id=1, source_target_pairs={{0,64},{64,0},{1,65},{65,1},{2,66},{66,2},{3,67},{67,3},{4,68},{68... | collective-permute-start | bytes 221192 | tf_op jit(solution)/shard_map/ppermute | solution.py:327
  (71 shorter events, 22.9 us)
Async XLA Ops:
  3.1 28.5 %all-to-all-start = ((bf16[8,48,768]{2,1,0:T(8,128)(2,1)}), bf16[8,48,768]{2,1,0:T(8,128)(2,1)}, u32[]{:S(2)}, u32[]{:S(2)}) async-start(bf16[8,48,768]{2,1,0:T(8,128)(2,1)} %broadcast_in_dim.8), calls=%async_computation | async-start | bytes 1179648 | tf_op jit(solution)/shard_map/all_to_all | solution.py:261
  12.2 15.8 %collective-permute-start.5 = (bf16[192,1536]{1,0:T(8,128)(2,1)}, bf16[192,1536]{1,0:T(8,128)(2,1)}, u32[]{:S(2)}, u32[]{:S(2)}) collective-permute-start(bf16[192,1536]{1,0:T(8,128)(2,1)} %bitcast.5.refs_0_.refs_4_), channel_id=1, source_target_pairs={{0,3},{1,0},{2,1},{3,2},{4,7},{5,4},{6,5},{7,6},{8,11},{9,8},{10,9... | collective-permute-start | bytes 1769480 | tf_op jit(solution)/shard_map/ppermute | solution.py:257
  14.9 15.4 %collective-permute-start.4 = (bf16[192,1536]{1,0:T(8,128)(2,1)}, bf16[192,1536]{1,0:T(8,128)(2,1)}, u32[]{:S(2)}, u32[]{:S(2)}) collective-permute-start(bf16[192,1536]{1,0:T(8,128)(2,1)} %bitcast.5.refs_0_.refs_4_), channel_id=1, source_target_pairs={{0,2},{1,3},{2,0},{3,1},{4,6},{5,7},{6,4},{7,5},{8,10},{9,11},{10,... | collective-permute-start | bytes 1769480 | tf_op jit(solution)/shard_map/ppermute | solution.py:257
  15.2 39.2 %collective-permute-start.2 = (bf16[2,192,1536]{2,1,0:T(8,128)(2,1)S(1)}, bf16[2,192,1536]{2,1,0:T(8,128)(2,1)S(1)}, u32[]{:S(2)}, u32[]{:S(2)}) collective-permute-start(bf16[2,192,1536]{2,1,0:T(8,128)(2,1)S(1)} %bitcast.27), channel_id=1, source_target_pairs={{32,64},{64,32},{33,65},{65,33},{34,66},{66,34},{35,67},{67,35},{3... | collective-permute-start | bytes 3538952 | tf_op jit(solution)/shard_map/ppermute | solution.py:282
  21.3 33.2 %collective-permute-start.1 = (bf16[2,192,1536]{2,1,0:T(8,128)(2,1)S(1)}, bf16[2,192,1536]{2,1,0:T(8,128)(2,1)S(1)}, u32[]{:S(2)}, u32[]{:S(2)}) collective-permute-start(bf16[2,192,1536]{2,1,0:T(8,128)(2,1)S(1)} %bitcast.28), channel_id=1, source_target_pairs={{0,32},{32,0},{1,33},{33,1},{2,34},{34,2},{3,35},{35,3},{4,36},{36... | collective-permute-start | bytes 3538952 | tf_op jit(solution)/shard_map/ppermute | solution.py:283
  21.4 39.2 %collective-permute-start = (bf16[2,192,1536]{2,1,0:T(8,128)(2,1)S(1)}, bf16[2,192,1536]{2,1,0:T(8,128)(2,1)}, u32[]{:S(2)}, u32[]{:S(2)}) collective-permute-start(bf16[2,192,1536]{2,1,0:T(8,128)(2,1)S(1)} %bitcast.29), channel_id=1, source_target_pairs={{0,128},{128,0},{1,129},{129,1},{2,130},{130,2},{3,131},{131,3},{4... | collective-permute-start | bytes 3538952 | tf_op jit(solution)/shard_map/ppermute | solution.py:281
  27.9 14.2 %collective-permute-start.3 = (bf16[192,1536]{1,0:T(8,128)(2,1)}, bf16[192,1536]{1,0:T(8,128)(2,1)}, u32[]{:S(2)}, u32[]{:S(2)}) collective-permute-start(bf16[192,1536]{1,0:T(8,128)(2,1)} %bitcast.5.refs_0_.refs_4_), channel_id=1, source_target_pairs={{0,1},{1,2},{2,3},{3,0},{4,5},{5,6},{6,7},{7,4},{8,9},{9,10},{10,1... | collective-permute-start | bytes 1769480 | tf_op jit(solution)/shard_map/ppermute | solution.py:257
  31.6 11.8 %collective-permute-start.6 = (bf16[384,768]{1,0:T(8,128)(2,1)}, bf16[384,768]{1,0:T(8,128)(2,1)}, u32[]{:S(2)}, u32[]{:S(2)}) collective-permute-start(bf16[384,768]{1,0:T(8,128)(2,1)} %bitcast.8.refs_4_), channel_id=1, source_target_pairs={{0,32},{32,0},{1,33},{33,1},{2,34},{34,2},{3,35},{35,3},{4,36},{36... | collective-permute-start | bytes 1769480 | tf_op jit(solution)/shard_map/ppermute | solution.py:289
  48.4 22.0 %all-to-all-start.2 = ((bf16[4,384,256]{2,1,0:T(8,128)(2,1)}), bf16[4,384,256]{2,1,0:T(8,128)(2,1)}, u32[]{:S(2)}, u32[]{:S(2)}) async-start(bf16[4,384,256]{2,1,0:T(8,128)(2,1)} %get-tuple-element.43), calls=%async_computation.2 | async-start | bytes 1572864 | tf_op jit(solution)/shard_map/all_to_all | solution.py:261
  70.4 12.2 %all-to-all-start.1 = ((bf16[4,384,256]{2,1,0:T(8,128)(2,1)}), bf16[4,384,256]{2,1,0:T(8,128)(2,1)S(1)}, u32[]{:S(2)}, u32[]{:S(2)}) async-start(bf16[4,384,256]{2,1,0:T(8,128)(2,1)} %bitcast.33), calls=%async_computation.1 | async-start | bytes 1572864 | tf_op jit(solution)/shard_map/all_to_all | solution.py:261
  89.3 16.4 %collective-permute-start.7 = (bf16[384,768]{1,0:T(8,128)(2,1)}, bf16[384,768]{1,0:T(8,128)(2,1)S(1)}, u32[]{:S(2)}, u32[]{:S(2)}) collective-permute-start(bf16[384,768]{1,0:T(8,128)(2,1)} %get-tuple-element.56), channel_id=1, source_target_pairs={{0,32},{32,0},{1,33},{33,1},{2,34},{34,2},{3,35},{35,3},{4,36},{36... | collective-permute-start | bytes 1769480 | tf_op jit(solution)/shard_map/ppermute | solution.py:314
  94.7 14.9 %collective-permute-start.8 = (bf16[2,192,768]{2,1,0:T(8,128)(2,1)S(1)}, bf16[2,192,768]{2,1,0:T(8,128)(2,1)S(1)}, u32[]{:S(2)}, u32[]{:S(2)}) collective-permute-start(bf16[2,192,768]{2,1,0:T(8,128)(2,1)S(1)} %copy-done.12), channel_id=1, source_target_pairs={{0,128},{128,0},{1,129},{129,1},{2,130},{130,2},{3,131},{131,3},{4... | collective-permute-start | bytes 1769480 | tf_op jit(solution)/shard_map/ppermute | solution.py:305
  95.9 22.8 %collective-permute-start.9 = (bf16[2,192,768]{2,1,0:T(8,128)(2,1)S(1)}, bf16[2,192,768]{2,1,0:T(8,128)(2,1)S(1)}, u32[]{:S(2)}, u32[]{:S(2)}) collective-permute-start(bf16[2,192,768]{2,1,0:T(8,128)(2,1)S(1)} %copy-done.11), channel_id=1, source_target_pairs={{32,64},{64,32},{33,65},{65,33},{34,66},{66,34},{35,67},{67,35},{3... | collective-permute-start | bytes 1769480 | tf_op jit(solution)/shard_map/ppermute | solution.py:306
  100.5 18.1 %collective-permute-start.10 = (bf16[2,192,768]{2,1,0:T(8,128)(2,1)S(1)}, bf16[2,192,768]{2,1,0:T(8,128)(2,1)S(1)}, u32[]{:S(2)}, u32[]{:S(2)}) collective-permute-start(bf16[2,192,768]{2,1,0:T(8,128)(2,1)S(1)} %copy-done.10), channel_id=1, source_target_pairs={{0,32},{32,0},{1,33},{33,1},{2,34},{34,2},{3,35},{35,3},{4,36},{36... | collective-permute-start | bytes 1769480 | tf_op jit(solution)/shard_map/ppermute | solution.py:307
  118.7 20.7 %collective-permute-start.11 = (bf16[192,1536]{1,0:T(8,128)(2,1)}, bf16[192,1536]{1,0:T(8,128)(2,1)}, u32[]{:S(2)}, u32[]{:S(2)}) collective-permute-start(bf16[192,1536]{1,0:T(8,128)(2,1)} %get-tuple-element.67), channel_id=1, source_target_pairs={{0,3},{1,0},{2,1},{3,2},{4,7},{5,4},{6,5},{7,6},{8,11},{9,8},{10,9... | collective-permute-start | bytes 1769480 | tf_op jit(solution)/shard_map/ppermute | solution.py:257
  119.2 21.7 %collective-permute-start.12 = (bf16[192,1536]{1,0:T(8,128)(2,1)}, bf16[192,1536]{1,0:T(8,128)(2,1)}, u32[]{:S(2)}, u32[]{:S(2)}) collective-permute-start(bf16[192,1536]{1,0:T(8,128)(2,1)} %get-tuple-element.68), channel_id=1, source_target_pairs={{0,2},{1,3},{2,0},{3,1},{4,6},{5,7},{6,4},{7,5},{8,10},{9,11},{10,... | collective-permute-start | bytes 1769480 | tf_op jit(solution)/shard_map/ppermute | solution.py:257
  120.3 21.9 %collective-permute-start.13 = (bf16[192,1536]{1,0:T(8,128)(2,1)}, bf16[192,1536]{1,0:T(8,128)(2,1)}, u32[]{:S(2)}, u32[]{:S(2)}) collective-permute-start(bf16[192,1536]{1,0:T(8,128)(2,1)} %get-tuple-element.69), channel_id=1, source_target_pairs={{0,1},{1,2},{2,3},{3,0},{4,5},{5,6},{6,7},{7,4},{8,9},{9,10},{10,1... | collective-permute-start | bytes 1769480 | tf_op jit(solution)/shard_map/ppermute | solution.py:257
  127.2 19.9 %all-to-all-start.3 = ((bf16[8,48,768]{2,1,0:T(8,128)(2,1)}), bf16[8,48,768]{2,1,0:T(8,128)(2,1)S(1)}, u32[]{:S(2)}, u32[]{:S(2)}) async-start(bf16[8,48,768]{2,1,0:T(8,128)(2,1)} %bitcast.11), calls=%async_computation.3 | async-start | bytes 1179648 | tf_op jit(solution)/shard_map/all_to_all | solution.py:261
  134.0 16.3 %collective-permute-start.14 = (bf16[2,192,768]{2,1,0:T(8,128)(2,1)}, bf16[2,192,768]{2,1,0:T(8,128)(2,1)}, u32[]{:S(2)}, u32[]{:S(2)}) collective-permute-start(bf16[2,192,768]{2,1,0:T(8,128)(2,1)} %get-tuple-element.78), channel_id=1, source_target_pairs={{0,128},{128,0},{1,129},{129,1},{2,130},{130,2},{3,131},{131,3},{4... | collective-permute-start | bytes 1769480 | tf_op jit(solution)/shard_map/ppermute | solution.py:305
  134.0 17.4 %collective-permute-start.15 = (bf16[2,192,768]{2,1,0:T(8,128)(2,1)}, bf16[2,192,768]{2,1,0:T(8,128)(2,1)}, u32[]{:S(2)}, u32[]{:S(2)}) collective-permute-start(bf16[2,192,768]{2,1,0:T(8,128)(2,1)} %get-tuple-element.79), channel_id=1, source_target_pairs={{32,64},{64,32},{33,65},{65,33},{34,66},{66,34},{35,67},{67,35},{3... | collective-permute-start | bytes 1769480 | tf_op jit(solution)/shard_map/ppermute | solution.py:306
  139.3 12.0 %collective-permute-start.16 = (bf16[2,192,768]{2,1,0:T(8,128)(2,1)}, bf16[2,192,768]{2,1,0:T(8,128)(2,1)S(1)}, u32[]{:S(2)}, u32[]{:S(2)}) collective-permute-start(bf16[2,192,768]{2,1,0:T(8,128)(2,1)} %get-tuple-element.80), channel_id=1, source_target_pairs={{0,32},{32,0},{1,33},{33,1},{2,34},{34,2},{3,35},{35,3},{4,36},{36... | collective-permute-start | bytes 1769480 | tf_op jit(solution)/shard_map/ppermute | solution.py:307
  147.2 6.6 %collective-permute-start.19 = (bf16[48,768]{1,0:T(8,128)(2,1)S(1)}, bf16[48,768]{1,0:T(8,128)(2,1)S(1)}, u32[]{:S(2)}, u32[]{:S(2)}) collective-permute-start(bf16[48,768]{1,0:T(8,128)(2,1)S(1)} %reduce_sum.12), channel_id=1, source_target_pairs={{0,192},{64,128},{128,64},{192,0},{1,193},{65,129},{129,65},{193,1... | collective-permute-start | bytes 221192 | tf_op jit(solution)/shard_map/ppermute | solution.py:328
  147.3 6.5 %collective-permute-start.18 = (bf16[48,768]{1,0:T(8,128)(2,1)S(1)}, bf16[48,768]{1,0:T(8,128)(2,1)S(1)}, u32[]{:S(2)}, u32[]{:S(2)}) collective-permute-start(bf16[48,768]{1,0:T(8,128)(2,1)S(1)} %reduce_sum.12), channel_id=1, source_target_pairs={{0,64},{64,0},{1,65},{65,1},{2,66},{66,2},{3,67},{67,3},{4,68},{68... | collective-permute-start | bytes 221192 | tf_op jit(solution)/shard_map/ppermute | solution.py:327
  150.3 4.4 %collective-permute-start.17 = (bf16[48,768]{1,0:T(8,128)(2,1)S(1)}, bf16[48,768]{1,0:T(8,128)(2,1)S(1)}, u32[]{:S(2)}, u32[]{:S(2)}) collective-permute-start(bf16[48,768]{1,0:T(8,128)(2,1)S(1)} %reduce_sum.12), channel_id=1, source_target_pairs={{0,128},{128,0},{1,129},{129,1},{2,130},{130,2},{3,131},{131,3},{4... | collective-permute-start | bytes 221192 | tf_op jit(solution)/shard_map/ppermute | solution.py:326
  (14 other events, 102.3 us)

commit v5 on v4

--- a/solution.py
+++ b/solution.py
@@ -8,6 +8,7 @@
 HEADS = 12
 HEAD_DIM = 128
 SCALE = HEAD_DIM ** (-0.5)
+LOG2E = 1.4426950408889634
 TILE = 192
 SLOTS = 4
 PER_STEP = 3
@@ -20,6 +21,7 @@
 TN = (((0,), (0,)), ((), ()))
 F32 = jnp.float32
 BF16 = jnp.bfloat16
+LIGHT = pl.CostEstimate(flops=1000, bytes_accessed=1000, transcendentals=0)
 PARAMS = pltpu.CompilerParams(vmem_limit_bytes=56 * 1024 * 1024)
 
 
@@ -27,29 +29,39 @@
     return jnp.concatenate([ref[which, :, cols] for ref in refs], axis=0)
 
 
-def probs_of(q, k, bound):
-    scores = lax.dot_general(q, k, NT, preferred_element_type=F32)
+def probs_of(scores, bound):
     tail = scores[:, MASKED:]
     column = lax.broadcasted_iota(jnp.int32, tail.shape, 1)
     tail = jnp.where(column + MASKED < bound, tail, -1e30)
     scores = jnp.concatenate([scores[:, :MASKED], tail], axis=1)
     top = jnp.max(scores, axis=1, keepdims=True)
-    weights = jnp.exp((scores - top) * SCALE)
+    weights = jnp.exp2((scores - top) * (SCALE * LOG2E))
     return weights * (1.0 / jnp.sum(weights, axis=1, keepdims=True))
+
+
+def head_cols(h):
+    return slice(h * HEAD_DIM, (h + 1) * HEAD_DIM)
 
 
 def forward_kernel(scalar_ref, q_ref, own_ref, time_ref, core_ref, cross_ref, out_ref, out_t_ref, probs_ref):
     kv = (own_ref, time_ref, core_ref, cross_ref)
+    scores = [
+        lax.dot_general(
+            q_ref[:, head_cols(h)], window_of(kv, 0, head_cols(h)), NT, preferred_element_type=F32
+        )
+        for h in range(PER_STEP)
+    ]
+    outs = []
     for h in range(PER_STEP):
-        cols = slice(h * HEAD_DIM, (h + 1) * HEAD_DIM)
-        k = window_of(kv, 0, cols)
-        v = window_of(kv, 1, cols)
-        probs = probs_of(q_ref[:, cols], k, scalar_ref[0])
-        probs_b = probs.astype(BF16)
+        probs_b = probs_of(scores[h], scalar_ref[0]).astype(BF16)
         probs_ref[h] = probs_b
-        out = jnp.dot(probs_b, v, preferred_element_type=F32)
-        out_ref[:, cols] = out.astype(BF16)
-    flipped = out_ref[...].astype(F32).T.astype(BF16)
+        v = window_of(kv, 1, head_cols(h))
+        outs.append(jnp.dot(probs_b, v, preferred_element_type=F32))
+    flipped = []
+    for h in range(PER_STEP):
+        out_ref[:, head_cols(h)] = outs[h].astype(BF16)
+        flipped.append(outs[h].T.astype(BF16))
+    flipped = jnp.concatenate(flipped, axis=0)
     for b in range(GROUP // ROWS):
         block = flipped[b * ROWS : (b + 1) * ROWS]
         out_t_ref[b % NY, b // NY] = jnp.concatenate([block, jnp.zeros((ROWS, PAD - TILE), BF16)], axis=1)
@@ -65,24 +77,24 @@
         [d_ref[b % NY, b // NY] for b in range(GROUP // ROWS)], axis=0
     )
     d_all = flipped.astype(F32).T[:TILE].astype(BF16)
+    ds = [d_all[:, head_cols(h)] for h in range(PER_STEP)]
+    d_probs = [
+        lax.dot_general(ds[h], window_of(kv, 1, head_cols(h)), NT, preferred_element_type=F32)
+        for h in range(PER_STEP)
+    ]
     for h in range(PER_STEP):
-        cols = slice(h * HEAD_DIM, (h + 1) * HEAD_DIM)
-        q = q_ref[:, cols]
-        k = window_of(kv, 0, cols)
-        v = window_of(kv, 1, cols)
-        d = d_all[:, cols]
-        probs = probs_ref[h]
-        delta = jnp.sum(d.astype(F32) * att_ref[:, cols].astype(F32), axis=1, keepdims=True)
-        d_probs = lax.dot_general(d, v, NT, preferred_element_type=F32)
-        d_scores = (probs.astype(F32) * (d_probs - delta)).astype(BF16)
-        value_terms = lax.dot_general(probs, d, TN, preferred_element_type=F32)
-        key_terms = lax.dot_general(d_scores, q, TN, preferred_element_type=F32) * SCALE
-        gq = jnp.dot(d_scores, k, preferred_element_type=F32) * SCALE
+        value_terms = lax.dot_general(probs_ref[h], ds[h], TN, preferred_element_type=F32)
+        for s, ref in enumerate(outs):
+            ref[1, :, head_cols(h)] = value_terms[s * TILE : (s + 1) * TILE].astype(ref.dtype)
+    for h in range(PER_STEP):
+        cols = head_cols(h)
+        delta = jnp.sum(ds[h].astype(F32) * att_ref[:, cols].astype(F32), axis=1, keepdims=True)
+        d_scores = (probs_ref[h].astype(F32) * (d_probs[h] - delta)).astype(BF16)
+        key_terms = lax.dot_general(d_scores, q_ref[:, cols], TN, preferred_element_type=F32) * SCALE
+        for s, ref in enumerate(outs):
+            ref[0, :, cols] = key_terms[s * TILE : (s + 1) * TILE].astype(ref.dtype)
+        gq = jnp.dot(d_scores, window_of(kv, 0, cols), preferred_element_type=F32) * SCALE
         gq_ref[:, cols] = gq.astype(BF16)
-        for s, ref in enumerate(outs):
-            rows = slice(s * TILE, (s + 1) * TILE)
-            ref[0, :, cols] = key_terms[rows].astype(ref.dtype)
-            ref[1, :, cols] = value_terms[rows].astype(ref.dtype)
 
 
 def flat_spec(first):
@@ -121,11 +133,7 @@
             jax.ShapeDtypeStruct((HEADS, TILE, SLOTS * TILE), BF16),
         ],
         compiler_params=PARAMS,
-        cost_estimate=pl.CostEstimate(
-            flops=4 * groups * TILE * SLOTS * TILE * GROUP,
-            bytes_accessed=20 * TILE * groups * GROUP,
-            transcendentals=groups * PER_STEP * TILE * SLOTS * TILE,
-        ),
+        cost_estimate=LIGHT,
     )(scalars, q, *kvs)
 
 
@@ -142,12 +150,32 @@
         out_shape=[jax.ShapeDtypeStruct((TILE, width), BF16)]
         + [jax.ShapeDtypeStruct((2, TILE, width), BF16)] * 4,
         compiler_params=PARAMS,
-        cost_estimate=pl.CostEstimate(
-            flops=12 * groups * TILE * SLOTS * TILE * GROUP,
-            bytes_accessed=48 * TILE * width,
-            transcendentals=groups * PER_STEP * TILE * SLOTS * TILE,
-        ),
+        cost_estimate=LIGHT,
     )(scalars, q, *kvs, att, d, probs)
+
+
+def panel_kernel(scalar_ref, weight_ref, after_ref, out_ref):
+    for k in range(out_ref.shape[0]):
+        out_ref[k] = weight_ref[0]
+
+
+def panel_copies(scalars, out_weight, copies, after):
+    half = out_weight.shape[2] // 2
+    return pl.pallas_call(
+        panel_kernel,
+        grid_spec=pltpu.PrefetchScalarGridSpec(
+            num_scalar_prefetch=1,
+            grid=(1,),
+            in_specs=[
+                pl.BlockSpec((1, ROWS, half), lambda i, b: (b[3], 0, b[1])),
+                pl.BlockSpec(memory_space=pl.ANY),
+            ],
+            out_specs=whole((copies, ROWS, half)),
+        ),
+        out_shape=jax.ShapeDtypeStruct((copies, ROWS, half), BF16),
+        compiler_params=PARAMS,
+        cost_estimate=LIGHT,
+    )(scalars, out_weight, after)
 
 
 def source(scalar_ref, k):
@@ -183,23 +211,22 @@
             jax.ShapeDtypeStruct((rows, dout), BF16),
         ],
         compiler_params=PARAMS,
-        cost_estimate=pl.CostEstimate(
-            flops=8 * TILE * rows * dout, bytes_accessed=8 * TILE * dout + 4 * rows * dout, transcendentals=0
-        ),
+        cost_estimate=LIGHT,
     )(scalars, *ups, w_mine, w_mate)
 
 
-def gradient_kernel(scalar_ref, att_ref, *refs):
+def gradient_kernel(scalar_ref, after_ref, att_ref, *refs):
     ups, outs = refs[: 2 * NY], refs[2 * NY :]
+    att = jnp.concatenate([att_ref[source(scalar_ref, k)] for k in range(NY)], axis=1)
+    rest = jnp.zeros((PAD - TILE, outs[0].shape[1]), BF16)
     for side, out_ref in enumerate(outs):
-        total = 0.0
-        for k in range(NY):
-            att = att_ref[source(scalar_ref, k)][:, :TILE]
-            total += jnp.dot(att, ups[side * NY + k][...], preferred_element_type=F32)
-        out_ref[...] = total.astype(out_ref.dtype)
-
-
-def weight_gradient(scalars, atts, ups):
+        up = jnp.concatenate(
+            [block for k in range(NY) for block in (ups[side * NY + k][...], rest)], axis=0
+        )
+        out_ref[...] = jnp.dot(att, up, preferred_element_type=F32).astype(BF16)
+
+
+def weight_gradient(scalars, atts, ups, after):
     half = ups[0].shape[1] // 2
     rows = atts.shape[1]
     step = 256
@@ -211,15 +238,13 @@
         grid_spec=pltpu.PrefetchScalarGridSpec(
             num_scalar_prefetch=1,
             grid=(steps,),
-            in_specs=[whole(atts.shape)] + [mine] * NY + [mate] * NY,
+            in_specs=[pl.BlockSpec(memory_space=pl.ANY), whole(atts.shape)] + [mine] * NY + [mate] * NY,
             out_specs=[pl.BlockSpec((rows, step), lambda i, b: (0, i))] * 2,
         ),
         out_shape=[jax.ShapeDtypeStruct((rows, half), BF16)] * 2,
         compiler_params=PARAMS,
-        cost_estimate=pl.CostEstimate(
-            flops=16 * TILE * rows * half, bytes_accessed=16 * TILE * (rows + half), transcendentals=0
-        ),
-    )(scalars, atts, *ups, *ups)
+        cost_estimate=LIGHT,
+    )(scalars, after, atts, *ups, *ups)
 
 
 def mixed_kernel(scalar_ref, att_ref, weight_ref, *outs):
@@ -242,9 +267,7 @@
         ),
         out_shape=[jax.ShapeDtypeStruct((TILE, dout), BF16)] * NY,
         compiler_params=PARAMS,
-        cost_estimate=pl.CostEstimate(
-            flops=8 * TILE * rows * dout, bytes_accessed=10 * TILE * dout, transcendentals=0
-        ),
+        cost_estimate=LIGHT,
     )(scalars, atts, weight)
 
 
@@ -276,20 +299,20 @@
 
     has_cross = lax.axis_index("xh") != co
     bound = jnp.where(has_cross, SLOTS * TILE, (SLOTS - 1) * TILE)
-    scalars = jnp.stack([bound, co, lax.axis_index("y")]).astype(jnp.int32)
+    scalars = jnp.stack([bound, co, lax.axis_index("y"), block_pick[0]]).astype(jnp.int32)
 
     from_time = lax.ppermute(kv, "xl", SWAP)
     from_cross = lax.ppermute(kv, ("xh", "co"), CROSS)
     from_core = lax.ppermute(kv, "co", SWAP)
-    kvs = (kv, from_time, from_core, from_cross)
-
-    panel = lax.dynamic_slice(out_weight, (block_pick[0], 0, co * half), (1, rows, half))
-    w_mine = swapped(jnp.broadcast_to(panel, (nz, rows, half)), "z").reshape(nz * rows, half)
+
+    panels = panel_copies(scalars, out_weight, nz, from_core)
+    w_mine = swapped(panels, "z").reshape(nz * rows, half)
     ups = [up] + [shifted(up, "y", k) for k in (1, 2, 3)]
     w_mate = lax.ppermute(w_mine, "co", SWAP)
     d_parts, w_rows = d_attention(scalars, ups, w_mine, w_mate)
     d_turned = swapped(d_parts, "y").reshape(ny, nz, rows, PAD)
 
+    kvs = (kv, from_time, from_core, from_cross)
     kvs, d_parts = lax.optimization_barrier((kvs, d_parts))
     att, att_turned, probs = attention_forward(scalars, q, kvs)
     atts = swapped(att_turned.reshape(ny, nz * rows, PAD), "y")
@@ -309,13 +332,12 @@
         return gq, own, terms
 
     gq_0, own_0, terms_0 = backward(0)
-    atts, gq_0 = lax.optimization_barrier((atts, gq_0))
-    grad_mine, grad_mate = weight_gradient(scalars, atts, ups)
+    grad_mine, grad_mate = weight_gradient(scalars, atts, ups, terms_0[2])
     from_mate = lax.ppermute(grad_mate, "co", SWAP)
     atts, w_rows, grad_mine = lax.optimization_barrier((atts, w_rows, grad_mine))
     mixed = mixed_parts(scalars, atts, w_rows)
     grad = (grad_mine.astype(F32) + from_mate.astype(F32)).astype(BF16).reshape(nz, rows, half)
-    probs, grad, mixed, terms_0 = lax.optimization_barrier((probs, grad, mixed, terms_0))
+    probs, grad, mixed = lax.optimization_barrier((probs, grad, mixed))
     gq_1, own_1, terms_1 = backward(1)
     gkv_parts = [
         own.astype(F32) + sum(t.astype(F32) for t in terms)

time: 159 us -> 154 us (0.969)
  starting transfers between devices: 67.3 us -> 62.7 us
  waiting for transfers between devices: 37.2 us -> 35 us
  other arithmetic: 8.79 us -> 10.6 us
  local copies, waits for them, and re-layouts: 3.28 us -> 5 us
    ppermute x1, waiting for transfers between devices: 6.07 us -> 0.01 us  [per_device(): from_time = lax.ppermute(kv, 'xl', SWAP)]
    ppermute x6, waiting for transfers between devices: 9.86 us -> 15 us  [shifted(): return lax.ppermute(x, axis, [(i, (i + by) % count) for i in range(count)])]
    all_to_all x4, starting transfers between devices: 25.8 us -> 20.9 us  [swapped(): return lax.all_to_all(x, axis, split_axis=0, concat_axis=0, tiled=True)]
    all_to_all x4, waiting for transfers between devices: 5.28 us -> 9.6 us  [swapped(): return lax.all_to_all(x, axis, split_axis=0, concat_axis=0, tiled=True)]
    unnamed x26 -> x28, local copies, waits for them, and re-layouts: 1.53 us -> 5 us
    ppermute x1, starting transfers between devices: 0.09 us -> 3.33 us  [per_device(): from_core = lax.ppermute(kv, 'co', SWAP)]
    ppermute x1, starting transfers between devices: 5.33 us -> 2.24 us  [per_device(): from_mate = lax.ppermute(grad_mate, 'co', SWAP)]
    ppermute x2, waiting for transfers between devices: 2.86 us -> 0.01 us  [backward(): lax.ppermute(to_time, 'xl', SWAP)]
  transfers between devices with their start and end apart: 25 -> 25, of which waited for: 13 -> 12; matrix products, arithmetic and copies ran while one was open for 5% -> 6% of each run, Pallas kernels for 21% -> 20%
where the time goes in v5:
time: 154 us; the launch traced here: 153 us
  starting transfers between devices  62.7 us (41%)
  Pallas kernels  38.4 us (25%)
  waiting for transfers between devices  35 us (23%)
  other arithmetic  10.6 us (7%)
  local copies, waits for them, and re-layouts  5 us (3%)
    all_to_all x4, starting transfers between devices, swapped(): return lax.all_to_all(x, axis, split_axis=0, concat_axis=0, tiled=True)  20.9 us
    ppermute x6, waiting for transfers between devices, shifted(): return lax.ppermute(x, axis, [(i, (i + by) % count) for i in range(count)])  15 us
    pallas_call x2, Pallas kernels, attention_backward(): pl.pallas_call(backward_kernel, grid_spec=pltpu.PrefetchScalarGridSpec(nu...  12.4 us
    ppermute x1, starting transfers between devices, per_device(): w_mate = lax.ppermute(w_mine, 'co', SWAP)  9.77 us
    all_to_all x4, waiting for transfers between devices, swapped(): return lax.all_to_all(x, axis, split_axis=0, concat_axis=0, tiled=True)  9.6 us
    ppermute x2, starting transfers between devices, backward(): lax.ppermute(to_cross, ('xh', 'co'), CROSS)  9.06 us
    ppermute x2, waiting for transfers between devices, backward(): lax.ppermute(to_cross, ('xh', 'co'), CROSS)  8.27 us
    pallas_call x1, Pallas kernels, attention_forward(): pl.pallas_call(forward_kernel, grid_spec=pltpu.PrefetchScalarGridSpec(num...  8.1 us
  transfers between devices with their start and end apart: 25, of which 12 were waited for; matrix products, arithmetic and copies ran while one was open for 6% of the time, Pallas kernels for 20%

profile of v5, /device:TPU:1, one launch (start us, length us, event | category | flops | bytes accessed | tf_op | source)
XLA Modules:
  0.0 153.2 jit_solution(5151350146999810750)
XLA Ops:
  0.6 3.3 %collective-permute-start.1 = (bf16[2,192,1536]{2,1,0:T(8,128)(2,1)}, bf16[2,192,1536]{2,1,0:T(8,128)(2,1)S(1)}, u32[]{:S(2)}, u32[]{:S(2)}) collective-permute-start(bf16[2,192,1536]{2,1,0:T(8,128)(2,1)} %bitcast.18), channel_id=1, source_target_pairs={{0,32},{32,0},{1,33},{33,1},{2,34},{34,2},{3,35},{35,3},{4,36},{36... | collective-permute-start | bytes 3538952 | tf_op jit(solution)/shard_map/ppermute | solution.py:306
  10.1 6.6 %all-to-all-start = ((bf16[8,48,768]{2,1,0:T(8,128)(2,1)}), bf16[8,48,768]{2,1,0:T(8,128)(2,1)}, u32[]{:S(2)}, u32[]{:S(2)}) async-start(bf16[8,48,768]{2,1,0:T(8,128)(2,1)} %shard_map.84), calls=%async_computation | async-start | bytes 1179648 | tf_op jit(solution)/shard_map/all_to_all | solution.py:284
  16.6 2.7 %collective-permute-start.5 = (bf16[192,1536]{1,0:T(8,128)(2,1)}, bf16[192,1536]{1,0:T(8,128)(2,1)}, u32[]{:S(2)}, u32[]{:S(2)}) collective-permute-start(bf16[192,1536]{1,0:T(8,128)(2,1)} %bitcast.5.refs_0_.refs_4_), channel_id=1, source_target_pairs={{0,3},{1,0},{2,1},{3,2},{4,7},{5,4},{6,5},{7,6},{8,11},{9,8},{10,9... | collective-permute-start | bytes 1769480 | tf_op jit(solution)/shard_map/ppermute | solution.py:280
  19.4 5.5 %collective-permute-start.2 = (bf16[2,192,1536]{2,1,0:T(8,128)(2,1)S(1)}, bf16[2,192,1536]{2,1,0:T(8,128)(2,1)S(1)}, u32[]{:S(2)}, u32[]{:S(2)}) collective-permute-start(bf16[2,192,1536]{2,1,0:T(8,128)(2,1)S(1)} %bitcast.22), channel_id=1, source_target_pairs={{32,64},{64,32},{33,65},{65,33},{34,66},{66,34},{35,67},{67,35},{3... | collective-permute-start | bytes 3538952 | tf_op jit(solution)/shard_map/ppermute | solution.py:305
  26.3 6.4 %collective-permute-done.5.refs_3_.refs_7_ = bf16[192,1536]{1,0:T(8,128)(2,1)} collective-permute-done((bf16[192,1536]{1,0:T(8,128)(2,1)}, bf16[192,1536]{1,0:T(8,128)(2,1)}, u32[]{:S(2)}, u32[]{:S(2)}) %collective-permute-start.5) | collective-permute-done | bytes 589856 | tf_op jit(solution)/shard_map/ppermute | solution.py:280
  32.7 3.4 %all-to-all-done = bf16[8,48,768]{2,1,0:T(8,128)(2,1)} async-done(((bf16[8,48,768]{2,1,0:T(8,128)(2,1)}), bf16[8,48,768]{2,1,0:T(8,128)(2,1)}, u32[]{:S(2)}, u32[]{:S(2)}) %all-to-all-start) | async-done | bytes 589856 | tf_op jit(solution)/shard_map/all_to_all | solution.py:284
  36.1 9.8 %collective-permute-start.6 = (bf16[384,768]{1,0:T(8,128)(2,1)}, bf16[384,768]{1,0:T(8,128)(2,1)S(1)}, u32[]{:S(2)}, u32[]{:S(2)}) collective-permute-start(bf16[384,768]{1,0:T(8,128)(2,1)} %bitcast.6.refs_4_), channel_id=1, source_target_pairs={{0,32},{32,0},{1,33},{33,1},{2,34},{34,2},{3,35},{35,3},{4,36},{36... | collective-permute-start | bytes 1769480 | tf_op jit(solution)/shard_map/ppermute | solution.py:311
  45.9 6.9 %collective-permute-done.3.refs_1_.refs_5_ = bf16[192,1536]{1,0:T(8,128)(2,1)} collective-permute-done((bf16[192,1536]{1,0:T(8,128)(2,1)}, bf16[192,1536]{1,0:T(8,128)(2,1)}, u32[]{:S(2)}, u32[]{:S(2)}) %collective-permute-start.3) | collective-permute-done | bytes 589856 | tf_op jit(solution)/shard_map/ppermute | solution.py:280
  53.6 4.9 %shard_map.85 = (bf16[4,384,256]{2,1,0:T(8,128)(2,1)}, bf16[384,1536]{1,0:T(8,128)(2,1)}) custom-call(s32[4]{0:T(128)} %pad_add_fusion.scalar_ref, bf16[192,1536]{1,0:T(8,128)(2,1)} %bitcast.5.refs_0_.refs_4_, bf16[192,1536]{1,0:T(8,128)(2,1)} %collective-permute-done.3.refs_1_.refs_5_, bf16[192,1536]{1,0:T(8,128)(2,1)} %collective-permute-done.4.refs_2_.refs_6_, ...), custom_call_target="tpu_custom_call" | custom-call | flops 1000 | bytes 1000 | tf_op jit(solution)/shard_map/pallas_call | solution.py:201
  58.6 4.2 %all-to-all-start.2 = ((bf16[4,384,256]{2,1,0:T(8,128)(2,1)}), bf16[4,384,256]{2,1,0:T(8,128)(2,1)}, u32[]{:S(2)}, u32[]{:S(2)}) async-start(bf16[4,384,256]{2,1,0:T(8,128)(2,1)} %get-tuple-element.38), calls=%async_computation.2 | async-start | bytes 1572864 | tf_op jit(solution)/shard_map/all_to_all | solution.py:284
  64.2 8.1 %shard_map.86 = (bf16[192,1536]{1,0:T(8,128)(2,1)}, bf16[4,8,48,256]{3,2,1,0:T(8,128)(2,1)}, bf16[12,192,768]{2,1,0:T(8,128)(2,1)}) custom-call(s32[4]{0:T(128)} %pad_add_fusion.scalar_ref, bf16[192,1536]{1,0:T(8,128)(2,1)} %bitcast.24, bf16[2,192,1536]{2,1,0:T(8,128)(2,1)} %bitcast.19, bf16[2,192,1536]{2,1,0:T(8,128)(2,1)} %copy-done.3, ...), custom_call_target="tpu_custom_call" | custom-call | flops 1000 | bytes 1000 | tf_op jit(solution)/shard_map/pallas_call | solution.py:122
  72.3 2.6 %all-to-all-done.2 = bf16[4,384,256]{2,1,0:T(8,128)(2,1)} async-done(((bf16[4,384,256]{2,1,0:T(8,128)(2,1)}), bf16[4,384,256]{2,1,0:T(8,128)(2,1)}, u32[]{:S(2)}, u32[]{:S(2)}) %all-to-all-start.2) | async-done | bytes 786464 | tf_op jit(solution)/shard_map/all_to_all | solution.py:284
  74.8 3.5 %all-to-all-start.1 = ((bf16[4,384,256]{2,1,0:T(8,128)(2,1)}), bf16[4,384,256]{2,1,0:T(8,128)(2,1)S(1)}, u32[]{:S(2)}, u32[]{:S(2)}) async-start(bf16[4,384,256]{2,1,0:T(8,128)(2,1)} %bitcast.27), calls=%async_computation.1 | async-start | bytes 1572864 | tf_op jit(solution)/shard_map/all_to_all | solution.py:284
  78.3 6.1 %shard_map.87 = (bf16[192,768]{1,0:T(8,128)(2,1)}, bf16[2,192,768]{2,1,0:T(8,128)(2,1)}, bf16[2,192,768]{2,1,0:T(8,128)(2,1)}, bf16[2,192,768]{2,1,0:T(8,128)(2,1)}, bf16[2,192,768]{2,1,0:T(8,128)(2,1)}) custom-call(s32[4]{0:T(128)} %pad_add_fusion.scalar_ref, bf16[192,1536]{1,0:T(8,128)(2,1)} %bitcast.25, bf16[2,192,1536]{2,1,0:T(8,128)(2,1)} %bitcast.20, ...), custom_call_target="tpu_custom_call" | custom-call | flops 1000 | bytes 1000 | tf_op jit(solution)/shard_map/pallas_call | solution.py:142
  85.7 3.6 %all-to-all-done.1.att_ref = bf16[4,384,256]{2,1,0:T(8,128)(2,1)S(1)} async-done(((bf16[4,384,256]{2,1,0:T(8,128)(2,1)}), bf16[4,384,256]{2,1,0:T(8,128)(2,1)S(1)}, u32[]{:S(2)}, u32[]{:S(2)}) %all-to-all-start.1) | async-done | bytes 786464 | tf_op jit(solution)/shard_map/all_to_all | solution.py:284
  91.2 5.6 %shard_map.88 = (bf16[384,768]{1,0:T(8,128)(2,1)}, bf16[384,768]{1,0:T(8,128)(2,1)}) custom-call(s32[4]{0:T(128)} %pad_add_fusion.scalar_ref, bf16[2,192,768]{2,1,0:T(8,128)(2,1)} %copy-done.5, bf16[4,384,256]{2,1,0:T(8,128)(2,1)} %copy-done.4, bf16[192,1536]{1,0:T(8,128)(2,1)} %bitcast.5.refs_0_.refs_4_, ...), custom_call_target="tpu_custom_call" | custom-call | flops 1000 | bytes 1000 | tf_op jit(solution)/shard_map/pallas_call | solution.py:236
  99.3 3.1 %collective-permute-start.13 = (bf16[2,192,768]{2,1,0:T(8,128)(2,1)}, bf16[2,192,768]{2,1,0:T(8,128)(2,1)}, u32[]{:S(2)}, u32[]{:S(2)}) collective-permute-start(bf16[2,192,768]{2,1,0:T(8,128)(2,1)} %get-tuple-element.66), channel_id=1, source_target_pairs={{32,64},{64,32},{33,65},{65,33},{34,66},{66,34},{35,67},{67,35},{3... | collective-permute-start | bytes 1769480 | tf_op jit(solution)/shard_map/ppermute | solution.py:329
  102.4 5.0 %shard_map.89 = (bf16[192,1536]{1,0:T(8,128)(2,1)}, bf16[192,1536]{1,0:T(8,128)(2,1)}, bf16[192,1536]{1,0:T(8,128)(2,1)}, bf16[192,1536]{1,0:T(8,128)(2,1)}) custom-call(s32[4]{0:T(128)} %pad_add_fusion.scalar_ref, bf16[4,384,256]{2,1,0:T(8,128)(2,1)} %copy-done.4, bf16[384,1536]{1,0:T(8,128)(2,1)} %get-tuple-element.52.weight_ref), custom_call_target="tpu_custom_call" | custom-call | flops 1000 | bytes 1000 | tf_op jit(solution)/shard_map/pallas_call | solution.py:260
  110.4 6.7 %all-to-all-start.3 = ((bf16[8,48,768]{2,1,0:T(8,128)(2,1)}), bf16[8,48,768]{2,1,0:T(8,128)(2,1)S(1)}, u32[]{:S(2)}, u32[]{:S(2)}) async-start(bf16[8,48,768]{2,1,0:T(8,128)(2,1)} %bitcast.9), calls=%async_computation.3 | async-start | bytes 1179648 | tf_op jit(solution)/shard_map/all_to_all | solution.py:284
  117.1 3.5 %collective-permute-done.13 = bf16[2,192,768]{2,1,0:T(8,128)(2,1)} collective-permute-done((bf16[2,192,768]{2,1,0:T(8,128)(2,1)}, bf16[2,192,768]{2,1,0:T(8,128)(2,1)}, u32[]{:S(2)}, u32[]{:S(2)}) %collective-permute-start.13) | collective-permute-done | bytes 589856 | tf_op jit(solution)/shard_map/ppermute | solution.py:329
  122.2 6.3 %shard_map.90 = (bf16[192,768]{1,0:T(8,128)(2,1)}, bf16[2,192,768]{2,1,0:T(8,128)(2,1)}, bf16[2,192,768]{2,1,0:T(8,128)(2,1)}, bf16[2,192,768]{2,1,0:T(8,128)(2,1)}, bf16[2,192,768]{2,1,0:T(8,128)(2,1)}) custom-call(s32[4]{0:T(128)} %pad_add_fusion.scalar_ref, bf16[192,1536]{1,0:T(8,128)(2,1)} %bitcast.26, bf16[2,192,1536]{2,1,0:T(8,128)(2,1)} %bitcast.21, ...), custom_call_target="tpu_custom_call" | custom-call | flops 1000 | bytes 1000 | tf_op jit(solution)/shard_map/pallas_call | solution.py:142
  129.0 6.0 %collective-permute-start.15 = (bf16[2,192,768]{2,1,0:T(8,128)(2,1)}, bf16[2,192,768]{2,1,0:T(8,128)(2,1)}, u32[]{:S(2)}, u32[]{:S(2)}) collective-permute-start(bf16[2,192,768]{2,1,0:T(8,128)(2,1)} %get-tuple-element.69), channel_id=1, source_target_pairs={{32,64},{64,32},{33,65},{65,33},{34,66},{66,34},{35,67},{67,35},{3... | collective-permute-start | bytes 1769480 | tf_op jit(solution)/shard_map/ppermute | solution.py:329
  140.9 2.5 %collective-permute-start.18 = (bf16[48,768]{1,0:T(8,128)(2,1)S(1)}, bf16[48,768]{1,0:T(8,128)(2,1)S(1)}, u32[]{:S(2)}, u32[]{:S(2)}) collective-permute-start(bf16[48,768]{1,0:T(8,128)(2,1)S(1)} %reduce_sum.12), channel_id=1, source_target_pairs={{0,64},{64,0},{1,65},{65,1},{2,66},{66,2},{3,67},{67,3},{4,68},{68... | collective-permute-start | bytes 221192 | tf_op jit(solution)/shard_map/ppermute | solution.py:349
  144.2 4.8 %collective-permute-done.15 = bf16[2,192,768]{2,1,0:T(8,128)(2,1)} collective-permute-done((bf16[2,192,768]{2,1,0:T(8,128)(2,1)}, bf16[2,192,768]{2,1,0:T(8,128)(2,1)}, u32[]{:S(2)}, u32[]{:S(2)}) %collective-permute-start.15) | collective-permute-done | bytes 589856 | tf_op jit(solution)/shard_map/ppermute | solution.py:329
  (72 shorter events, 30.7 us)
Async XLA Ops:
  0.6 6.0 %collective-permute-start.1 = (bf16[2,192,1536]{2,1,0:T(8,128)(2,1)}, bf16[2,192,1536]{2,1,0:T(8,128)(2,1)S(1)}, u32[]{:S(2)}, u32[]{:S(2)}) collective-permute-start(bf16[2,192,1536]{2,1,0:T(8,128)(2,1)} %bitcast.18), channel_id=1, source_target_pairs={{0,32},{32,0},{1,33},{33,1},{2,34},{34,2},{3,35},{35,3},{4,36},{36... | collective-permute-start | bytes 3538952 | tf_op jit(solution)/shard_map/ppermute | solution.py:306
  10.1 26.0 %all-to-all-start = ((bf16[8,48,768]{2,1,0:T(8,128)(2,1)}), bf16[8,48,768]{2,1,0:T(8,128)(2,1)}, u32[]{:S(2)}, u32[]{:S(2)}) async-start(bf16[8,48,768]{2,1,0:T(8,128)(2,1)} %shard_map.84), calls=%async_computation | async-start | bytes 1179648 | tf_op jit(solution)/shard_map/all_to_all | solution.py:284
  16.6 16.1 %collective-permute-start.5 = (bf16[192,1536]{1,0:T(8,128)(2,1)}, bf16[192,1536]{1,0:T(8,128)(2,1)}, u32[]{:S(2)}, u32[]{:S(2)}) collective-permute-start(bf16[192,1536]{1,0:T(8,128)(2,1)} %bitcast.5.refs_0_.refs_4_), channel_id=1, source_target_pairs={{0,3},{1,0},{2,1},{3,2},{4,7},{5,4},{6,5},{7,6},{8,11},{9,8},{10,9... | collective-permute-start | bytes 1769480 | tf_op jit(solution)/shard_map/ppermute | solution.py:280
  19.4 43.4 %collective-permute-start.2 = (bf16[2,192,1536]{2,1,0:T(8,128)(2,1)S(1)}, bf16[2,192,1536]{2,1,0:T(8,128)(2,1)S(1)}, u32[]{:S(2)}, u32[]{:S(2)}) collective-permute-start(bf16[2,192,1536]{2,1,0:T(8,128)(2,1)S(1)} %bitcast.22), channel_id=1, source_target_pairs={{32,64},{64,32},{33,65},{65,33},{34,66},{66,34},{35,67},{67,35},{3... | collective-permute-start | bytes 3538952 | tf_op jit(solution)/shard_map/ppermute | solution.py:305
  24.9 37.9 %collective-permute-start = (bf16[2,192,1536]{2,1,0:T(8,128)(2,1)S(1)}, bf16[2,192,1536]{2,1,0:T(8,128)(2,1)S(1)}, u32[]{:S(2)}, u32[]{:S(2)}) collective-permute-start(bf16[2,192,1536]{2,1,0:T(8,128)(2,1)S(1)} %bitcast.23), channel_id=1, source_target_pairs={{0,128},{128,0},{1,129},{129,1},{2,130},{130,2},{3,131},{131,3},{4... | collective-permute-start | bytes 3538952 | tf_op jit(solution)/shard_map/ppermute | solution.py:304
  25.3 20.6 %collective-permute-start.4 = (bf16[192,1536]{1,0:T(8,128)(2,1)}, bf16[192,1536]{1,0:T(8,128)(2,1)}, u32[]{:S(2)}, u32[]{:S(2)}) collective-permute-start(bf16[192,1536]{1,0:T(8,128)(2,1)} %bitcast.5.refs_0_.refs_4_), channel_id=1, source_target_pairs={{0,2},{1,3},{2,0},{3,1},{4,6},{5,7},{6,4},{7,5},{8,10},{9,11},{10,... | collective-permute-start | bytes 1769480 | tf_op jit(solution)/shard_map/ppermute | solution.py:280
  25.6 27.2 %collective-permute-start.3 = (bf16[192,1536]{1,0:T(8,128)(2,1)}, bf16[192,1536]{1,0:T(8,128)(2,1)}, u32[]{:S(2)}, u32[]{:S(2)}) collective-permute-start(bf16[192,1536]{1,0:T(8,128)(2,1)} %bitcast.5.refs_0_.refs_4_), channel_id=1, source_target_pairs={{0,1},{1,2},{2,3},{3,0},{4,5},{5,6},{6,7},{7,4},{8,9},{9,10},{10,1... | collective-permute-start | bytes 1769480 | tf_op jit(solution)/shard_map/ppermute | solution.py:280
  36.1 16.7 %collective-permute-start.6 = (bf16[384,768]{1,0:T(8,128)(2,1)}, bf16[384,768]{1,0:T(8,128)(2,1)S(1)}, u32[]{:S(2)}, u32[]{:S(2)}) collective-permute-start(bf16[384,768]{1,0:T(8,128)(2,1)} %bitcast.6.refs_4_), channel_id=1, source_target_pairs={{0,32},{32,0},{1,33},{33,1},{2,34},{34,2},{3,35},{35,3},{4,36},{36... | collective-permute-start | bytes 1769480 | tf_op jit(solution)/shard_map/ppermute | solution.py:311
  58.6 16.3 %all-to-all-start.2 = ((bf16[4,384,256]{2,1,0:T(8,128)(2,1)}), bf16[4,384,256]{2,1,0:T(8,128)(2,1)}, u32[]{:S(2)}, u32[]{:S(2)}) async-start(bf16[4,384,256]{2,1,0:T(8,128)(2,1)} %get-tuple-element.38), calls=%async_computation.2 | async-start | bytes 1572864 | tf_op jit(solution)/shard_map/all_to_all | solution.py:284
  74.8 14.6 %all-to-all-start.1 = ((bf16[4,384,256]{2,1,0:T(8,128)(2,1)}), bf16[4,384,256]{2,1,0:T(8,128)(2,1)S(1)}, u32[]{:S(2)}, u32[]{:S(2)}) async-start(bf16[4,384,256]{2,1,0:T(8,128)(2,1)} %bitcast.27), calls=%async_computation.1 | async-start | bytes 1572864 | tf_op jit(solution)/shard_map/all_to_all | solution.py:284
  84.4 5.0 %collective-permute-start.7 = (bf16[2,192,768]{2,1,0:T(8,128)(2,1)}, bf16[2,192,768]{2,1,0:T(8,128)(2,1)S(1)}, u32[]{:S(2)}, u32[]{:S(2)}) collective-permute-start(bf16[2,192,768]{2,1,0:T(8,128)(2,1)} %get-tuple-element.47), channel_id=1, source_target_pairs={{0,32},{32,0},{1,33},{33,1},{2,34},{34,2},{3,35},{35,3},{4,36},{36... | collective-permute-start | bytes 1769480 | tf_op jit(solution)/shard_map/ppermute | solution.py:330
  96.8 10.6 %collective-permute-start.8 = (bf16[384,768]{1,0:T(8,128)(2,1)}, bf16[384,768]{1,0:T(8,128)(2,1)S(1)}, u32[]{:S(2)}, u32[]{:S(2)}) collective-permute-start(bf16[384,768]{1,0:T(8,128)(2,1)} %get-tuple-element.50), channel_id=1, source_target_pairs={{0,32},{32,0},{1,33},{33,1},{2,34},{34,2},{3,35},{35,3},{4,36},{36... | collective-permute-start | bytes 1769480 | tf_op jit(solution)/shard_map/ppermute | solution.py:336
  99.0 18.1 %collective-permute-start.12 = (bf16[2,192,768]{2,1,0:T(8,128)(2,1)}, bf16[2,192,768]{2,1,0:T(8,128)(2,1)S(1)}, u32[]{:S(2)}, u32[]{:S(2)}) collective-permute-start(bf16[2,192,768]{2,1,0:T(8,128)(2,1)} %get-tuple-element.65), channel_id=1, source_target_pairs={{0,128},{128,0},{1,129},{129,1},{2,130},{130,2},{3,131},{131,3},{4... | collective-permute-start | bytes 1769480 | tf_op jit(solution)/shard_map/ppermute | solution.py:328
  99.3 21.4 %collective-permute-start.13 = (bf16[2,192,768]{2,1,0:T(8,128)(2,1)}, bf16[2,192,768]{2,1,0:T(8,128)(2,1)}, u32[]{:S(2)}, u32[]{:S(2)}) collective-permute-start(bf16[2,192,768]{2,1,0:T(8,128)(2,1)} %get-tuple-element.66), channel_id=1, source_target_pairs={{32,64},{64,32},{33,65},{65,33},{34,66},{66,34},{35,67},{67,35},{3... | collective-permute-start | bytes 1769480 | tf_op jit(solution)/shard_map/ppermute | solution.py:329
  108.3 26.6 %collective-permute-start.9 = (bf16[192,1536]{1,0:T(8,128)(2,1)}, bf16[192,1536]{1,0:T(8,128)(2,1)S(1)}, u32[]{:S(2)}, u32[]{:S(2)}) collective-permute-start(bf16[192,1536]{1,0:T(8,128)(2,1)} %get-tuple-element.58), channel_id=1, source_target_pairs={{0,3},{1,0},{2,1},{3,2},{4,7},{5,4},{6,5},{7,6},{8,11},{9,8},{10,9... | collective-permute-start | bytes 1769480 | tf_op jit(solution)/shard_map/ppermute | solution.py:280
  109.2 27.7 %collective-permute-start.10 = (bf16[192,1536]{1,0:T(8,128)(2,1)}, bf16[192,1536]{1,0:T(8,128)(2,1)S(1)}, u32[]{:S(2)}, u32[]{:S(2)}) collective-permute-start(bf16[192,1536]{1,0:T(8,128)(2,1)} %get-tuple-element.59), channel_id=1, source_target_pairs={{0,2},{1,3},{2,0},{3,1},{4,6},{5,7},{6,4},{7,5},{8,10},{9,11},{10,... | collective-permute-start | bytes 1769480 | tf_op jit(solution)/shard_map/ppermute | solution.py:280
  110.4 28.1 %collective-permute-start.11 = (bf16[192,1536]{1,0:T(8,128)(2,1)}, bf16[192,1536]{1,0:T(8,128)(2,1)}, u32[]{:S(2)}, u32[]{:S(2)}) collective-permute-start(bf16[192,1536]{1,0:T(8,128)(2,1)} %get-tuple-element.60), channel_id=1, source_target_pairs={{0,1},{1,2},{2,3},{3,0},{4,5},{5,6},{6,7},{7,4},{8,9},{9,10},{10,1... | collective-permute-start | bytes 1769480 | tf_op jit(solution)/shard_map/ppermute | solution.py:280
  110.4 30.3 %all-to-all-start.3 = ((bf16[8,48,768]{2,1,0:T(8,128)(2,1)}), bf16[8,48,768]{2,1,0:T(8,128)(2,1)S(1)}, u32[]{:S(2)}, u32[]{:S(2)}) async-start(bf16[8,48,768]{2,1,0:T(8,128)(2,1)} %bitcast.9), calls=%async_computation.3 | async-start | bytes 1179648 | tf_op jit(solution)/shard_map/all_to_all | solution.py:284
  128.4 15.0 %collective-permute-start.14 = (bf16[2,192,768]{2,1,0:T(8,128)(2,1)}, bf16[2,192,768]{2,1,0:T(8,128)(2,1)S(1)}, u32[]{:S(2)}, u32[]{:S(2)}) collective-permute-start(bf16[2,192,768]{2,1,0:T(8,128)(2,1)} %get-tuple-element.68), channel_id=1, source_target_pairs={{0,128},{128,0},{1,129},{129,1},{2,130},{130,2},{3,131},{131,3},{4... | collective-permute-start | bytes 1769480 | tf_op jit(solution)/shard_map/ppermute | solution.py:328
  129.0 20.0 %collective-permute-start.15 = (bf16[2,192,768]{2,1,0:T(8,128)(2,1)}, bf16[2,192,768]{2,1,0:T(8,128)(2,1)}, u32[]{:S(2)}, u32[]{:S(2)}) collective-permute-start(bf16[2,192,768]{2,1,0:T(8,128)(2,1)} %get-tuple-element.69), channel_id=1, source_target_pairs={{32,64},{64,32},{33,65},{65,33},{34,66},{66,34},{35,67},{67,35},{3... | collective-permute-start | bytes 1769480 | tf_op jit(solution)/shard_map/ppermute | solution.py:329
  135.0 14.0 %collective-permute-start.16 = (bf16[2,192,768]{2,1,0:T(8,128)(2,1)}, bf16[2,192,768]{2,1,0:T(8,128)(2,1)}, u32[]{:S(2)}, u32[]{:S(2)}) collective-permute-start(bf16[2,192,768]{2,1,0:T(8,128)(2,1)} %get-tuple-element.70), channel_id=1, source_target_pairs={{0,32},{32,0},{1,33},{33,1},{2,34},{34,2},{3,35},{35,3},{4,36},{36... | collective-permute-start | bytes 1769480 | tf_op jit(solution)/shard_map/ppermute | solution.py:330
  140.8 9.7 %collective-permute-start.19 = (bf16[48,768]{1,0:T(8,128)(2,1)S(1)}, bf16[48,768]{1,0:T(8,128)(2,1)S(1)}, u32[]{:S(2)}, u32[]{:S(2)}) collective-permute-start(bf16[48,768]{1,0:T(8,128)(2,1)S(1)} %reduce_sum.12), channel_id=1, source_target_pairs={{0,192},{64,128},{128,64},{192,0},{1,193},{65,129},{129,65},{193,1... | collective-permute-start | bytes 221192 | tf_op jit(solution)/shard_map/ppermute | solution.py:350
  140.9 9.6 %collective-permute-start.18 = (bf16[48,768]{1,0:T(8,128)(2,1)S(1)}, bf16[48,768]{1,0:T(8,128)(2,1)S(1)}, u32[]{:S(2)}, u32[]{:S(2)}) collective-permute-start(bf16[48,768]{1,0:T(8,128)(2,1)S(1)} %reduce_sum.12), channel_id=1, source_target_pairs={{0,64},{64,0},{1,65},{65,1},{2,66},{66,2},{3,67},{67,3},{4,68},{68... | collective-permute-start | bytes 221192 | tf_op jit(solution)/shard_map/ppermute | solution.py:349
  143.4 7.5 %collective-permute-start.17 = (bf16[48,768]{1,0:T(8,128)(2,1)S(1)}, bf16[48,768]{1,0:T(8,128)(2,1)S(1)}, u32[]{:S(2)}, u32[]{:S(2)}) collective-permute-start(bf16[48,768]{1,0:T(8,128)(2,1)S(1)} %reduce_sum.12), channel_id=1, source_target_pairs={{0,128},{128,0},{1,129},{129,1},{2,130},{130,2},{3,131},{131,3},{4... | collective-permute-start | bytes 221192 | tf_op jit(solution)/shard_map/ppermute | solution.py:348
  (15 other events, 92.6 us)

commit v6 on v5

--- a/solution.py
+++ b/solution.py
@@ -215,7 +215,7 @@
     )(scalars, *ups, w_mine, w_mate)
 
 
-def gradient_kernel(scalar_ref, after_ref, att_ref, *refs):
+def gradient_kernel(scalar_ref, att_ref, *refs):
     ups, outs = refs[: 2 * NY], refs[2 * NY :]
     att = jnp.concatenate([att_ref[source(scalar_ref, k)] for k in range(NY)], axis=1)
     rest = jnp.zeros((PAD - TILE, outs[0].shape[1]), BF16)
@@ -226,7 +226,7 @@
         out_ref[...] = jnp.dot(att, up, preferred_element_type=F32).astype(BF16)
 
 
-def weight_gradient(scalars, atts, ups, after):
+def weight_gradient(scalars, atts, ups):
     half = ups[0].shape[1] // 2
     rows = atts.shape[1]
     step = 256
@@ -238,13 +238,13 @@
         grid_spec=pltpu.PrefetchScalarGridSpec(
             num_scalar_prefetch=1,
             grid=(steps,),
-            in_specs=[pl.BlockSpec(memory_space=pl.ANY), whole(atts.shape)] + [mine] * NY + [mate] * NY,
+            in_specs=[whole(atts.shape)] + [mine] * NY + [mate] * NY,
             out_specs=[pl.BlockSpec((rows, step), lambda i, b: (0, i))] * 2,
         ),
         out_shape=[jax.ShapeDtypeStruct((rows, half), BF16)] * 2,
         compiler_params=PARAMS,
         cost_estimate=LIGHT,
-    )(scalars, after, atts, *ups, *ups)
+    )(scalars, atts, *ups, *ups)
 
 
 def mixed_kernel(scalar_ref, att_ref, weight_ref, *outs):
@@ -313,7 +313,6 @@
     d_turned = swapped(d_parts, "y").reshape(ny, nz, rows, PAD)
 
     kvs = (kv, from_time, from_core, from_cross)
-    kvs, d_parts = lax.optimization_barrier((kvs, d_parts))
     att, att_turned, probs = attention_forward(scalars, q, kvs)
     atts = swapped(att_turned.reshape(ny, nz * rows, PAD), "y")
 
@@ -332,7 +331,8 @@
         return gq, own, terms
 
     gq_0, own_0, terms_0 = backward(0)
-    grad_mine, grad_mate = weight_gradient(scalars, atts, ups, terms_0[2])
+    atts, gq_0 = lax.optimization_barrier((atts, gq_0))
+    grad_mine, grad_mate = weight_gradient(scalars, atts, ups)
     from_mate = lax.ppermute(grad_mate, "co", SWAP)
     atts, w_rows, grad_mine = lax.optimization_barrier((atts, w_rows, grad_mine))
     mixed = mixed_parts(scalars, atts, w_rows)

time: 154 us -> 153 us (level)
  waiting for transfers between devices: 35 us -> 38.3 us
  other arithmetic: 10.6 us -> 8.61 us
  starting transfers between devices: 62.7 us -> 61 us
    ppermute x1, waiting for transfers between devices: 0.01 us -> 4.82 us  [per_device(): from_time = lax.ppermute(kv, 'xl', SWAP)]
    ppermute x2, waiting for transfers between devices: 8.27 us -> 5.1 us  [backward(): lax.ppermute(to_cross, ('xh', 'co'), CROSS)]
    ppermute x2, waiting for transfers between devices: 0.01 us -> 2.6 us  [backward(): lax.ppermute(to_time, 'xl', SWAP)]
    ppermute x1, starting transfers between devices: 2.52 us -> 0.46 us  [per_device(): x_far = lax.ppermute(over_z, 'xh', SWAP)]
    ppermute x1, starting transfers between devices: 0.09 us -> 1.95 us  [per_device(): x_both = lax.ppermute(over_z, ('xl', 'xh'), [(i, 3 - i) for i in range(4)])]
    ppermute x1, starting transfers between devices: 2.24 us -> 0.48 us  [per_device(): from_mate = lax.ppermute(grad_mate, 'co', SWAP)]
    ppermute x2, starting transfers between devices: 0.8 us -> 2.48 us  [backward(): lax.ppermute(to_time, 'xl', SWAP)]
    unnamed x28 -> x26, local copies, waits for them, and re-layouts: 5 us -> 4.42 us
  transfers between devices with their start and end apart: 25 -> 25, of which waited for: 12 -> 10; matrix products, arithmetic and copies ran while one was open for 6% -> 5% of each run, Pallas kernels for 20% -> 20%
where the time goes in v6:
time: 153 us; the launch traced here: 152 us
  starting transfers between devices  61 us (40%)
  Pallas kernels  38.5 us (25%)
  waiting for transfers between devices  38.3 us (25%)
  other arithmetic  8.61 us (6%)
  local copies, waits for them, and re-layouts  4.42 us (3%)
    all_to_all x4, starting transfers between devices, swapped(): return lax.all_to_all(x, axis, split_axis=0, concat_axis=0, tiled=True)  20.5 us
    ppermute x6, waiting for transfers between devices, shifted(): return lax.ppermute(x, axis, [(i, (i + by) % count) for i in range(count)])  14.2 us
    pallas_call x2, Pallas kernels, attention_backward(): pl.pallas_call(backward_kernel, grid_spec=pltpu.PrefetchScalarGridSpec(nu...  12.4 us
    ppermute x1, starting transfers between devices, per_device(): w_mate = lax.ppermute(w_mine, 'co', SWAP)  9.77 us
    all_to_all x4, waiting for transfers between devices, swapped(): return lax.all_to_all(x, axis, split_axis=0, concat_axis=0, tiled=True)  9.71 us
    pallas_call x1, Pallas kernels, attention_forward(): pl.pallas_call(forward_kernel, grid_spec=pltpu.PrefetchScalarGridSpec(num...  8.09 us
    ppermute x2, starting transfers between devices, backward(): lax.ppermute(to_cross, ('xh', 'co'), CROSS)  7.76 us
    ppermute x6, starting transfers between devices, shifted(): return lax.ppermute(x, axis, [(i, (i + by) % count) for i in range(count)])  6.14 us
  transfers between devices with their start and end apart: 25, of which 10 were waited for; matrix products, arithmetic and copies ran while one was open for 5% of the time, Pallas kernels for 20%

profile of v6, /device:TPU:1, one launch (start us, length us, event | category | flops | bytes accessed | tf_op | source)
XLA Modules:
  0.0 152.3 jit_solution(12885980921158993981)
XLA Ops:
  0.6 3.3 %collective-permute-start.1 = (bf16[2,192,1536]{2,1,0:T(8,128)(2,1)}, bf16[2,192,1536]{2,1,0:T(8,128)(2,1)S(1)}, u32[]{:S(2)}, u32[]{:S(2)}) collective-permute-start(bf16[2,192,1536]{2,1,0:T(8,128)(2,1)} %bitcast.18), channel_id=1, source_target_pairs={{0,32},{32,0},{1,33},{33,1},{2,34},{34,2},{3,35},{35,3},{4,36},{36... | collective-permute-start | bytes 3538952 | tf_op jit(solution)/shard_map/ppermute | solution.py:306
  10.1 6.6 %all-to-all-start.1 = ((bf16[8,48,768]{2,1,0:T(8,128)(2,1)}), bf16[8,48,768]{2,1,0:T(8,128)(2,1)}, u32[]{:S(2)}, u32[]{:S(2)}) async-start(bf16[8,48,768]{2,1,0:T(8,128)(2,1)} %shard_map.85), calls=%async_computation.1 | async-start | bytes 1179648 | tf_op jit(solution)/shard_map/all_to_all | solution.py:284
  16.7 2.7 %collective-permute-start.5 = (bf16[192,1536]{1,0:T(8,128)(2,1)}, bf16[192,1536]{1,0:T(8,128)(2,1)}, u32[]{:S(2)}, u32[]{:S(2)}) collective-permute-start(bf16[192,1536]{1,0:T(8,128)(2,1)} %bitcast.6.refs_0_.refs_4_), channel_id=1, source_target_pairs={{0,3},{1,0},{2,1},{3,2},{4,7},{5,4},{6,5},{7,6},{8,11},{9,8},{10,9... | collective-permute-start | bytes 1769480 | tf_op jit(solution)/shard_map/ppermute | solution.py:280
  20.4 6.0 %collective-permute-start.2 = (bf16[2,192,1536]{2,1,0:T(8,128)(2,1)S(1)}, bf16[2,192,1536]{2,1,0:T(8,128)(2,1)S(1)}, u32[]{:S(2)}, u32[]{:S(2)}) collective-permute-start(bf16[2,192,1536]{2,1,0:T(8,128)(2,1)S(1)} %bitcast.22), channel_id=1, source_target_pairs={{32,64},{64,32},{33,65},{65,33},{34,66},{66,34},{35,67},{67,35},{3... | collective-permute-start | bytes 3538952 | tf_op jit(solution)/shard_map/ppermute | solution.py:305
  26.9 5.9 %collective-permute-done.5.refs_3_.refs_7_ = bf16[192,1536]{1,0:T(8,128)(2,1)} collective-permute-done((bf16[192,1536]{1,0:T(8,128)(2,1)}, bf16[192,1536]{1,0:T(8,128)(2,1)}, u32[]{:S(2)}, u32[]{:S(2)}) %collective-permute-start.5) | collective-permute-done | bytes 589856 | tf_op jit(solution)/shard_map/ppermute | solution.py:280
  32.7 3.4 %all-to-all-done.1 = bf16[8,48,768]{2,1,0:T(8,128)(2,1)} async-done(((bf16[8,48,768]{2,1,0:T(8,128)(2,1)}), bf16[8,48,768]{2,1,0:T(8,128)(2,1)}, u32[]{:S(2)}, u32[]{:S(2)}) %all-to-all-start.1) | async-done | bytes 589856 | tf_op jit(solution)/shard_map/all_to_all | solution.py:284
  36.1 9.8 %collective-permute-start.6 = (bf16[384,768]{1,0:T(8,128)(2,1)}, bf16[384,768]{1,0:T(8,128)(2,1)S(1)}, u32[]{:S(2)}, u32[]{:S(2)}) collective-permute-start(bf16[384,768]{1,0:T(8,128)(2,1)} %bitcast.7.refs_4_), channel_id=1, source_target_pairs={{0,32},{32,0},{1,33},{33,1},{2,34},{34,2},{3,35},{35,3},{4,36},{36... | collective-permute-start | bytes 1769480 | tf_op jit(solution)/shard_map/ppermute | solution.py:311
  45.9 3.2 %collective-permute-done.3.refs_1_.refs_5_ = bf16[192,1536]{1,0:T(8,128)(2,1)} collective-permute-done((bf16[192,1536]{1,0:T(8,128)(2,1)}, bf16[192,1536]{1,0:T(8,128)(2,1)}, u32[]{:S(2)}, u32[]{:S(2)}) %collective-permute-start.3) | collective-permute-done | bytes 589856 | tf_op jit(solution)/shard_map/ppermute | solution.py:280
  49.9 5.0 %shard_map.86 = (bf16[4,384,256]{2,1,0:T(8,128)(2,1)}, bf16[384,1536]{1,0:T(8,128)(2,1)}) custom-call(s32[4]{0:T(128)} %pad_add_fusion.scalar_ref, bf16[192,1536]{1,0:T(8,128)(2,1)} %bitcast.6.refs_0_.refs_4_, bf16[192,1536]{1,0:T(8,128)(2,1)} %collective-permute-done.3.refs_1_.refs_5_, bf16[192,1536]{1,0:T(8,128)(2,1)} %collective-permute-done.4.refs_2_.refs_6_, ...), custom_call_target="tpu_custom_call" | custom-call | flops 1000 | bytes 1000 | tf_op jit(solution)/shard_map/pallas_call | solution.py:201
  54.9 4.2 %all-to-all-start.2 = ((bf16[4,384,256]{2,1,0:T(8,128)(2,1)}), bf16[4,384,256]{2,1,0:T(8,128)(2,1)}, u32[]{:S(2)}, u32[]{:S(2)}) async-start(bf16[4,384,256]{2,1,0:T(8,128)(2,1)} %get-tuple-element.39), calls=%async_computation.2 | async-start | bytes 1572864 | tf_op jit(solution)/shard_map/all_to_all | solution.py:284
  59.1 4.8 %collective-permute-done.time_ref = bf16[2,192,1536]{2,1,0:T(8,128)(2,1)S(1)} collective-permute-done((bf16[2,192,1536]{2,1,0:T(8,128)(2,1)S(1)}, bf16[2,192,1536]{2,1,0:T(8,128)(2,1)S(1)}, u32[]{:S(2)}, u32[]{:S(2)}) %collective-permute-start) | collective-permute-done | bytes 1179680 | tf_op jit(solution)/shard_map/ppermute | solution.py:304
  65.0 8.1 %shard_map.84 = (bf16[192,1536]{1,0:T(8,128)(2,1)}, bf16[4,8,48,256]{3,2,1,0:T(8,128)(2,1)}, bf16[12,192,768]{2,1,0:T(8,128)(2,1)}) custom-call(s32[4]{0:T(128)} %pad_add_fusion.scalar_ref, bf16[192,1536]{1,0:T(8,128)(2,1)} %bitcast.24, bf16[2,192,1536]{2,1,0:T(8,128)(2,1)} %bitcast.19, bf16[2,192,1536]{2,1,0:T(8,128)(2,1)} %copy-done.3, ...), custom_call_target="tpu_custom_call" | custom-call | flops 1000 | bytes 1000 | tf_op jit(solution)/shard_map/pallas_call | solution.py:122
  73.1 3.5 %all-to-all-start = ((bf16[4,384,256]{2,1,0:T(8,128)(2,1)}), bf16[4,384,256]{2,1,0:T(8,128)(2,1)S(1)}, u32[]{:S(2)}, u32[]{:S(2)}) async-start(bf16[4,384,256]{2,1,0:T(8,128)(2,1)} %bitcast.27), calls=%async_computation | async-start | bytes 1572864 | tf_op jit(solution)/shard_map/all_to_all | solution.py:284
  76.6 6.1 %shard_map.87 = (bf16[192,768]{1,0:T(8,128)(2,1)}, bf16[2,192,768]{2,1,0:T(8,128)(2,1)}, bf16[2,192,768]{2,1,0:T(8,128)(2,1)}, bf16[2,192,768]{2,1,0:T(8,128)(2,1)}, bf16[2,192,768]{2,1,0:T(8,128)(2,1)}) custom-call(s32[4]{0:T(128)} %pad_add_fusion.scalar_ref, bf16[192,1536]{1,0:T(8,128)(2,1)} %bitcast.25, bf16[2,192,1536]{2,1,0:T(8,128)(2,1)} %bitcast.20, ...), custom_call_target="tpu_custom_call" | custom-call | flops 1000 | bytes 1000 | tf_op jit(solution)/shard_map/pallas_call | solution.py:142
  82.7 6.3 %all-to-all-done.att_ref = bf16[4,384,256]{2,1,0:T(8,128)(2,1)S(1)} async-done(((bf16[4,384,256]{2,1,0:T(8,128)(2,1)}), bf16[4,384,256]{2,1,0:T(8,128)(2,1)S(1)}, u32[]{:S(2)}, u32[]{:S(2)}) %all-to-all-start) | async-done | bytes 786464 | tf_op jit(solution)/shard_map/all_to_all | solution.py:284
  89.9 5.7 %shard_map.88 = (bf16[384,768]{1,0:T(8,128)(2,1)}, bf16[384,768]{1,0:T(8,128)(2,1)}) custom-call(s32[4]{0:T(128)} %pad_add_fusion.scalar_ref, bf16[4,384,256]{2,1,0:T(8,128)(2,1)} %copy-done.4, bf16[192,1536]{1,0:T(8,128)(2,1)} %bitcast.6.refs_0_.refs_4_, bf16[192,1536]{1,0:T(8,128)(2,1)} %collective-permute-done.3.refs_1_.refs_5_, ...), custom_call_target="tpu_custom_call" | custom-call | flops 1000 | bytes 1000 | tf_op jit(solution)/shard_map/pallas_call | solution.py:236
  97.3 3.0 %collective-permute-start.12 = (bf16[2,192,768]{2,1,0:T(8,128)(2,1)}, bf16[2,192,768]{2,1,0:T(8,128)(2,1)S(1)}, u32[]{:S(2)}, u32[]{:S(2)}) collective-permute-start(bf16[2,192,768]{2,1,0:T(8,128)(2,1)} %get-tuple-element.61), channel_id=1, source_target_pairs={{32,64},{64,32},{33,65},{65,33},{34,66},{66,34},{35,67},{67,35},{3... | collective-permute-start | bytes 1769480 | tf_op jit(solution)/shard_map/ppermute | solution.py:328
  100.5 4.9 %shard_map.89 = (bf16[192,1536]{1,0:T(8,128)(2,1)}, bf16[192,1536]{1,0:T(8,128)(2,1)}, bf16[192,1536]{1,0:T(8,128)(2,1)}, bf16[192,1536]{1,0:T(8,128)(2,1)}) custom-call(s32[4]{0:T(128)} %pad_add_fusion.scalar_ref, bf16[4,384,256]{2,1,0:T(8,128)(2,1)} %copy-done.4, bf16[384,1536]{1,0:T(8,128)(2,1)} %get-tuple-element.47.weight_ref), custom_call_target="tpu_custom_call" | custom-call | flops 1000 | bytes 1000 | tf_op jit(solution)/shard_map/pallas_call | solution.py:260
  108.4 2.6 %collective-permute-done.11 = bf16[2,192,768]{2,1,0:T(8,128)(2,1)S(1)} collective-permute-done((bf16[2,192,768]{2,1,0:T(8,128)(2,1)S(1)}, bf16[2,192,768]{2,1,0:T(8,128)(2,1)S(1)}, u32[]{:S(2)}, u32[]{:S(2)}) %collective-permute-start.11) | collective-permute-done | bytes 589856 | tf_op jit(solution)/shard_map/ppermute | solution.py:327
  111.3 6.3 %all-to-all-start.3 = ((bf16[8,48,768]{2,1,0:T(8,128)(2,1)}), bf16[8,48,768]{2,1,0:T(8,128)(2,1)S(1)}, u32[]{:S(2)}, u32[]{:S(2)}) async-start(bf16[8,48,768]{2,1,0:T(8,128)(2,1)} %bitcast.9), calls=%async_computation.3 | async-start | bytes 1179648 | tf_op jit(solution)/shard_map/all_to_all | solution.py:284
  117.6 6.2 %shard_map.90 = (bf16[192,768]{1,0:T(8,128)(2,1)}, bf16[2,192,768]{2,1,0:T(8,128)(2,1)}, bf16[2,192,768]{2,1,0:T(8,128)(2,1)}, bf16[2,192,768]{2,1,0:T(8,128)(2,1)}, bf16[2,192,768]{2,1,0:T(8,128)(2,1)}) custom-call(s32[4]{0:T(128)} %pad_add_fusion.scalar_ref, bf16[192,1536]{1,0:T(8,128)(2,1)} %bitcast.26, bf16[2,192,1536]{2,1,0:T(8,128)(2,1)} %bitcast.21, ...), custom_call_target="tpu_custom_call" | custom-call | flops 1000 | bytes 1000 | tf_op jit(solution)/shard_map/pallas_call | solution.py:142
  125.1 4.7 %collective-permute-start.15 = (bf16[2,192,768]{2,1,0:T(8,128)(2,1)}, bf16[2,192,768]{2,1,0:T(8,128)(2,1)}, u32[]{:S(2)}, u32[]{:S(2)}) collective-permute-start(bf16[2,192,768]{2,1,0:T(8,128)(2,1)} %get-tuple-element.65), channel_id=1, source_target_pairs={{32,64},{64,32},{33,65},{65,33},{34,66},{66,34},{35,67},{67,35},{3... | collective-permute-start | bytes 1769480 | tf_op jit(solution)/shard_map/ppermute | solution.py:328
  131.8 5.1 %collective-permute-done.10 = bf16[192,1536]{1,0:T(8,128)(2,1)} collective-permute-done((bf16[192,1536]{1,0:T(8,128)(2,1)}, bf16[192,1536]{1,0:T(8,128)(2,1)}, u32[]{:S(2)}, u32[]{:S(2)}) %collective-permute-start.10) | collective-permute-done | bytes 589856 | tf_op jit(solution)/shard_map/ppermute | solution.py:280
  142.7 5.1 %collective-permute-done.15 = bf16[2,192,768]{2,1,0:T(8,128)(2,1)} collective-permute-done((bf16[2,192,768]{2,1,0:T(8,128)(2,1)}, bf16[2,192,768]{2,1,0:T(8,128)(2,1)}, u32[]{:S(2)}, u32[]{:S(2)}) %collective-permute-start.15) | collective-permute-done | bytes 589856 | tf_op jit(solution)/shard_map/ppermute | solution.py:328
  (70 shorter events, 28.2 us)
Async XLA Ops:
  0.6 6.0 %collective-permute-start.1 = (bf16[2,192,1536]{2,1,0:T(8,128)(2,1)}, bf16[2,192,1536]{2,1,0:T(8,128)(2,1)S(1)}, u32[]{:S(2)}, u32[]{:S(2)}) collective-permute-start(bf16[2,192,1536]{2,1,0:T(8,128)(2,1)} %bitcast.18), channel_id=1, source_target_pairs={{0,32},{32,0},{1,33},{33,1},{2,34},{34,2},{3,35},{35,3},{4,36},{36... | collective-permute-start | bytes 3538952 | tf_op jit(solution)/shard_map/ppermute | solution.py:306
  10.1 26.0 %all-to-all-start.1 = ((bf16[8,48,768]{2,1,0:T(8,128)(2,1)}), bf16[8,48,768]{2,1,0:T(8,128)(2,1)}, u32[]{:S(2)}, u32[]{:S(2)}) async-start(bf16[8,48,768]{2,1,0:T(8,128)(2,1)} %shard_map.85), calls=%async_computation.1 | async-start | bytes 1179648 | tf_op jit(solution)/shard_map/all_to_all | solution.py:284
  16.7 16.1 %collective-permute-start.5 = (bf16[192,1536]{1,0:T(8,128)(2,1)}, bf16[192,1536]{1,0:T(8,128)(2,1)}, u32[]{:S(2)}, u32[]{:S(2)}) collective-permute-start(bf16[192,1536]{1,0:T(8,128)(2,1)} %bitcast.6.refs_0_.refs_4_), channel_id=1, source_target_pairs={{0,3},{1,0},{2,1},{3,2},{4,7},{5,4},{6,5},{7,6},{8,11},{9,8},{10,9... | collective-permute-start | bytes 1769480 | tf_op jit(solution)/shard_map/ppermute | solution.py:280
  19.4 26.5 %collective-permute-start.4 = (bf16[192,1536]{1,0:T(8,128)(2,1)}, bf16[192,1536]{1,0:T(8,128)(2,1)}, u32[]{:S(2)}, u32[]{:S(2)}) collective-permute-start(bf16[192,1536]{1,0:T(8,128)(2,1)} %bitcast.6.refs_0_.refs_4_), channel_id=1, source_target_pairs={{0,2},{1,3},{2,0},{3,1},{4,6},{5,7},{6,4},{7,5},{8,10},{9,11},{10,... | collective-permute-start | bytes 1769480 | tf_op jit(solution)/shard_map/ppermute | solution.py:280
  19.7 29.4 %collective-permute-start.3 = (bf16[192,1536]{1,0:T(8,128)(2,1)}, bf16[192,1536]{1,0:T(8,128)(2,1)}, u32[]{:S(2)}, u32[]{:S(2)}) collective-permute-start(bf16[192,1536]{1,0:T(8,128)(2,1)} %bitcast.6.refs_0_.refs_4_), channel_id=1, source_target_pairs={{0,1},{1,2},{2,3},{3,0},{4,5},{5,6},{6,7},{7,4},{8,9},{9,10},{10,1... | collective-permute-start | bytes 1769480 | tf_op jit(solution)/shard_map/ppermute | solution.py:280
  20.4 38.7 %collective-permute-start.2 = (bf16[2,192,1536]{2,1,0:T(8,128)(2,1)S(1)}, bf16[2,192,1536]{2,1,0:T(8,128)(2,1)S(1)}, u32[]{:S(2)}, u32[]{:S(2)}) collective-permute-start(bf16[2,192,1536]{2,1,0:T(8,128)(2,1)S(1)} %bitcast.22), channel_id=1, source_target_pairs={{32,64},{64,32},{33,65},{65,33},{34,66},{66,34},{35,67},{67,35},{3... | collective-permute-start | bytes 3538952 | tf_op jit(solution)/shard_map/ppermute | solution.py:305
  26.5 37.5 %collective-permute-start = (bf16[2,192,1536]{2,1,0:T(8,128)(2,1)S(1)}, bf16[2,192,1536]{2,1,0:T(8,128)(2,1)S(1)}, u32[]{:S(2)}, u32[]{:S(2)}) collective-permute-start(bf16[2,192,1536]{2,1,0:T(8,128)(2,1)S(1)} %bitcast.23), channel_id=1, source_target_pairs={{0,128},{128,0},{1,129},{129,1},{2,130},{130,2},{3,131},{131,3},{4... | collective-permute-start | bytes 3538952 | tf_op jit(solution)/shard_map/ppermute | solution.py:304
  36.1 13.0 %collective-permute-start.6 = (bf16[384,768]{1,0:T(8,128)(2,1)}, bf16[384,768]{1,0:T(8,128)(2,1)S(1)}, u32[]{:S(2)}, u32[]{:S(2)}) collective-permute-start(bf16[384,768]{1,0:T(8,128)(2,1)} %bitcast.7.refs_4_), channel_id=1, source_target_pairs={{0,32},{32,0},{1,33},{33,1},{2,34},{34,2},{3,35},{35,3},{4,36},{36... | collective-permute-start | bytes 1769480 | tf_op jit(solution)/shard_map/ppermute | solution.py:311
  54.9 18.1 %all-to-all-start.2 = ((bf16[4,384,256]{2,1,0:T(8,128)(2,1)}), bf16[4,384,256]{2,1,0:T(8,128)(2,1)}, u32[]{:S(2)}, u32[]{:S(2)}) async-start(bf16[4,384,256]{2,1,0:T(8,128)(2,1)} %get-tuple-element.39), calls=%async_computation.2 | async-start | bytes 1572864 | tf_op jit(solution)/shard_map/all_to_all | solution.py:284
  73.1 15.9 %all-to-all-start = ((bf16[4,384,256]{2,1,0:T(8,128)(2,1)}), bf16[4,384,256]{2,1,0:T(8,128)(2,1)S(1)}, u32[]{:S(2)}, u32[]{:S(2)}) async-start(bf16[4,384,256]{2,1,0:T(8,128)(2,1)} %bitcast.27), calls=%async_computation | async-start | bytes 1572864 | tf_op jit(solution)/shard_map/all_to_all | solution.py:284
  95.6 9.8 %collective-permute-start.7 = (bf16[384,768]{1,0:T(8,128)(2,1)}, bf16[384,768]{1,0:T(8,128)(2,1)S(1)}, u32[]{:S(2)}, u32[]{:S(2)}) collective-permute-start(bf16[384,768]{1,0:T(8,128)(2,1)} %get-tuple-element.45), channel_id=1, source_target_pairs={{0,32},{32,0},{1,33},{33,1},{2,34},{34,2},{3,35},{35,3},{4,36},{36... | collective-permute-start | bytes 1769480 | tf_op jit(solution)/shard_map/ppermute | solution.py:336
  96.1 14.9 %collective-permute-start.11 = (bf16[2,192,768]{2,1,0:T(8,128)(2,1)S(1)}, bf16[2,192,768]{2,1,0:T(8,128)(2,1)S(1)}, u32[]{:S(2)}, u32[]{:S(2)}) collective-permute-start(bf16[2,192,768]{2,1,0:T(8,128)(2,1)S(1)} %copy-done.12), channel_id=1, source_target_pairs={{0,128},{128,0},{1,129},{129,1},{2,130},{130,2},{3,131},{131,3},{4... | collective-permute-start | bytes 1769480 | tf_op jit(solution)/shard_map/ppermute | solution.py:327
  97.3 26.5 %collective-permute-start.12 = (bf16[2,192,768]{2,1,0:T(8,128)(2,1)}, bf16[2,192,768]{2,1,0:T(8,128)(2,1)S(1)}, u32[]{:S(2)}, u32[]{:S(2)}) collective-permute-start(bf16[2,192,768]{2,1,0:T(8,128)(2,1)} %get-tuple-element.61), channel_id=1, source_target_pairs={{32,64},{64,32},{33,65},{65,33},{34,66},{66,34},{35,67},{67,35},{3... | collective-permute-start | bytes 1769480 | tf_op jit(solution)/shard_map/ppermute | solution.py:328
  100.4 24.8 %collective-permute-start.13 = (bf16[2,192,768]{2,1,0:T(8,128)(2,1)}, bf16[2,192,768]{2,1,0:T(8,128)(2,1)S(1)}, u32[]{:S(2)}, u32[]{:S(2)}) collective-permute-start(bf16[2,192,768]{2,1,0:T(8,128)(2,1)} %get-tuple-element.62), channel_id=1, source_target_pairs={{0,32},{32,0},{1,33},{33,1},{2,34},{34,2},{3,35},{35,3},{4,36},{36... | collective-permute-start | bytes 1769480 | tf_op jit(solution)/shard_map/ppermute | solution.py:329
  106.4 23.9 %collective-permute-start.8 = (bf16[192,1536]{1,0:T(8,128)(2,1)}, bf16[192,1536]{1,0:T(8,128)(2,1)S(1)}, u32[]{:S(2)}, u32[]{:S(2)}) collective-permute-start(bf16[192,1536]{1,0:T(8,128)(2,1)} %get-tuple-element.53), channel_id=1, source_target_pairs={{0,3},{1,0},{2,1},{3,2},{4,7},{5,4},{6,5},{7,6},{8,11},{9,8},{10,9... | collective-permute-start | bytes 1769480 | tf_op jit(solution)/shard_map/ppermute | solution.py:280
  107.2 24.6 %collective-permute-start.9 = (bf16[192,1536]{1,0:T(8,128)(2,1)}, bf16[192,1536]{1,0:T(8,128)(2,1)}, u32[]{:S(2)}, u32[]{:S(2)}) collective-permute-start(bf16[192,1536]{1,0:T(8,128)(2,1)} %get-tuple-element.54), channel_id=1, source_target_pairs={{0,2},{1,3},{2,0},{3,1},{4,6},{5,7},{6,4},{7,5},{8,10},{9,11},{10,... | collective-permute-start | bytes 1769480 | tf_op jit(solution)/shard_map/ppermute | solution.py:280
  111.0 25.9 %collective-permute-start.10 = (bf16[192,1536]{1,0:T(8,128)(2,1)}, bf16[192,1536]{1,0:T(8,128)(2,1)}, u32[]{:S(2)}, u32[]{:S(2)}) collective-permute-start(bf16[192,1536]{1,0:T(8,128)(2,1)} %get-tuple-element.55), channel_id=1, source_target_pairs={{0,1},{1,2},{2,3},{3,0},{4,5},{5,6},{6,7},{7,4},{8,9},{9,10},{10,1... | collective-permute-start | bytes 1769480 | tf_op jit(solution)/shard_map/ppermute | solution.py:280
  111.3 28.0 %all-to-all-start.3 = ((bf16[8,48,768]{2,1,0:T(8,128)(2,1)}), bf16[8,48,768]{2,1,0:T(8,128)(2,1)S(1)}, u32[]{:S(2)}, u32[]{:S(2)}) async-start(bf16[8,48,768]{2,1,0:T(8,128)(2,1)} %bitcast.9), calls=%async_computation.3 | async-start | bytes 1179648 | tf_op jit(solution)/shard_map/all_to_all | solution.py:284
  123.8 18.0 %collective-permute-start.14 = (bf16[2,192,768]{2,1,0:T(8,128)(2,1)}, bf16[2,192,768]{2,1,0:T(8,128)(2,1)}, u32[]{:S(2)}, u32[]{:S(2)}) collective-permute-start(bf16[2,192,768]{2,1,0:T(8,128)(2,1)} %get-tuple-element.64), channel_id=1, source_target_pairs={{0,128},{128,0},{1,129},{129,1},{2,130},{130,2},{3,131},{131,3},{4... | collective-permute-start | bytes 1769480 | tf_op jit(solution)/shard_map/ppermute | solution.py:327
  125.1 22.7 %collective-permute-start.15 = (bf16[2,192,768]{2,1,0:T(8,128)(2,1)}, bf16[2,192,768]{2,1,0:T(8,128)(2,1)}, u32[]{:S(2)}, u32[]{:S(2)}) collective-permute-start(bf16[2,192,768]{2,1,0:T(8,128)(2,1)} %get-tuple-element.65), channel_id=1, source_target_pairs={{32,64},{64,32},{33,65},{65,33},{34,66},{66,34},{35,67},{67,35},{3... | collective-permute-start | bytes 1769480 | tf_op jit(solution)/shard_map/ppermute | solution.py:328
  130.2 17.6 %collective-permute-start.16 = (bf16[2,192,768]{2,1,0:T(8,128)(2,1)}, bf16[2,192,768]{2,1,0:T(8,128)(2,1)S(1)}, u32[]{:S(2)}, u32[]{:S(2)}) collective-permute-start(bf16[2,192,768]{2,1,0:T(8,128)(2,1)} %get-tuple-element.66), channel_id=1, source_target_pairs={{0,32},{32,0},{1,33},{33,1},{2,34},{34,2},{3,35},{35,3},{4,36},{36... | collective-permute-start | bytes 1769480 | tf_op jit(solution)/shard_map/ppermute | solution.py:329
  139.4 10.5 %collective-permute-start.19 = (bf16[48,768]{1,0:T(8,128)(2,1)S(1)}, bf16[48,768]{1,0:T(8,128)(2,1)S(1)}, u32[]{:S(2)}, u32[]{:S(2)}) collective-permute-start(bf16[48,768]{1,0:T(8,128)(2,1)S(1)} %reduce_sum.12), channel_id=1, source_target_pairs={{0,192},{64,128},{128,64},{192,0},{1,193},{65,129},{129,65},{193,1... | collective-permute-start | bytes 221192 | tf_op jit(solution)/shard_map/ppermute | solution.py:350
  141.3 8.5 %collective-permute-start.18 = (bf16[48,768]{1,0:T(8,128)(2,1)S(1)}, bf16[48,768]{1,0:T(8,128)(2,1)S(1)}, u32[]{:S(2)}, u32[]{:S(2)}) collective-permute-start(bf16[48,768]{1,0:T(8,128)(2,1)S(1)} %reduce_sum.12), channel_id=1, source_target_pairs={{0,64},{64,0},{1,65},{65,1},{2,66},{66,2},{3,67},{67,3},{4,68},{68... | collective-permute-start | bytes 221192 | tf_op jit(solution)/shard_map/ppermute | solution.py:349
  141.8 8.1 %collective-permute-start.17 = (bf16[48,768]{1,0:T(8,128)(2,1)S(1)}, bf16[48,768]{1,0:T(8,128)(2,1)S(1)}, u32[]{:S(2)}, u32[]{:S(2)}) collective-permute-start(bf16[48,768]{1,0:T(8,128)(2,1)S(1)} %reduce_sum.12), channel_id=1, source_target_pairs={{0,128},{128,0},{1,129},{129,1},{2,130},{130,2},{3,131},{131,3},{4... | collective-permute-start | bytes 221192 | tf_op jit(solution)/shard_map/ppermute | solution.py:348
  (14 other events, 73.7 us)

commit v7 on v6

--- a/solution.py
+++ b/solution.py
@@ -64,7 +64,8 @@
     flipped = jnp.concatenate(flipped, axis=0)
     for b in range(GROUP // ROWS):
         block = flipped[b * ROWS : (b + 1) * ROWS]
-        out_t_ref[b % NY, b // NY] = jnp.concatenate([block, jnp.zeros((ROWS, PAD - TILE), BF16)], axis=1)
+        to = lax.rem(b % NY - scalar_ref[2] + NY, NY)
+        out_t_ref[to, b // NY] = jnp.concatenate([block, jnp.zeros((ROWS, PAD - TILE), BF16)], axis=1)
 
 
 def backward_kernel(
@@ -154,28 +155,25 @@
     )(scalars, q, *kvs, att, d, probs)
 
 
-def panel_kernel(scalar_ref, weight_ref, after_ref, out_ref):
+def panel_kernel(scalar_ref, weight_ref, out_ref):
     for k in range(out_ref.shape[0]):
         out_ref[k] = weight_ref[0]
 
 
-def panel_copies(scalars, out_weight, copies, after):
+def panel_copies(scalars, out_weight, copies):
     half = out_weight.shape[2] // 2
     return pl.pallas_call(
         panel_kernel,
         grid_spec=pltpu.PrefetchScalarGridSpec(
             num_scalar_prefetch=1,
             grid=(1,),
-            in_specs=[
-                pl.BlockSpec((1, ROWS, half), lambda i, b: (b[3], 0, b[1])),
-                pl.BlockSpec(memory_space=pl.ANY),
-            ],
+            in_specs=[pl.BlockSpec((1, ROWS, half), lambda i, b: (b[3], 0, b[1]))],
             out_specs=whole((copies, ROWS, half)),
         ),
         out_shape=jax.ShapeDtypeStruct((copies, ROWS, half), BF16),
         compiler_params=PARAMS,
         cost_estimate=LIGHT,
-    )(scalars, out_weight, after)
+    )(scalars, out_weight)
 
 
 def source(scalar_ref, k):
@@ -215,9 +213,9 @@
     )(scalars, *ups, w_mine, w_mate)
 
 
-def gradient_kernel(scalar_ref, att_ref, *refs):
-    ups, outs = refs[: 2 * NY], refs[2 * NY :]
-    att = jnp.concatenate([att_ref[source(scalar_ref, k)] for k in range(NY)], axis=1)
+def gradient_kernel(scalar_ref, *refs):
+    atts, ups, outs = refs[:NY], refs[NY : 3 * NY], refs[3 * NY :]
+    att = jnp.concatenate([ref[...] for ref in atts], axis=1)
     rest = jnp.zeros((PAD - TILE, outs[0].shape[1]), BF16)
     for side, out_ref in enumerate(outs):
         up = jnp.concatenate(
@@ -228,7 +226,7 @@
 
 def weight_gradient(scalars, atts, ups):
     half = ups[0].shape[1] // 2
-    rows = atts.shape[1]
+    rows = atts[0].shape[0]
     step = 256
     steps = half // step
     mine = pl.BlockSpec((TILE, step), lambda i, b: (0, b[1] * steps + i))
@@ -238,37 +236,35 @@
         grid_spec=pltpu.PrefetchScalarGridSpec(
             num_scalar_prefetch=1,
             grid=(steps,),
-            in_specs=[whole(atts.shape)] + [mine] * NY + [mate] * NY,
+            in_specs=[whole((rows, PAD))] * NY + [mine] * NY + [mate] * NY,
             out_specs=[pl.BlockSpec((rows, step), lambda i, b: (0, i))] * 2,
         ),
         out_shape=[jax.ShapeDtypeStruct((rows, half), BF16)] * 2,
         compiler_params=PARAMS,
         cost_estimate=LIGHT,
-    )(scalars, atts, *ups, *ups)
-
-
-def mixed_kernel(scalar_ref, att_ref, weight_ref, *outs):
-    for k, out_ref in enumerate(outs):
-        att = att_ref[source(scalar_ref, k)][:, :TILE]
+    )(scalars, *atts, *ups, *ups)
+
+
+def mixed_kernel(*refs):
+    atts, weight_ref, outs = refs[:NY], refs[NY], refs[NY + 1 :]
+    for att_ref, out_ref in zip(atts, outs):
+        att = att_ref[...][:, :TILE]
         out = lax.dot_general(att, weight_ref[...], TN, preferred_element_type=F32)
         out_ref[...] = out.astype(BF16)
 
 
-def mixed_parts(scalars, atts, weight):
+def mixed_parts(atts, weight):
     rows, dout = weight.shape
     step = 512
     return pl.pallas_call(
         mixed_kernel,
-        grid_spec=pltpu.PrefetchScalarGridSpec(
-            num_scalar_prefetch=1,
-            grid=(dout // step,),
-            in_specs=[whole(atts.shape), pl.BlockSpec((rows, step), lambda i, b: (0, i))],
-            out_specs=[pl.BlockSpec((TILE, step), lambda i, b: (0, i))] * NY,
-        ),
+        grid=(dout // step,),
+        in_specs=[whole((rows, PAD))] * NY + [pl.BlockSpec((rows, step), lambda i: (0, i))],
+        out_specs=[pl.BlockSpec((TILE, step), lambda i: (0, i))] * NY,
         out_shape=[jax.ShapeDtypeStruct((TILE, dout), BF16)] * NY,
         compiler_params=PARAMS,
         cost_estimate=LIGHT,
-    )(scalars, atts, weight)
+    )(*atts, weight)
 
 
 SWAP = [(0, 1), (1, 0)]
@@ -305,16 +301,17 @@
     from_cross = lax.ppermute(kv, ("xh", "co"), CROSS)
     from_core = lax.ppermute(kv, "co", SWAP)
 
-    panels = panel_copies(scalars, out_weight, nz, from_core)
+    panels = panel_copies(scalars, out_weight, nz)
     w_mine = swapped(panels, "z").reshape(nz * rows, half)
     ups = [up] + [shifted(up, "y", k) for k in (1, 2, 3)]
     w_mate = lax.ppermute(w_mine, "co", SWAP)
+    kvs = (kv, from_time, from_core, from_cross)
+    att, att_turned, probs = attention_forward(scalars, q, kvs)
+    att_turned = att_turned.reshape(ny, nz * rows, PAD)
+    atts = [att_turned[0]] + [shifted(att_turned[k], "y", k) for k in (1, 2, 3)]
+    att, w_mine, w_mate = lax.optimization_barrier((att, w_mine, w_mate))
     d_parts, w_rows = d_attention(scalars, ups, w_mine, w_mate)
     d_turned = swapped(d_parts, "y").reshape(ny, nz, rows, PAD)
-
-    kvs = (kv, from_time, from_core, from_cross)
-    att, att_turned, probs = attention_forward(scalars, q, kvs)
-    atts = swapped(att_turned.reshape(ny, nz * rows, PAD), "y")
 
     parts = 2
     groups = HEADS // PER_STEP // parts
@@ -335,7 +332,7 @@
     grad_mine, grad_mate = weight_gradient(scalars, atts, ups)
     from_mate = lax.ppermute(grad_mate, "co", SWAP)
     atts, w_rows, grad_mine = lax.optimization_barrier((atts, w_rows, grad_mine))
-    mixed = mixed_parts(scalars, atts, w_rows)
+    mixed = mixed_parts(atts, w_rows)
     grad = (grad_mine.astype(F32) + from_mate.astype(F32)).astype(BF16).reshape(nz, rows, half)
     probs, grad, mixed = lax.optimization_barrier((probs, grad, mixed))
     gq_1, own_1, terms_1 = backward(1)

time: 153 us -> 165 us (1.078)
  waiting for transfers between devices: 38.3 us -> 59 us
  starting transfers between devices: 61 us -> 53.3 us
    all_to_all x4 -> x3, waiting for transfers between devices: 9.71 us -> 25.8 us  [swapped(): return lax.all_to_all(x, axis, split_axis=0, concat_axis=0, tiled=True)]
    ppermute x6 -> x9, waiting for transfers between devices: 14.2 us -> 25 us  [shifted(): return lax.ppermute(x, axis, [(i, (i + by) % count) for i in range(count)])]
    ppermute x6 -> x9, starting transfers between devices: 6.14 us -> 16.2 us  [shifted(): return lax.ppermute(x, axis, [(i, (i + by) % count) for i in range(count)])]
    ppermute x1, starting transfers between devices: 9.77 us -> 0.49 us  [per_device(): w_mate = lax.ppermute(w_mine, 'co', SWAP)]
    all_to_all x4 -> x3, starting transfers between devices: 20.5 us -> 15.3 us  [swapped(): return lax.all_to_all(x, axis, split_axis=0, concat_axis=0, tiled=True)]
    ppermute x1, starting transfers between devices: 3.33 us -> 0.09 us  [per_device(): from_core = lax.ppermute(kv, 'co', SWAP)]
    ppermute x2, waiting for transfers between devices: 2.6 us -> 0.33 us  [backward(): lax.ppermute(to_time, 'xl', SWAP)]
    ppermute x2, waiting for transfers between devices: 5.1 us -> 3.17 us  [backward(): lax.ppermute(to_cross, ('xh', 'co'), CROSS)]
  transfers between devices with their start and end apart: 25 -> 27, of which waited for: 10 -> 10; matrix products, arithmetic and copies ran while one was open for 5% -> 5% of each run, Pallas kernels for 20% -> 17%
where the time goes in v7:
time: 165 us; the launch traced here: 164 us
  waiting for transfers between devices  59 us (36%)
  starting transfers between devices  53.3 us (32%)
  Pallas kernels  38.1 us (23%)
  other arithmetic  8.57 us (5%)
  local copies, waits for them, and re-layouts  3.85 us (2%)
    all_to_all x3, waiting for transfers between devices, swapped(): return lax.all_to_all(x, axis, split_axis=0, concat_axis=0, tiled=True)  25.8 us
    ppermute x9, waiting for transfers between devices, shifted(): return lax.ppermute(x, axis, [(i, (i + by) % count) for i in range(count)])  25 us
    ppermute x9, starting transfers between devices, shifted(): return lax.ppermute(x, axis, [(i, (i + by) % count) for i in range(count)])  16.2 us
    all_to_all x3, starting transfers between devices, swapped(): return lax.all_to_all(x, axis, split_axis=0, concat_axis=0, tiled=True)  15.3 us
    pallas_call x2, Pallas kernels, attention_backward(): pl.pallas_call(backward_kernel, grid_spec=pltpu.PrefetchScalarGridSpec(nu...  12.4 us
    ppermute x2, starting transfers between devices, backward(): lax.ppermute(to_cross, ('xh', 'co'), CROSS)  8.54 us
    pallas_call x1, Pallas kernels, attention_forward(): pl.pallas_call(forward_kernel, grid_spec=pltpu.PrefetchScalarGridSpec(num...  8.1 us
    ppermute x1, starting transfers between devices, per_device(): from_cross = lax.ppermute(kv, ('xh', 'co'), CROSS)  6.04 us
  transfers between devices with their start and end apart: 27, of which 10 were waited for; matrix products, arithmetic and copies ran while one was open for 5% of the time, Pallas kernels for 17%

profile of v7, /device:TPU:1, one launch (start us, length us, event | category | flops | bytes accessed | tf_op | source)
XLA Modules:
  0.0 164.5 jit_solution(4952191971530777559)
XLA Ops:
  0.6 6.0 %collective-permute-start.2 = (bf16[2,192,1536]{2,1,0:T(8,128)(2,1)}, bf16[2,192,1536]{2,1,0:T(8,128)(2,1)S(1)}, u32[]{:S(2)}, u32[]{:S(2)}) collective-permute-start(bf16[2,192,1536]{2,1,0:T(8,128)(2,1)} %bitcast.21), channel_id=1, source_target_pairs={{32,64},{64,32},{33,65},{65,33},{34,66},{66,34},{35,67},{67,35},{3... | collective-permute-start | bytes 3538952 | tf_op jit(solution)/shard_map/ppermute | solution.py:301
  8.0 2.5 %shard_map.85 = bf16[8,48,768]{2,1,0:T(8,128)(2,1)} custom-call(s32[4]{0:T(128)} %pad_add_fusion.scalar_ref, bf16[32,48,1536]{2,1,0:T(8,128)(2,1)} %weight_ref.1), custom_call_target="tpu_custom_call" | custom-call | flops 1000 | bytes 1000 | tf_op jit(solution)/shard_map/pallas_call | solution.py:165
  10.6 8.2 %all-to-all-start = ((bf16[8,48,768]{2,1,0:T(8,128)(2,1)}), bf16[8,48,768]{2,1,0:T(8,128)(2,1)}, u32[]{:S(2)}, u32[]{:S(2)}) async-start(bf16[8,48,768]{2,1,0:T(8,128)(2,1)} %shard_map.85), calls=%async_computation | async-start | bytes 1179648 | tf_op jit(solution)/shard_map/all_to_all | solution.py:280
  19.2 19.1 %all-to-all-done = bf16[8,48,768]{2,1,0:T(8,128)(2,1)} async-done(((bf16[8,48,768]{2,1,0:T(8,128)(2,1)}), bf16[8,48,768]{2,1,0:T(8,128)(2,1)}, u32[]{:S(2)}, u32[]{:S(2)}) %all-to-all-start) | async-done | bytes 589856 | tf_op jit(solution)/shard_map/all_to_all | solution.py:280
  38.7 2.7 %collective-permute-start.9 = (bf16[192,1536]{1,0:T(8,128)(2,1)}, bf16[192,1536]{1,0:T(8,128)(2,1)S(1)}, u32[]{:S(2)}, u32[]{:S(2)}) collective-permute-start(bf16[192,1536]{1,0:T(8,128)(2,1)} %bitcast.32), channel_id=1, source_target_pairs={{0,3},{1,0},{2,1},{3,2},{4,7},{5,4},{6,5},{7,6},{8,11},{9,8},{10,9... | collective-permute-start | bytes 1769480 | tf_op jit(solution)/shard_map/ppermute | solution.py:276
  42.5 3.2 %collective-permute-done.time_ref = bf16[2,192,1536]{2,1,0:T(8,128)(2,1)} collective-permute-done((bf16[2,192,1536]{2,1,0:T(8,128)(2,1)S(1)}, bf16[2,192,1536]{2,1,0:T(8,128)(2,1)}, u32[]{:S(2)}, u32[]{:S(2)}) %collective-permute-start) | collective-permute-done | bytes 1179680 | tf_op jit(solution)/shard_map/ppermute | solution.py:300
  45.7 8.1 %shard_map.84 = (bf16[192,1536]{1,0:T(8,128)(2,1)}, bf16[4,8,48,256]{3,2,1,0:T(8,128)(2,1)}, bf16[12,192,768]{2,1,0:T(8,128)(2,1)}) custom-call(s32[4]{0:T(128)} %pad_add_fusion.scalar_ref, bf16[192,1536]{1,0:T(8,128)(2,1)} %bitcast.29, bf16[2,192,1536]{2,1,0:T(8,128)(2,1)} %bitcast.23, bf16[2,192,1536]{2,1,0:T(8,128)(2,1)} %collective-permute-done.time_ref, ...), custom_call_target="tpu_custom_call" | custom-call | flops 1000 | bytes 1000 | tf_op jit(solution)/shard_map/pallas_call | solution.py:123
  53.8 13.2 %collective-permute-done.9.refs_3_.refs_7_.refs_11_ = bf16[192,1536]{1,0:T(8,128)(2,1)S(1)} collective-permute-done((bf16[192,1536]{1,0:T(8,128)(2,1)}, bf16[192,1536]{1,0:T(8,128)(2,1)S(1)}, u32[]{:S(2)}, u32[]{:S(2)}) %collective-permute-start.9) | collective-permute-done | bytes 589856 | tf_op jit(solution)/shard_map/ppermute | solution.py:276
  67.0 4.0 %collective-permute-done.7.refs_1_.refs_5_.refs_9_ = bf16[192,1536]{1,0:T(8,128)(2,1)S(1)} collective-permute-done((bf16[192,1536]{1,0:T(8,128)(2,1)}, bf16[192,1536]{1,0:T(8,128)(2,1)S(1)}, u32[]{:S(2)}, u32[]{:S(2)}) %collective-permute-start.7) | collective-permute-done | bytes 589856 | tf_op jit(solution)/shard_map/ppermute | solution.py:276
  71.9 5.0 %shard_map.86 = (bf16[4,384,256]{2,1,0:T(8,128)(2,1)}, bf16[384,1536]{1,0:T(8,128)(2,1)}) custom-call(s32[4]{0:T(128)} %pad_add_fusion.scalar_ref, bf16[192,1536]{1,0:T(8,128)(2,1)} %bitcast.35, bf16[192,1536]{1,0:T(8,128)(2,1)} %copy-done.6, bf16[192,1536]{1,0:T(8,128)(2,1)} %copy-done.5, bf16[192,1536]{1,0:T(8,128)(2,1)} %copy-done.4, ...), custom_call_target="tpu_custom_call" | custom-call | flops 1000 | bytes 1000 | tf_op jit(solution)/shard_map/pallas_call | solution.py:199
  76.9 3.6 %all-to-all-start.1 = ((bf16[4,384,256]{2,1,0:T(8,128)(2,1)}), bf16[4,384,256]{2,1,0:T(8,128)(2,1)S(1)}, u32[]{:S(2)}, u32[]{:S(2)}) async-start(bf16[4,384,256]{2,1,0:T(8,128)(2,1)} %get-tuple-element.51), calls=%async_computation.1 | async-start | bytes 1572864 | tf_op jit(solution)/shard_map/all_to_all | solution.py:280
  81.3 2.9 %collective-permute-start.4 = (bf16[384,256]{1,0:T(8,128)(2,1)S(1)}, bf16[384,256]{1,0:T(8,128)(2,1)S(1)}, u32[]{:S(2)}, u32[]{:S(2)}) collective-permute-start(bf16[384,256]{1,0:T(8,128)(2,1)S(1)} %bitcast.42), channel_id=1, source_target_pairs={{0,2},{1,3},{2,0},{3,1},{4,6},{5,7},{6,4},{7,5},{8,10},{9,11},{10,... | collective-permute-start | bytes 589832 | tf_op jit(solution)/shard_map/ppermute | solution.py:276
  85.7 6.8 %all-to-all-done.1 = bf16[4,384,256]{2,1,0:T(8,128)(2,1)S(1)} async-done(((bf16[4,384,256]{2,1,0:T(8,128)(2,1)}), bf16[4,384,256]{2,1,0:T(8,128)(2,1)S(1)}, u32[]{:S(2)}, u32[]{:S(2)}) %all-to-all-start.1) | async-done | bytes 786464 | tf_op jit(solution)/shard_map/all_to_all | solution.py:280
  93.4 6.2 %shard_map.87 = (bf16[192,768]{1,0:T(8,128)(2,1)}, bf16[2,192,768]{2,1,0:T(8,128)(2,1)}, bf16[2,192,768]{2,1,0:T(8,128)(2,1)}, bf16[2,192,768]{2,1,0:T(8,128)(2,1)}, bf16[2,192,768]{2,1,0:T(8,128)(2,1)}) custom-call(s32[4]{0:T(128)} %pad_add_fusion.scalar_ref, bf16[192,1536]{1,0:T(8,128)(2,1)} %bitcast.30, bf16[2,192,1536]{2,1,0:T(8,128)(2,1)} %bitcast.24, ...), custom_call_target="tpu_custom_call" | custom-call | flops 1000 | bytes 1000 | tf_op jit(solution)/shard_map/pallas_call | solution.py:143
  101.7 5.8 %shard_map.88 = (bf16[384,768]{1,0:T(8,128)(2,1)}, bf16[384,768]{1,0:T(8,128)(2,1)}) custom-call(s32[4]{0:T(128)} %pad_add_fusion.scalar_ref, bf16[384,256]{1,0:T(8,128)(2,1)} %bitcast.38, bf16[384,256]{1,0:T(8,128)(2,1)} %copy-done.9, bf16[384,256]{1,0:T(8,128)(2,1)} %copy-done.7, bf16[384,256]{1,0:T(8,128)(2,1)} %copy-done.8, bf16[192,1536]{1,0:T(8,128)(2,1)} %bitcast.36, ...), custom_call_target="tpu_custom_call" | custom-call | flops 1000 | bytes 1000 | tf_op jit(solution)/shard_map/pallas_call | solution.py:234
  109.0 3.7 %collective-permute-start.15 = (bf16[2,192,768]{2,1,0:T(8,128)(2,1)}, bf16[2,192,768]{2,1,0:T(8,128)(2,1)S(1)}, u32[]{:S(2)}, u32[]{:S(2)}) collective-permute-start(bf16[2,192,768]{2,1,0:T(8,128)(2,1)} %get-tuple-element.79), channel_id=1, source_target_pairs={{32,64},{64,32},{33,65},{65,33},{34,66},{66,34},{35,67},{67,35},{3... | collective-permute-start | bytes 1769480 | tf_op jit(solution)/shard_map/ppermute | solution.py:325
  113.0 4.3 %shard_map.89 = (bf16[192,1536]{1,0:T(8,128)(2,1)}, bf16[192,1536]{1,0:T(8,128)(2,1)}, bf16[192,1536]{1,0:T(8,128)(2,1)}, bf16[192,1536]{1,0:T(8,128)(2,1)}) custom-call(bf16[384,256]{1,0:T(8,128)(2,1)} %bitcast.39, bf16[384,256]{1,0:T(8,128)(2,1)} %copy-done.9, bf16[384,256]{1,0:T(8,128)(2,1)} %copy-done.7, bf16[384,256]{1,0:T(8,128)(2,1)} %copy-done.8, ...), custom_call_target="tpu_custom_call" | custom-call | flops 1000 | bytes 1000 | tf_op jit(solution)/shard_map/pallas_call | solution.py:259
  119.2 4.0 %collective-permute-start.12 = (bf16[192,1536]{1,0:T(8,128)(2,1)}, bf16[192,1536]{1,0:T(8,128)(2,1)}, u32[]{:S(2)}, u32[]{:S(2)}) collective-permute-start(bf16[192,1536]{1,0:T(8,128)(2,1)} %get-tuple-element.72), channel_id=1, source_target_pairs={{0,2},{1,3},{2,0},{3,1},{4,6},{5,7},{6,4},{7,5},{8,10},{9,11},{10,... | collective-permute-start | bytes 1769480 | tf_op jit(solution)/shard_map/ppermute | solution.py:276
  123.6 3.1 %collective-permute-start.13 = (bf16[192,1536]{1,0:T(8,128)(2,1)}, bf16[192,1536]{1,0:T(8,128)(2,1)}, u32[]{:S(2)}, u32[]{:S(2)}) collective-permute-start(bf16[192,1536]{1,0:T(8,128)(2,1)} %get-tuple-element.73), channel_id=1, source_target_pairs={{0,1},{1,2},{2,3},{3,0},{4,5},{5,6},{6,7},{7,4},{8,9},{9,10},{10,1... | collective-permute-start | bytes 1769480 | tf_op jit(solution)/shard_map/ppermute | solution.py:276
  126.7 3.5 %all-to-all-start.2 = ((bf16[8,48,768]{2,1,0:T(8,128)(2,1)}), bf16[8,48,768]{2,1,0:T(8,128)(2,1)S(1)}, u32[]{:S(2)}, u32[]{:S(2)}) async-start(bf16[8,48,768]{2,1,0:T(8,128)(2,1)} %bitcast.12), calls=%async_computation.2 | async-start | bytes 1179648 | tf_op jit(solution)/shard_map/all_to_all | solution.py:280
  130.2 6.2 %shard_map.90 = (bf16[192,768]{1,0:T(8,128)(2,1)}, bf16[2,192,768]{2,1,0:T(8,128)(2,1)}, bf16[2,192,768]{2,1,0:T(8,128)(2,1)}, bf16[2,192,768]{2,1,0:T(8,128)(2,1)}, bf16[2,192,768]{2,1,0:T(8,128)(2,1)}) custom-call(s32[4]{0:T(128)} %pad_add_fusion.scalar_ref, bf16[192,1536]{1,0:T(8,128)(2,1)} %bitcast.31, bf16[2,192,1536]{2,1,0:T(8,128)(2,1)} %bitcast.25, ...), custom_call_target="tpu_custom_call" | custom-call | flops 1000 | bytes 1000 | tf_op jit(solution)/shard_map/pallas_call | solution.py:143
  136.9 4.8 %collective-permute-start.18 = (bf16[2,192,768]{2,1,0:T(8,128)(2,1)}, bf16[2,192,768]{2,1,0:T(8,128)(2,1)}, u32[]{:S(2)}, u32[]{:S(2)}) collective-permute-start(bf16[2,192,768]{2,1,0:T(8,128)(2,1)} %get-tuple-element.83), channel_id=1, source_target_pairs={{32,64},{64,32},{33,65},{65,33},{34,66},{66,34},{35,67},{67,35},{3... | collective-permute-start | bytes 1769480 | tf_op jit(solution)/shard_map/ppermute | solution.py:325
  143.6 6.3 %collective-permute-done.13 = bf16[192,1536]{1,0:T(8,128)(2,1)} collective-permute-done((bf16[192,1536]{1,0:T(8,128)(2,1)}, bf16[192,1536]{1,0:T(8,128)(2,1)}, u32[]{:S(2)}, u32[]{:S(2)}) %collective-permute-start.13) | collective-permute-done | bytes 589856 | tf_op jit(solution)/shard_map/ppermute | solution.py:276
  155.8 3.2 %collective-permute-done.18 = bf16[2,192,768]{2,1,0:T(8,128)(2,1)} collective-permute-done((bf16[2,192,768]{2,1,0:T(8,128)(2,1)}, bf16[2,192,768]{2,1,0:T(8,128)(2,1)}, u32[]{:S(2)}, u32[]{:S(2)}) %collective-permute-start.18) | collective-permute-done | bytes 589856 | tf_op jit(solution)/shard_map/ppermute | solution.py:325
  (87 shorter events, 26.3 us)
Async XLA Ops:
  0.6 40.8 %collective-permute-start.2 = (bf16[2,192,1536]{2,1,0:T(8,128)(2,1)}, bf16[2,192,1536]{2,1,0:T(8,128)(2,1)S(1)}, u32[]{:S(2)}, u32[]{:S(2)}) collective-permute-start(bf16[2,192,1536]{2,1,0:T(8,128)(2,1)} %bitcast.21), channel_id=1, source_target_pairs={{32,64},{64,32},{33,65},{65,33},{34,66},{66,34},{35,67},{67,35},{3... | collective-permute-start | bytes 3538952 | tf_op jit(solution)/shard_map/ppermute | solution.py:301
  6.7 35.1 %collective-permute-start.1 = (bf16[2,192,1536]{2,1,0:T(8,128)(2,1)}, bf16[2,192,1536]{2,1,0:T(8,128)(2,1)S(1)}, u32[]{:S(2)}, u32[]{:S(2)}) collective-permute-start(bf16[2,192,1536]{2,1,0:T(8,128)(2,1)} %bitcast.22), channel_id=1, source_target_pairs={{0,32},{32,0},{1,33},{33,1},{2,34},{34,2},{3,35},{35,3},{4,36},{36... | collective-permute-start | bytes 3538952 | tf_op jit(solution)/shard_map/ppermute | solution.py:302
  10.6 27.7 %all-to-all-start = ((bf16[8,48,768]{2,1,0:T(8,128)(2,1)}), bf16[8,48,768]{2,1,0:T(8,128)(2,1)}, u32[]{:S(2)}, u32[]{:S(2)}) async-start(bf16[8,48,768]{2,1,0:T(8,128)(2,1)} %shard_map.85), calls=%async_computation | async-start | bytes 1179648 | tf_op jit(solution)/shard_map/all_to_all | solution.py:280
  18.8 26.9 %collective-permute-start = (bf16[2,192,1536]{2,1,0:T(8,128)(2,1)S(1)}, bf16[2,192,1536]{2,1,0:T(8,128)(2,1)}, u32[]{:S(2)}, u32[]{:S(2)}) collective-permute-start(bf16[2,192,1536]{2,1,0:T(8,128)(2,1)S(1)} %bitcast.26), channel_id=1, source_target_pairs={{0,128},{128,0},{1,129},{129,1},{2,130},{130,2},{3,131},{131,3},{4... | collective-permute-start | bytes 3538952 | tf_op jit(solution)/shard_map/ppermute | solution.py:300
  38.2 15.6 %collective-permute-start.6 = (bf16[384,768]{1,0:T(8,128)(2,1)}, bf16[384,768]{1,0:T(8,128)(2,1)S(1)}, u32[]{:S(2)}, u32[]{:S(2)}) collective-permute-start(bf16[384,768]{1,0:T(8,128)(2,1)} %bitcast.9.refs_4_), channel_id=1, source_target_pairs={{0,32},{32,0},{1,33},{33,1},{2,34},{34,2},{3,35},{35,3},{4,36},{36... | collective-permute-start | bytes 1769480 | tf_op jit(solution)/shard_map/ppermute | solution.py:307
  38.7 28.3 %collective-permute-start.9 = (bf16[192,1536]{1,0:T(8,128)(2,1)}, bf16[192,1536]{1,0:T(8,128)(2,1)S(1)}, u32[]{:S(2)}, u32[]{:S(2)}) collective-permute-start(bf16[192,1536]{1,0:T(8,128)(2,1)} %bitcast.32), channel_id=1, source_target_pairs={{0,3},{1,0},{2,1},{3,2},{4,7},{5,4},{6,5},{7,6},{8,11},{9,8},{10,9... | collective-permute-start | bytes 1769480 | tf_op jit(solution)/shard_map/ppermute | solution.py:276
  41.5 25.6 %collective-permute-start.8 = (bf16[192,1536]{1,0:T(8,128)(2,1)}, bf16[192,1536]{1,0:T(8,128)(2,1)S(1)}, u32[]{:S(2)}, u32[]{:S(2)}) collective-permute-start(bf16[192,1536]{1,0:T(8,128)(2,1)} %bitcast.33), channel_id=1, source_target_pairs={{0,2},{1,3},{2,0},{3,1},{4,6},{5,7},{6,4},{7,5},{8,10},{9,11},{10,... | collective-permute-start | bytes 1769480 | tf_op jit(solution)/shard_map/ppermute | solution.py:276
  41.8 29.2 %collective-permute-start.7 = (bf16[192,1536]{1,0:T(8,128)(2,1)}, bf16[192,1536]{1,0:T(8,128)(2,1)S(1)}, u32[]{:S(2)}, u32[]{:S(2)}) collective-permute-start(bf16[192,1536]{1,0:T(8,128)(2,1)} %bitcast.34), channel_id=1, source_target_pairs={{0,1},{1,2},{2,3},{3,0},{4,5},{5,6},{6,7},{7,4},{8,9},{9,10},{10,1... | collective-permute-start | bytes 1769480 | tf_op jit(solution)/shard_map/ppermute | solution.py:276
  76.9 15.5 %all-to-all-start.1 = ((bf16[4,384,256]{2,1,0:T(8,128)(2,1)}), bf16[4,384,256]{2,1,0:T(8,128)(2,1)S(1)}, u32[]{:S(2)}, u32[]{:S(2)}) async-start(bf16[4,384,256]{2,1,0:T(8,128)(2,1)} %get-tuple-element.51), calls=%async_computation.1 | async-start | bytes 1572864 | tf_op jit(solution)/shard_map/all_to_all | solution.py:280
  81.3 18.3 %collective-permute-start.4 = (bf16[384,256]{1,0:T(8,128)(2,1)S(1)}, bf16[384,256]{1,0:T(8,128)(2,1)S(1)}, u32[]{:S(2)}, u32[]{:S(2)}) collective-permute-start(bf16[384,256]{1,0:T(8,128)(2,1)S(1)} %bitcast.42), channel_id=1, source_target_pairs={{0,2},{1,3},{2,0},{3,1},{4,6},{5,7},{6,4},{7,5},{8,10},{9,11},{10,... | collective-permute-start | bytes 589832 | tf_op jit(solution)/shard_map/ppermute | solution.py:276
  84.2 15.4 %collective-permute-start.5 = (bf16[384,256]{1,0:T(8,128)(2,1)S(1)}, bf16[384,256]{1,0:T(8,128)(2,1)S(1)}, u32[]{:S(2)}, u32[]{:S(2)}) collective-permute-start(bf16[384,256]{1,0:T(8,128)(2,1)S(1)} %bitcast.41), channel_id=1, source_target_pairs={{0,3},{1,0},{2,1},{3,2},{4,7},{5,4},{6,5},{7,6},{8,11},{9,8},{10,9... | collective-permute-start | bytes 589832 | tf_op jit(solution)/shard_map/ppermute | solution.py:276
  85.1 15.9 %collective-permute-start.3 = (bf16[384,256]{1,0:T(8,128)(2,1)S(1)}, bf16[384,256]{1,0:T(8,128)(2,1)S(1)}, u32[]{:S(2)}, u32[]{:S(2)}) collective-permute-start(bf16[384,256]{1,0:T(8,128)(2,1)S(1)} %bitcast.40), channel_id=1, source_target_pairs={{0,1},{1,2},{2,3},{3,0},{4,5},{5,6},{6,7},{7,4},{8,9},{9,10},{10,1... | collective-permute-start | bytes 589832 | tf_op jit(solution)/shard_map/ppermute | solution.py:276
  107.5 9.8 %collective-permute-start.10 = (bf16[384,768]{1,0:T(8,128)(2,1)}, bf16[384,768]{1,0:T(8,128)(2,1)S(1)}, u32[]{:S(2)}, u32[]{:S(2)}) collective-permute-start(bf16[384,768]{1,0:T(8,128)(2,1)} %get-tuple-element.60), channel_id=1, source_target_pairs={{0,32},{32,0},{1,33},{33,1},{2,34},{34,2},{3,35},{35,3},{4,36},{36... | collective-permute-start | bytes 1769480 | tf_op jit(solution)/shard_map/ppermute | solution.py:333
  108.7 14.9 %collective-permute-start.14 = (bf16[2,192,768]{2,1,0:T(8,128)(2,1)S(1)}, bf16[2,192,768]{2,1,0:T(8,128)(2,1)S(1)}, u32[]{:S(2)}, u32[]{:S(2)}) collective-permute-start(bf16[2,192,768]{2,1,0:T(8,128)(2,1)S(1)} %copy-done.18), channel_id=1, source_target_pairs={{0,128},{128,0},{1,129},{129,1},{2,130},{130,2},{3,131},{131,3},{4... | collective-permute-start | bytes 1769480 | tf_op jit(solution)/shard_map/ppermute | solution.py:324
  109.0 27.5 %collective-permute-start.15 = (bf16[2,192,768]{2,1,0:T(8,128)(2,1)}, bf16[2,192,768]{2,1,0:T(8,128)(2,1)S(1)}, u32[]{:S(2)}, u32[]{:S(2)}) collective-permute-start(bf16[2,192,768]{2,1,0:T(8,128)(2,1)} %get-tuple-element.79), channel_id=1, source_target_pairs={{32,64},{64,32},{33,65},{65,33},{34,66},{66,34},{35,67},{67,35},{3... | collective-permute-start | bytes 1769480 | tf_op jit(solution)/shard_map/ppermute | solution.py:325
  112.7 24.2 %collective-permute-start.16 = (bf16[2,192,768]{2,1,0:T(8,128)(2,1)}, bf16[2,192,768]{2,1,0:T(8,128)(2,1)S(1)}, u32[]{:S(2)}, u32[]{:S(2)}) collective-permute-start(bf16[2,192,768]{2,1,0:T(8,128)(2,1)} %get-tuple-element.80), channel_id=1, source_target_pairs={{0,32},{32,0},{1,33},{33,1},{2,34},{34,2},{3,35},{35,3},{4,36},{36... | collective-permute-start | bytes 1769480 | tf_op jit(solution)/shard_map/ppermute | solution.py:326
  118.3 23.8 %collective-permute-start.11 = (bf16[192,1536]{1,0:T(8,128)(2,1)}, bf16[192,1536]{1,0:T(8,128)(2,1)S(1)}, u32[]{:S(2)}, u32[]{:S(2)}) collective-permute-start(bf16[192,1536]{1,0:T(8,128)(2,1)} %get-tuple-element.71), channel_id=1, source_target_pairs={{0,3},{1,0},{2,1},{3,2},{4,7},{5,4},{6,5},{7,6},{8,11},{9,8},{10,9... | collective-permute-start | bytes 1769480 | tf_op jit(solution)/shard_map/ppermute | solution.py:276
  119.2 24.4 %collective-permute-start.12 = (bf16[192,1536]{1,0:T(8,128)(2,1)}, bf16[192,1536]{1,0:T(8,128)(2,1)}, u32[]{:S(2)}, u32[]{:S(2)}) collective-permute-start(bf16[192,1536]{1,0:T(8,128)(2,1)} %get-tuple-element.72), channel_id=1, source_target_pairs={{0,2},{1,3},{2,0},{3,1},{4,6},{5,7},{6,4},{7,5},{8,10},{9,11},{10,... | collective-permute-start | bytes 1769480 | tf_op jit(solution)/shard_map/ppermute | solution.py:276
  123.6 26.4 %collective-permute-start.13 = (bf16[192,1536]{1,0:T(8,128)(2,1)}, bf16[192,1536]{1,0:T(8,128)(2,1)}, u32[]{:S(2)}, u32[]{:S(2)}) collective-permute-start(bf16[192,1536]{1,0:T(8,128)(2,1)} %get-tuple-element.73), channel_id=1, source_target_pairs={{0,1},{1,2},{2,3},{3,0},{4,5},{5,6},{6,7},{7,4},{8,9},{9,10},{10,1... | collective-permute-start | bytes 1769480 | tf_op jit(solution)/shard_map/ppermute | solution.py:276
  126.7 25.6 %all-to-all-start.2 = ((bf16[8,48,768]{2,1,0:T(8,128)(2,1)}), bf16[8,48,768]{2,1,0:T(8,128)(2,1)S(1)}, u32[]{:S(2)}, u32[]{:S(2)}) async-start(bf16[8,48,768]{2,1,0:T(8,128)(2,1)} %bitcast.12), calls=%async_computation.2 | async-start | bytes 1179648 | tf_op jit(solution)/shard_map/all_to_all | solution.py:280
  136.5 18.1 %collective-permute-start.17 = (bf16[2,192,768]{2,1,0:T(8,128)(2,1)}, bf16[2,192,768]{2,1,0:T(8,128)(2,1)}, u32[]{:S(2)}, u32[]{:S(2)}) collective-permute-start(bf16[2,192,768]{2,1,0:T(8,128)(2,1)} %get-tuple-element.82), channel_id=1, source_target_pairs={{0,128},{128,0},{1,129},{129,1},{2,130},{130,2},{3,131},{131,3},{4... | collective-permute-start | bytes 1769480 | tf_op jit(solution)/shard_map/ppermute | solution.py:324
  136.9 22.0 %collective-permute-start.18 = (bf16[2,192,768]{2,1,0:T(8,128)(2,1)}, bf16[2,192,768]{2,1,0:T(8,128)(2,1)}, u32[]{:S(2)}, u32[]{:S(2)}) collective-permute-start(bf16[2,192,768]{2,1,0:T(8,128)(2,1)} %get-tuple-element.83), channel_id=1, source_target_pairs={{32,64},{64,32},{33,65},{65,33},{34,66},{66,34},{35,67},{67,35},{3... | collective-permute-start | bytes 1769480 | tf_op jit(solution)/shard_map/ppermute | solution.py:325
  142.1 16.9 %collective-permute-start.19 = (bf16[2,192,768]{2,1,0:T(8,128)(2,1)}, bf16[2,192,768]{2,1,0:T(8,128)(2,1)S(1)}, u32[]{:S(2)}, u32[]{:S(2)}) collective-permute-start(bf16[2,192,768]{2,1,0:T(8,128)(2,1)} %get-tuple-element.84), channel_id=1, source_target_pairs={{0,32},{32,0},{1,33},{33,1},{2,34},{34,2},{3,35},{35,3},{4,36},{36... | collective-permute-start | bytes 1769480 | tf_op jit(solution)/shard_map/ppermute | solution.py:326
  152.4 9.6 %collective-permute-start.22 = (bf16[48,768]{1,0:T(8,128)(2,1)S(1)}, bf16[48,768]{1,0:T(8,128)(2,1)S(1)}, u32[]{:S(2)}, u32[]{:S(2)}) collective-permute-start(bf16[48,768]{1,0:T(8,128)(2,1)S(1)} %reduce_sum.12), channel_id=1, source_target_pairs={{0,192},{64,128},{128,64},{192,0},{1,193},{65,129},{129,65},{193,1... | collective-permute-start | bytes 221192 | tf_op jit(solution)/shard_map/ppermute | solution.py:347
  (22 other events, 123.1 us)

commit v8 on v6

--- a/solution.py
+++ b/solution.py
@@ -154,28 +154,25 @@
     )(scalars, q, *kvs, att, d, probs)
 
 
-def panel_kernel(scalar_ref, weight_ref, after_ref, out_ref):
+def panel_kernel(scalar_ref, weight_ref, out_ref):
     for k in range(out_ref.shape[0]):
         out_ref[k] = weight_ref[0]
 
 
-def panel_copies(scalars, out_weight, copies, after):
+def panel_copies(scalars, out_weight, copies):
     half = out_weight.shape[2] // 2
     return pl.pallas_call(
         panel_kernel,
         grid_spec=pltpu.PrefetchScalarGridSpec(
             num_scalar_prefetch=1,
             grid=(1,),
-            in_specs=[
-                pl.BlockSpec((1, ROWS, half), lambda i, b: (b[3], 0, b[1])),
-                pl.BlockSpec(memory_space=pl.ANY),
-            ],
+            in_specs=[pl.BlockSpec((1, ROWS, half), lambda i, b: (b[3], 0, b[1]))],
             out_specs=whole((copies, ROWS, half)),
         ),
         out_shape=jax.ShapeDtypeStruct((copies, ROWS, half), BF16),
         compiler_params=PARAMS,
         cost_estimate=LIGHT,
-    )(scalars, out_weight, after)
+    )(scalars, out_weight)
 
 
 def source(scalar_ref, k):
@@ -305,7 +302,7 @@
     from_cross = lax.ppermute(kv, ("xh", "co"), CROSS)
     from_core = lax.ppermute(kv, "co", SWAP)
 
-    panels = panel_copies(scalars, out_weight, nz, from_core)
+    panels = panel_copies(scalars, out_weight, nz)
     w_mine = swapped(panels, "z").reshape(nz * rows, half)
     ups = [up] + [shifted(up, "y", k) for k in (1, 2, 3)]
     w_mate = lax.ppermute(w_mine, "co", SWAP)
@@ -331,14 +328,13 @@
         return gq, own, terms
 
     gq_0, own_0, terms_0 = backward(0)
-    atts, gq_0 = lax.optimization_barrier((atts, gq_0))
+    gq_1, own_1, terms_1 = backward(1)
+    atts, gq_0, gq_1 = lax.optimization_barrier((atts, gq_0, gq_1))
     grad_mine, grad_mate = weight_gradient(scalars, atts, ups)
     from_mate = lax.ppermute(grad_mate, "co", SWAP)
-    atts, w_rows, grad_mine = lax.optimization_barrier((atts, w_rows, grad_mine))
+    grad = (grad_mine.astype(F32) + from_mate.astype(F32)).astype(BF16).reshape(nz, rows, half)
+    atts, w_rows, grad = lax.optimization_barrier((atts, w_rows, grad))
     mixed = mixed_parts(scalars, atts, w_rows)
-    grad = (grad_mine.astype(F32) + from_mate.astype(F32)).astype(BF16).reshape(nz, rows, half)
-    probs, grad, mixed = lax.optimization_barrier((probs, grad, mixed))
-    gq_1, own_1, terms_1 = backward(1)
     gkv_parts = [
         own.astype(F32) + sum(t.astype(F32) for t in terms)
         for own, terms in ((own_0, terms_0), (own_1, terms_1))

time: 153 us -> 157 us (1.026)
  starting transfers between devices: 61 us -> 69.8 us
  waiting for transfers between devices: 38.3 us -> 32.8 us
  other arithmetic: 8.61 us -> 10.5 us
    all_to_all x4, waiting for transfers between devices: 9.71 us -> 3.6 us  [swapped(): return lax.all_to_all(x, axis, split_axis=0, concat_axis=0, tiled=True)]
    all_to_all x4, starting transfers between devices: 20.5 us -> 26.5 us  [swapped(): return lax.all_to_all(x, axis, split_axis=0, concat_axis=0, tiled=True)]
    ppermute x1, waiting for transfers between devices: 4.82 us -> 0.01 us  [per_device(): from_time = lax.ppermute(kv, 'xl', SWAP)]
    ppermute x2, waiting for transfers between devices: 5.1 us -> 8.92 us  [backward(): lax.ppermute(to_cross, ('xh', 'co'), CROSS)]
    ppermute x1, starting transfers between devices: 3.33 us -> 0.09 us  [per_device(): from_core = lax.ppermute(kv, 'co', SWAP)]
    ppermute x6, starting transfers between devices: 6.14 us -> 8.92 us  [shifted(): return lax.ppermute(x, axis, [(i, (i + by) % count) for i in range(count)])]
    ppermute x2, waiting for transfers between devices: 2.6 us -> 0.01 us  [backward(): lax.ppermute(to_time, 'xl', SWAP)]
    ppermute x1, starting transfers between devices: 0.46 us -> 2.94 us  [per_device(): x_far = lax.ppermute(over_z, 'xh', SWAP)]
  transfers between devices with their start and end apart: 25 -> 25, of which waited for: 10 -> 14; matrix products, arithmetic and copies ran while one was open for 5% -> 6% of each run, Pallas kernels for 20% -> 20%
where the time goes in v8:
time: 157 us; the launch traced here: 156 us
  starting transfers between devices  69.8 us (44%)
  Pallas kernels  38.5 us (25%)
  waiting for transfers between devices  32.8 us (21%)
  other arithmetic  10.5 us (7%)
  local copies, waits for them, and re-layouts  3.11 us (2%)
    all_to_all x4, starting transfers between devices, swapped(): return lax.all_to_all(x, axis, split_axis=0, concat_axis=0, tiled=True)  26.5 us
    ppermute x6, waiting for transfers between devices, shifted(): return lax.ppermute(x, axis, [(i, (i + by) % count) for i in range(count)])  16.5 us
    pallas_call x2, Pallas kernels, attention_backward(): pl.pallas_call(backward_kernel, grid_spec=pltpu.PrefetchScalarGridSpec(nu...  12.4 us
    ppermute x1, starting transfers between devices, per_device(): w_mate = lax.ppermute(w_mine, 'co', SWAP)  11.4 us
    ppermute x2, starting transfers between devices, backward(): lax.ppermute(to_cross, ('xh', 'co'), CROSS)  9.06 us
    ppermute x6, starting transfers between devices, shifted(): return lax.ppermute(x, axis, [(i, (i + by) % count) for i in range(count)])  8.92 us
    ppermute x2, waiting for transfers between devices, backward(): lax.ppermute(to_cross, ('xh', 'co'), CROSS)  8.92 us
    pallas_call x1, Pallas kernels, attention_forward(): pl.pallas_call(forward_kernel, grid_spec=pltpu.PrefetchScalarGridSpec(num...  8.09 us
  transfers between devices with their start and end apart: 25, of which 14 were waited for; matrix products, arithmetic and copies ran while one was open for 6% of the time, Pallas kernels for 20%

profile of v8, /device:TPU:1, one launch (start us, length us, event | category | flops | bytes accessed | tf_op | source)
XLA Modules:
  0.0 156.3 jit_solution(9063953441547947386)
XLA Ops:
  1.8 2.4 %shard_map.85 = bf16[8,48,768]{2,1,0:T(8,128)(2,1)} custom-call(s32[4]{0:T(128)} %pad_add_fusion.scalar_ref, bf16[32,48,1536]{2,1,0:T(8,128)(2,1)} %weight_ref.1), custom_call_target="tpu_custom_call" | custom-call | flops 1000 | bytes 1000 | tf_op jit(solution)/shard_map/pallas_call | solution.py:164
  4.2 9.1 %all-to-all-start.1 = ((bf16[8,48,768]{2,1,0:T(8,128)(2,1)}), bf16[8,48,768]{2,1,0:T(8,128)(2,1)}, u32[]{:S(2)}, u32[]{:S(2)}) async-start(bf16[8,48,768]{2,1,0:T(8,128)(2,1)} %shard_map.85), calls=%async_computation.1 | async-start | bytes 1179648 | tf_op jit(solution)/shard_map/all_to_all | solution.py:281
  13.4 2.7 %collective-permute-start.5 = (bf16[192,1536]{1,0:T(8,128)(2,1)}, bf16[192,1536]{1,0:T(8,128)(2,1)S(1)}, u32[]{:S(2)}, u32[]{:S(2)}) collective-permute-start(bf16[192,1536]{1,0:T(8,128)(2,1)} %bitcast.6.refs_0_.refs_4_), channel_id=1, source_target_pairs={{0,3},{1,0},{2,1},{3,2},{4,7},{5,4},{6,5},{7,6},{8,11},{9,8},{10,9... | collective-permute-start | bytes 1769480 | tf_op jit(solution)/shard_map/ppermute | solution.py:277
  17.2 6.3 %collective-permute-start.2 = (bf16[2,192,1536]{2,1,0:T(8,128)(2,1)S(1)}, bf16[2,192,1536]{2,1,0:T(8,128)(2,1)S(1)}, u32[]{:S(2)}, u32[]{:S(2)}) collective-permute-start(bf16[2,192,1536]{2,1,0:T(8,128)(2,1)S(1)} %bitcast.21), channel_id=1, source_target_pairs={{32,64},{64,32},{33,65},{65,33},{34,66},{66,34},{35,67},{67,35},{3... | collective-permute-start | bytes 3538952 | tf_op jit(solution)/shard_map/ppermute | solution.py:302
  23.6 5.6 %collective-permute-done.5.refs_3_.refs_7_ = bf16[192,1536]{1,0:T(8,128)(2,1)S(1)} collective-permute-done((bf16[192,1536]{1,0:T(8,128)(2,1)}, bf16[192,1536]{1,0:T(8,128)(2,1)S(1)}, u32[]{:S(2)}, u32[]{:S(2)}) %collective-permute-start.5) | collective-permute-done | bytes 589856 | tf_op jit(solution)/shard_map/ppermute | solution.py:277
  32.9 11.4 %collective-permute-start.6 = (bf16[384,768]{1,0:T(8,128)(2,1)}, bf16[384,768]{1,0:T(8,128)(2,1)S(1)}, u32[]{:S(2)}, u32[]{:S(2)}) collective-permute-start(bf16[384,768]{1,0:T(8,128)(2,1)} %bitcast.7.refs_4_), channel_id=1, source_target_pairs={{0,32},{32,0},{1,33},{33,1},{2,34},{34,2},{3,35},{35,3},{4,36},{36... | collective-permute-start | bytes 1769480 | tf_op jit(solution)/shard_map/ppermute | solution.py:308
  46.9 5.0 %shard_map.86 = (bf16[4,384,256]{2,1,0:T(8,128)(2,1)}, bf16[384,1536]{1,0:T(8,128)(2,1)}) custom-call(s32[4]{0:T(128)} %pad_add_fusion.scalar_ref, bf16[192,1536]{1,0:T(8,128)(2,1)} %bitcast.6.refs_0_.refs_4_, bf16[192,1536]{1,0:T(8,128)(2,1)} %collective-permute-done.3.refs_1_.refs_5_, bf16[192,1536]{1,0:T(8,128)(2,1)} %collective-permute-done.4.refs_2_.refs_6_, ...), custom_call_target="tpu_custom_call" | custom-call | flops 1000 | bytes 1000 | tf_op jit(solution)/shard_map/pallas_call | solution.py:198
  51.8 4.6 %all-to-all-start.2 = ((bf16[4,384,256]{2,1,0:T(8,128)(2,1)}), bf16[4,384,256]{2,1,0:T(8,128)(2,1)}, u32[]{:S(2)}, u32[]{:S(2)}) async-start(bf16[4,384,256]{2,1,0:T(8,128)(2,1)} %get-tuple-element.33), calls=%async_computation.2 | async-start | bytes 1572864 | tf_op jit(solution)/shard_map/all_to_all | solution.py:281
  57.8 8.1 %shard_map.84 = (bf16[192,1536]{1,0:T(8,128)(2,1)}, bf16[4,8,48,256]{3,2,1,0:T(8,128)(2,1)}, bf16[12,192,768]{2,1,0:T(8,128)(2,1)}) custom-call(s32[4]{0:T(128)} %pad_add_fusion.scalar_ref, bf16[192,1536]{1,0:T(8,128)(2,1)} %bitcast.24, bf16[2,192,1536]{2,1,0:T(8,128)(2,1)} %bitcast.18, bf16[2,192,1536]{2,1,0:T(8,128)(2,1)} %collective-permute-done.time_ref, ...), custom_call_target="tpu_custom_call" | custom-call | flops 1000 | bytes 1000 | tf_op jit(solution)/shard_map/pallas_call | solution.py:122
  65.9 2.3 %all-to-all-done.2 = bf16[4,384,256]{2,1,0:T(8,128)(2,1)} async-done(((bf16[4,384,256]{2,1,0:T(8,128)(2,1)}), bf16[4,384,256]{2,1,0:T(8,128)(2,1)}, u32[]{:S(2)}, u32[]{:S(2)}) %all-to-all-start.2) | async-done | bytes 786464 | tf_op jit(solution)/shard_map/all_to_all | solution.py:281
  68.2 5.9 %all-to-all-start = ((bf16[4,384,256]{2,1,0:T(8,128)(2,1)}), bf16[4,384,256]{2,1,0:T(8,128)(2,1)S(1)}, u32[]{:S(2)}, u32[]{:S(2)}) async-start(bf16[4,384,256]{2,1,0:T(8,128)(2,1)} %bitcast.27), calls=%async_computation | async-start | bytes 1572864 | tf_op jit(solution)/shard_map/all_to_all | solution.py:281
  74.1 6.2 %shard_map.88 = (bf16[192,768]{1,0:T(8,128)(2,1)}, bf16[2,192,768]{2,1,0:T(8,128)(2,1)}, bf16[2,192,768]{2,1,0:T(8,128)(2,1)}, bf16[2,192,768]{2,1,0:T(8,128)(2,1)}, bf16[2,192,768]{2,1,0:T(8,128)(2,1)}) custom-call(s32[4]{0:T(128)} %pad_add_fusion.scalar_ref, bf16[192,1536]{1,0:T(8,128)(2,1)} %bitcast.25, bf16[2,192,1536]{2,1,0:T(8,128)(2,1)} %bitcast.19, ...), custom_call_target="tpu_custom_call" | custom-call | flops 1000 | bytes 1000 | tf_op jit(solution)/shard_map/pallas_call | solution.py:142
  80.3 6.2 %shard_map.87 = (bf16[192,768]{1,0:T(8,128)(2,1)}, bf16[2,192,768]{2,1,0:T(8,128)(2,1)}, bf16[2,192,768]{2,1,0:T(8,128)(2,1)}, bf16[2,192,768]{2,1,0:T(8,128)(2,1)}, bf16[2,192,768]{2,1,0:T(8,128)(2,1)}) custom-call(s32[4]{0:T(128)} %pad_add_fusion.scalar_ref, bf16[192,1536]{1,0:T(8,128)(2,1)} %bitcast.26, bf16[2,192,1536]{2,1,0:T(8,128)(2,1)} %bitcast.20, ...), custom_call_target="tpu_custom_call" | custom-call | flops 1000 | bytes 1000 | tf_op jit(solution)/shard_map/pallas_call | solution.py:142
  87.4 5.6 %shard_map.89 = (bf16[384,768]{1,0:T(8,128)(2,1)}, bf16[384,768]{1,0:T(8,128)(2,1)}) custom-call(s32[4]{0:T(128)} %pad_add_fusion.scalar_ref, bf16[4,384,256]{2,1,0:T(8,128)(2,1)} %copy-done.3, bf16[192,1536]{1,0:T(8,128)(2,1)} %bitcast.6.refs_0_.refs_4_, bf16[192,1536]{1,0:T(8,128)(2,1)} %collective-permute-done.3.refs_1_.refs_5_, ...), custom_call_target="tpu_custom_call" | custom-call | flops 1000 | bytes 1000 | tf_op jit(solution)/shard_map/pallas_call | solution.py:233
  98.0 6.9 %all-to-all-start.3 = ((bf16[8,48,768]{2,1,0:T(8,128)(2,1)}), bf16[8,48,768]{2,1,0:T(8,128)(2,1)S(1)}, u32[]{:S(2)}, u32[]{:S(2)}) async-start(bf16[8,48,768]{2,1,0:T(8,128)(2,1)} %bitcast.9), calls=%async_computation.3 | async-start | bytes 1179648 | tf_op jit(solution)/shard_map/all_to_all | solution.py:281
  104.9 3.3 %collective-permute-start.15 = (bf16[2,192,768]{2,1,0:T(8,128)(2,1)}, bf16[2,192,768]{2,1,0:T(8,128)(2,1)S(1)}, u32[]{:S(2)}, u32[]{:S(2)}) collective-permute-start(bf16[2,192,768]{2,1,0:T(8,128)(2,1)} %get-tuple-element.55), channel_id=1, source_target_pairs={{32,64},{64,32},{33,65},{65,33},{34,66},{66,34},{35,67},{67,35},{3... | collective-permute-start | bytes 1769480 | tf_op jit(solution)/shard_map/ppermute | solution.py:325
  108.6 5.7 %collective-permute-start.12 = (bf16[2,192,768]{2,1,0:T(8,128)(2,1)}, bf16[2,192,768]{2,1,0:T(8,128)(2,1)}, u32[]{:S(2)}, u32[]{:S(2)}) collective-permute-start(bf16[2,192,768]{2,1,0:T(8,128)(2,1)} %get-tuple-element.51), channel_id=1, source_target_pairs={{32,64},{64,32},{33,65},{65,33},{34,66},{66,34},{35,67},{67,35},{3... | collective-permute-start | bytes 1769480 | tf_op jit(solution)/shard_map/ppermute | solution.py:325
  115.4 5.1 %shard_map.90 = (bf16[192,1536]{1,0:T(8,128)(2,1)}, bf16[192,1536]{1,0:T(8,128)(2,1)}, bf16[192,1536]{1,0:T(8,128)(2,1)}, bf16[192,1536]{1,0:T(8,128)(2,1)}) custom-call(s32[4]{0:T(128)} %pad_add_fusion.scalar_ref, bf16[4,384,256]{2,1,0:T(8,128)(2,1)} %copy-done.3, bf16[384,1536]{1,0:T(8,128)(2,1)} %get-tuple-element.42.weight_ref), custom_call_target="tpu_custom_call" | custom-call | flops 1000 | bytes 1000 | tf_op jit(solution)/shard_map/pallas_call | solution.py:257
  120.5 2.2 %collective-permute-done.15 = bf16[2,192,768]{2,1,0:T(8,128)(2,1)S(1)} collective-permute-done((bf16[2,192,768]{2,1,0:T(8,128)(2,1)}, bf16[2,192,768]{2,1,0:T(8,128)(2,1)S(1)}, u32[]{:S(2)}, u32[]{:S(2)}) %collective-permute-start.15) | collective-permute-done | bytes 589856 | tf_op jit(solution)/shard_map/ppermute | solution.py:325
  122.7 2.9 %collective-permute-start.8 = (bf16[192,1536]{1,0:T(8,128)(2,1)}, bf16[192,1536]{1,0:T(8,128)(2,1)S(1)}, u32[]{:S(2)}, u32[]{:S(2)}) collective-permute-start(bf16[192,1536]{1,0:T(8,128)(2,1)} %get-tuple-element.44), channel_id=1, source_target_pairs={{0,3},{1,0},{2,1},{3,2},{4,7},{5,4},{6,5},{7,6},{8,11},{9,8},{10,9... | collective-permute-start | bytes 1769480 | tf_op jit(solution)/shard_map/ppermute | solution.py:277
  130.3 6.7 %collective-permute-done.12 = bf16[2,192,768]{2,1,0:T(8,128)(2,1)} collective-permute-done((bf16[2,192,768]{2,1,0:T(8,128)(2,1)}, bf16[2,192,768]{2,1,0:T(8,128)(2,1)}, u32[]{:S(2)}, u32[]{:S(2)}) %collective-permute-start.12) | collective-permute-done | bytes 589856 | tf_op jit(solution)/shard_map/ppermute | solution.py:325
  138.7 2.9 %collective-permute-start.18 = (bf16[48,768]{1,0:T(8,128)(2,1)S(1)}, bf16[48,768]{1,0:T(8,128)(2,1)S(1)}, u32[]{:S(2)}, u32[]{:S(2)}) collective-permute-start(bf16[48,768]{1,0:T(8,128)(2,1)S(1)} %copy-done.12), channel_id=1, source_target_pairs={{0,64},{64,0},{1,65},{65,1},{2,66},{66,2},{3,67},{67,3},{4,68},{68... | collective-permute-start | bytes 221192 | tf_op jit(solution)/shard_map/ppermute | solution.py:345
  146.3 4.2 %collective-permute-done.8 = bf16[192,1536]{1,0:T(8,128)(2,1)S(1)} collective-permute-done((bf16[192,1536]{1,0:T(8,128)(2,1)}, bf16[192,1536]{1,0:T(8,128)(2,1)S(1)}, u32[]{:S(2)}, u32[]{:S(2)}) %collective-permute-start.8) | collective-permute-done | bytes 589856 | tf_op jit(solution)/shard_map/ppermute | solution.py:277
  150.5 3.9 %collective-permute-done.10 = bf16[192,1536]{1,0:T(8,128)(2,1)S(1)} collective-permute-done((bf16[192,1536]{1,0:T(8,128)(2,1)}, bf16[192,1536]{1,0:T(8,128)(2,1)S(1)}, u32[]{:S(2)}, u32[]{:S(2)}) %collective-permute-start.10) | collective-permute-done | bytes 589856 | tf_op jit(solution)/shard_map/ppermute | solution.py:277
  (74 shorter events, 29.5 us)
Async XLA Ops:
  4.2 28.6 %all-to-all-start.1 = ((bf16[8,48,768]{2,1,0:T(8,128)(2,1)}), bf16[8,48,768]{2,1,0:T(8,128)(2,1)}, u32[]{:S(2)}, u32[]{:S(2)}) async-start(bf16[8,48,768]{2,1,0:T(8,128)(2,1)} %shard_map.85), calls=%async_computation.1 | async-start | bytes 1179648 | tf_op jit(solution)/shard_map/all_to_all | solution.py:281
  13.4 15.8 %collective-permute-start.5 = (bf16[192,1536]{1,0:T(8,128)(2,1)}, bf16[192,1536]{1,0:T(8,128)(2,1)S(1)}, u32[]{:S(2)}, u32[]{:S(2)}) collective-permute-start(bf16[192,1536]{1,0:T(8,128)(2,1)} %bitcast.6.refs_0_.refs_4_), channel_id=1, source_target_pairs={{0,3},{1,0},{2,1},{3,2},{4,7},{5,4},{6,5},{7,6},{8,11},{9,8},{10,9... | collective-permute-start | bytes 1769480 | tf_op jit(solution)/shard_map/ppermute | solution.py:277
  16.1 15.5 %collective-permute-start.4 = (bf16[192,1536]{1,0:T(8,128)(2,1)}, bf16[192,1536]{1,0:T(8,128)(2,1)}, u32[]{:S(2)}, u32[]{:S(2)}) collective-permute-start(bf16[192,1536]{1,0:T(8,128)(2,1)} %bitcast.6.refs_0_.refs_4_), channel_id=1, source_target_pairs={{0,2},{1,3},{2,0},{3,1},{4,6},{5,7},{6,4},{7,5},{8,10},{9,11},{10,... | collective-permute-start | bytes 1769480 | tf_op jit(solution)/shard_map/ppermute | solution.py:277
  16.5 29.4 %collective-permute-start.3 = (bf16[192,1536]{1,0:T(8,128)(2,1)}, bf16[192,1536]{1,0:T(8,128)(2,1)}, u32[]{:S(2)}, u32[]{:S(2)}) collective-permute-start(bf16[192,1536]{1,0:T(8,128)(2,1)} %bitcast.6.refs_0_.refs_4_), channel_id=1, source_target_pairs={{0,1},{1,2},{2,3},{3,0},{4,5},{5,6},{6,7},{7,4},{8,9},{9,10},{10,1... | collective-permute-start | bytes 1769480 | tf_op jit(solution)/shard_map/ppermute | solution.py:277
  17.2 39.2 %collective-permute-start.2 = (bf16[2,192,1536]{2,1,0:T(8,128)(2,1)S(1)}, bf16[2,192,1536]{2,1,0:T(8,128)(2,1)S(1)}, u32[]{:S(2)}, u32[]{:S(2)}) collective-permute-start(bf16[2,192,1536]{2,1,0:T(8,128)(2,1)S(1)} %bitcast.21), channel_id=1, source_target_pairs={{32,64},{64,32},{33,65},{65,33},{34,66},{66,34},{35,67},{67,35},{3... | collective-permute-start | bytes 3538952 | tf_op jit(solution)/shard_map/ppermute | solution.py:302
  23.5 32.9 %collective-permute-start.1 = (bf16[2,192,1536]{2,1,0:T(8,128)(2,1)S(1)}, bf16[2,192,1536]{2,1,0:T(8,128)(2,1)S(1)}, u32[]{:S(2)}, u32[]{:S(2)}) collective-permute-start(bf16[2,192,1536]{2,1,0:T(8,128)(2,1)S(1)} %bitcast.22), channel_id=1, source_target_pairs={{0,32},{32,0},{1,33},{33,1},{2,34},{34,2},{3,35},{35,3},{4,36},{36... | collective-permute-start | bytes 3538952 | tf_op jit(solution)/shard_map/ppermute | solution.py:303
  29.2 27.3 %collective-permute-start = (bf16[2,192,1536]{2,1,0:T(8,128)(2,1)S(1)}, bf16[2,192,1536]{2,1,0:T(8,128)(2,1)}, u32[]{:S(2)}, u32[]{:S(2)}) collective-permute-start(bf16[2,192,1536]{2,1,0:T(8,128)(2,1)S(1)} %bitcast.23), channel_id=1, source_target_pairs={{0,128},{128,0},{1,129},{129,1},{2,130},{130,2},{3,131},{131,3},{4... | collective-permute-start | bytes 3538952 | tf_op jit(solution)/shard_map/ppermute | solution.py:301
  32.9 13.2 %collective-permute-start.6 = (bf16[384,768]{1,0:T(8,128)(2,1)}, bf16[384,768]{1,0:T(8,128)(2,1)S(1)}, u32[]{:S(2)}, u32[]{:S(2)}) collective-permute-start(bf16[384,768]{1,0:T(8,128)(2,1)} %bitcast.7.refs_4_), channel_id=1, source_target_pairs={{0,32},{32,0},{1,33},{33,1},{2,34},{34,2},{3,35},{35,3},{4,36},{36... | collective-permute-start | bytes 1769480 | tf_op jit(solution)/shard_map/ppermute | solution.py:308
  51.8 16.4 %all-to-all-start.2 = ((bf16[4,384,256]{2,1,0:T(8,128)(2,1)}), bf16[4,384,256]{2,1,0:T(8,128)(2,1)}, u32[]{:S(2)}, u32[]{:S(2)}) async-start(bf16[4,384,256]{2,1,0:T(8,128)(2,1)} %get-tuple-element.33), calls=%async_computation.2 | async-start | bytes 1572864 | tf_op jit(solution)/shard_map/all_to_all | solution.py:281
  68.2 18.3 %all-to-all-start = ((bf16[4,384,256]{2,1,0:T(8,128)(2,1)}), bf16[4,384,256]{2,1,0:T(8,128)(2,1)S(1)}, u32[]{:S(2)}, u32[]{:S(2)}) async-start(bf16[4,384,256]{2,1,0:T(8,128)(2,1)} %bitcast.27), calls=%async_computation | async-start | bytes 1572864 | tf_op jit(solution)/shard_map/all_to_all | solution.py:281
  94.1 20.3 %collective-permute-start.14 = (bf16[2,192,768]{2,1,0:T(8,128)(2,1)}, bf16[2,192,768]{2,1,0:T(8,128)(2,1)S(1)}, u32[]{:S(2)}, u32[]{:S(2)}) collective-permute-start(bf16[2,192,768]{2,1,0:T(8,128)(2,1)} %get-tuple-element.54), channel_id=1, source_target_pairs={{0,128},{128,0},{1,129},{129,1},{2,130},{130,2},{3,131},{131,3},{4... | collective-permute-start | bytes 1769480 | tf_op jit(solution)/shard_map/ppermute | solution.py:324
  98.0 30.5 %all-to-all-start.3 = ((bf16[8,48,768]{2,1,0:T(8,128)(2,1)}), bf16[8,48,768]{2,1,0:T(8,128)(2,1)S(1)}, u32[]{:S(2)}, u32[]{:S(2)}) async-start(bf16[8,48,768]{2,1,0:T(8,128)(2,1)} %bitcast.9), calls=%async_computation.3 | async-start | bytes 1179648 | tf_op jit(solution)/shard_map/all_to_all | solution.py:281
  104.9 17.8 %collective-permute-start.15 = (bf16[2,192,768]{2,1,0:T(8,128)(2,1)}, bf16[2,192,768]{2,1,0:T(8,128)(2,1)S(1)}, u32[]{:S(2)}, u32[]{:S(2)}) collective-permute-start(bf16[2,192,768]{2,1,0:T(8,128)(2,1)} %get-tuple-element.55), channel_id=1, source_target_pairs={{32,64},{64,32},{33,65},{65,33},{34,66},{66,34},{35,67},{67,35},{3... | collective-permute-start | bytes 1769480 | tf_op jit(solution)/shard_map/ppermute | solution.py:325
  108.3 17.4 %collective-permute-start.16 = (bf16[2,192,768]{2,1,0:T(8,128)(2,1)}, bf16[2,192,768]{2,1,0:T(8,128)(2,1)S(1)}, u32[]{:S(2)}, u32[]{:S(2)}) collective-permute-start(bf16[2,192,768]{2,1,0:T(8,128)(2,1)} %get-tuple-element.56), channel_id=1, source_target_pairs={{0,32},{32,0},{1,33},{33,1},{2,34},{34,2},{3,35},{35,3},{4,36},{36... | collective-permute-start | bytes 1769480 | tf_op jit(solution)/shard_map/ppermute | solution.py:326
  108.4 20.9 %collective-permute-start.11 = (bf16[2,192,768]{2,1,0:T(8,128)(2,1)}, bf16[2,192,768]{2,1,0:T(8,128)(2,1)S(1)}, u32[]{:S(2)}, u32[]{:S(2)}) collective-permute-start(bf16[2,192,768]{2,1,0:T(8,128)(2,1)} %get-tuple-element.50), channel_id=1, source_target_pairs={{0,128},{128,0},{1,129},{129,1},{2,130},{130,2},{3,131},{131,3},{4... | collective-permute-start | bytes 1769480 | tf_op jit(solution)/shard_map/ppermute | solution.py:324
  108.6 28.4 %collective-permute-start.12 = (bf16[2,192,768]{2,1,0:T(8,128)(2,1)}, bf16[2,192,768]{2,1,0:T(8,128)(2,1)}, u32[]{:S(2)}, u32[]{:S(2)}) collective-permute-start(bf16[2,192,768]{2,1,0:T(8,128)(2,1)} %get-tuple-element.51), channel_id=1, source_target_pairs={{32,64},{64,32},{33,65},{65,33},{34,66},{66,34},{35,67},{67,35},{3... | collective-permute-start | bytes 1769480 | tf_op jit(solution)/shard_map/ppermute | solution.py:325
  114.4 22.7 %collective-permute-start.13 = (bf16[2,192,768]{2,1,0:T(8,128)(2,1)}, bf16[2,192,768]{2,1,0:T(8,128)(2,1)}, u32[]{:S(2)}, u32[]{:S(2)}) collective-permute-start(bf16[2,192,768]{2,1,0:T(8,128)(2,1)} %get-tuple-element.52), channel_id=1, source_target_pairs={{0,32},{32,0},{1,33},{33,1},{2,34},{34,2},{3,35},{35,3},{4,36},{36... | collective-permute-start | bytes 1769480 | tf_op jit(solution)/shard_map/ppermute | solution.py:326
  122.7 27.9 %collective-permute-start.8 = (bf16[192,1536]{1,0:T(8,128)(2,1)}, bf16[192,1536]{1,0:T(8,128)(2,1)S(1)}, u32[]{:S(2)}, u32[]{:S(2)}) collective-permute-start(bf16[192,1536]{1,0:T(8,128)(2,1)} %get-tuple-element.44), channel_id=1, source_target_pairs={{0,3},{1,0},{2,1},{3,2},{4,7},{5,4},{6,5},{7,6},{8,11},{9,8},{10,9... | collective-permute-start | bytes 1769480 | tf_op jit(solution)/shard_map/ppermute | solution.py:277
  125.6 24.9 %collective-permute-start.9 = (bf16[192,1536]{1,0:T(8,128)(2,1)}, bf16[192,1536]{1,0:T(8,128)(2,1)S(1)}, u32[]{:S(2)}, u32[]{:S(2)}) collective-permute-start(bf16[192,1536]{1,0:T(8,128)(2,1)} %get-tuple-element.45), channel_id=1, source_target_pairs={{0,2},{1,3},{2,0},{3,1},{4,6},{5,7},{6,4},{7,5},{8,10},{9,11},{10,... | collective-permute-start | bytes 1769480 | tf_op jit(solution)/shard_map/ppermute | solution.py:277
  129.2 25.2 %collective-permute-start.10 = (bf16[192,1536]{1,0:T(8,128)(2,1)}, bf16[192,1536]{1,0:T(8,128)(2,1)S(1)}, u32[]{:S(2)}, u32[]{:S(2)}) collective-permute-start(bf16[192,1536]{1,0:T(8,128)(2,1)} %get-tuple-element.46), channel_id=1, source_target_pairs={{0,1},{1,2},{2,3},{3,0},{4,5},{5,6},{6,7},{7,4},{8,9},{9,10},{10,1... | collective-permute-start | bytes 1769480 | tf_op jit(solution)/shard_map/ppermute | solution.py:277
  137.1 4.9 %collective-permute-start.19 = (bf16[48,768]{1,0:T(8,128)(2,1)}, bf16[48,768]{1,0:T(8,128)(2,1)S(1)}, u32[]{:S(2)}, u32[]{:S(2)}) collective-permute-start(bf16[48,768]{1,0:T(8,128)(2,1)} %reduce_sum.12), channel_id=1, source_target_pairs={{0,192},{64,128},{128,64},{192,0},{1,193},{65,129},{129,65},{193,1... | collective-permute-start | bytes 221192 | tf_op jit(solution)/shard_map/ppermute | solution.py:346
  138.7 4.8 %collective-permute-start.18 = (bf16[48,768]{1,0:T(8,128)(2,1)S(1)}, bf16[48,768]{1,0:T(8,128)(2,1)S(1)}, u32[]{:S(2)}, u32[]{:S(2)}) collective-permute-start(bf16[48,768]{1,0:T(8,128)(2,1)S(1)} %copy-done.12), channel_id=1, source_target_pairs={{0,64},{64,0},{1,65},{65,1},{2,66},{66,2},{3,67},{67,3},{4,68},{68... | collective-permute-start | bytes 221192 | tf_op jit(solution)/shard_map/ppermute | solution.py:345
  142.0 3.6 %collective-permute-start.17 = (bf16[48,768]{1,0:T(8,128)(2,1)S(1)}, bf16[48,768]{1,0:T(8,128)(2,1)S(1)}, u32[]{:S(2)}, u32[]{:S(2)}) collective-permute-start(bf16[48,768]{1,0:T(8,128)(2,1)S(1)} %copy-done.12), channel_id=1, source_target_pairs={{0,128},{128,0},{1,129},{129,1},{2,130},{130,2},{3,131},{131,3},{4... | collective-permute-start | bytes 221192 | tf_op jit(solution)/shard_map/ppermute | solution.py:344
  145.7 9.9 %collective-permute-start.20 = (f32[48,768]{1,0:T(8,128)S(1)}, f32[48,768]{1,0:T(8,128)S(1)}, u32[]{:S(2)}, u32[]{:S(2)}) collective-permute-start(f32[48,768]{1,0:T(8,128)S(1)} %add_add_fusion), channel_id=1, source_target_pairs={{0,32},{32,0},{1,33},{33,1},{2,34},{34,2},{3,35},{35,3},{4,36},{36... | collective-permute-start | bytes 442376 | tf_op jit(solution)/shard_map/ppermute | solution.py:348
  (16 other events, 107.5 us)

commit v9 on v8

--- a/solution.py
+++ b/solution.py
@@ -332,15 +332,13 @@
     atts, gq_0, gq_1 = lax.optimization_barrier((atts, gq_0, gq_1))
     grad_mine, grad_mate = weight_gradient(scalars, atts, ups)
     from_mate = lax.ppermute(grad_mate, "co", SWAP)
+    atts, w_rows, grad_mine = lax.optimization_barrier((atts, w_rows, grad_mine))
+    mixed = mixed_parts(scalars, atts, w_rows)
     grad = (grad_mine.astype(F32) + from_mate.astype(F32)).astype(BF16).reshape(nz, rows, half)
-    atts, w_rows, grad = lax.optimization_barrier((atts, w_rows, grad))
-    mixed = mixed_parts(scalars, atts, w_rows)
-    gkv_parts = [
-        own.astype(F32) + sum(t.astype(F32) for t in terms)
-        for own, terms in ((own_0, terms_0), (own_1, terms_1))
-    ]
+    grad, mixed = lax.optimization_barrier((grad, mixed))
     gq_parts = (gq_0, gq_1)
     over_z = jnp.sum(swapped(grad, "z").astype(F32), axis=0).astype(BF16)
+    over_z, terms_0 = lax.optimization_barrier((over_z, terms_0))
     x_near = lax.ppermute(over_z, "xl", SWAP)
     x_far = lax.ppermute(over_z, "xh", SWAP)
     x_both = lax.ppermute(over_z, ("xl", "xh"), [(i, 3 - i) for i in range(4)])
@@ -352,6 +350,10 @@
 
     back = [shifted(mixed[k], "y", -k).astype(F32) for k in (1, 2, 3)]
     mixed = (mixed[0].astype(F32) + sum(back)).astype(BF16)
+    gkv_parts = [
+        own.astype(F32) + sum(t.astype(F32) for t in terms)
+        for own, terms in ((own_0, terms_0), (own_1, terms_1))
+    ]
     grad_q = jnp.concatenate(gq_parts, axis=1)
     grad_kv = jnp.concatenate([p.astype(BF16) for p in gkv_parts], axis=2)
     return (

time: 157 us -> 154 us (0.981)
  waiting for transfers between devices: 32.8 us -> 27.7 us
  starting transfers between devices: 69.8 us -> 72.2 us
    ppermute x2, waiting for transfers between devices: 8.92 us -> 2.34 us  [backward(): lax.ppermute(to_cross, ('xh', 'co'), CROSS)]
    ppermute x2, starting transfers between devices: 9.06 us -> 6.25 us  [backward(): lax.ppermute(to_cross, ('xh', 'co'), CROSS)]
    ppermute x1, starting transfers between devices: 0.68 us -> 2.82 us  [per_device(): mate = lax.ppermute(mine, 'co', SWAP)]
    ppermute x6, waiting for transfers between devices: 16.5 us -> 18.5 us  [shifted(): return lax.ppermute(x, axis, [(i, (i + by) % count) for i in range(count)])]
  transfers between devices with their start and end apart: 25 -> 25, of which waited for: 14 -> 12; matrix products, arithmetic and copies ran while one was open for 6% -> 5% of each run, Pallas kernels for 20% -> 20%
where the time goes in v9:
time: 154 us; the launch traced here: 153 us
  starting transfers between devices  72.2 us (47%)
  Pallas kernels  38.4 us (25%)
  waiting for transfers between devices  27.7 us (18%)
  other arithmetic  9.77 us (6%)
  local copies, waits for them, and re-layouts  3.1 us (2%)
    all_to_all x4, starting transfers between devices, swapped(): return lax.all_to_all(x, axis, split_axis=0, concat_axis=0, tiled=True)  26.7 us
    ppermute x6, waiting for transfers between devices, shifted(): return lax.ppermute(x, axis, [(i, (i + by) % count) for i in range(count)])  18.5 us
    pallas_call x2, Pallas kernels, attention_backward(): pl.pallas_call(backward_kernel, grid_spec=pltpu.PrefetchScalarGridSpec(nu...  12.3 us
    ppermute x1, starting transfers between devices, per_device(): w_mate = lax.ppermute(w_mine, 'co', SWAP)  11.4 us
    ppermute x6, starting transfers between devices, shifted(): return lax.ppermute(x, axis, [(i, (i + by) % count) for i in range(count)])  9.05 us
    pallas_call x1, Pallas kernels, attention_forward(): pl.pallas_call(forward_kernel, grid_spec=pltpu.PrefetchScalarGridSpec(num...  8.11 us
    ppermute x1, starting transfers between devices, per_device(): from_cross = lax.ppermute(kv, ('xh', 'co'), CROSS)  6.32 us
    ppermute x2, starting transfers between devices, backward(): lax.ppermute(to_cross, ('xh', 'co'), CROSS)  6.25 us
  transfers between devices with their start and end apart: 25, of which 12 were waited for; matrix products, arithmetic and copies ran while one was open for 5% of the time, Pallas kernels for 20%

profile of v9, /device:TPU:1, one launch (start us, length us, event | category | flops | bytes accessed | tf_op | source)
XLA Modules:
  0.0 152.7 jit_solution(4227695633700766560)
XLA Ops:
  1.9 2.4 %shard_map.85 = bf16[8,48,768]{2,1,0:T(8,128)(2,1)} custom-call(s32[4]{0:T(128)} %pad_add_fusion.scalar_ref, bf16[32,48,1536]{2,1,0:T(8,128)(2,1)} %weight_ref.1), custom_call_target="tpu_custom_call" | custom-call | flops 1000 | bytes 1000 | tf_op jit(solution)/shard_map/pallas_call | solution.py:164
  4.3 9.1 %all-to-all-start.1 = ((bf16[8,48,768]{2,1,0:T(8,128)(2,1)}), bf16[8,48,768]{2,1,0:T(8,128)(2,1)}, u32[]{:S(2)}, u32[]{:S(2)}) async-start(bf16[8,48,768]{2,1,0:T(8,128)(2,1)} %shard_map.85), calls=%async_computation.1 | async-start | bytes 1179648 | tf_op jit(solution)/shard_map/all_to_all | solution.py:281
  13.4 2.7 %collective-permute-start.5 = (bf16[192,1536]{1,0:T(8,128)(2,1)}, bf16[192,1536]{1,0:T(8,128)(2,1)S(1)}, u32[]{:S(2)}, u32[]{:S(2)}) collective-permute-start(bf16[192,1536]{1,0:T(8,128)(2,1)} %bitcast.6.refs_0_.refs_4_), channel_id=1, source_target_pairs={{0,3},{1,0},{2,1},{3,2},{4,7},{5,4},{6,5},{7,6},{8,11},{9,8},{10,9... | collective-permute-start | bytes 1769480 | tf_op jit(solution)/shard_map/ppermute | solution.py:277
  17.2 6.3 %collective-permute-start.2 = (bf16[2,192,1536]{2,1,0:T(8,128)(2,1)S(1)}, bf16[2,192,1536]{2,1,0:T(8,128)(2,1)S(1)}, u32[]{:S(2)}, u32[]{:S(2)}) collective-permute-start(bf16[2,192,1536]{2,1,0:T(8,128)(2,1)S(1)} %bitcast.21), channel_id=1, source_target_pairs={{32,64},{64,32},{33,65},{65,33},{34,66},{66,34},{35,67},{67,35},{3... | collective-permute-start | bytes 3538952 | tf_op jit(solution)/shard_map/ppermute | solution.py:302
  23.6 5.6 %collective-permute-done.5.refs_3_.refs_7_ = bf16[192,1536]{1,0:T(8,128)(2,1)S(1)} collective-permute-done((bf16[192,1536]{1,0:T(8,128)(2,1)}, bf16[192,1536]{1,0:T(8,128)(2,1)S(1)}, u32[]{:S(2)}, u32[]{:S(2)}) %collective-permute-start.5) | collective-permute-done | bytes 589856 | tf_op jit(solution)/shard_map/ppermute | solution.py:277
  32.9 11.4 %collective-permute-start.6 = (bf16[384,768]{1,0:T(8,128)(2,1)}, bf16[384,768]{1,0:T(8,128)(2,1)S(1)}, u32[]{:S(2)}, u32[]{:S(2)}) collective-permute-start(bf16[384,768]{1,0:T(8,128)(2,1)} %bitcast.7.refs_4_), channel_id=1, source_target_pairs={{0,32},{32,0},{1,33},{33,1},{2,34},{34,2},{3,35},{35,3},{4,36},{36... | collective-permute-start | bytes 1769480 | tf_op jit(solution)/shard_map/ppermute | solution.py:308
  46.9 4.9 %shard_map.86 = (bf16[4,384,256]{2,1,0:T(8,128)(2,1)}, bf16[384,1536]{1,0:T(8,128)(2,1)}) custom-call(s32[4]{0:T(128)} %pad_add_fusion.scalar_ref, bf16[192,1536]{1,0:T(8,128)(2,1)} %bitcast.6.refs_0_.refs_4_, bf16[192,1536]{1,0:T(8,128)(2,1)} %collective-permute-done.3.refs_1_.refs_5_, bf16[192,1536]{1,0:T(8,128)(2,1)} %collective-permute-done.4.refs_2_.refs_6_, ...), custom_call_target="tpu_custom_call" | custom-call | flops 1000 | bytes 1000 | tf_op jit(solution)/shard_map/pallas_call | solution.py:198
  51.9 4.6 %all-to-all-start.2 = ((bf16[4,384,256]{2,1,0:T(8,128)(2,1)}), bf16[4,384,256]{2,1,0:T(8,128)(2,1)}, u32[]{:S(2)}, u32[]{:S(2)}) async-start(bf16[4,384,256]{2,1,0:T(8,128)(2,1)} %get-tuple-element.42), calls=%async_computation.2 | async-start | bytes 1572864 | tf_op jit(solution)/shard_map/all_to_all | solution.py:281
  57.8 8.1 %shard_map.84 = (bf16[192,1536]{1,0:T(8,128)(2,1)}, bf16[4,8,48,256]{3,2,1,0:T(8,128)(2,1)}, bf16[12,192,768]{2,1,0:T(8,128)(2,1)}) custom-call(s32[4]{0:T(128)} %pad_add_fusion.scalar_ref, bf16[192,1536]{1,0:T(8,128)(2,1)} %bitcast.24, bf16[2,192,1536]{2,1,0:T(8,128)(2,1)} %bitcast.18, bf16[2,192,1536]{2,1,0:T(8,128)(2,1)} %collective-permute-done.time_ref, ...), custom_call_target="tpu_custom_call" | custom-call | flops 1000 | bytes 1000 | tf_op jit(solution)/shard_map/pallas_call | solution.py:122
  65.9 2.3 %all-to-all-done.2 = bf16[4,384,256]{2,1,0:T(8,128)(2,1)} async-done(((bf16[4,384,256]{2,1,0:T(8,128)(2,1)}), bf16[4,384,256]{2,1,0:T(8,128)(2,1)}, u32[]{:S(2)}, u32[]{:S(2)}) %all-to-all-start.2) | async-done | bytes 786464 | tf_op jit(solution)/shard_map/all_to_all | solution.py:281
  68.2 5.9 %all-to-all-start = ((bf16[4,384,256]{2,1,0:T(8,128)(2,1)}), bf16[4,384,256]{2,1,0:T(8,128)(2,1)S(1)}, u32[]{:S(2)}, u32[]{:S(2)}) async-start(bf16[4,384,256]{2,1,0:T(8,128)(2,1)} %bitcast.27), calls=%async_computation | async-start | bytes 1572864 | tf_op jit(solution)/shard_map/all_to_all | solution.py:281
  74.2 6.1 %shard_map.88 = (bf16[192,768]{1,0:T(8,128)(2,1)}, bf16[2,192,768]{2,1,0:T(8,128)(2,1)}, bf16[2,192,768]{2,1,0:T(8,128)(2,1)}, bf16[2,192,768]{2,1,0:T(8,128)(2,1)}, bf16[2,192,768]{2,1,0:T(8,128)(2,1)}) custom-call(s32[4]{0:T(128)} %pad_add_fusion.scalar_ref, bf16[192,1536]{1,0:T(8,128)(2,1)} %bitcast.25, bf16[2,192,1536]{2,1,0:T(8,128)(2,1)} %bitcast.19, ...), custom_call_target="tpu_custom_call" | custom-call | flops 1000 | bytes 1000 | tf_op jit(solution)/shard_map/pallas_call | solution.py:142
  80.3 6.2 %shard_map.87 = (bf16[192,768]{1,0:T(8,128)(2,1)}, bf16[2,192,768]{2,1,0:T(8,128)(2,1)}, bf16[2,192,768]{2,1,0:T(8,128)(2,1)}, bf16[2,192,768]{2,1,0:T(8,128)(2,1)}, bf16[2,192,768]{2,1,0:T(8,128)(2,1)}) custom-call(s32[4]{0:T(128)} %pad_add_fusion.scalar_ref, bf16[192,1536]{1,0:T(8,128)(2,1)} %bitcast.26, bf16[2,192,1536]{2,1,0:T(8,128)(2,1)} %bitcast.20, ...), custom_call_target="tpu_custom_call" | custom-call | flops 1000 | bytes 1000 | tf_op jit(solution)/shard_map/pallas_call | solution.py:142
  87.3 5.7 %shard_map.89 = (bf16[384,768]{1,0:T(8,128)(2,1)}, bf16[384,768]{1,0:T(8,128)(2,1)}) custom-call(s32[4]{0:T(128)} %pad_add_fusion.scalar_ref, bf16[4,384,256]{2,1,0:T(8,128)(2,1)} %copy-done.3, bf16[192,1536]{1,0:T(8,128)(2,1)} %bitcast.6.refs_0_.refs_4_, bf16[192,1536]{1,0:T(8,128)(2,1)} %collective-permute-done.3.refs_1_.refs_5_, ...), custom_call_target="tpu_custom_call" | custom-call | flops 1000 | bytes 1000 | tf_op jit(solution)/shard_map/pallas_call | solution.py:233
  95.4 2.4 %collective-permute-start.15 = (bf16[2,192,768]{2,1,0:T(8,128)(2,1)}, bf16[2,192,768]{2,1,0:T(8,128)(2,1)S(1)}, u32[]{:S(2)}, u32[]{:S(2)}) collective-permute-start(bf16[2,192,768]{2,1,0:T(8,128)(2,1)} %get-tuple-element.73), channel_id=1, source_target_pairs={{32,64},{64,32},{33,65},{65,33},{34,66},{66,34},{35,67},{67,35},{3... | collective-permute-start | bytes 1769480 | tf_op jit(solution)/shard_map/ppermute | solution.py:325
  98.1 5.0 %shard_map.90 = (bf16[192,1536]{1,0:T(8,128)(2,1)}, bf16[192,1536]{1,0:T(8,128)(2,1)}, bf16[192,1536]{1,0:T(8,128)(2,1)}, bf16[192,1536]{1,0:T(8,128)(2,1)}) custom-call(s32[4]{0:T(128)} %pad_add_fusion.scalar_ref, bf16[4,384,256]{2,1,0:T(8,128)(2,1)} %copy-done.3, bf16[384,1536]{1,0:T(8,128)(2,1)} %get-tuple-element.52.weight_ref), custom_call_target="tpu_custom_call" | custom-call | flops 1000 | bytes 1000 | tf_op jit(solution)/shard_map/pallas_call | solution.py:257
  104.0 3.0 %collective-permute-start.8 = (bf16[192,1536]{1,0:T(8,128)(2,1)}, bf16[192,1536]{1,0:T(8,128)(2,1)S(1)}, u32[]{:S(2)}, u32[]{:S(2)}) collective-permute-start(bf16[192,1536]{1,0:T(8,128)(2,1)} %get-tuple-element.58), channel_id=1, source_target_pairs={{0,3},{1,0},{2,1},{3,2},{4,7},{5,4},{6,5},{7,6},{8,11},{9,8},{10,9... | collective-permute-start | bytes 1769480 | tf_op jit(solution)/shard_map/ppermute | solution.py:277
  110.8 7.1 %all-to-all-start.3 = ((bf16[8,48,768]{2,1,0:T(8,128)(2,1)}), bf16[8,48,768]{2,1,0:T(8,128)(2,1)S(1)}, u32[]{:S(2)}, u32[]{:S(2)}) async-start(bf16[8,48,768]{2,1,0:T(8,128)(2,1)} %bitcast.9), calls=%async_computation.3 | async-start | bytes 1179648 | tf_op jit(solution)/shard_map/all_to_all | solution.py:281
  120.9 3.8 %collective-permute-start.12 = (bf16[2,192,768]{2,1,0:T(8,128)(2,1)}, bf16[2,192,768]{2,1,0:T(8,128)(2,1)}, u32[]{:S(2)}, u32[]{:S(2)}) collective-permute-start(bf16[2,192,768]{2,1,0:T(8,128)(2,1)} %get-tuple-element.66), channel_id=1, source_target_pairs={{32,64},{64,32},{33,65},{65,33},{34,66},{66,34},{35,67},{67,35},{3... | collective-permute-start | bytes 1769480 | tf_op jit(solution)/shard_map/ppermute | solution.py:325
  124.8 7.2 %collective-permute-done.8 = bf16[192,1536]{1,0:T(8,128)(2,1)S(1)} collective-permute-done((bf16[192,1536]{1,0:T(8,128)(2,1)}, bf16[192,1536]{1,0:T(8,128)(2,1)S(1)}, u32[]{:S(2)}, u32[]{:S(2)}) %collective-permute-start.8) | collective-permute-done | bytes 589856 | tf_op jit(solution)/shard_map/ppermute | solution.py:277
  133.8 2.9 %collective-permute-done.10 = bf16[192,1536]{1,0:T(8,128)(2,1)} collective-permute-done((bf16[192,1536]{1,0:T(8,128)(2,1)}, bf16[192,1536]{1,0:T(8,128)(2,1)}, u32[]{:S(2)}, u32[]{:S(2)}) %collective-permute-start.10) | collective-permute-done | bytes 589856 | tf_op jit(solution)/shard_map/ppermute | solution.py:277
  136.7 2.3 %fusion = bf16[1,1,1,192,1536]{4,3,2,1,0:T(8,128)(2,1)} fusion(bf16[192,1536]{1,0:T(8,128)(2,1)} %collective-permute-done.10, bf16[192,1536]{1,0:T(8,128)(2,1)} %collective-permute-done.9, bf16[192,1536]{1,0:T(8,128)(2,1)S(1)} %copy-done.10, bf16[192,1536]{1,0:T(8,128)(2,1)S(1)} %copy-done.8), kind=kLoop, calls=%fused_computation.5 | loop fusion | flops 2359296 | bytes 2949120 | tf_op jit(solution)/shard_map/reshape | solution.py:360
  139.1 2.3 %collective-permute-done.12 = bf16[2,192,768]{2,1,0:T(8,128)(2,1)} collective-permute-done((bf16[2,192,768]{2,1,0:T(8,128)(2,1)}, bf16[2,192,768]{2,1,0:T(8,128)(2,1)}, u32[]{:S(2)}, u32[]{:S(2)}) %collective-permute-start.12) | collective-permute-done | bytes 589856 | tf_op jit(solution)/shard_map/ppermute | solution.py:325
  148.0 2.8 %collective-permute-start.20 = (f32[48,768]{1,0:T(8,128)S(1)}, f32[48,768]{1,0:T(8,128)S(1)}, u32[]{:S(2)}, u32[]{:S(2)}) collective-permute-start(f32[48,768]{1,0:T(8,128)S(1)} %add_add_fusion), channel_id=1, source_target_pairs={{0,32},{32,0},{1,33},{33,1},{2,34},{34,2},{3,35},{35,3},{4,36},{36... | collective-permute-start | bytes 442376 | tf_op jit(solution)/shard_map/ppermute | solution.py:346
  (70 shorter events, 31.0 us)
Async XLA Ops:
  4.3 28.6 %all-to-all-start.1 = ((bf16[8,48,768]{2,1,0:T(8,128)(2,1)}), bf16[8,48,768]{2,1,0:T(8,128)(2,1)}, u32[]{:S(2)}, u32[]{:S(2)}) async-start(bf16[8,48,768]{2,1,0:T(8,128)(2,1)} %shard_map.85), calls=%async_computation.1 | async-start | bytes 1179648 | tf_op jit(solution)/shard_map/all_to_all | solution.py:281
  13.4 15.8 %collective-permute-start.5 = (bf16[192,1536]{1,0:T(8,128)(2,1)}, bf16[192,1536]{1,0:T(8,128)(2,1)S(1)}, u32[]{:S(2)}, u32[]{:S(2)}) collective-permute-start(bf16[192,1536]{1,0:T(8,128)(2,1)} %bitcast.6.refs_0_.refs_4_), channel_id=1, source_target_pairs={{0,3},{1,0},{2,1},{3,2},{4,7},{5,4},{6,5},{7,6},{8,11},{9,8},{10,9... | collective-permute-start | bytes 1769480 | tf_op jit(solution)/shard_map/ppermute | solution.py:277
  16.2 15.5 %collective-permute-start.4 = (bf16[192,1536]{1,0:T(8,128)(2,1)}, bf16[192,1536]{1,0:T(8,128)(2,1)}, u32[]{:S(2)}, u32[]{:S(2)}) collective-permute-start(bf16[192,1536]{1,0:T(8,128)(2,1)} %bitcast.6.refs_0_.refs_4_), channel_id=1, source_target_pairs={{0,2},{1,3},{2,0},{3,1},{4,6},{5,7},{6,4},{7,5},{8,10},{9,11},{10,... | collective-permute-start | bytes 1769480 | tf_op jit(solution)/shard_map/ppermute | solution.py:277
  16.5 29.4 %collective-permute-start.3 = (bf16[192,1536]{1,0:T(8,128)(2,1)}, bf16[192,1536]{1,0:T(8,128)(2,1)}, u32[]{:S(2)}, u32[]{:S(2)}) collective-permute-start(bf16[192,1536]{1,0:T(8,128)(2,1)} %bitcast.6.refs_0_.refs_4_), channel_id=1, source_target_pairs={{0,1},{1,2},{2,3},{3,0},{4,5},{5,6},{6,7},{7,4},{8,9},{9,10},{10,1... | collective-permute-start | bytes 1769480 | tf_op jit(solution)/shard_map/ppermute | solution.py:277
  17.2 39.2 %collective-permute-start.2 = (bf16[2,192,1536]{2,1,0:T(8,128)(2,1)S(1)}, bf16[2,192,1536]{2,1,0:T(8,128)(2,1)S(1)}, u32[]{:S(2)}, u32[]{:S(2)}) collective-permute-start(bf16[2,192,1536]{2,1,0:T(8,128)(2,1)S(1)} %bitcast.21), channel_id=1, source_target_pairs={{32,64},{64,32},{33,65},{65,33},{34,66},{66,34},{35,67},{67,35},{3... | collective-permute-start | bytes 3538952 | tf_op jit(solution)/shard_map/ppermute | solution.py:302
  23.5 32.9 %collective-permute-start.1 = (bf16[2,192,1536]{2,1,0:T(8,128)(2,1)S(1)}, bf16[2,192,1536]{2,1,0:T(8,128)(2,1)S(1)}, u32[]{:S(2)}, u32[]{:S(2)}) collective-permute-start(bf16[2,192,1536]{2,1,0:T(8,128)(2,1)S(1)} %bitcast.22), channel_id=1, source_target_pairs={{0,32},{32,0},{1,33},{33,1},{2,34},{34,2},{3,35},{35,3},{4,36},{36... | collective-permute-start | bytes 3538952 | tf_op jit(solution)/shard_map/ppermute | solution.py:303
  29.2 27.2 %collective-permute-start = (bf16[2,192,1536]{2,1,0:T(8,128)(2,1)S(1)}, bf16[2,192,1536]{2,1,0:T(8,128)(2,1)}, u32[]{:S(2)}, u32[]{:S(2)}) collective-permute-start(bf16[2,192,1536]{2,1,0:T(8,128)(2,1)S(1)} %bitcast.23), channel_id=1, source_target_pairs={{0,128},{128,0},{1,129},{129,1},{2,130},{130,2},{3,131},{131,3},{4... | collective-permute-start | bytes 3538952 | tf_op jit(solution)/shard_map/ppermute | solution.py:301
  32.9 13.2 %collective-permute-start.6 = (bf16[384,768]{1,0:T(8,128)(2,1)}, bf16[384,768]{1,0:T(8,128)(2,1)S(1)}, u32[]{:S(2)}, u32[]{:S(2)}) collective-permute-start(bf16[384,768]{1,0:T(8,128)(2,1)} %bitcast.7.refs_4_), channel_id=1, source_target_pairs={{0,32},{32,0},{1,33},{33,1},{2,34},{34,2},{3,35},{35,3},{4,36},{36... | collective-permute-start | bytes 1769480 | tf_op jit(solution)/shard_map/ppermute | solution.py:308
  51.9 16.4 %all-to-all-start.2 = ((bf16[4,384,256]{2,1,0:T(8,128)(2,1)}), bf16[4,384,256]{2,1,0:T(8,128)(2,1)}, u32[]{:S(2)}, u32[]{:S(2)}) async-start(bf16[4,384,256]{2,1,0:T(8,128)(2,1)} %get-tuple-element.42), calls=%async_computation.2 | async-start | bytes 1572864 | tf_op jit(solution)/shard_map/all_to_all | solution.py:281
  68.2 18.2 %all-to-all-start = ((bf16[4,384,256]{2,1,0:T(8,128)(2,1)}), bf16[4,384,256]{2,1,0:T(8,128)(2,1)S(1)}, u32[]{:S(2)}, u32[]{:S(2)}) async-start(bf16[4,384,256]{2,1,0:T(8,128)(2,1)} %bitcast.27), calls=%async_computation | async-start | bytes 1572864 | tf_op jit(solution)/shard_map/all_to_all | solution.py:281
  93.1 10.0 %collective-permute-start.7 = (bf16[384,768]{1,0:T(8,128)(2,1)}, bf16[384,768]{1,0:T(8,128)(2,1)S(1)}, u32[]{:S(2)}, u32[]{:S(2)}) collective-permute-start(bf16[384,768]{1,0:T(8,128)(2,1)} %get-tuple-element.50), channel_id=1, source_target_pairs={{0,32},{32,0},{1,33},{33,1},{2,34},{34,2},{3,35},{35,3},{4,36},{36... | collective-permute-start | bytes 1769480 | tf_op jit(solution)/shard_map/ppermute | solution.py:334
  94.2 14.9 %collective-permute-start.14 = (bf16[2,192,768]{2,1,0:T(8,128)(2,1)S(1)}, bf16[2,192,768]{2,1,0:T(8,128)(2,1)S(1)}, u32[]{:S(2)}, u32[]{:S(2)}) collective-permute-start(bf16[2,192,768]{2,1,0:T(8,128)(2,1)S(1)} %copy-done.12), channel_id=1, source_target_pairs={{0,128},{128,0},{1,129},{129,1},{2,130},{130,2},{3,131},{131,3},{4... | collective-permute-start | bytes 1769480 | tf_op jit(solution)/shard_map/ppermute | solution.py:324
  95.4 24.4 %collective-permute-start.15 = (bf16[2,192,768]{2,1,0:T(8,128)(2,1)}, bf16[2,192,768]{2,1,0:T(8,128)(2,1)S(1)}, u32[]{:S(2)}, u32[]{:S(2)}) collective-permute-start(bf16[2,192,768]{2,1,0:T(8,128)(2,1)} %get-tuple-element.73), channel_id=1, source_target_pairs={{32,64},{64,32},{33,65},{65,33},{34,66},{66,34},{35,67},{67,35},{3... | collective-permute-start | bytes 1769480 | tf_op jit(solution)/shard_map/ppermute | solution.py:325
  97.8 23.1 %collective-permute-start.16 = (bf16[2,192,768]{2,1,0:T(8,128)(2,1)}, bf16[2,192,768]{2,1,0:T(8,128)(2,1)S(1)}, u32[]{:S(2)}, u32[]{:S(2)}) collective-permute-start(bf16[2,192,768]{2,1,0:T(8,128)(2,1)} %get-tuple-element.74), channel_id=1, source_target_pairs={{0,32},{32,0},{1,33},{33,1},{2,34},{34,2},{3,35},{35,3},{4,36},{36... | collective-permute-start | bytes 1769480 | tf_op jit(solution)/shard_map/ppermute | solution.py:326
  104.0 28.0 %collective-permute-start.8 = (bf16[192,1536]{1,0:T(8,128)(2,1)}, bf16[192,1536]{1,0:T(8,128)(2,1)S(1)}, u32[]{:S(2)}, u32[]{:S(2)}) collective-permute-start(bf16[192,1536]{1,0:T(8,128)(2,1)} %get-tuple-element.58), channel_id=1, source_target_pairs={{0,3},{1,0},{2,1},{3,2},{4,7},{5,4},{6,5},{7,6},{8,11},{9,8},{10,9... | collective-permute-start | bytes 1769480 | tf_op jit(solution)/shard_map/ppermute | solution.py:277
  107.0 26.8 %collective-permute-start.9 = (bf16[192,1536]{1,0:T(8,128)(2,1)}, bf16[192,1536]{1,0:T(8,128)(2,1)}, u32[]{:S(2)}, u32[]{:S(2)}) collective-permute-start(bf16[192,1536]{1,0:T(8,128)(2,1)} %get-tuple-element.59), channel_id=1, source_target_pairs={{0,2},{1,3},{2,0},{3,1},{4,6},{5,7},{6,4},{7,5},{8,10},{9,11},{10,... | collective-permute-start | bytes 1769480 | tf_op jit(solution)/shard_map/ppermute | solution.py:277
  109.1 27.6 %collective-permute-start.10 = (bf16[192,1536]{1,0:T(8,128)(2,1)}, bf16[192,1536]{1,0:T(8,128)(2,1)}, u32[]{:S(2)}, u32[]{:S(2)}) collective-permute-start(bf16[192,1536]{1,0:T(8,128)(2,1)} %get-tuple-element.60), channel_id=1, source_target_pairs={{0,1},{1,2},{2,3},{3,0},{4,5},{5,6},{6,7},{7,4},{8,9},{9,10},{10,1... | collective-permute-start | bytes 1769480 | tf_op jit(solution)/shard_map/ppermute | solution.py:277
  110.8 28.2 %all-to-all-start.3 = ((bf16[8,48,768]{2,1,0:T(8,128)(2,1)}), bf16[8,48,768]{2,1,0:T(8,128)(2,1)S(1)}, u32[]{:S(2)}, u32[]{:S(2)}) async-start(bf16[8,48,768]{2,1,0:T(8,128)(2,1)} %bitcast.9), calls=%async_computation.3 | async-start | bytes 1179648 | tf_op jit(solution)/shard_map/all_to_all | solution.py:281
  119.8 19.3 %collective-permute-start.11 = (bf16[2,192,768]{2,1,0:T(8,128)(2,1)}, bf16[2,192,768]{2,1,0:T(8,128)(2,1)}, u32[]{:S(2)}, u32[]{:S(2)}) collective-permute-start(bf16[2,192,768]{2,1,0:T(8,128)(2,1)} %get-tuple-element.65), channel_id=1, source_target_pairs={{0,128},{128,0},{1,129},{129,1},{2,130},{130,2},{3,131},{131,3},{4... | collective-permute-start | bytes 1769480 | tf_op jit(solution)/shard_map/ppermute | solution.py:324
  120.9 20.5 %collective-permute-start.12 = (bf16[2,192,768]{2,1,0:T(8,128)(2,1)}, bf16[2,192,768]{2,1,0:T(8,128)(2,1)}, u32[]{:S(2)}, u32[]{:S(2)}) collective-permute-start(bf16[2,192,768]{2,1,0:T(8,128)(2,1)} %get-tuple-element.66), channel_id=1, source_target_pairs={{32,64},{64,32},{33,65},{65,33},{34,66},{66,34},{35,67},{67,35},{3... | collective-permute-start | bytes 1769480 | tf_op jit(solution)/shard_map/ppermute | solution.py:325
  132.0 9.5 %collective-permute-start.13 = (bf16[2,192,768]{2,1,0:T(8,128)(2,1)}, bf16[2,192,768]{2,1,0:T(8,128)(2,1)}, u32[]{:S(2)}, u32[]{:S(2)}) collective-permute-start(bf16[2,192,768]{2,1,0:T(8,128)(2,1)} %get-tuple-element.67), channel_id=1, source_target_pairs={{0,32},{32,0},{1,33},{33,1},{2,34},{34,2},{3,35},{35,3},{4,36},{36... | collective-permute-start | bytes 1769480 | tf_op jit(solution)/shard_map/ppermute | solution.py:326
  141.5 5.8 %collective-permute-start.19 = (bf16[48,768]{1,0:T(8,128)(2,1)S(1)}, bf16[48,768]{1,0:T(8,128)(2,1)S(1)}, u32[]{:S(2)}, u32[]{:S(2)}) collective-permute-start(bf16[48,768]{1,0:T(8,128)(2,1)S(1)} %reduce_sum.12), channel_id=1, source_target_pairs={{0,192},{64,128},{128,64},{192,0},{1,193},{65,129},{129,65},{193,1... | collective-permute-start | bytes 221192 | tf_op jit(solution)/shard_map/ppermute | solution.py:344
  141.8 5.5 %collective-permute-start.18 = (bf16[48,768]{1,0:T(8,128)(2,1)S(1)}, bf16[48,768]{1,0:T(8,128)(2,1)S(1)}, u32[]{:S(2)}, u32[]{:S(2)}) collective-permute-start(bf16[48,768]{1,0:T(8,128)(2,1)S(1)} %reduce_sum.12), channel_id=1, source_target_pairs={{0,64},{64,0},{1,65},{65,1},{2,66},{66,2},{3,67},{67,3},{4,68},{68... | collective-permute-start | bytes 221192 | tf_op jit(solution)/shard_map/ppermute | solution.py:343
  143.6 4.4 %collective-permute-start.17 = (bf16[48,768]{1,0:T(8,128)(2,1)S(1)}, bf16[48,768]{1,0:T(8,128)(2,1)S(1)}, u32[]{:S(2)}, u32[]{:S(2)}) collective-permute-start(bf16[48,768]{1,0:T(8,128)(2,1)S(1)} %reduce_sum.12), channel_id=1, source_target_pairs={{0,128},{128,0},{1,129},{129,1},{2,130},{130,2},{3,131},{131,3},{4... | collective-permute-start | bytes 221192 | tf_op jit(solution)/shard_map/ppermute | solution.py:342
  (14 other events, 80.5 us)

commit v10 on v9

--- a/solution.py
+++ b/solution.py
@@ -320,15 +320,13 @@
         gq, own, to_time, to_core, to_cross = attention_backward(
             scalars, q, kvs, att, d_turned, probs, c * groups, groups
         )
-        terms = (
-            lax.ppermute(to_time, "xl", SWAP),
-            lax.ppermute(to_cross, ("xh", "co"), CROSS),
-            lax.ppermute(to_core, "co", SWAP),
-        )
-        return gq, own, terms
-
-    gq_0, own_0, terms_0 = backward(0)
-    gq_1, own_1, terms_1 = backward(1)
+        from_time = lax.ppermute(to_time, "xl", SWAP)
+        from_cross = lax.ppermute(to_cross, ("xh", "co"), CROSS)
+        return gq, own, (from_time, from_cross), to_core
+
+    gq_0, own_0, terms_0, to_core = backward(0)
+    terms_0 += (lax.ppermute(to_core, "co", SWAP),)
+    gq_1, own_1, terms_1, to_core = backward(1)
     atts, gq_0, gq_1 = lax.optimization_barrier((atts, gq_0, gq_1))
     grad_mine, grad_mate = weight_gradient(scalars, atts, ups)
     from_mate = lax.ppermute(grad_mate, "co", SWAP)
@@ -338,7 +336,7 @@
     grad, mixed = lax.optimization_barrier((grad, mixed))
     gq_parts = (gq_0, gq_1)
     over_z = jnp.sum(swapped(grad, "z").astype(F32), axis=0).astype(BF16)
-    over_z, terms_0 = lax.optimization_barrier((over_z, terms_0))
+    over_z, terms_0, to_core = lax.optimization_barrier((over_z, terms_0, to_core))
     x_near = lax.ppermute(over_z, "xl", SWAP)
     x_far = lax.ppermute(over_z, "xh", SWAP)
     x_both = lax.ppermute(over_z, ("xl", "xh"), [(i, 3 - i) for i in range(4)])
@@ -348,8 +346,10 @@
         [jnp.where(first, mine, mate), jnp.where(first, mate, mine)], axis=1
     )
 
-    back = [shifted(mixed[k], "y", -k).astype(F32) for k in (1, 2, 3)]
-    mixed = (mixed[0].astype(F32) + sum(back)).astype(BF16)
+    back = [shifted(mixed[k], "y", -k) for k in (1, 2, 3)]
+    back, _ = lax.optimization_barrier((back, x_near))
+    mixed = (mixed[0].astype(F32) + sum(b.astype(F32) for b in back)).astype(BF16)
+    terms_1 += (lax.ppermute(to_core, "co", SWAP),)
     gkv_parts = [
         own.astype(F32) + sum(t.astype(F32) for t in terms)
         for own, terms in ((own_0, terms_0), (own_1, terms_1))

time: 154 us -> 162 us (1.052)
  waiting for transfers between devices: 27.7 us -> 38.1 us
    all_to_all x4, waiting for transfers between devices: 3.58 us -> 15 us  [swapped(): return lax.all_to_all(x, axis, split_axis=0, concat_axis=0, tiled=True)]
    ppermute x6, waiting for transfers between devices: 18.5 us -> 8.4 us  [shifted(): return lax.ppermute(x, axis, [(i, (i + by) % count) for i in range(count)])]
    ppermute x6, waiting for transfers between devices: 3.88 us -> 12.6 us  [the longest x2 11.8 us: backward(): from_cross = lax.ppermute(to_cross, ('xh', 'co'), CROSS)]
    ppermute x1, starting transfers between devices: 2.82 us -> 0.49 us  [per_device(): mate = lax.ppermute(mine, 'co', SWAP)]
  transfers between devices with their start and end apart: 25 -> 25, of which waited for: 12 -> 14; matrix products, arithmetic and copies ran while one was open for 5% -> 4% of each run, Pallas kernels for 20% -> 19%
where the time goes in v10:
time: 162 us; the launch traced here: 161 us
  starting transfers between devices  71.2 us (44%)
  Pallas kernels  38.2 us (24%)
  waiting for transfers between devices  38.1 us (24%)
  other arithmetic  8.93 us (6%)
  local copies, waits for them, and re-layouts  3.1 us (2%)
    all_to_all x4, starting transfers between devices, swapped(): return lax.all_to_all(x, axis, split_axis=0, concat_axis=0, tiled=True)  26.5 us
    all_to_all x4, waiting for transfers between devices, swapped(): return lax.all_to_all(x, axis, split_axis=0, concat_axis=0, tiled=True)  15 us
    pallas_call x2, Pallas kernels, attention_backward(): pl.pallas_call(backward_kernel, grid_spec=pltpu.PrefetchScalarGridSpec(nu...  12.3 us
    ppermute x2, waiting for transfers between devices, backward(): from_cross = lax.ppermute(to_cross, ('xh', 'co'), CROSS)  11.8 us
    ppermute x1, starting transfers between devices, per_device(): w_mate = lax.ppermute(w_mine, 'co', SWAP)  11.4 us
    ppermute x6, starting transfers between devices, shifted(): return lax.ppermute(x, axis, [(i, (i + by) % count) for i in range(count)])  9.13 us
    ppermute x2, starting transfers between devices, backward(): from_cross = lax.ppermute(to_cross, ('xh', 'co'), CROSS)  9.05 us
    ppermute x6, waiting for transfers between devices, shifted(): return lax.ppermute(x, axis, [(i, (i + by) % count) for i in range(count)])  8.4 us
  transfers between devices with their start and end apart: 25, of which 14 were waited for; matrix products, arithmetic and copies ran while one was open for 4% of the time, Pallas kernels for 19%

profile of v10, /device:TPU:1, one launch (start us, length us, event | category | flops | bytes accessed | tf_op | source)
XLA Modules:
  0.0 161.1 jit_solution(11433031504858674842)
XLA Ops:
  1.8 2.4 %shard_map.85 = bf16[8,48,768]{2,1,0:T(8,128)(2,1)} custom-call(s32[4]{0:T(128)} %pad_add_fusion.scalar_ref, bf16[32,48,1536]{2,1,0:T(8,128)(2,1)} %weight_ref.1), custom_call_target="tpu_custom_call" | custom-call | flops 1000 | bytes 1000 | tf_op jit(solution)/shard_map/pallas_call | solution.py:164
  4.2 9.1 %all-to-all-start.1 = ((bf16[8,48,768]{2,1,0:T(8,128)(2,1)}), bf16[8,48,768]{2,1,0:T(8,128)(2,1)}, u32[]{:S(2)}, u32[]{:S(2)}) async-start(bf16[8,48,768]{2,1,0:T(8,128)(2,1)} %shard_map.85), calls=%async_computation.1 | async-start | bytes 1179648 | tf_op jit(solution)/shard_map/all_to_all | solution.py:281
  13.4 2.7 %collective-permute-start.5 = (bf16[192,1536]{1,0:T(8,128)(2,1)}, bf16[192,1536]{1,0:T(8,128)(2,1)S(1)}, u32[]{:S(2)}, u32[]{:S(2)}) collective-permute-start(bf16[192,1536]{1,0:T(8,128)(2,1)} %bitcast.6.refs_0_.refs_4_), channel_id=1, source_target_pairs={{0,3},{1,0},{2,1},{3,2},{4,7},{5,4},{6,5},{7,6},{8,11},{9,8},{10,9... | collective-permute-start | bytes 1769480 | tf_op jit(solution)/shard_map/ppermute | solution.py:277
  17.2 6.3 %collective-permute-start.2 = (bf16[2,192,1536]{2,1,0:T(8,128)(2,1)S(1)}, bf16[2,192,1536]{2,1,0:T(8,128)(2,1)S(1)}, u32[]{:S(2)}, u32[]{:S(2)}) collective-permute-start(bf16[2,192,1536]{2,1,0:T(8,128)(2,1)S(1)} %bitcast.21), channel_id=1, source_target_pairs={{32,64},{64,32},{33,65},{65,33},{34,66},{66,34},{35,67},{67,35},{3... | collective-permute-start | bytes 3538952 | tf_op jit(solution)/shard_map/ppermute | solution.py:302
  23.6 5.6 %collective-permute-done.5.refs_3_.refs_7_ = bf16[192,1536]{1,0:T(8,128)(2,1)S(1)} collective-permute-done((bf16[192,1536]{1,0:T(8,128)(2,1)}, bf16[192,1536]{1,0:T(8,128)(2,1)S(1)}, u32[]{:S(2)}, u32[]{:S(2)}) %collective-permute-start.5) | collective-permute-done | bytes 589856 | tf_op jit(solution)/shard_map/ppermute | solution.py:277
  32.9 11.4 %collective-permute-start.6 = (bf16[384,768]{1,0:T(8,128)(2,1)}, bf16[384,768]{1,0:T(8,128)(2,1)S(1)}, u32[]{:S(2)}, u32[]{:S(2)}) collective-permute-start(bf16[384,768]{1,0:T(8,128)(2,1)} %bitcast.7.refs_4_), channel_id=1, source_target_pairs={{0,32},{32,0},{1,33},{33,1},{2,34},{34,2},{3,35},{35,3},{4,36},{36... | collective-permute-start | bytes 1769480 | tf_op jit(solution)/shard_map/ppermute | solution.py:308
  46.9 4.9 %shard_map.86 = (bf16[4,384,256]{2,1,0:T(8,128)(2,1)}, bf16[384,1536]{1,0:T(8,128)(2,1)}) custom-call(s32[4]{0:T(128)} %pad_add_fusion.scalar_ref, bf16[192,1536]{1,0:T(8,128)(2,1)} %bitcast.6.refs_0_.refs_4_, bf16[192,1536]{1,0:T(8,128)(2,1)} %collective-permute-done.3.refs_1_.refs_5_, bf16[192,1536]{1,0:T(8,128)(2,1)} %collective-permute-done.4.refs_2_.refs_6_, ...), custom_call_target="tpu_custom_call" | custom-call | flops 1000 | bytes 1000 | tf_op jit(solution)/shard_map/pallas_call | solution.py:198
  51.8 4.6 %all-to-all-start.2 = ((bf16[4,384,256]{2,1,0:T(8,128)(2,1)}), bf16[4,384,256]{2,1,0:T(8,128)(2,1)}, u32[]{:S(2)}, u32[]{:S(2)}) async-start(bf16[4,384,256]{2,1,0:T(8,128)(2,1)} %get-tuple-element.46), calls=%async_computation.2 | async-start | bytes 1572864 | tf_op jit(solution)/shard_map/all_to_all | solution.py:281
  57.8 8.1 %shard_map.84 = (bf16[192,1536]{1,0:T(8,128)(2,1)}, bf16[4,8,48,256]{3,2,1,0:T(8,128)(2,1)}, bf16[12,192,768]{2,1,0:T(8,128)(2,1)}) custom-call(s32[4]{0:T(128)} %pad_add_fusion.scalar_ref, bf16[192,1536]{1,0:T(8,128)(2,1)} %bitcast.24, bf16[2,192,1536]{2,1,0:T(8,128)(2,1)} %bitcast.18, bf16[2,192,1536]{2,1,0:T(8,128)(2,1)} %collective-permute-done.time_ref, ...), custom_call_target="tpu_custom_call" | custom-call | flops 1000 | bytes 1000 | tf_op jit(solution)/shard_map/pallas_call | solution.py:122
  65.9 2.3 %all-to-all-done.2 = bf16[4,384,256]{2,1,0:T(8,128)(2,1)} async-done(((bf16[4,384,256]{2,1,0:T(8,128)(2,1)}), bf16[4,384,256]{2,1,0:T(8,128)(2,1)}, u32[]{:S(2)}, u32[]{:S(2)}) %all-to-all-start.2) | async-done | bytes 786464 | tf_op jit(solution)/shard_map/all_to_all | solution.py:281
  68.2 5.9 %all-to-all-start = ((bf16[4,384,256]{2,1,0:T(8,128)(2,1)}), bf16[4,384,256]{2,1,0:T(8,128)(2,1)S(1)}, u32[]{:S(2)}, u32[]{:S(2)}) async-start(bf16[4,384,256]{2,1,0:T(8,128)(2,1)} %bitcast.27), calls=%async_computation | async-start | bytes 1572864 | tf_op jit(solution)/shard_map/all_to_all | solution.py:281
  74.1 6.1 %shard_map.88 = (bf16[192,768]{1,0:T(8,128)(2,1)}, bf16[2,192,768]{2,1,0:T(8,128)(2,1)}, bf16[2,192,768]{2,1,0:T(8,128)(2,1)}, bf16[2,192,768]{2,1,0:T(8,128)(2,1)}, bf16[2,192,768]{2,1,0:T(8,128)(2,1)}) custom-call(s32[4]{0:T(128)} %pad_add_fusion.scalar_ref, bf16[192,1536]{1,0:T(8,128)(2,1)} %bitcast.25, bf16[2,192,1536]{2,1,0:T(8,128)(2,1)} %bitcast.19, ...), custom_call_target="tpu_custom_call" | custom-call | flops 1000 | bytes 1000 | tf_op jit(solution)/shard_map/pallas_call | solution.py:142
  80.2 6.2 %shard_map.87 = (bf16[192,768]{1,0:T(8,128)(2,1)}, bf16[2,192,768]{2,1,0:T(8,128)(2,1)}, bf16[2,192,768]{2,1,0:T(8,128)(2,1)}, bf16[2,192,768]{2,1,0:T(8,128)(2,1)}, bf16[2,192,768]{2,1,0:T(8,128)(2,1)}) custom-call(s32[4]{0:T(128)} %pad_add_fusion.scalar_ref, bf16[192,1536]{1,0:T(8,128)(2,1)} %bitcast.26, bf16[2,192,1536]{2,1,0:T(8,128)(2,1)} %bitcast.20, ...), custom_call_target="tpu_custom_call" | custom-call | flops 1000 | bytes 1000 | tf_op jit(solution)/shard_map/pallas_call | solution.py:142
  87.3 5.6 %shard_map.89 = (bf16[384,768]{1,0:T(8,128)(2,1)}, bf16[384,768]{1,0:T(8,128)(2,1)}) custom-call(s32[4]{0:T(128)} %pad_add_fusion.scalar_ref, bf16[4,384,256]{2,1,0:T(8,128)(2,1)} %copy-done.3, bf16[192,1536]{1,0:T(8,128)(2,1)} %bitcast.6.refs_0_.refs_4_, bf16[192,1536]{1,0:T(8,128)(2,1)} %collective-permute-done.3.refs_1_.refs_5_, ...), custom_call_target="tpu_custom_call" | custom-call | flops 1000 | bytes 1000 | tf_op jit(solution)/shard_map/pallas_call | solution.py:233
  94.0 4.9 %shard_map.90 = (bf16[192,1536]{1,0:T(8,128)(2,1)}, bf16[192,1536]{1,0:T(8,128)(2,1)}, bf16[192,1536]{1,0:T(8,128)(2,1)}, bf16[192,1536]{1,0:T(8,128)(2,1)}) custom-call(s32[4]{0:T(128)} %pad_add_fusion.scalar_ref, bf16[4,384,256]{2,1,0:T(8,128)(2,1)} %copy-done.3, bf16[384,1536]{1,0:T(8,128)(2,1)} %get-tuple-element.56.weight_ref), custom_call_target="tpu_custom_call" | custom-call | flops 1000 | bytes 1000 | tf_op jit(solution)/shard_map/pallas_call | solution.py:257
  99.9 6.9 %all-to-all-start.3 = ((bf16[8,48,768]{2,1,0:T(8,128)(2,1)}), bf16[8,48,768]{2,1,0:T(8,128)(2,1)S(1)}, u32[]{:S(2)}, u32[]{:S(2)}) async-start(bf16[8,48,768]{2,1,0:T(8,128)(2,1)} %bitcast.9), calls=%async_computation.3 | async-start | bytes 1179648 | tf_op jit(solution)/shard_map/all_to_all | solution.py:281
  108.0 2.8 %collective-permute-start.12 = (bf16[2,192,768]{2,1,0:T(8,128)(2,1)}, bf16[2,192,768]{2,1,0:T(8,128)(2,1)S(1)}, u32[]{:S(2)}, u32[]{:S(2)}) collective-permute-start(bf16[2,192,768]{2,1,0:T(8,128)(2,1)} %get-tuple-element.67), channel_id=1, source_target_pairs={{32,64},{64,32},{33,65},{65,33},{34,66},{66,34},{35,67},{67,35},{3... | collective-permute-start | bytes 1769480 | tf_op jit(solution)/shard_map/ppermute | solution.py:324
  111.1 3.0 %collective-permute-start.8 = (bf16[192,1536]{1,0:T(8,128)(2,1)}, bf16[192,1536]{1,0:T(8,128)(2,1)S(1)}, u32[]{:S(2)}, u32[]{:S(2)}) collective-permute-start(bf16[192,1536]{1,0:T(8,128)(2,1)} %get-tuple-element.62), channel_id=1, source_target_pairs={{0,3},{1,0},{2,1},{3,2},{4,7},{5,4},{6,5},{7,6},{8,11},{9,8},{10,9... | collective-permute-start | bytes 1769480 | tf_op jit(solution)/shard_map/ppermute | solution.py:277
  114.7 11.5 %all-to-all-done.3 = bf16[8,48,768]{2,1,0:T(8,128)(2,1)S(1)} async-done(((bf16[8,48,768]{2,1,0:T(8,128)(2,1)}), bf16[8,48,768]{2,1,0:T(8,128)(2,1)S(1)}, u32[]{:S(2)}, u32[]{:S(2)}) %all-to-all-start.3) | async-done | bytes 589856 | tf_op jit(solution)/shard_map/all_to_all | solution.py:281
  126.9 1.7 %collective-permute-start.10 = (bf16[192,1536]{1,0:T(8,128)(2,1)}, bf16[192,1536]{1,0:T(8,128)(2,1)S(1)}, u32[]{:S(2)}, u32[]{:S(2)}) collective-permute-start(bf16[192,1536]{1,0:T(8,128)(2,1)} %get-tuple-element.64), channel_id=1, source_target_pairs={{0,1},{1,2},{2,3},{3,0},{4,5},{5,6},{6,7},{7,4},{8,9},{9,10},{10,1... | collective-permute-start | bytes 1769480 | tf_op jit(solution)/shard_map/ppermute | solution.py:277
  128.9 1.9 %maximum_bitcast_fusion.1 = bf16[1,1,1,192,1536]{4,3,2,1,0:T(8,128)(2,1)} fusion(bf16[192,768]{1,0:T(8,128)(2,1)} %get-tuple-element.75, bf16[192,768]{1,0:T(8,128)(2,1)} %get-tuple-element.74), kind=kLoop, calls=%fused_computation.6 | loop fusion | flops 1179648 | bytes 1179648 | tf_op jit(solution)/shard_map/reshape | solution.py:361
  130.8 2.7 %collective-permute-start.18 = (bf16[48,768]{1,0:T(8,128)(2,1)S(1)}, bf16[48,768]{1,0:T(8,128)(2,1)S(1)}, u32[]{:S(2)}, u32[]{:S(2)}) collective-permute-start(bf16[48,768]{1,0:T(8,128)(2,1)S(1)} %copy-done.10), channel_id=1, source_target_pairs={{0,64},{64,0},{1,65},{65,1},{2,66},{66,2},{3,67},{67,3},{4,68},{68... | collective-permute-start | bytes 221192 | tf_op jit(solution)/shard_map/ppermute | solution.py:341
  137.8 6.2 %collective-permute-start.16 = (bf16[2,192,768]{2,1,0:T(8,128)(2,1)S(1)}, bf16[2,192,768]{2,1,0:T(8,128)(2,1)S(1)}, u32[]{:S(2)}, u32[]{:S(2)}) collective-permute-start(bf16[2,192,768]{2,1,0:T(8,128)(2,1)S(1)} %copy-done.12), channel_id=1, source_target_pairs={{32,64},{64,32},{33,65},{65,33},{34,66},{66,34},{35,67},{67,35},{3... | collective-permute-start | bytes 1769480 | tf_op jit(solution)/shard_map/ppermute | solution.py:324
  147.9 11.7 %collective-permute-done.16 = bf16[2,192,768]{2,1,0:T(8,128)(2,1)S(1)} collective-permute-done((bf16[2,192,768]{2,1,0:T(8,128)(2,1)S(1)}, bf16[2,192,768]{2,1,0:T(8,128)(2,1)S(1)}, u32[]{:S(2)}, u32[]{:S(2)}) %collective-permute-start.16) | collective-permute-done | bytes 589856 | tf_op jit(solution)/shard_map/ppermute | solution.py:324
  (72 shorter events, 24.9 us)
Async XLA Ops:
  4.2 28.6 %all-to-all-start.1 = ((bf16[8,48,768]{2,1,0:T(8,128)(2,1)}), bf16[8,48,768]{2,1,0:T(8,128)(2,1)}, u32[]{:S(2)}, u32[]{:S(2)}) async-start(bf16[8,48,768]{2,1,0:T(8,128)(2,1)} %shard_map.85), calls=%async_computation.1 | async-start | bytes 1179648 | tf_op jit(solution)/shard_map/all_to_all | solution.py:281
  13.4 15.8 %collective-permute-start.5 = (bf16[192,1536]{1,0:T(8,128)(2,1)}, bf16[192,1536]{1,0:T(8,128)(2,1)S(1)}, u32[]{:S(2)}, u32[]{:S(2)}) collective-permute-start(bf16[192,1536]{1,0:T(8,128)(2,1)} %bitcast.6.refs_0_.refs_4_), channel_id=1, source_target_pairs={{0,3},{1,0},{2,1},{3,2},{4,7},{5,4},{6,5},{7,6},{8,11},{9,8},{10,9... | collective-permute-start | bytes 1769480 | tf_op jit(solution)/shard_map/ppermute | solution.py:277
  16.1 15.5 %collective-permute-start.4 = (bf16[192,1536]{1,0:T(8,128)(2,1)}, bf16[192,1536]{1,0:T(8,128)(2,1)}, u32[]{:S(2)}, u32[]{:S(2)}) collective-permute-start(bf16[192,1536]{1,0:T(8,128)(2,1)} %bitcast.6.refs_0_.refs_4_), channel_id=1, source_target_pairs={{0,2},{1,3},{2,0},{3,1},{4,6},{5,7},{6,4},{7,5},{8,10},{9,11},{10,... | collective-permute-start | bytes 1769480 | tf_op jit(solution)/shard_map/ppermute | solution.py:277
  16.5 29.4 %collective-permute-start.3 = (bf16[192,1536]{1,0:T(8,128)(2,1)}, bf16[192,1536]{1,0:T(8,128)(2,1)}, u32[]{:S(2)}, u32[]{:S(2)}) collective-permute-start(bf16[192,1536]{1,0:T(8,128)(2,1)} %bitcast.6.refs_0_.refs_4_), channel_id=1, source_target_pairs={{0,1},{1,2},{2,3},{3,0},{4,5},{5,6},{6,7},{7,4},{8,9},{9,10},{10,1... | collective-permute-start | bytes 1769480 | tf_op jit(solution)/shard_map/ppermute | solution.py:277
  17.2 39.2 %collective-permute-start.2 = (bf16[2,192,1536]{2,1,0:T(8,128)(2,1)S(1)}, bf16[2,192,1536]{2,1,0:T(8,128)(2,1)S(1)}, u32[]{:S(2)}, u32[]{:S(2)}) collective-permute-start(bf16[2,192,1536]{2,1,0:T(8,128)(2,1)S(1)} %bitcast.21), channel_id=1, source_target_pairs={{32,64},{64,32},{33,65},{65,33},{34,66},{66,34},{35,67},{67,35},{3... | collective-permute-start | bytes 3538952 | tf_op jit(solution)/shard_map/ppermute | solution.py:302
  23.5 32.9 %collective-permute-start.1 = (bf16[2,192,1536]{2,1,0:T(8,128)(2,1)S(1)}, bf16[2,192,1536]{2,1,0:T(8,128)(2,1)S(1)}, u32[]{:S(2)}, u32[]{:S(2)}) collective-permute-start(bf16[2,192,1536]{2,1,0:T(8,128)(2,1)S(1)} %bitcast.22), channel_id=1, source_target_pairs={{0,32},{32,0},{1,33},{33,1},{2,34},{34,2},{3,35},{35,3},{4,36},{36... | collective-permute-start | bytes 3538952 | tf_op jit(solution)/shard_map/ppermute | solution.py:303
  29.2 27.2 %collective-permute-start = (bf16[2,192,1536]{2,1,0:T(8,128)(2,1)S(1)}, bf16[2,192,1536]{2,1,0:T(8,128)(2,1)}, u32[]{:S(2)}, u32[]{:S(2)}) collective-permute-start(bf16[2,192,1536]{2,1,0:T(8,128)(2,1)S(1)} %bitcast.23), channel_id=1, source_target_pairs={{0,128},{128,0},{1,129},{129,1},{2,130},{130,2},{3,131},{131,3},{4... | collective-permute-start | bytes 3538952 | tf_op jit(solution)/shard_map/ppermute | solution.py:301
  32.9 13.2 %collective-permute-start.6 = (bf16[384,768]{1,0:T(8,128)(2,1)}, bf16[384,768]{1,0:T(8,128)(2,1)S(1)}, u32[]{:S(2)}, u32[]{:S(2)}) collective-permute-start(bf16[384,768]{1,0:T(8,128)(2,1)} %bitcast.7.refs_4_), channel_id=1, source_target_pairs={{0,32},{32,0},{1,33},{33,1},{2,34},{34,2},{3,35},{35,3},{4,36},{36... | collective-permute-start | bytes 1769480 | tf_op jit(solution)/shard_map/ppermute | solution.py:308
  51.8 16.4 %all-to-all-start.2 = ((bf16[4,384,256]{2,1,0:T(8,128)(2,1)}), bf16[4,384,256]{2,1,0:T(8,128)(2,1)}, u32[]{:S(2)}, u32[]{:S(2)}) async-start(bf16[4,384,256]{2,1,0:T(8,128)(2,1)} %get-tuple-element.46), calls=%async_computation.2 | async-start | bytes 1572864 | tf_op jit(solution)/shard_map/all_to_all | solution.py:281
  68.2 18.2 %all-to-all-start = ((bf16[4,384,256]{2,1,0:T(8,128)(2,1)}), bf16[4,384,256]{2,1,0:T(8,128)(2,1)S(1)}, u32[]{:S(2)}, u32[]{:S(2)}) async-start(bf16[4,384,256]{2,1,0:T(8,128)(2,1)} %bitcast.27), calls=%async_computation | async-start | bytes 1572864 | tf_op jit(solution)/shard_map/all_to_all | solution.py:281
  92.9 6.0 %collective-permute-start.7 = (bf16[384,768]{1,0:T(8,128)(2,1)}, bf16[384,768]{1,0:T(8,128)(2,1)S(1)}, u32[]{:S(2)}, u32[]{:S(2)}) collective-permute-start(bf16[384,768]{1,0:T(8,128)(2,1)} %get-tuple-element.54), channel_id=1, source_target_pairs={{0,32},{32,0},{1,33},{33,1},{2,34},{34,2},{3,35},{35,3},{4,36},{36... | collective-permute-start | bytes 1769480 | tf_op jit(solution)/shard_map/ppermute | solution.py:332
  99.9 26.3 %all-to-all-start.3 = ((bf16[8,48,768]{2,1,0:T(8,128)(2,1)}), bf16[8,48,768]{2,1,0:T(8,128)(2,1)S(1)}, u32[]{:S(2)}, u32[]{:S(2)}) async-start(bf16[8,48,768]{2,1,0:T(8,128)(2,1)} %bitcast.9), calls=%async_computation.3 | async-start | bytes 1179648 | tf_op jit(solution)/shard_map/all_to_all | solution.py:281
  106.8 20.1 %collective-permute-start.11 = (bf16[2,192,768]{2,1,0:T(8,128)(2,1)}, bf16[2,192,768]{2,1,0:T(8,128)(2,1)S(1)}, u32[]{:S(2)}, u32[]{:S(2)}) collective-permute-start(bf16[2,192,768]{2,1,0:T(8,128)(2,1)} %get-tuple-element.66), channel_id=1, source_target_pairs={{0,128},{128,0},{1,129},{129,1},{2,130},{130,2},{3,131},{131,3},{4... | collective-permute-start | bytes 1769480 | tf_op jit(solution)/shard_map/ppermute | solution.py:323
  108.0 20.7 %collective-permute-start.12 = (bf16[2,192,768]{2,1,0:T(8,128)(2,1)}, bf16[2,192,768]{2,1,0:T(8,128)(2,1)S(1)}, u32[]{:S(2)}, u32[]{:S(2)}) collective-permute-start(bf16[2,192,768]{2,1,0:T(8,128)(2,1)} %get-tuple-element.67), channel_id=1, source_target_pairs={{32,64},{64,32},{33,65},{65,33},{34,66},{66,34},{35,67},{67,35},{3... | collective-permute-start | bytes 1769480 | tf_op jit(solution)/shard_map/ppermute | solution.py:324
  110.8 17.9 %collective-permute-start.13 = (bf16[2,192,768]{2,1,0:T(8,128)(2,1)}, bf16[2,192,768]{2,1,0:T(8,128)(2,1)}, u32[]{:S(2)}, u32[]{:S(2)}) collective-permute-start(bf16[2,192,768]{2,1,0:T(8,128)(2,1)} %get-tuple-element.68), channel_id=1, source_target_pairs={{0,32},{32,0},{1,33},{33,1},{2,34},{34,2},{3,35},{35,3},{4,36},{36... | collective-permute-start | bytes 1769480 | tf_op jit(solution)/shard_map/ppermute | solution.py:328
  111.1 32.9 %collective-permute-start.8 = (bf16[192,1536]{1,0:T(8,128)(2,1)}, bf16[192,1536]{1,0:T(8,128)(2,1)S(1)}, u32[]{:S(2)}, u32[]{:S(2)}) collective-permute-start(bf16[192,1536]{1,0:T(8,128)(2,1)} %get-tuple-element.62), channel_id=1, source_target_pairs={{0,3},{1,0},{2,1},{3,2},{4,7},{5,4},{6,5},{7,6},{8,11},{9,8},{10,9... | collective-permute-start | bytes 1769480 | tf_op jit(solution)/shard_map/ppermute | solution.py:277
  114.2 30.0 %collective-permute-start.9 = (bf16[192,1536]{1,0:T(8,128)(2,1)}, bf16[192,1536]{1,0:T(8,128)(2,1)S(1)}, u32[]{:S(2)}, u32[]{:S(2)}) collective-permute-start(bf16[192,1536]{1,0:T(8,128)(2,1)} %get-tuple-element.63), channel_id=1, source_target_pairs={{0,2},{1,3},{2,0},{3,1},{4,6},{5,7},{6,4},{7,5},{8,10},{9,11},{10,... | collective-permute-start | bytes 1769480 | tf_op jit(solution)/shard_map/ppermute | solution.py:277
  126.9 17.8 %collective-permute-start.10 = (bf16[192,1536]{1,0:T(8,128)(2,1)}, bf16[192,1536]{1,0:T(8,128)(2,1)S(1)}, u32[]{:S(2)}, u32[]{:S(2)}) collective-permute-start(bf16[192,1536]{1,0:T(8,128)(2,1)} %get-tuple-element.64), channel_id=1, source_target_pairs={{0,1},{1,2},{2,3},{3,0},{4,5},{5,6},{6,7},{7,4},{8,9},{9,10},{10,1... | collective-permute-start | bytes 1769480 | tf_op jit(solution)/shard_map/ppermute | solution.py:277
  128.7 4.9 %collective-permute-start.19 = (bf16[48,768]{1,0:T(8,128)(2,1)}, bf16[48,768]{1,0:T(8,128)(2,1)S(1)}, u32[]{:S(2)}, u32[]{:S(2)}) collective-permute-start(bf16[48,768]{1,0:T(8,128)(2,1)} %reduce_sum.12), channel_id=1, source_target_pairs={{0,192},{64,128},{128,64},{192,0},{1,193},{65,129},{129,65},{193,1... | collective-permute-start | bytes 221192 | tf_op jit(solution)/shard_map/ppermute | solution.py:342
  130.8 4.7 %collective-permute-start.18 = (bf16[48,768]{1,0:T(8,128)(2,1)S(1)}, bf16[48,768]{1,0:T(8,128)(2,1)S(1)}, u32[]{:S(2)}, u32[]{:S(2)}) collective-permute-start(bf16[48,768]{1,0:T(8,128)(2,1)S(1)} %copy-done.10), channel_id=1, source_target_pairs={{0,64},{64,0},{1,65},{65,1},{2,66},{66,2},{3,67},{67,3},{4,68},{68... | collective-permute-start | bytes 221192 | tf_op jit(solution)/shard_map/ppermute | solution.py:341
  133.7 4.1 %collective-permute-start.14 = (bf16[48,768]{1,0:T(8,128)(2,1)S(1)}, bf16[48,768]{1,0:T(8,128)(2,1)S(1)}, u32[]{:S(2)}, u32[]{:S(2)}) collective-permute-start(bf16[48,768]{1,0:T(8,128)(2,1)S(1)} %copy-done.10), channel_id=1, source_target_pairs={{0,128},{128,0},{1,129},{129,1},{2,130},{130,2},{3,131},{131,3},{4... | collective-permute-start | bytes 221192 | tf_op jit(solution)/shard_map/ppermute | solution.py:340
  135.6 12.4 %collective-permute-start.15 = (bf16[2,192,768]{2,1,0:T(8,128)(2,1)S(1)}, bf16[2,192,768]{2,1,0:T(8,128)(2,1)S(1)}, u32[]{:S(2)}, u32[]{:S(2)}) collective-permute-start(bf16[2,192,768]{2,1,0:T(8,128)(2,1)S(1)} %copy-done.13), channel_id=1, source_target_pairs={{0,128},{128,0},{1,129},{129,1},{2,130},{130,2},{3,131},{131,3},{4... | collective-permute-start | bytes 1769480 | tf_op jit(solution)/shard_map/ppermute | solution.py:323
  137.8 21.9 %collective-permute-start.16 = (bf16[2,192,768]{2,1,0:T(8,128)(2,1)S(1)}, bf16[2,192,768]{2,1,0:T(8,128)(2,1)S(1)}, u32[]{:S(2)}, u32[]{:S(2)}) collective-permute-start(bf16[2,192,768]{2,1,0:T(8,128)(2,1)S(1)} %copy-done.12), channel_id=1, source_target_pairs={{32,64},{64,32},{33,65},{65,33},{34,66},{66,34},{35,67},{67,35},{3... | collective-permute-start | bytes 1769480 | tf_op jit(solution)/shard_map/ppermute | solution.py:324
  144.1 15.6 %collective-permute-start.17 = (bf16[2,192,768]{2,1,0:T(8,128)(2,1)S(1)}, bf16[2,192,768]{2,1,0:T(8,128)(2,1)S(1)}, u32[]{:S(2)}, u32[]{:S(2)}) collective-permute-start(bf16[2,192,768]{2,1,0:T(8,128)(2,1)S(1)} %copy-done.11), channel_id=1, source_target_pairs={{0,32},{32,0},{1,33},{33,1},{2,34},{34,2},{3,35},{35,3},{4,36},{36... | collective-permute-start | bytes 1769480 | tf_op jit(solution)/shard_map/ppermute | solution.py:352
  (15 other events, 97.8 us)

commit v11 on v8

--- a/solution.py
+++ b/solution.py
@@ -328,13 +328,14 @@
         return gq, own, terms
 
     gq_0, own_0, terms_0 = backward(0)
-    gq_1, own_1, terms_1 = backward(1)
-    atts, gq_0, gq_1 = lax.optimization_barrier((atts, gq_0, gq_1))
+    atts, gq_0 = lax.optimization_barrier((atts, gq_0))
     grad_mine, grad_mate = weight_gradient(scalars, atts, ups)
     from_mate = lax.ppermute(grad_mate, "co", SWAP)
+    atts, w_rows, grad_mine = lax.optimization_barrier((atts, w_rows, grad_mine))
+    mixed = mixed_parts(scalars, atts, w_rows)
     grad = (grad_mine.astype(F32) + from_mate.astype(F32)).astype(BF16).reshape(nz, rows, half)
-    atts, w_rows, grad = lax.optimization_barrier((atts, w_rows, grad))
-    mixed = mixed_parts(scalars, atts, w_rows)
+    probs, grad, mixed = lax.optimization_barrier((probs, grad, mixed))
+    gq_1, own_1, terms_1 = backward(1)
     gkv_parts = [
         own.astype(F32) + sum(t.astype(F32) for t in terms)
         for own, terms in ((own_0, terms_0), (own_1, terms_1))
@@ -350,8 +351,9 @@
         [jnp.where(first, mine, mate), jnp.where(first, mate, mine)], axis=1
     )
 
-    back = [shifted(mixed[k], "y", -k).astype(F32) for k in (1, 2, 3)]
-    mixed = (mixed[0].astype(F32) + sum(back)).astype(BF16)
+    back = [shifted(mixed[k], "y", -k) for k in (1, 2, 3)]
+    back, _ = lax.optimization_barrier((back, x_near))
+    mixed = (mixed[0].astype(F32) + sum(b.astype(F32) for b in back)).astype(BF16)
     grad_q = jnp.concatenate(gq_parts, axis=1)
     grad_kv = jnp.concatenate([p.astype(BF16) for p in gkv_parts], axis=2)
     return (

time: 157 us -> 159 us (1.013)
  waiting for transfers between devices: 32.8 us -> 38.5 us
  starting transfers between devices: 69.8 us -> 66.4 us
    all_to_all x4, waiting for transfers between devices: 3.6 us -> 8.75 us  [swapped(): return lax.all_to_all(x, axis, split_axis=0, concat_axis=0, tiled=True)]
    ppermute x6, starting transfers between devices: 8.92 us -> 6.12 us  [shifted(): return lax.ppermute(x, axis, [(i, (i + by) % count) for i in range(count)])]
    ppermute x2, waiting for transfers between devices: 0.01 us -> 2.73 us  [backward(): lax.ppermute(to_time, 'xl', SWAP)]
    ppermute x6, waiting for transfers between devices: 16.5 us -> 14.2 us  [shifted(): return lax.ppermute(x, axis, [(i, (i + by) % count) for i in range(count)])]
  transfers between devices with their start and end apart: 25 -> 25, of which waited for: 14 -> 13; matrix products, arithmetic and copies ran while one was open for 6% -> 5% of each run, Pallas kernels for 20% -> 19%
where the time goes in v11:
time: 159 us; the launch traced here: 158 us
  starting transfers between devices  66.4 us (42%)
  waiting for transfers between devices  38.5 us (24%)
  Pallas kernels  38.3 us (24%)
  other arithmetic  9.83 us (6%)
  local copies, waits for them, and re-layouts  3.18 us (2%)
    all_to_all x4, starting transfers between devices, swapped(): return lax.all_to_all(x, axis, split_axis=0, concat_axis=0, tiled=True)  26.5 us
    ppermute x6, waiting for transfers between devices, shifted(): return lax.ppermute(x, axis, [(i, (i + by) % count) for i in range(count)])  14.2 us
    pallas_call x2, Pallas kernels, attention_backward(): pl.pallas_call(backward_kernel, grid_spec=pltpu.PrefetchScalarGridSpec(nu...  12.3 us
    ppermute x1, starting transfers between devices, per_device(): w_mate = lax.ppermute(w_mine, 'co', SWAP)  11.4 us
    ppermute x2, waiting for transfers between devices, backward(): lax.ppermute(to_cross, ('xh', 'co'), CROSS)  9.66 us
    all_to_all x4, waiting for transfers between devices, swapped(): return lax.all_to_all(x, axis, split_axis=0, concat_axis=0, tiled=True)  8.75 us
    pallas_call x1, Pallas kernels, attention_forward(): pl.pallas_call(forward_kernel, grid_spec=pltpu.PrefetchScalarGridSpec(num...  8.07 us
    ppermute x2, starting transfers between devices, backward(): lax.ppermute(to_cross, ('xh', 'co'), CROSS)  7.95 us
  transfers between devices with their start and end apart: 25, of which 13 were waited for; matrix products, arithmetic and copies ran while one was open for 5% of the time, Pallas kernels for 19%

profile of v11, /device:TPU:1, one launch (start us, length us, event | category | flops | bytes accessed | tf_op | source)
XLA Modules:
  0.0 157.7 jit_solution(7375859107412836973)
XLA Ops:
  1.8 2.4 %shard_map.85 = bf16[8,48,768]{2,1,0:T(8,128)(2,1)} custom-call(s32[4]{0:T(128)} %pad_add_fusion.scalar_ref, bf16[32,48,1536]{2,1,0:T(8,128)(2,1)} %weight_ref.1), custom_call_target="tpu_custom_call" | custom-call | flops 1000 | bytes 1000 | tf_op jit(solution)/shard_map/pallas_call | solution.py:164
  4.2 9.1 %all-to-all-start.1 = ((bf16[8,48,768]{2,1,0:T(8,128)(2,1)}), bf16[8,48,768]{2,1,0:T(8,128)(2,1)}, u32[]{:S(2)}, u32[]{:S(2)}) async-start(bf16[8,48,768]{2,1,0:T(8,128)(2,1)} %shard_map.85), calls=%async_computation.1 | async-start | bytes 1179648 | tf_op jit(solution)/shard_map/all_to_all | solution.py:281
  13.4 2.7 %collective-permute-start.5 = (bf16[192,1536]{1,0:T(8,128)(2,1)}, bf16[192,1536]{1,0:T(8,128)(2,1)S(1)}, u32[]{:S(2)}, u32[]{:S(2)}) collective-permute-start(bf16[192,1536]{1,0:T(8,128)(2,1)} %bitcast.6.refs_0_.refs_4_), channel_id=1, source_target_pairs={{0,3},{1,0},{2,1},{3,2},{4,7},{5,4},{6,5},{7,6},{8,11},{9,8},{10,9... | collective-permute-start | bytes 1769480 | tf_op jit(solution)/shard_map/ppermute | solution.py:277
  17.2 6.3 %collective-permute-start.2 = (bf16[2,192,1536]{2,1,0:T(8,128)(2,1)S(1)}, bf16[2,192,1536]{2,1,0:T(8,128)(2,1)S(1)}, u32[]{:S(2)}, u32[]{:S(2)}) collective-permute-start(bf16[2,192,1536]{2,1,0:T(8,128)(2,1)S(1)} %bitcast.21), channel_id=1, source_target_pairs={{32,64},{64,32},{33,65},{65,33},{34,66},{66,34},{35,67},{67,35},{3... | collective-permute-start | bytes 3538952 | tf_op jit(solution)/shard_map/ppermute | solution.py:302
  23.6 5.6 %collective-permute-done.5.refs_3_.refs_7_ = bf16[192,1536]{1,0:T(8,128)(2,1)S(1)} collective-permute-done((bf16[192,1536]{1,0:T(8,128)(2,1)}, bf16[192,1536]{1,0:T(8,128)(2,1)S(1)}, u32[]{:S(2)}, u32[]{:S(2)}) %collective-permute-start.5) | collective-permute-done | bytes 589856 | tf_op jit(solution)/shard_map/ppermute | solution.py:277
  32.9 11.4 %collective-permute-start.6 = (bf16[384,768]{1,0:T(8,128)(2,1)}, bf16[384,768]{1,0:T(8,128)(2,1)S(1)}, u32[]{:S(2)}, u32[]{:S(2)}) collective-permute-start(bf16[384,768]{1,0:T(8,128)(2,1)} %bitcast.7.refs_4_), channel_id=1, source_target_pairs={{0,32},{32,0},{1,33},{33,1},{2,34},{34,2},{3,35},{35,3},{4,36},{36... | collective-permute-start | bytes 1769480 | tf_op jit(solution)/shard_map/ppermute | solution.py:308
  46.9 4.9 %shard_map.86 = (bf16[4,384,256]{2,1,0:T(8,128)(2,1)}, bf16[384,1536]{1,0:T(8,128)(2,1)}) custom-call(s32[4]{0:T(128)} %pad_add_fusion.scalar_ref, bf16[192,1536]{1,0:T(8,128)(2,1)} %bitcast.6.refs_0_.refs_4_, bf16[192,1536]{1,0:T(8,128)(2,1)} %collective-permute-done.3.refs_1_.refs_5_, bf16[192,1536]{1,0:T(8,128)(2,1)} %collective-permute-done.4.refs_2_.refs_6_, ...), custom_call_target="tpu_custom_call" | custom-call | flops 1000 | bytes 1000 | tf_op jit(solution)/shard_map/pallas_call | solution.py:198
  51.8 4.6 %all-to-all-start.2 = ((bf16[4,384,256]{2,1,0:T(8,128)(2,1)}), bf16[4,384,256]{2,1,0:T(8,128)(2,1)}, u32[]{:S(2)}, u32[]{:S(2)}) async-start(bf16[4,384,256]{2,1,0:T(8,128)(2,1)} %get-tuple-element.42), calls=%async_computation.2 | async-start | bytes 1572864 | tf_op jit(solution)/shard_map/all_to_all | solution.py:281
  57.8 8.1 %shard_map.84 = (bf16[192,1536]{1,0:T(8,128)(2,1)}, bf16[4,8,48,256]{3,2,1,0:T(8,128)(2,1)}, bf16[12,192,768]{2,1,0:T(8,128)(2,1)}) custom-call(s32[4]{0:T(128)} %pad_add_fusion.scalar_ref, bf16[192,1536]{1,0:T(8,128)(2,1)} %bitcast.24, bf16[2,192,1536]{2,1,0:T(8,128)(2,1)} %bitcast.18, bf16[2,192,1536]{2,1,0:T(8,128)(2,1)} %collective-permute-done.time_ref, ...), custom_call_target="tpu_custom_call" | custom-call | flops 1000 | bytes 1000 | tf_op jit(solution)/shard_map/pallas_call | solution.py:122
  65.9 2.3 %all-to-all-done.2 = bf16[4,384,256]{2,1,0:T(8,128)(2,1)} async-done(((bf16[4,384,256]{2,1,0:T(8,128)(2,1)}), bf16[4,384,256]{2,1,0:T(8,128)(2,1)}, u32[]{:S(2)}, u32[]{:S(2)}) %all-to-all-start.2) | async-done | bytes 786464 | tf_op jit(solution)/shard_map/all_to_all | solution.py:281
  68.2 5.9 %all-to-all-start = ((bf16[4,384,256]{2,1,0:T(8,128)(2,1)}), bf16[4,384,256]{2,1,0:T(8,128)(2,1)S(1)}, u32[]{:S(2)}, u32[]{:S(2)}) async-start(bf16[4,384,256]{2,1,0:T(8,128)(2,1)} %bitcast.27), calls=%async_computation | async-start | bytes 1572864 | tf_op jit(solution)/shard_map/all_to_all | solution.py:281
  74.1 6.2 %shard_map.87 = (bf16[192,768]{1,0:T(8,128)(2,1)}, bf16[2,192,768]{2,1,0:T(8,128)(2,1)}, bf16[2,192,768]{2,1,0:T(8,128)(2,1)}, bf16[2,192,768]{2,1,0:T(8,128)(2,1)}, bf16[2,192,768]{2,1,0:T(8,128)(2,1)}) custom-call(s32[4]{0:T(128)} %pad_add_fusion.scalar_ref, bf16[192,1536]{1,0:T(8,128)(2,1)} %bitcast.25, bf16[2,192,1536]{2,1,0:T(8,128)(2,1)} %bitcast.19, ...), custom_call_target="tpu_custom_call" | custom-call | flops 1000 | bytes 1000 | tf_op jit(solution)/shard_map/pallas_call | solution.py:142
  80.3 5.1 %all-to-all-done.att_ref = bf16[4,384,256]{2,1,0:T(8,128)(2,1)S(1)} async-done(((bf16[4,384,256]{2,1,0:T(8,128)(2,1)}), bf16[4,384,256]{2,1,0:T(8,128)(2,1)S(1)}, u32[]{:S(2)}, u32[]{:S(2)}) %all-to-all-start) | async-done | bytes 786464 | tf_op jit(solution)/shard_map/all_to_all | solution.py:281
  86.3 5.6 %shard_map.88 = (bf16[384,768]{1,0:T(8,128)(2,1)}, bf16[384,768]{1,0:T(8,128)(2,1)}) custom-call(s32[4]{0:T(128)} %pad_add_fusion.scalar_ref, bf16[4,384,256]{2,1,0:T(8,128)(2,1)} %copy-done.3, bf16[192,1536]{1,0:T(8,128)(2,1)} %bitcast.6.refs_0_.refs_4_, bf16[192,1536]{1,0:T(8,128)(2,1)} %collective-permute-done.3.refs_1_.refs_5_, ...), custom_call_target="tpu_custom_call" | custom-call | flops 1000 | bytes 1000 | tf_op jit(solution)/shard_map/pallas_call | solution.py:233
  91.9 2.0 %collective-permute-start.7 = (bf16[384,768]{1,0:T(8,128)(2,1)}, bf16[384,768]{1,0:T(8,128)(2,1)S(1)}, u32[]{:S(2)}, u32[]{:S(2)}) collective-permute-start(bf16[384,768]{1,0:T(8,128)(2,1)} %get-tuple-element.48), channel_id=1, source_target_pairs={{0,32},{32,0},{1,33},{33,1},{2,34},{34,2},{3,35},{35,3},{4,36},{36... | collective-permute-start | bytes 1769480 | tf_op jit(solution)/shard_map/ppermute | solution.py:333
  95.1 5.0 %shard_map.89 = (bf16[192,1536]{1,0:T(8,128)(2,1)}, bf16[192,1536]{1,0:T(8,128)(2,1)}, bf16[192,1536]{1,0:T(8,128)(2,1)}, bf16[192,1536]{1,0:T(8,128)(2,1)}) custom-call(s32[4]{0:T(128)} %pad_add_fusion.scalar_ref, bf16[4,384,256]{2,1,0:T(8,128)(2,1)} %copy-done.3, bf16[384,1536]{1,0:T(8,128)(2,1)} %get-tuple-element.50.weight_ref), custom_call_target="tpu_custom_call" | custom-call | flops 1000 | bytes 1000 | tf_op jit(solution)/shard_map/pallas_call | solution.py:257
  101.1 6.9 %all-to-all-start.3 = ((bf16[8,48,768]{2,1,0:T(8,128)(2,1)}), bf16[8,48,768]{2,1,0:T(8,128)(2,1)S(1)}, u32[]{:S(2)}, u32[]{:S(2)}) async-start(bf16[8,48,768]{2,1,0:T(8,128)(2,1)} %bitcast.9), calls=%async_computation.3 | async-start | bytes 1179648 | tf_op jit(solution)/shard_map/all_to_all | solution.py:281
  108.0 1.9 %collective-permute-start.13 = (bf16[2,192,768]{2,1,0:T(8,128)(2,1)S(1)}, bf16[2,192,768]{2,1,0:T(8,128)(2,1)}, u32[]{:S(2)}, u32[]{:S(2)}) collective-permute-start(bf16[2,192,768]{2,1,0:T(8,128)(2,1)S(1)} %copy-done.11), channel_id=1, source_target_pairs={{32,64},{64,32},{33,65},{65,33},{34,66},{66,34},{35,67},{67,35},{3... | collective-permute-start | bytes 1769480 | tf_op jit(solution)/shard_map/ppermute | solution.py:325
  110.2 6.1 %shard_map.90 = (bf16[192,768]{1,0:T(8,128)(2,1)}, bf16[2,192,768]{2,1,0:T(8,128)(2,1)}, bf16[2,192,768]{2,1,0:T(8,128)(2,1)}, bf16[2,192,768]{2,1,0:T(8,128)(2,1)}, bf16[2,192,768]{2,1,0:T(8,128)(2,1)}) custom-call(s32[4]{0:T(128)} %pad_add_fusion.scalar_ref, bf16[192,1536]{1,0:T(8,128)(2,1)} %bitcast.26, bf16[2,192,1536]{2,1,0:T(8,128)(2,1)} %bitcast.20, ...), custom_call_target="tpu_custom_call" | custom-call | flops 1000 | bytes 1000 | tf_op jit(solution)/shard_map/pallas_call | solution.py:142
  116.8 6.0 %collective-permute-start.16 = (bf16[2,192,768]{2,1,0:T(8,128)(2,1)}, bf16[2,192,768]{2,1,0:T(8,128)(2,1)}, u32[]{:S(2)}, u32[]{:S(2)}) collective-permute-start(bf16[2,192,768]{2,1,0:T(8,128)(2,1)} %get-tuple-element.72), channel_id=1, source_target_pairs={{32,64},{64,32},{33,65},{65,33},{34,66},{66,34},{35,67},{67,35},{3... | collective-permute-start | bytes 1769480 | tf_op jit(solution)/shard_map/ppermute | solution.py:325
  128.5 2.7 %collective-permute-done.15 = bf16[2,192,768]{2,1,0:T(8,128)(2,1)} collective-permute-done((bf16[2,192,768]{2,1,0:T(8,128)(2,1)}, bf16[2,192,768]{2,1,0:T(8,128)(2,1)}, u32[]{:S(2)}, u32[]{:S(2)}) %collective-permute-start.15) | collective-permute-done | bytes 589856 | tf_op jit(solution)/shard_map/ppermute | solution.py:324
  131.5 9.7 %collective-permute-done.16 = bf16[2,192,768]{2,1,0:T(8,128)(2,1)} collective-permute-done((bf16[2,192,768]{2,1,0:T(8,128)(2,1)}, bf16[2,192,768]{2,1,0:T(8,128)(2,1)}, u32[]{:S(2)}, u32[]{:S(2)}) %collective-permute-start.16) | collective-permute-done | bytes 589856 | tf_op jit(solution)/shard_map/ppermute | solution.py:325
  141.1 1.9 %add_convert_fusion = bf16[2,192,768]{2,1,0:T(8,128)(2,1)S(1)} fusion(bf16[2,192,768]{2,1,0:T(8,128)(2,1)} %collective-permute-done.17, bf16[2,192,768]{2,1,0:T(8,128)(2,1)} %collective-permute-done.16, bf16[2,192,768]{2,1,0:T(8,128)(2,1)} %collective-permute-done.15, bf16[2,192,768]{2,1,0:T(8,128)(2,1)} %get-tuple-element.70), kind=kLoop, calls=%fused_computation.1 | loop fusion | flops 2359296 | bytes 2949120 | tf_op jit(solution)/shard_map/convert_element_type | solution.py:358
  150.0 5.8 %collective-permute-done.10 = bf16[192,1536]{1,0:T(8,128)(2,1)S(1)} collective-permute-done((bf16[192,1536]{1,0:T(8,128)(2,1)}, bf16[192,1536]{1,0:T(8,128)(2,1)S(1)}, u32[]{:S(2)}, u32[]{:S(2)}) %collective-permute-start.10) | collective-permute-done | bytes 589856 | tf_op jit(solution)/shard_map/ppermute | solution.py:277
  (68 shorter events, 27.9 us)
Async XLA Ops:
  4.2 28.6 %all-to-all-start.1 = ((bf16[8,48,768]{2,1,0:T(8,128)(2,1)}), bf16[8,48,768]{2,1,0:T(8,128)(2,1)}, u32[]{:S(2)}, u32[]{:S(2)}) async-start(bf16[8,48,768]{2,1,0:T(8,128)(2,1)} %shard_map.85), calls=%async_computation.1 | async-start | bytes 1179648 | tf_op jit(solution)/shard_map/all_to_all | solution.py:281
  13.4 15.8 %collective-permute-start.5 = (bf16[192,1536]{1,0:T(8,128)(2,1)}, bf16[192,1536]{1,0:T(8,128)(2,1)S(1)}, u32[]{:S(2)}, u32[]{:S(2)}) collective-permute-start(bf16[192,1536]{1,0:T(8,128)(2,1)} %bitcast.6.refs_0_.refs_4_), channel_id=1, source_target_pairs={{0,3},{1,0},{2,1},{3,2},{4,7},{5,4},{6,5},{7,6},{8,11},{9,8},{10,9... | collective-permute-start | bytes 1769480 | tf_op jit(solution)/shard_map/ppermute | solution.py:277
  16.1 15.5 %collective-permute-start.4 = (bf16[192,1536]{1,0:T(8,128)(2,1)}, bf16[192,1536]{1,0:T(8,128)(2,1)}, u32[]{:S(2)}, u32[]{:S(2)}) collective-permute-start(bf16[192,1536]{1,0:T(8,128)(2,1)} %bitcast.6.refs_0_.refs_4_), channel_id=1, source_target_pairs={{0,2},{1,3},{2,0},{3,1},{4,6},{5,7},{6,4},{7,5},{8,10},{9,11},{10,... | collective-permute-start | bytes 1769480 | tf_op jit(solution)/shard_map/ppermute | solution.py:277
  16.5 29.4 %collective-permute-start.3 = (bf16[192,1536]{1,0:T(8,128)(2,1)}, bf16[192,1536]{1,0:T(8,128)(2,1)}, u32[]{:S(2)}, u32[]{:S(2)}) collective-permute-start(bf16[192,1536]{1,0:T(8,128)(2,1)} %bitcast.6.refs_0_.refs_4_), channel_id=1, source_target_pairs={{0,1},{1,2},{2,3},{3,0},{4,5},{5,6},{6,7},{7,4},{8,9},{9,10},{10,1... | collective-permute-start | bytes 1769480 | tf_op jit(solution)/shard_map/ppermute | solution.py:277
  17.2 39.2 %collective-permute-start.2 = (bf16[2,192,1536]{2,1,0:T(8,128)(2,1)S(1)}, bf16[2,192,1536]{2,1,0:T(8,128)(2,1)S(1)}, u32[]{:S(2)}, u32[]{:S(2)}) collective-permute-start(bf16[2,192,1536]{2,1,0:T(8,128)(2,1)S(1)} %bitcast.21), channel_id=1, source_target_pairs={{32,64},{64,32},{33,65},{65,33},{34,66},{66,34},{35,67},{67,35},{3... | collective-permute-start | bytes 3538952 | tf_op jit(solution)/shard_map/ppermute | solution.py:302
  23.5 32.9 %collective-permute-start.1 = (bf16[2,192,1536]{2,1,0:T(8,128)(2,1)S(1)}, bf16[2,192,1536]{2,1,0:T(8,128)(2,1)S(1)}, u32[]{:S(2)}, u32[]{:S(2)}) collective-permute-start(bf16[2,192,1536]{2,1,0:T(8,128)(2,1)S(1)} %bitcast.22), channel_id=1, source_target_pairs={{0,32},{32,0},{1,33},{33,1},{2,34},{34,2},{3,35},{35,3},{4,36},{36... | collective-permute-start | bytes 3538952 | tf_op jit(solution)/shard_map/ppermute | solution.py:303
  29.2 27.2 %collective-permute-start = (bf16[2,192,1536]{2,1,0:T(8,128)(2,1)S(1)}, bf16[2,192,1536]{2,1,0:T(8,128)(2,1)}, u32[]{:S(2)}, u32[]{:S(2)}) collective-permute-start(bf16[2,192,1536]{2,1,0:T(8,128)(2,1)S(1)} %bitcast.23), channel_id=1, source_target_pairs={{0,128},{128,0},{1,129},{129,1},{2,130},{130,2},{3,131},{131,3},{4... | collective-permute-start | bytes 3538952 | tf_op jit(solution)/shard_map/ppermute | solution.py:301
  32.9 13.2 %collective-permute-start.6 = (bf16[384,768]{1,0:T(8,128)(2,1)}, bf16[384,768]{1,0:T(8,128)(2,1)S(1)}, u32[]{:S(2)}, u32[]{:S(2)}) collective-permute-start(bf16[384,768]{1,0:T(8,128)(2,1)} %bitcast.7.refs_4_), channel_id=1, source_target_pairs={{0,32},{32,0},{1,33},{33,1},{2,34},{34,2},{3,35},{35,3},{4,36},{36... | collective-permute-start | bytes 1769480 | tf_op jit(solution)/shard_map/ppermute | solution.py:308
  51.8 16.4 %all-to-all-start.2 = ((bf16[4,384,256]{2,1,0:T(8,128)(2,1)}), bf16[4,384,256]{2,1,0:T(8,128)(2,1)}, u32[]{:S(2)}, u32[]{:S(2)}) async-start(bf16[4,384,256]{2,1,0:T(8,128)(2,1)} %get-tuple-element.42), calls=%async_computation.2 | async-start | bytes 1572864 | tf_op jit(solution)/shard_map/all_to_all | solution.py:281
  68.2 17.2 %all-to-all-start = ((bf16[4,384,256]{2,1,0:T(8,128)(2,1)}), bf16[4,384,256]{2,1,0:T(8,128)(2,1)S(1)}, u32[]{:S(2)}, u32[]{:S(2)}) async-start(bf16[4,384,256]{2,1,0:T(8,128)(2,1)} %bitcast.27), calls=%async_computation | async-start | bytes 1572864 | tf_op jit(solution)/shard_map/all_to_all | solution.py:281
  91.9 8.2 %collective-permute-start.7 = (bf16[384,768]{1,0:T(8,128)(2,1)}, bf16[384,768]{1,0:T(8,128)(2,1)S(1)}, u32[]{:S(2)}, u32[]{:S(2)}) collective-permute-start(bf16[384,768]{1,0:T(8,128)(2,1)} %get-tuple-element.48), channel_id=1, source_target_pairs={{0,32},{32,0},{1,33},{33,1},{2,34},{34,2},{3,35},{35,3},{4,36},{36... | collective-permute-start | bytes 1769480 | tf_op jit(solution)/shard_map/ppermute | solution.py:333
  94.0 28.8 %collective-permute-start.12 = (bf16[2,192,768]{2,1,0:T(8,128)(2,1)}, bf16[2,192,768]{2,1,0:T(8,128)(2,1)S(1)}, u32[]{:S(2)}, u32[]{:S(2)}) collective-permute-start(bf16[2,192,768]{2,1,0:T(8,128)(2,1)} %get-tuple-element.67), channel_id=1, source_target_pairs={{0,128},{128,0},{1,129},{129,1},{2,130},{130,2},{3,131},{131,3},{4... | collective-permute-start | bytes 1769480 | tf_op jit(solution)/shard_map/ppermute | solution.py:324
  101.1 27.3 %all-to-all-start.3 = ((bf16[8,48,768]{2,1,0:T(8,128)(2,1)}), bf16[8,48,768]{2,1,0:T(8,128)(2,1)S(1)}, u32[]{:S(2)}, u32[]{:S(2)}) async-start(bf16[8,48,768]{2,1,0:T(8,128)(2,1)} %bitcast.9), calls=%async_computation.3 | async-start | bytes 1179648 | tf_op jit(solution)/shard_map/all_to_all | solution.py:281
  108.0 16.7 %collective-permute-start.13 = (bf16[2,192,768]{2,1,0:T(8,128)(2,1)S(1)}, bf16[2,192,768]{2,1,0:T(8,128)(2,1)}, u32[]{:S(2)}, u32[]{:S(2)}) collective-permute-start(bf16[2,192,768]{2,1,0:T(8,128)(2,1)S(1)} %copy-done.11), channel_id=1, source_target_pairs={{32,64},{64,32},{33,65},{65,33},{34,66},{66,34},{35,67},{67,35},{3... | collective-permute-start | bytes 1769480 | tf_op jit(solution)/shard_map/ppermute | solution.py:325
  110.0 16.2 %collective-permute-start.14 = (bf16[2,192,768]{2,1,0:T(8,128)(2,1)S(1)}, bf16[2,192,768]{2,1,0:T(8,128)(2,1)}, u32[]{:S(2)}, u32[]{:S(2)}) collective-permute-start(bf16[2,192,768]{2,1,0:T(8,128)(2,1)S(1)} %copy-done.10), channel_id=1, source_target_pairs={{0,32},{32,0},{1,33},{33,1},{2,34},{34,2},{3,35},{35,3},{4,36},{36... | collective-permute-start | bytes 1769480 | tf_op jit(solution)/shard_map/ppermute | solution.py:326
  116.4 14.8 %collective-permute-start.15 = (bf16[2,192,768]{2,1,0:T(8,128)(2,1)}, bf16[2,192,768]{2,1,0:T(8,128)(2,1)}, u32[]{:S(2)}, u32[]{:S(2)}) collective-permute-start(bf16[2,192,768]{2,1,0:T(8,128)(2,1)} %get-tuple-element.71), channel_id=1, source_target_pairs={{0,128},{128,0},{1,129},{129,1},{2,130},{130,2},{3,131},{131,3},{4... | collective-permute-start | bytes 1769480 | tf_op jit(solution)/shard_map/ppermute | solution.py:324
  116.8 24.3 %collective-permute-start.16 = (bf16[2,192,768]{2,1,0:T(8,128)(2,1)}, bf16[2,192,768]{2,1,0:T(8,128)(2,1)}, u32[]{:S(2)}, u32[]{:S(2)}) collective-permute-start(bf16[2,192,768]{2,1,0:T(8,128)(2,1)} %get-tuple-element.72), channel_id=1, source_target_pairs={{32,64},{64,32},{33,65},{65,33},{34,66},{66,34},{35,67},{67,35},{3... | collective-permute-start | bytes 1769480 | tf_op jit(solution)/shard_map/ppermute | solution.py:325
  122.8 18.3 %collective-permute-start.17 = (bf16[2,192,768]{2,1,0:T(8,128)(2,1)}, bf16[2,192,768]{2,1,0:T(8,128)(2,1)}, u32[]{:S(2)}, u32[]{:S(2)}) collective-permute-start(bf16[2,192,768]{2,1,0:T(8,128)(2,1)} %get-tuple-element.73), channel_id=1, source_target_pairs={{0,32},{32,0},{1,33},{33,1},{2,34},{34,2},{3,35},{35,3},{4,36},{36... | collective-permute-start | bytes 1769480 | tf_op jit(solution)/shard_map/ppermute | solution.py:326
  124.7 25.2 %collective-permute-start.8 = (bf16[192,1536]{1,0:T(8,128)(2,1)}, bf16[192,1536]{1,0:T(8,128)(2,1)S(1)}, u32[]{:S(2)}, u32[]{:S(2)}) collective-permute-start(bf16[192,1536]{1,0:T(8,128)(2,1)} %get-tuple-element.56), channel_id=1, source_target_pairs={{0,3},{1,0},{2,1},{3,2},{4,7},{5,4},{6,5},{7,6},{8,11},{9,8},{10,9... | collective-permute-start | bytes 1769480 | tf_op jit(solution)/shard_map/ppermute | solution.py:277
  126.2 23.8 %collective-permute-start.9 = (bf16[192,1536]{1,0:T(8,128)(2,1)}, bf16[192,1536]{1,0:T(8,128)(2,1)S(1)}, u32[]{:S(2)}, u32[]{:S(2)}) collective-permute-start(bf16[192,1536]{1,0:T(8,128)(2,1)} %get-tuple-element.57), channel_id=1, source_target_pairs={{0,2},{1,3},{2,0},{3,1},{4,6},{5,7},{6,4},{7,5},{8,10},{9,11},{10,... | collective-permute-start | bytes 1769480 | tf_op jit(solution)/shard_map/ppermute | solution.py:277
  131.2 24.6 %collective-permute-start.10 = (bf16[192,1536]{1,0:T(8,128)(2,1)}, bf16[192,1536]{1,0:T(8,128)(2,1)S(1)}, u32[]{:S(2)}, u32[]{:S(2)}) collective-permute-start(bf16[192,1536]{1,0:T(8,128)(2,1)} %get-tuple-element.58), channel_id=1, source_target_pairs={{0,1},{1,2},{2,3},{3,0},{4,5},{5,6},{6,7},{7,4},{8,9},{9,10},{10,1... | collective-permute-start | bytes 1769480 | tf_op jit(solution)/shard_map/ppermute | solution.py:277
  141.1 4.7 %collective-permute-start.19 = (bf16[48,768]{1,0:T(8,128)(2,1)S(1)}, bf16[48,768]{1,0:T(8,128)(2,1)S(1)}, u32[]{:S(2)}, u32[]{:S(2)}) collective-permute-start(bf16[48,768]{1,0:T(8,128)(2,1)S(1)} %reduce_sum.12), channel_id=1, source_target_pairs={{0,192},{64,128},{128,64},{192,0},{1,193},{65,129},{129,65},{193,1... | collective-permute-start | bytes 221192 | tf_op jit(solution)/shard_map/ppermute | solution.py:347
  143.0 4.8 %collective-permute-start.18 = (bf16[48,768]{1,0:T(8,128)(2,1)S(1)}, bf16[48,768]{1,0:T(8,128)(2,1)S(1)}, u32[]{:S(2)}, u32[]{:S(2)}) collective-permute-start(bf16[48,768]{1,0:T(8,128)(2,1)S(1)} %reduce_sum.12), channel_id=1, source_target_pairs={{0,64},{64,0},{1,65},{65,1},{2,66},{66,2},{3,67},{67,3},{4,68},{68... | collective-permute-start | bytes 221192 | tf_op jit(solution)/shard_map/ppermute | solution.py:346
  149.4 7.5 %collective-permute-start.20 = (f32[48,768]{1,0:T(8,128)S(1)}, f32[48,768]{1,0:T(8,128)S(1)}, u32[]{:S(2)}, u32[]{:S(2)}) collective-permute-start(f32[48,768]{1,0:T(8,128)S(1)} %add_add_fusion), channel_id=1, source_target_pairs={{0,32},{32,0},{1,33},{33,1},{2,34},{34,2},{3,35},{35,3},{4,36},{36... | collective-permute-start | bytes 442376 | tf_op jit(solution)/shard_map/ppermute | solution.py:349
  (13 other events, 84.0 us)
